TPU v7x, 512 devices: a whole 4x8x8 slice. The times are simulated.
512 devices in a mesh: dp: 64 (over y, z_hi, core), narrow: 8 (over x, z_lo).
Axes of the slice: x: 4, y: 8, z: 8 (z_hi: 4, z_lo: 2; z = z_hi * 2 + z_lo), core: 2. Of those that a mesh axis runs over, the one named last changes fastest.
Arguments:
- image_emb: bfloat16 [16384, 1152], P('dp'), may hold values from -0.1796875 to 0.1796875
- text_emb: bfloat16 [16384, 1152], P(('dp', 'narrow')), may hold values from -0.1796875 to 0.1796875
- positive: int32 [16384], P(('dp', 'narrow')), may hold values from 0 to 16383, as said below
- log_scale: float32 [1], replicated, may hold values from 2.3 to 3.4
- bias: float32 [1], replicated, may hold values from -4 to -2
Outputs:
- grad_image: bfloat16 [16384, 1152], P('dp')
- grad_text: bfloat16 [16384, 1152], P(('dp', 'narrow'))
Inputs may be any that keep to these rules, and one draw needn't show every extreme that they name: `positive`: each image is paired with exactly one text: the b-th block of 256 texts names every image of the b-th block of 256 images once.
All inputs are finite; a program needn't handle non-finite values.
Results may differ from a plain program's by a relative error of at most 0.0066.
Values may be sent and summed in bfloat16 or wider, within the bound.
No kernel may reach another device: no remote copies, remote signals or barrier semaphores. Data moves between devices by JAX's collectives and lax.ppermute only.
A program may use at most 64 MiB of HBM per device.

v0:
```python
import jax
import jax.numpy as jnp
from jax import lax
from jax.sharding import PartitionSpec as P

epsilon = 1e-06


def as_sent(shard):

    def short(part):
        return part.astype(jnp.bfloat16) if part.dtype == jnp.float32 else part

    return jax.tree.map(short, shard)


def passed_along(block, axis, distance):
    devices = range(lax.axis_size(axis))
    route = [((i - distance) % len(devices), i) for i in devices]
    return lax.ppermute(block, axis, route)


def unit_rows(values):
    as_float = values.astype(jnp.float32)
    row_norm = jnp.sqrt(jnp.sum(as_float * as_float, axis=1, keepdims=True) + epsilon)
    return (as_float / row_norm, row_norm)


def walk(image_bf, streams, cycle_size, logit_scale, offset):

    def visit(step_index, carried_streams):
        at_home = (step_index == 0).astype(jnp.float32)
        updated = []
        for carried, stream in zip(carried_streams, streams):
            visitor, accumulator, grad_tiles, text_store = carried
            home_mask = stream[1]
            half_rows = visitor.shape[0]
            cosine = lax.dot_general(
                image_bf, visitor, (((1,), (1,)), ((), ())), preferred_element_type=jnp.float32
            )
            logits = logit_scale * cosine + offset
            live_hits = home_mask * at_home
            pair_grad = jax.nn.sigmoid(logits) - live_hits
            grad_bf = pair_grad.astype(jnp.bfloat16)
            accumulator = accumulator + lax.dot_general(
                grad_bf, image_bf, (((0,), (0,)), ((), ())), preferred_element_type=jnp.float32
            )
            grad_tiles = lax.dynamic_update_slice(
                grad_tiles, grad_bf, (jnp.int32(0), (step_index * half_rows).astype(jnp.int32))
            )
            text_store = lax.dynamic_update_slice(
                text_store, visitor, ((step_index * half_rows).astype(jnp.int32), jnp.int32(0))
            )
            updated.append((visitor, accumulator, grad_tiles, text_store))
        return tuple(updated)

    def turn(step_index, carried):
        visited = visit(step_index, carried)
        return tuple(
            (
                (stream[2](entry[0]), stream[3](entry[1]), entry[2], entry[3])
                for entry, stream in zip(visited, streams)
            )
        )

    image_rows = image_bf.shape[0]
    feature_width = image_bf.shape[1]
    begin = tuple(
        (
            (
                stream[0],
                jnp.zeros((stream[0].shape[0], feature_width), jnp.float32),
                jnp.zeros((image_rows, cycle_size * stream[0].shape[0]), jnp.bfloat16),
                jnp.zeros((cycle_size * stream[0].shape[0], feature_width), jnp.bfloat16),
            )
            for stream in streams
        )
    )
    streams_now = lax.fori_loop(0, cycle_size - 1, turn, begin)
    visited = visit(jnp.int32(cycle_size - 1), streams_now)
    accumulators = [stream[3](entry[1]) for entry, stream in zip(visited, streams)]
    partial_value = jnp.zeros((image_rows, feature_width), jnp.float32)
    for entry in visited:
        partial_value = partial_value + jnp.dot(
            entry[2], entry[3], preferred_element_type=jnp.float32
        )
    return (partial_value, jnp.concatenate(accumulators, axis=0))


def local(image_emb, text_emb, positive, log_scale, bias):
    logit_scale = jnp.exp(log_scale[0])
    offset = bias[0]
    image_unit, image_norm = unit_rows(image_emb)
    text_unit, text_norm = unit_rows(text_emb)
    image_bf = image_unit.astype(jnp.bfloat16)
    text_bf = text_unit.astype(jnp.bfloat16)
    image_rows = image_emb.shape[0]
    cycle_size = lax.axis_size("dp")
    home_index = lax.axis_index("dp")
    local_pos = positive - home_index * image_rows
    positive_mask = (jnp.arange(image_rows, dtype=jnp.int32)[:, None] == local_pos[None, :]).astype(
        jnp.float32
    )

    def cycle_text(block):
        return jax.tree.map(
            lambda part, own: part.astype(own.dtype), passed_along(as_sent(block), "dp", 1), block
        )

    def cycle_accum(block):
        return passed_along(block, "dp", 1)

    streams = [(text_bf, positive_mask, cycle_text, cycle_accum)]
    partial_value, text_accum = walk(image_bf, streams, cycle_size, logit_scale, offset)
    grad_unit_text = logit_scale * text_accum
    grad_text = (
        grad_unit_text - text_unit * jnp.sum(text_unit * grad_unit_text, axis=1, keepdims=True)
    ) / text_norm
    grad_unit_image = logit_scale * lax.psum(partial_value, "narrow")
    grad_image = (
        (
            grad_unit_image
            - image_unit * jnp.sum(image_unit * grad_unit_image, axis=1, keepdims=True)
        )
        / image_norm
    ).astype(jnp.bfloat16)
    return (grad_image, grad_text.astype(jnp.bfloat16))


def solution(mesh):
    in_specs = (P("dp", None), P(("dp", "narrow"), None), P(("dp", "narrow")), P(), P())
    out_specs = (P("dp", None), P(("dp", "narrow"), None))
    return jax.shard_map(local, mesh=mesh, in_specs=in_specs, out_specs=out_specs, check_vma=False)
```

profile of v0, /device:TPU:56, one launch (start us, length us, event | category | flops | bytes accessed | tf_op | source)
XLA Modules:
  0.0 1012.3 jit_solution(11227392573247436885)
XLA Ops:
  14.0 881.7 %while.20 = (s32[]{:T(128)}, bf16[32,1152]{1,0:T(8,128)(2,1)S(1)}, f32[32,1152]{1,0:T(8,128)S(1)}, bf16[256,2048]{0,1:T(8,128)(2,1)S(1)}, bf16[2048,1152]{1,0:T(...) while((s32[]{:T(128)}, bf16[32,1152]{1,0:T(8,128)(2,1)S(1)}, ...), condition=%wide.region_3.0_spmd.clone, body=%wide.region_2.0_spmd.clone.sunk | while | flops 37859336 | bytes 2777885 | solution.py:79
  17.1 6.2 collective-permute-start.1
  28.0 4.7 collective-permute-done.1
  83.8 5.1 collective-permute-done.1
  125.9 5.1 collective-permute-done.1
  250.7 4.8 collective-permute-done.1
  264.4 5.1 collective-permute-done.1
  278.6 4.9 collective-permute-done.1
  292.6 4.8 collective-permute-done.1
  320.1 4.9 collective-permute-done.1
  334.1 4.9 collective-permute-done.1
  348.0 4.9 collective-permute-done.1
  361.9 4.9 collective-permute-done.1
  375.8 4.9 collective-permute-done.1
  389.7 4.9 collective-permute-done.1
  403.7 5.0 collective-permute-done.1
  417.9 4.9 collective-permute-done.1
  432.0 4.8 collective-permute-done.1
  446.0 4.7 collective-permute-done.1
  459.9 4.9 collective-permute-done.1
  501.4 4.8 collective-permute-done.1
  515.2 4.8 collective-permute-done.1
  529.0 4.8 collective-permute-done.1
  542.8 4.8 collective-permute-done.1
  556.6 4.9 collective-permute-done.1
  570.6 4.8 collective-permute-done.1
  584.3 4.9 collective-permute-done.1
  598.3 4.9 collective-permute-done.1
  612.3 5.0 collective-permute-done.1
  626.5 4.9 collective-permute-done.1
  640.6 4.8 collective-permute-done.1
  668.4 4.9 collective-permute-done.1
  696.1 4.7 collective-permute-done.1
  709.8 5.0 collective-permute-done.1
  723.9 4.9 collective-permute-done.1
  765.4 4.8 collective-permute-done.1
  779.1 5.0 collective-permute-done.1
  793.2 4.8 collective-permute-done.1
  807.0 4.9 collective-permute-done.1
  820.9 5.0 collective-permute-done.1
  835.0 4.9 collective-permute-done.1
  849.0 4.9 collective-permute-done.1
  863.0 4.9 collective-permute-done.1
  876.9 4.8 collective-permute-done.1
  890.8 4.9 collective-permute-done.1
  896.7 5.0 fusion.19
  903.8 8.7 collective-permute-done.2
  913.4 89.2 %all-reduce.2.cloned.1.call-done = f32[256,1152]{1,0:T(8,128)} async-done(((f32[256,1152]{1,0:T(8,128)}), f32[256,1152]{1,0:T(8,128)}) %all-reduce.2.cloned.1.call-update) | async-done | bytes 1179664 | tf_op jit(solution)/shard_map/psum | solution.py:119
  (488 shorter events, 675.2 us)
Async XLA Ops:
  7.2 995.4 %all-reduce.2.cloned.1.call-start = ((), (), s32[]{:S(2)}) async-start(), calls=%async_computation | async-start | bytes 2359296 | tf_op jit(solution)/shard_map/psum | solution.py:119
  14.0 14.0 %collective-permute-start = (bf16[32,1152]{1,0:T(8,128)(2,1)S(1)}, bf16[32,1152]{1,0:T(8,128)(2,1)S(1)}, u32[]{:S(2)}, u32[]{:S(2)}) collective-permute-start(bf16[32,1152]{1,0:T(8,128)(2,1)S(1)} %copy.15), channel_id=1, source_target_pairs={{504,0},{0,8},{8,16},{16,24},{24,32},{32,40},{40,48},{48,56},{56,6... | collective-permute-start | bytes 221192 | tf_op jit(solution)/shard_map/while/body/eval_jaxpr/ppermute | solution.py:20
  17.1 15.6 %collective-permute-start.1 = (f32[32,1152]{1,0:T(8,128)S(1)}, f32[32,1152]{1,0:T(8,128)S(1)}, u32[]{:S(2)}, u32[]{:S(2)}) collective-permute-start(f32[32,1152]{1,0:T(8,128)S(1)} %convolution_add_fusion.3), channel_id=1, source_target_pairs={{504,0},{0,8},{8,16},{16,24},{24,32},{32,40},{40,48},{48,56},{56,6... | collective-permute-start | bytes 442376 | tf_op jit(solution)/shard_map/while/body/eval_jaxpr/ppermute | solution.py:20
  35.8 11.0 %collective-permute-start.1 = (f32[32,1152]{1,0:T(8,128)S(1)}, f32[32,1152]{1,0:T(8,128)S(1)}, u32[]{:S(2)}, u32[]{:S(2)}) collective-permute-start(f32[32,1152]{1,0:T(8,128)S(1)} %convolution_add_fusion.3), channel_id=1, source_target_pairs={{504,0},{0,8},{8,16},{16,24},{24,32},{32,40},{40,48},{48,56},{56,6... | collective-permute-start | bytes 442376 | tf_op jit(solution)/shard_map/while/body/eval_jaxpr/ppermute | solution.py:20
  49.9 10.9 %collective-permute-start.1 = (f32[32,1152]{1,0:T(8,128)S(1)}, f32[32,1152]{1,0:T(8,128)S(1)}, u32[]{:S(2)}, u32[]{:S(2)}) collective-permute-start(f32[32,1152]{1,0:T(8,128)S(1)} %convolution_add_fusion.3), channel_id=1, source_target_pairs={{504,0},{0,8},{8,16},{16,24},{24,32},{32,40},{40,48},{48,56},{56,6... | collective-permute-start | bytes 442376 | tf_op jit(solution)/shard_map/while/body/eval_jaxpr/ppermute | solution.py:20
  63.9 10.8 %collective-permute-start.1 = (f32[32,1152]{1,0:T(8,128)S(1)}, f32[32,1152]{1,0:T(8,128)S(1)}, u32[]{:S(2)}, u32[]{:S(2)}) collective-permute-start(f32[32,1152]{1,0:T(8,128)S(1)} %convolution_add_fusion.3), channel_id=1, source_target_pairs={{504,0},{0,8},{8,16},{16,24},{24,32},{32,40},{40,48},{48,56},{56,6... | collective-permute-start | bytes 442376 | tf_op jit(solution)/shard_map/while/body/eval_jaxpr/ppermute | solution.py:20
  77.8 11.2 %collective-permute-start.1 = (f32[32,1152]{1,0:T(8,128)S(1)}, f32[32,1152]{1,0:T(8,128)S(1)}, u32[]{:S(2)}, u32[]{:S(2)}) collective-permute-start(f32[32,1152]{1,0:T(8,128)S(1)} %convolution_add_fusion.3), channel_id=1, source_target_pairs={{504,0},{0,8},{8,16},{16,24},{24,32},{32,40},{40,48},{48,56},{56,6... | collective-permute-start | bytes 442376 | tf_op jit(solution)/shard_map/while/body/eval_jaxpr/ppermute | solution.py:20
  92.1 10.9 %collective-permute-start.1 = (f32[32,1152]{1,0:T(8,128)S(1)}, f32[32,1152]{1,0:T(8,128)S(1)}, u32[]{:S(2)}, u32[]{:S(2)}) collective-permute-start(f32[32,1152]{1,0:T(8,128)S(1)} %convolution_add_fusion.3), channel_id=1, source_target_pairs={{504,0},{0,8},{8,16},{16,24},{24,32},{32,40},{40,48},{48,56},{56,6... | collective-permute-start | bytes 442376 | tf_op jit(solution)/shard_map/while/body/eval_jaxpr/ppermute | solution.py:20
  106.1 10.7 %collective-permute-start.1 = (f32[32,1152]{1,0:T(8,128)S(1)}, f32[32,1152]{1,0:T(8,128)S(1)}, u32[]{:S(2)}, u32[]{:S(2)}) collective-permute-start(f32[32,1152]{1,0:T(8,128)S(1)} %convolution_add_fusion.3), channel_id=1, source_target_pairs={{504,0},{0,8},{8,16},{16,24},{24,32},{32,40},{40,48},{48,56},{56,6... | collective-permute-start | bytes 442376 | tf_op jit(solution)/shard_map/while/body/eval_jaxpr/ppermute | solution.py:20
  119.9 11.1 %collective-permute-start.1 = (f32[32,1152]{1,0:T(8,128)S(1)}, f32[32,1152]{1,0:T(8,128)S(1)}, u32[]{:S(2)}, u32[]{:S(2)}) collective-permute-start(f32[32,1152]{1,0:T(8,128)S(1)} %convolution_add_fusion.3), channel_id=1, source_target_pairs={{504,0},{0,8},{8,16},{16,24},{24,32},{32,40},{40,48},{48,56},{56,6... | collective-permute-start | bytes 442376 | tf_op jit(solution)/shard_map/while/body/eval_jaxpr/ppermute | solution.py:20
  134.2 11.0 %collective-permute-start.1 = (f32[32,1152]{1,0:T(8,128)S(1)}, f32[32,1152]{1,0:T(8,128)S(1)}, u32[]{:S(2)}, u32[]{:S(2)}) collective-permute-start(f32[32,1152]{1,0:T(8,128)S(1)} %convolution_add_fusion.3), channel_id=1, source_target_pairs={{504,0},{0,8},{8,16},{16,24},{24,32},{32,40},{40,48},{48,56},{56,6... | collective-permute-start | bytes 442376 | tf_op jit(solution)/shard_map/while/body/eval_jaxpr/ppermute | solution.py:20
  148.2 10.9 %collective-permute-start.1 = (f32[32,1152]{1,0:T(8,128)S(1)}, f32[32,1152]{1,0:T(8,128)S(1)}, u32[]{:S(2)}, u32[]{:S(2)}) collective-permute-start(f32[32,1152]{1,0:T(8,128)S(1)} %convolution_add_fusion.3), channel_id=1, source_target_pairs={{504,0},{0,8},{8,16},{16,24},{24,32},{32,40},{40,48},{48,56},{56,6... | collective-permute-start | bytes 442376 | tf_op jit(solution)/shard_map/while/body/eval_jaxpr/ppermute | solution.py:20
  162.3 10.8 %collective-permute-start.1 = (f32[32,1152]{1,0:T(8,128)S(1)}, f32[32,1152]{1,0:T(8,128)S(1)}, u32[]{:S(2)}, u32[]{:S(2)}) collective-permute-start(f32[32,1152]{1,0:T(8,128)S(1)} %convolution_add_fusion.3), channel_id=1, source_target_pairs={{504,0},{0,8},{8,16},{16,24},{24,32},{32,40},{40,48},{48,56},{56,6... | collective-permute-start | bytes 442376 | tf_op jit(solution)/shard_map/while/body/eval_jaxpr/ppermute | solution.py:20
  176.2 10.7 %collective-permute-start.1 = (f32[32,1152]{1,0:T(8,128)S(1)}, f32[32,1152]{1,0:T(8,128)S(1)}, u32[]{:S(2)}, u32[]{:S(2)}) collective-permute-start(f32[32,1152]{1,0:T(8,128)S(1)} %convolution_add_fusion.3), channel_id=1, source_target_pairs={{504,0},{0,8},{8,16},{16,24},{24,32},{32,40},{40,48},{48,56},{56,6... | collective-permute-start | bytes 442376 | tf_op jit(solution)/shard_map/while/body/eval_jaxpr/ppermute | solution.py:20
  258.6 10.9 %collective-permute-start.1 = (f32[32,1152]{1,0:T(8,128)S(1)}, f32[32,1152]{1,0:T(8,128)S(1)}, u32[]{:S(2)}, u32[]{:S(2)}) collective-permute-start(f32[32,1152]{1,0:T(8,128)S(1)} %convolution_add_fusion.3), channel_id=1, source_target_pairs={{504,0},{0,8},{8,16},{16,24},{24,32},{32,40},{40,48},{48,56},{56,6... | collective-permute-start | bytes 442376 | tf_op jit(solution)/shard_map/while/body/eval_jaxpr/ppermute | solution.py:20
  272.6 10.9 %collective-permute-start.1 = (f32[32,1152]{1,0:T(8,128)S(1)}, f32[32,1152]{1,0:T(8,128)S(1)}, u32[]{:S(2)}, u32[]{:S(2)}) collective-permute-start(f32[32,1152]{1,0:T(8,128)S(1)} %convolution_add_fusion.3), channel_id=1, source_target_pairs={{504,0},{0,8},{8,16},{16,24},{24,32},{32,40},{40,48},{48,56},{56,6... | collective-permute-start | bytes 442376 | tf_op jit(solution)/shard_map/while/body/eval_jaxpr/ppermute | solution.py:20
  286.6 10.8 %collective-permute-start.1 = (f32[32,1152]{1,0:T(8,128)S(1)}, f32[32,1152]{1,0:T(8,128)S(1)}, u32[]{:S(2)}, u32[]{:S(2)}) collective-permute-start(f32[32,1152]{1,0:T(8,128)S(1)} %convolution_add_fusion.3), channel_id=1, source_target_pairs={{504,0},{0,8},{8,16},{16,24},{24,32},{32,40},{40,48},{48,56},{56,6... | collective-permute-start | bytes 442376 | tf_op jit(solution)/shard_map/while/body/eval_jaxpr/ppermute | solution.py:20
  314.2 10.8 %collective-permute-start.1 = (f32[32,1152]{1,0:T(8,128)S(1)}, f32[32,1152]{1,0:T(8,128)S(1)}, u32[]{:S(2)}, u32[]{:S(2)}) collective-permute-start(f32[32,1152]{1,0:T(8,128)S(1)} %convolution_add_fusion.3), channel_id=1, source_target_pairs={{504,0},{0,8},{8,16},{16,24},{24,32},{32,40},{40,48},{48,56},{56,6... | collective-permute-start | bytes 442376 | tf_op jit(solution)/shard_map/while/body/eval_jaxpr/ppermute | solution.py:20
  328.2 10.8 %collective-permute-start.1 = (f32[32,1152]{1,0:T(8,128)S(1)}, f32[32,1152]{1,0:T(8,128)S(1)}, u32[]{:S(2)}, u32[]{:S(2)}) collective-permute-start(f32[32,1152]{1,0:T(8,128)S(1)} %convolution_add_fusion.3), channel_id=1, source_target_pairs={{504,0},{0,8},{8,16},{16,24},{24,32},{32,40},{40,48},{48,56},{56,6... | collective-permute-start | bytes 442376 | tf_op jit(solution)/shard_map/while/body/eval_jaxpr/ppermute | solution.py:20
  342.1 10.8 %collective-permute-start.1 = (f32[32,1152]{1,0:T(8,128)S(1)}, f32[32,1152]{1,0:T(8,128)S(1)}, u32[]{:S(2)}, u32[]{:S(2)}) collective-permute-start(f32[32,1152]{1,0:T(8,128)S(1)} %convolution_add_fusion.3), channel_id=1, source_target_pairs={{504,0},{0,8},{8,16},{16,24},{24,32},{32,40},{40,48},{48,56},{56,6... | collective-permute-start | bytes 442376 | tf_op jit(solution)/shard_map/while/body/eval_jaxpr/ppermute | solution.py:20
  356.0 10.8 %collective-permute-start.1 = (f32[32,1152]{1,0:T(8,128)S(1)}, f32[32,1152]{1,0:T(8,128)S(1)}, u32[]{:S(2)}, u32[]{:S(2)}) collective-permute-start(f32[32,1152]{1,0:T(8,128)S(1)} %convolution_add_fusion.3), channel_id=1, source_target_pairs={{504,0},{0,8},{8,16},{16,24},{24,32},{32,40},{40,48},{48,56},{56,6... | collective-permute-start | bytes 442376 | tf_op jit(solution)/shard_map/while/body/eval_jaxpr/ppermute | solution.py:20
  369.9 10.8 %collective-permute-start.1 = (f32[32,1152]{1,0:T(8,128)S(1)}, f32[32,1152]{1,0:T(8,128)S(1)}, u32[]{:S(2)}, u32[]{:S(2)}) collective-permute-start(f32[32,1152]{1,0:T(8,128)S(1)} %convolution_add_fusion.3), channel_id=1, source_target_pairs={{504,0},{0,8},{8,16},{16,24},{24,32},{32,40},{40,48},{48,56},{56,6... | collective-permute-start | bytes 442376 | tf_op jit(solution)/shard_map/while/body/eval_jaxpr/ppermute | solution.py:20
  383.8 10.8 %collective-permute-start.1 = (f32[32,1152]{1,0:T(8,128)S(1)}, f32[32,1152]{1,0:T(8,128)S(1)}, u32[]{:S(2)}, u32[]{:S(2)}) collective-permute-start(f32[32,1152]{1,0:T(8,128)S(1)} %convolution_add_fusion.3), channel_id=1, source_target_pairs={{504,0},{0,8},{8,16},{16,24},{24,32},{32,40},{40,48},{48,56},{56,6... | collective-permute-start | bytes 442376 | tf_op jit(solution)/shard_map/while/body/eval_jaxpr/ppermute | solution.py:20
  397.8 11.0 %collective-permute-start.1 = (f32[32,1152]{1,0:T(8,128)S(1)}, f32[32,1152]{1,0:T(8,128)S(1)}, u32[]{:S(2)}, u32[]{:S(2)}) collective-permute-start(f32[32,1152]{1,0:T(8,128)S(1)} %convolution_add_fusion.3), channel_id=1, source_target_pairs={{504,0},{0,8},{8,16},{16,24},{24,32},{32,40},{40,48},{48,56},{56,6... | collective-permute-start | bytes 442376 | tf_op jit(solution)/shard_map/while/body/eval_jaxpr/ppermute | solution.py:20
  411.8 11.0 %collective-permute-start.1 = (f32[32,1152]{1,0:T(8,128)S(1)}, f32[32,1152]{1,0:T(8,128)S(1)}, u32[]{:S(2)}, u32[]{:S(2)}) collective-permute-start(f32[32,1152]{1,0:T(8,128)S(1)} %convolution_add_fusion.3), channel_id=1, source_target_pairs={{504,0},{0,8},{8,16},{16,24},{24,32},{32,40},{40,48},{48,56},{56,6... | collective-permute-start | bytes 442376 | tf_op jit(solution)/shard_map/while/body/eval_jaxpr/ppermute | solution.py:20
  425.9 10.9 %collective-permute-start.1 = (f32[32,1152]{1,0:T(8,128)S(1)}, f32[32,1152]{1,0:T(8,128)S(1)}, u32[]{:S(2)}, u32[]{:S(2)}) collective-permute-start(f32[32,1152]{1,0:T(8,128)S(1)} %convolution_add_fusion.3), channel_id=1, source_target_pairs={{504,0},{0,8},{8,16},{16,24},{24,32},{32,40},{40,48},{48,56},{56,6... | collective-permute-start | bytes 442376 | tf_op jit(solution)/shard_map/while/body/eval_jaxpr/ppermute | solution.py:20
  440.0 10.8 %collective-permute-start.1 = (f32[32,1152]{1,0:T(8,128)S(1)}, f32[32,1152]{1,0:T(8,128)S(1)}, u32[]{:S(2)}, u32[]{:S(2)}) collective-permute-start(f32[32,1152]{1,0:T(8,128)S(1)} %convolution_add_fusion.3), channel_id=1, source_target_pairs={{504,0},{0,8},{8,16},{16,24},{24,32},{32,40},{40,48},{48,56},{56,6... | collective-permute-start | bytes 442376 | tf_op jit(solution)/shard_map/while/body/eval_jaxpr/ppermute | solution.py:20
  453.9 10.9 %collective-permute-start.1 = (f32[32,1152]{1,0:T(8,128)S(1)}, f32[32,1152]{1,0:T(8,128)S(1)}, u32[]{:S(2)}, u32[]{:S(2)}) collective-permute-start(f32[32,1152]{1,0:T(8,128)S(1)} %convolution_add_fusion.3), channel_id=1, source_target_pairs={{504,0},{0,8},{8,16},{16,24},{24,32},{32,40},{40,48},{48,56},{56,6... | collective-permute-start | bytes 442376 | tf_op jit(solution)/shard_map/while/body/eval_jaxpr/ppermute | solution.py:20
  467.9 10.7 %collective-permute-start.1 = (f32[32,1152]{1,0:T(8,128)S(1)}, f32[32,1152]{1,0:T(8,128)S(1)}, u32[]{:S(2)}, u32[]{:S(2)}) collective-permute-start(f32[32,1152]{1,0:T(8,128)S(1)} %convolution_add_fusion.3), channel_id=1, source_target_pairs={{504,0},{0,8},{8,16},{16,24},{24,32},{32,40},{40,48},{48,56},{56,6... | collective-permute-start | bytes 442376 | tf_op jit(solution)/shard_map/while/body/eval_jaxpr/ppermute | solution.py:20
  495.5 10.7 %collective-permute-start.1 = (f32[32,1152]{1,0:T(8,128)S(1)}, f32[32,1152]{1,0:T(8,128)S(1)}, u32[]{:S(2)}, u32[]{:S(2)}) collective-permute-start(f32[32,1152]{1,0:T(8,128)S(1)} %convolution_add_fusion.3), channel_id=1, source_target_pairs={{504,0},{0,8},{8,16},{16,24},{24,32},{32,40},{40,48},{48,56},{56,6... | collective-permute-start | bytes 442376 | tf_op jit(solution)/shard_map/while/body/eval_jaxpr/ppermute | solution.py:20
  550.8 10.8 %collective-permute-start.1 = (f32[32,1152]{1,0:T(8,128)S(1)}, f32[32,1152]{1,0:T(8,128)S(1)}, u32[]{:S(2)}, u32[]{:S(2)}) collective-permute-start(f32[32,1152]{1,0:T(8,128)S(1)} %convolution_add_fusion.3), channel_id=1, source_target_pairs={{504,0},{0,8},{8,16},{16,24},{24,32},{32,40},{40,48},{48,56},{56,6... | collective-permute-start | bytes 442376 | tf_op jit(solution)/shard_map/while/body/eval_jaxpr/ppermute | solution.py:20
  578.5 10.8 %collective-permute-start.1 = (f32[32,1152]{1,0:T(8,128)S(1)}, f32[32,1152]{1,0:T(8,128)S(1)}, u32[]{:S(2)}, u32[]{:S(2)}) collective-permute-start(f32[32,1152]{1,0:T(8,128)S(1)} %convolution_add_fusion.3), channel_id=1, source_target_pairs={{504,0},{0,8},{8,16},{16,24},{24,32},{32,40},{40,48},{48,56},{56,6... | collective-permute-start | bytes 442376 | tf_op jit(solution)/shard_map/while/body/eval_jaxpr/ppermute | solution.py:20
  592.4 10.8 %collective-permute-start.1 = (f32[32,1152]{1,0:T(8,128)S(1)}, f32[32,1152]{1,0:T(8,128)S(1)}, u32[]{:S(2)}, u32[]{:S(2)}) collective-permute-start(f32[32,1152]{1,0:T(8,128)S(1)} %convolution_add_fusion.3), channel_id=1, source_target_pairs={{504,0},{0,8},{8,16},{16,24},{24,32},{32,40},{40,48},{48,56},{56,6... | collective-permute-start | bytes 442376 | tf_op jit(solution)/shard_map/while/body/eval_jaxpr/ppermute | solution.py:20
  606.3 11.0 %collective-permute-start.1 = (f32[32,1152]{1,0:T(8,128)S(1)}, f32[32,1152]{1,0:T(8,128)S(1)}, u32[]{:S(2)}, u32[]{:S(2)}) collective-permute-start(f32[32,1152]{1,0:T(8,128)S(1)} %convolution_add_fusion.3), channel_id=1, source_target_pairs={{504,0},{0,8},{8,16},{16,24},{24,32},{32,40},{40,48},{48,56},{56,6... | collective-permute-start | bytes 442376 | tf_op jit(solution)/shard_map/while/body/eval_jaxpr/ppermute | solution.py:20
  620.4 11.0 %collective-permute-start.1 = (f32[32,1152]{1,0:T(8,128)S(1)}, f32[32,1152]{1,0:T(8,128)S(1)}, u32[]{:S(2)}, u32[]{:S(2)}) collective-permute-start(f32[32,1152]{1,0:T(8,128)S(1)} %convolution_add_fusion.3), channel_id=1, source_target_pairs={{504,0},{0,8},{8,16},{16,24},{24,32},{32,40},{40,48},{48,56},{56,6... | collective-permute-start | bytes 442376 | tf_op jit(solution)/shard_map/while/body/eval_jaxpr/ppermute | solution.py:20
  634.5 10.9 %collective-permute-start.1 = (f32[32,1152]{1,0:T(8,128)S(1)}, f32[32,1152]{1,0:T(8,128)S(1)}, u32[]{:S(2)}, u32[]{:S(2)}) collective-permute-start(f32[32,1152]{1,0:T(8,128)S(1)} %convolution_add_fusion.3), channel_id=1, source_target_pairs={{504,0},{0,8},{8,16},{16,24},{24,32},{32,40},{40,48},{48,56},{56,6... | collective-permute-start | bytes 442376 | tf_op jit(solution)/shard_map/while/body/eval_jaxpr/ppermute | solution.py:20
  648.5 10.7 %collective-permute-start.1 = (f32[32,1152]{1,0:T(8,128)S(1)}, f32[32,1152]{1,0:T(8,128)S(1)}, u32[]{:S(2)}, u32[]{:S(2)}) collective-permute-start(f32[32,1152]{1,0:T(8,128)S(1)} %convolution_add_fusion.3), channel_id=1, source_target_pairs={{504,0},{0,8},{8,16},{16,24},{24,32},{32,40},{40,48},{48,56},{56,6... | collective-permute-start | bytes 442376 | tf_op jit(solution)/shard_map/while/body/eval_jaxpr/ppermute | solution.py:20
  662.4 10.9 %collective-permute-start.1 = (f32[32,1152]{1,0:T(8,128)S(1)}, f32[32,1152]{1,0:T(8,128)S(1)}, u32[]{:S(2)}, u32[]{:S(2)}) collective-permute-start(f32[32,1152]{1,0:T(8,128)S(1)} %convolution_add_fusion.3), channel_id=1, source_target_pairs={{504,0},{0,8},{8,16},{16,24},{24,32},{32,40},{40,48},{48,56},{56,6... | collective-permute-start | bytes 442376 | tf_op jit(solution)/shard_map/while/body/eval_jaxpr/ppermute | solution.py:20
  703.9 10.9 %collective-permute-start.1 = (f32[32,1152]{1,0:T(8,128)S(1)}, f32[32,1152]{1,0:T(8,128)S(1)}, u32[]{:S(2)}, u32[]{:S(2)}) collective-permute-start(f32[32,1152]{1,0:T(8,128)S(1)} %convolution_add_fusion.3), channel_id=1, source_target_pairs={{504,0},{0,8},{8,16},{16,24},{24,32},{32,40},{40,48},{48,56},{56,6... | collective-permute-start | bytes 442376 | tf_op jit(solution)/shard_map/while/body/eval_jaxpr/ppermute | solution.py:20
  717.9 10.9 %collective-permute-start.1 = (f32[32,1152]{1,0:T(8,128)S(1)}, f32[32,1152]{1,0:T(8,128)S(1)}, u32[]{:S(2)}, u32[]{:S(2)}) collective-permute-start(f32[32,1152]{1,0:T(8,128)S(1)} %convolution_add_fusion.3), channel_id=1, source_target_pairs={{504,0},{0,8},{8,16},{16,24},{24,32},{32,40},{40,48},{48,56},{56,6... | collective-permute-start | bytes 442376 | tf_op jit(solution)/shard_map/while/body/eval_jaxpr/ppermute | solution.py:20
  773.3 10.9 %collective-permute-start.1 = (f32[32,1152]{1,0:T(8,128)S(1)}, f32[32,1152]{1,0:T(8,128)S(1)}, u32[]{:S(2)}, u32[]{:S(2)}) collective-permute-start(f32[32,1152]{1,0:T(8,128)S(1)} %convolution_add_fusion.3), channel_id=1, source_target_pairs={{504,0},{0,8},{8,16},{16,24},{24,32},{32,40},{40,48},{48,56},{56,6... | collective-permute-start | bytes 442376 | tf_op jit(solution)/shard_map/while/body/eval_jaxpr/ppermute | solution.py:20
  801.0 10.8 %collective-permute-start.1 = (f32[32,1152]{1,0:T(8,128)S(1)}, f32[32,1152]{1,0:T(8,128)S(1)}, u32[]{:S(2)}, u32[]{:S(2)}) collective-permute-start(f32[32,1152]{1,0:T(8,128)S(1)} %convolution_add_fusion.3), channel_id=1, source_target_pairs={{504,0},{0,8},{8,16},{16,24},{24,32},{32,40},{40,48},{48,56},{56,6... | collective-permute-start | bytes 442376 | tf_op jit(solution)/shard_map/while/body/eval_jaxpr/ppermute | solution.py:20
  815.0 10.9 %collective-permute-start.1 = (f32[32,1152]{1,0:T(8,128)S(1)}, f32[32,1152]{1,0:T(8,128)S(1)}, u32[]{:S(2)}, u32[]{:S(2)}) collective-permute-start(f32[32,1152]{1,0:T(8,128)S(1)} %convolution_add_fusion.3), channel_id=1, source_target_pairs={{504,0},{0,8},{8,16},{16,24},{24,32},{32,40},{40,48},{48,56},{56,6... | collective-permute-start | bytes 442376 | tf_op jit(solution)/shard_map/while/body/eval_jaxpr/ppermute | solution.py:20
  829.0 10.9 %collective-permute-start.1 = (f32[32,1152]{1,0:T(8,128)S(1)}, f32[32,1152]{1,0:T(8,128)S(1)}, u32[]{:S(2)}, u32[]{:S(2)}) collective-permute-start(f32[32,1152]{1,0:T(8,128)S(1)} %convolution_add_fusion.3), channel_id=1, source_target_pairs={{504,0},{0,8},{8,16},{16,24},{24,32},{32,40},{40,48},{48,56},{56,6... | collective-permute-start | bytes 442376 | tf_op jit(solution)/shard_map/while/body/eval_jaxpr/ppermute | solution.py:20
  843.0 10.9 %collective-permute-start.1 = (f32[32,1152]{1,0:T(8,128)S(1)}, f32[32,1152]{1,0:T(8,128)S(1)}, u32[]{:S(2)}, u32[]{:S(2)}) collective-permute-start(f32[32,1152]{1,0:T(8,128)S(1)} %convolution_add_fusion.3), channel_id=1, source_target_pairs={{504,0},{0,8},{8,16},{16,24},{24,32},{32,40},{40,48},{48,56},{56,6... | collective-permute-start | bytes 442376 | tf_op jit(solution)/shard_map/while/body/eval_jaxpr/ppermute | solution.py:20
  857.0 10.8 %collective-permute-start.1 = (f32[32,1152]{1,0:T(8,128)S(1)}, f32[32,1152]{1,0:T(8,128)S(1)}, u32[]{:S(2)}, u32[]{:S(2)}) collective-permute-start(f32[32,1152]{1,0:T(8,128)S(1)} %convolution_add_fusion.3), channel_id=1, source_target_pairs={{504,0},{0,8},{8,16},{16,24},{24,32},{32,40},{40,48},{48,56},{56,6... | collective-permute-start | bytes 442376 | tf_op jit(solution)/shard_map/while/body/eval_jaxpr/ppermute | solution.py:20
  870.9 10.8 %collective-permute-start.1 = (f32[32,1152]{1,0:T(8,128)S(1)}, f32[32,1152]{1,0:T(8,128)S(1)}, u32[]{:S(2)}, u32[]{:S(2)}) collective-permute-start(f32[32,1152]{1,0:T(8,128)S(1)} %convolution_add_fusion.3), channel_id=1, source_target_pairs={{504,0},{0,8},{8,16},{16,24},{24,32},{32,40},{40,48},{48,56},{56,6... | collective-permute-start | bytes 442376 | tf_op jit(solution)/shard_map/while/body/eval_jaxpr/ppermute | solution.py:20
  884.8 10.9 %collective-permute-start.1 = (f32[32,1152]{1,0:T(8,128)S(1)}, f32[32,1152]{1,0:T(8,128)S(1)}, u32[]{:S(2)}, u32[]{:S(2)}) collective-permute-start(f32[32,1152]{1,0:T(8,128)S(1)} %convolution_add_fusion.3), channel_id=1, source_target_pairs={{504,0},{0,8},{8,16},{16,24},{24,32},{32,40},{40,48},{48,56},{56,6... | collective-permute-start | bytes 442376 | tf_op jit(solution)/shard_map/while/body/eval_jaxpr/ppermute | solution.py:20
  (84 other events, 866.8 us)
Sparse Core Ops, SparseCore 0:
  901.8 100.7 all-reduce.1
where the time goes:
time: 1020 us; the launch traced here: 1010 us
  waiting for transfers between devices  617 us (60%)
  starting transfers between devices  248 us (24%)
  matrix products  79.1 us (8%)
  local copies, waits for them, and re-layouts  43.8 us (4%)
  between operations  15.5 us (2%)
    ppermute x127, waiting for transfers between devices, passed_along(): return lax.ppermute(block, axis, route)  528 us
    ppermute x127, starting transfers between devices, passed_along(): return lax.ppermute(block, axis, route)  248 us
    psum x1, waiting for transfers between devices, local(): grad_unit_image = logit_scale * lax.psum(partial_value, 'narrow')  89.2 us
    dot_general x64, matrix products, visit(): lax.dot_general(image_bf, visitor, (((1,), (1,)), ((), ())), preferred_el...  61.1 us
    dynamic_update_slice x64, local copies, waits for them, and re-layouts, visit(): lax.dynamic_update_slice(text_store, visitor, ((step_index * half_rows).a...  40.8 us
  transfers between devices with their start and end apart: 128, of which 128 were waited for; matrix products, arithmetic and copies ran while one was open for 11% of the time, Pallas kernels for 0%

commit v1 on v0

v1 whole, which is shorter than its diff:
```python
import jax
import jax.numpy as jnp
from jax import lax
from jax.sharding import Mesh, PartitionSpec as P

epsilon = 1e-06
AXES = ("y", "w", "c", "x", "l")
TEXT_AXES = ("y", "w")
IMAGE_AXES = ("c", "x", "l")
NARROW = ("x", "l")


def unit_rows(values):
    as_float = values.astype(jnp.float32)
    row_norm = jnp.sqrt(jnp.sum(as_float * as_float, axis=1, keepdims=True) + epsilon)
    return as_float / row_norm, row_norm


def spread(block, axes):
    count = lax.axis_size(axes)
    copies = jnp.broadcast_to(block[None], (count,) + block.shape)
    return lax.all_to_all(copies, axes, 0, 0, tiled=True)


def collect(terms, axes):
    count = lax.axis_size(axes)
    sent = terms.astype(jnp.bfloat16).reshape((count, -1, terms.shape[-1]))
    return jnp.sum(lax.all_to_all(sent, axes, 0, 0, tiled=True).astype(jnp.float32), axis=0)


def finish(grad_unit, unit, norm):
    along = jnp.sum(unit * grad_unit, axis=1, keepdims=True)
    return ((grad_unit - unit * along) / norm).astype(jnp.bfloat16)


def local(image_emb, text_emb, positive, log_scale, bias):
    scale = jnp.exp(log_scale[0])
    rows, width = image_emb.shape
    image_unit, image_norm = unit_rows(image_emb)
    text_unit, text_norm = unit_rows(text_emb)
    image_bf = image_unit.astype(jnp.bfloat16)
    text_bf = text_unit.astype(jnp.bfloat16)

    images = spread(image_bf, "c").reshape(-1, width)
    texts = spread(text_bf, TEXT_AXES).reshape(-1, width)
    slot = lax.axis_index(TEXT_AXES) * positive.shape[0]
    hits = lax.dynamic_update_slice_in_dim(jnp.full((texts.shape[0],), -1, jnp.int32), positive, slot, 0)

    first = lax.axis_index(TEXT_AXES) * images.shape[0]
    image_index = first + jnp.arange(images.shape[0], dtype=jnp.int32)
    cosine = lax.dot_general(images, texts, (((1,), (1,)), ((), ())), preferred_element_type=jnp.float32)
    hit = (image_index[:, None] == hits[None, :]).astype(jnp.float32)
    grad_bf = (jax.nn.sigmoid(scale * cosine + bias[0]) - hit).astype(jnp.bfloat16)
    text_terms = lax.dot_general(grad_bf, images, (((0,), (0,)), ((), ())), preferred_element_type=jnp.float32)
    image_terms = jnp.dot(grad_bf, texts, preferred_element_type=jnp.float32)

    own = lax.axis_index(NARROW) * (rows // 8)
    image_sum = scale * collect(image_terms, IMAGE_AXES)
    part = lax.dynamic_slice_in_dim(image_unit, own, rows // 8, 0)
    part_norm = lax.dynamic_slice_in_dim(image_norm, own, rows // 8, 0)
    grad_image = spread(finish(image_sum, part, part_norm), NARROW).reshape(rows, width)

    grad_text = finish(scale * collect(text_terms, TEXT_AXES), text_unit, text_norm)
    return grad_image, grad_text


def solution(mesh):
    fine = Mesh(mesh.devices.reshape(8, 4, 2, 4, 2), AXES)
    dp, every = ("y", "w", "c"), AXES
    in_specs = (P(dp, None), P(every, None), P(every), P(), P())
    out_specs = (P(dp, None), P(every, None))
    return jax.shard_map(local, mesh=fine, in_specs=in_specs, out_specs=out_specs, check_vma=False)
```

time: 1020 us -> 218 us (0.21)
  the two profiles are of different devices: /device:TPU:56 before, /device:TPU:145 now
where the time goes in v1:
time: 218 us; the launch traced here: 217 us
  waiting for transfers between devices  153 us (70%)
  starting transfers between devices  44.1 us (20%)
  matrix products  8.67 us (4%)
  local copies, waits for them, and re-layouts  4.89 us (2%)
  other arithmetic  4.43 us (2%)
    all_to_all x2, waiting for transfers between devices, collect(): lax.all_to_all(sent, axes, 0, 0, tiled=True).astype(jnp.float32)  88 us
    all_to_all x3, waiting for transfers between devices, spread(): return lax.all_to_all(copies, axes, 0, 0, tiled=True)  64.9 us
    all_to_all x2, starting transfers between devices, collect(): lax.all_to_all(sent, axes, 0, 0, tiled=True).astype(jnp.float32)  22.6 us
    all_to_all x3, starting transfers between devices, spread(): return lax.all_to_all(copies, axes, 0, 0, tiled=True)  21.5 us
  transfers between devices with their start and end apart: 5, of which 5 were waited for; matrix products, arithmetic and copies ran while one was open for 2% of the time, Pallas kernels for 0%

profile of v1, /device:TPU:145, one launch (start us, length us, event | category | flops | bytes accessed | tf_op | source)
XLA Modules:
  0.0 217.2 jit_solution(9280777760562447644)
XLA Ops:
  0.6 1.3 fusion
  1.9 1.3 convert_divide_fusion
  3.2 0.0 copy-start.2
  3.2 1.1 broadcast_in_dim.6
  4.3 4.3 %all-to-all-start = ((bf16[2,256,1152]{2,1,0:T(8,128)(2,1)}), bf16[2,256,1152]{2,1,0:T(8,128)(2,1)S(1)}, u32[]{:S(2)}, u32[]{:S(2)}) async-start(bf16[2,256,1152]{2,1,0:T(8,128)(2,1)} %broadcast_in_dim.6), calls=%async_computation | async-start | bytes 2359296 | tf_op jit(solution)/shard_map/all_to_all | solution.py:22
  8.6 0.0 copy-done.2
  8.6 0.1 fusion.1
  8.7 0.1 fusion.2
  8.8 1.6 all-to-all-done
  10.4 0.0 copy-start
  10.4 1.7 broadcast_in_dim.7
  12.1 0.0 copy-start.4
  12.1 0.1 copy-done
  12.2 13.7 %all-to-all-start.1 = ((bf16[32,32,1152]{2,1,0:T(8,128)(2,1)}), bf16[32,32,1152]{2,1,0:T(8,128)(2,1)S(1)}, u32[]{:S(2)}, u32[]{:S(2)}) async-start(bf16[32,32,1152]{2,1,0:T(8,128)(2,1)} %broadcast_in_dim.7), calls=%async_computation.1 | async-start | bytes 4718592 | tf_op jit(solution)/shard_map/all_to_all | solution.py:22
  27.2 0.0 copy-done.4
  27.2 0.2 dynamic_update_slice.5
  27.5 56.5 %all-to-all-done.1 = bf16[32,32,1152]{2,1,0:T(8,128)(2,1)S(1)} async-done(((bf16[32,32,1152]{2,1,0:T(8,128)(2,1)}), bf16[32,32,1152]{2,1,0:T(8,128)(2,1)S(1)}, u32[]{:S(2)}, u32[]{:S(2)}) %all-to-all-start.1) | async-done | bytes 2359328 | tf_op jit(solution)/shard_map/all_to_all | solution.py:22
  84.0 3.1 %subtract_convert_fusion = bf16[512,1024]{1,0:T(8,128)(2,1)S(1)} fusion(bf16[512,1152]{1,0:T(8,128)(2,1)} %bitcast.18, bf16[1024,1152]{1,0:T(8,128)(2,1)S(1)} %bitcast.14, s32[1024]{0:T(1024)S(1)} %dynamic_update_slice.5, f32[]{:T(128)} %bitcast.13, f32[]{:T(128)} %bitcast, s32[512]{0:T(512)S(1)} %iota_add_fusion), kind=kOutput, calls=%fused_computation.4 | convolution fusion | flops 1212678144 | bytes 4593672 | tf_op jit(solution)/shard_map/dot_general | solution.py:51
  87.2 0.0 copy-start.5
  87.2 2.5 %convolution_convert_fusion.1 = bf16[512,1152]{1,0:T(8,128)(2,1)} fusion(bf16[512,1024]{1,0:T(8,128)(2,1)S(1)} %subtract_convert_fusion, bf16[1024,1152]{1,0:T(8,128)(2,1)S(1)} %bitcast.15), kind=kOutput, calls=%fused_computation.2 | convolution fusion | flops 1208549376 | bytes 4587520 | tf_op jit(solution)/shard_map/dot_general | solution.py:55
  89.7 0.0 copy-done.5
  89.7 5.9 %all-to-all-start.2 = ((bf16[16,32,1152]{2,1,0:T(8,128)(2,1)}), bf16[16,32,1152]{2,1,0:T(8,128)(2,1)S(1)}, u32[]{:S(2)}, u32[]{:S(2)}) async-start(bf16[16,32,1152]{2,1,0:T(8,128)(2,1)} %bitcast.20), calls=%async_computation.2 | async-start | bytes 2359296 | tf_op jit(solution)/shard_map/all_to_all | solution.py:28
  95.6 0.0 copy-start.1
  95.6 0.1 dynamic-slice.3
  95.7 16.3 %all-to-all-done.2 = bf16[16,32,1152]{2,1,0:T(8,128)(2,1)S(1)} async-done(((bf16[16,32,1152]{2,1,0:T(8,128)(2,1)}), bf16[16,32,1152]{2,1,0:T(8,128)(2,1)S(1)}, u32[]{:S(2)}, u32[]{:S(2)}) %all-to-all-start.2) | async-done | bytes 1179680 | tf_op jit(solution)/shard_map/all_to_all | solution.py:28
  112.0 0.2 convert_reduce_fusion.1
  112.1 0.0 copy-start.6
  112.1 0.1 multiply_reduce_fusion.1
  112.3 0.1 divide_convert_fusion.1
  112.4 0.9 broadcast_in_dim.8
  113.2 3.5 %all-to-all-start.3 = ((bf16[8,32,1152]{2,1,0:T(8,128)(2,1)}), bf16[8,32,1152]{2,1,0:T(8,128)(2,1)S(1)}, u32[]{:S(2)}, u32[]{:S(2)}) async-start(bf16[8,32,1152]{2,1,0:T(8,128)(2,1)} %broadcast_in_dim.8), calls=%async_computation.3 | async-start | bytes 1179648 | tf_op jit(solution)/shard_map/all_to_all | solution.py:22
  116.8 0.0 copy-done.1
  116.8 0.0 copy-done.6
  116.8 3.0 %convolution_convert_fusion = bf16[1024,1152]{1,0:T(8,128)(2,1)} fusion(bf16[512,1024]{1,0:T(8,128)(2,1)S(1)} %copy-done.6, bf16[512,1152]{1,0:T(8,128)(2,1)S(1)} %bitcast.19), kind=kOutput, calls=%fused_computation.1 | convolution fusion | flops 1209139200 | bytes 4587520 | tf_op jit(solution)/shard_map/dot_general | solution.py:54
  119.8 6.8 %all-to-all-done.3 = bf16[8,32,1152]{2,1,0:T(8,128)(2,1)S(1)} async-done(((bf16[8,32,1152]{2,1,0:T(8,128)(2,1)}), bf16[8,32,1152]{2,1,0:T(8,128)(2,1)S(1)}, u32[]{:S(2)}, u32[]{:S(2)}) %all-to-all-start.3) | async-done | bytes 589856 | tf_op jit(solution)/shard_map/all_to_all | solution.py:22
  126.6 16.7 %all-to-all-start.4 = ((bf16[32,32,1152]{2,1,0:T(8,128)(2,1)}), bf16[32,32,1152]{2,1,0:T(8,128)(2,1)S(1)}, u32[]{:S(2)}, u32[]{:S(2)}) async-start(bf16[32,32,1152]{2,1,0:T(8,128)(2,1)} %bitcast.16), calls=%async_computation.4 | async-start | bytes 4718592 | tf_op jit(solution)/shard_map/all_to_all | solution.py:28
  143.3 0.0 copy-start.3
  143.3 71.7 %all-to-all-done.4 = bf16[32,32,1152]{2,1,0:T(8,128)(2,1)S(1)} async-done(((bf16[32,32,1152]{2,1,0:T(8,128)(2,1)}), bf16[32,32,1152]{2,1,0:T(8,128)(2,1)S(1)}, u32[]{:S(2)}, u32[]{:S(2)}) %all-to-all-start.4) | async-done | bytes 2359328 | tf_op jit(solution)/shard_map/all_to_all | solution.py:28
  215.1 0.3 convert_reduce_fusion
  215.4 0.0 copy-done.3
  215.4 0.2 multiply_reduce_fusion
  215.6 0.7 divide_convert_fusion
  216.4 0.8 copy.11
  (4 shorter events, 0.0 us)
Async XLA Ops:
  3.2 5.4 %copy-start.2 = (bf16[32,1152]{1,0:T(8,128)(2,1)S(1)}, bf16[32,1152]{1,0:T(8,128)(2,1)}, u32[]{:S(2)}) copy-start(bf16[32,1152]{1,0:T(8,128)(2,1)} %param.6) | copy-start | bytes 221188
  4.3 6.1 %all-to-all-start = ((bf16[2,256,1152]{2,1,0:T(8,128)(2,1)}), bf16[2,256,1152]{2,1,0:T(8,128)(2,1)S(1)}, u32[]{:S(2)}, u32[]{:S(2)}) async-start(bf16[2,256,1152]{2,1,0:T(8,128)(2,1)} %broadcast_in_dim.6), calls=%async_computation | async-start | bytes 2359296 | tf_op jit(solution)/shard_map/all_to_all | solution.py:22
  10.4 1.8 copy-start
  12.1 15.1 %copy-start.4 = (s32[32]{0:T(128)S(1)}, s32[32]{0:T(128)}, u32[]{:S(2)}) copy-start(s32[32]{0:T(128)} %param.7) | copy-start | bytes 388
  12.2 71.8 %all-to-all-start.1 = ((bf16[32,32,1152]{2,1,0:T(8,128)(2,1)}), bf16[32,32,1152]{2,1,0:T(8,128)(2,1)S(1)}, u32[]{:S(2)}, u32[]{:S(2)}) async-start(bf16[32,32,1152]{2,1,0:T(8,128)(2,1)} %broadcast_in_dim.7), calls=%async_computation.1 | async-start | bytes 4718592 | tf_op jit(solution)/shard_map/all_to_all | solution.py:22
  87.2 2.6 %copy-start.5 = (bf16[512,1024]{1,0:T(8,128)(2,1)}, bf16[512,1024]{1,0:T(8,128)(2,1)S(1)}, u32[]{:S(2)}) copy-start(bf16[512,1024]{1,0:T(8,128)(2,1)S(1)} %subtract_convert_fusion) | copy-start | bytes 3145732
  89.7 22.2 %all-to-all-start.2 = ((bf16[16,32,1152]{2,1,0:T(8,128)(2,1)}), bf16[16,32,1152]{2,1,0:T(8,128)(2,1)S(1)}, u32[]{:S(2)}, u32[]{:S(2)}) async-start(bf16[16,32,1152]{2,1,0:T(8,128)(2,1)} %bitcast.20), calls=%async_computation.2 | async-start | bytes 2359296 | tf_op jit(solution)/shard_map/all_to_all | solution.py:28
  95.6 21.2 %copy-start.1 = (bf16[2,256,1152]{2,1,0:T(8,128)(2,1)S(1)}, bf16[2,256,1152]{2,1,0:T(8,128)(2,1)}, u32[]{:S(2)}) copy-start(bf16[2,256,1152]{2,1,0:T(8,128)(2,1)} %copy-done) | copy-start | bytes 3538948
  112.1 4.7 %copy-start.6 = (bf16[512,1024]{1,0:T(8,128)(2,1)S(1)}, bf16[512,1024]{1,0:T(8,128)(2,1)}, u32[]{:S(2)}) copy-start(bf16[512,1024]{1,0:T(8,128)(2,1)} %copy-done.5) | copy-start | bytes 3145732
  113.2 13.4 %all-to-all-start.3 = ((bf16[8,32,1152]{2,1,0:T(8,128)(2,1)}), bf16[8,32,1152]{2,1,0:T(8,128)(2,1)S(1)}, u32[]{:S(2)}, u32[]{:S(2)}) async-start(bf16[8,32,1152]{2,1,0:T(8,128)(2,1)} %broadcast_in_dim.8), calls=%async_computation.3 | async-start | bytes 1179648 | tf_op jit(solution)/shard_map/all_to_all | solution.py:22
  126.6 88.5 %all-to-all-start.4 = ((bf16[32,32,1152]{2,1,0:T(8,128)(2,1)}), bf16[32,32,1152]{2,1,0:T(8,128)(2,1)S(1)}, u32[]{:S(2)}, u32[]{:S(2)}) async-start(bf16[32,32,1152]{2,1,0:T(8,128)(2,1)} %bitcast.16), calls=%async_computation.4 | async-start | bytes 4718592 | tf_op jit(solution)/shard_map/all_to_all | solution.py:28
  143.3 72.1 %copy-start.3 = (bf16[32,1152]{1,0:T(8,128)(2,1)S(1)}, bf16[32,1152]{1,0:T(8,128)(2,1)}, u32[]{:S(2)}) copy-start(bf16[32,1152]{1,0:T(8,128)(2,1)} %param.6) | copy-start | bytes 221188

commit v2 on v1

v2 whole, which is shorter than its diff:
```python
import jax
import jax.numpy as jnp
from jax import lax
from jax.sharding import Mesh, PartitionSpec as P

epsilon = 1e-06
AXES = ("yh", "yl", "w", "c", "x", "l")
Y, Z = ("yh", "yl"), ("w", "l")
NARROW = ("x", "l")
GROUP = ("yl", "x", "l")
BF16, F32 = jnp.bfloat16, jnp.float32


def unit_rows(values):
    as_float = values.astype(F32)
    row_norm = jnp.sqrt(jnp.sum(as_float * as_float, axis=1, keepdims=True) + epsilon)
    return as_float / row_norm, row_norm


def swap(block, axis):
    return lax.ppermute(block, axis, [(0, 1), (1, 0)])


def route(axes, distance):
    count = lax.axis_size(axes)
    pairs = []
    for i in range(count):
        sign = 1 if (i + distance) % 2 == 0 else -1
        pairs.append((i, (i + sign * distance) % count))
    return pairs


def fan_out(block, axes, distance):
    return lax.ppermute(block, axes, route(axes, distance))


def fan_in(terms, axes, distance):
    back = [(target, source) for source, target in route(axes, distance)]
    return lax.ppermute(terms.astype(BF16), axes, back).astype(F32)


def finish(grad_unit, unit, norm):
    along = jnp.sum(unit * grad_unit, axis=1, keepdims=True)
    return ((grad_unit - unit * along) / norm).astype(BF16)


def local(image_emb, text_emb, positive, log_scale, bias):
    scale = jnp.exp(log_scale[0])
    rows, width = image_emb.shape
    mine = text_emb.shape[0]
    text_unit, text_norm = unit_rows(text_emb)
    text_bf = text_unit.astype(BF16)
    along_y = jnp.concatenate([text_bf] + [fan_out(text_bf, Y, d) for d in (1, 2, 3)], axis=0)

    image_unit, image_norm = unit_rows(image_emb)
    image_bf = image_unit.astype(BF16)
    beyond = swap(image_bf, "yl")
    images = jnp.concatenate([image_bf, swap(image_bf, "c"), beyond, swap(beyond, "c")], axis=0)

    wanted = positive - lax.axis_index(("yh", "yl", "w", "c")) * rows
    hit = jnp.arange(rows, dtype=jnp.int32)[:, None] == wanted[None, :]

    grads, texts, returned = [], [], []
    for d in (0, 1, 2, 3):
        block = along_y if d == 0 else fan_out(along_y, Z, d)
        cosine = lax.dot_general(images, block, (((1,), (1,)), ((), ())), preferred_element_type=F32)
        grad = jax.nn.sigmoid(scale * cosine + bias[0])
        if d == 0:
            padded = jnp.pad(hit.astype(F32), ((0, grad.shape[0] - rows), (0, grad.shape[1] - mine)))
            grad = grad - padded
        grad = grad.astype(BF16)
        terms = lax.dot_general(grad, images, (((0,), (0,)), ((), ())), preferred_element_type=F32)
        returned.append(terms if d == 0 else fan_in(terms, Z, d))
        grads.append(grad)
        texts.append(block)

    image_terms = jnp.dot(jnp.concatenate(grads, axis=1), jnp.concatenate(texts, axis=0), preferred_element_type=F32)
    image_terms = image_terms.reshape(2, 2, rows, width)
    pairs = image_terms[:, 0] + swap(image_terms[:, 1].astype(BF16), "c").astype(F32)
    upper = lax.axis_index("yl") == 1
    pairs = jnp.where(upper, pairs[::-1], pairs).astype(BF16).reshape(16, rows // 8, width)
    image_sum = scale * jnp.sum(lax.all_to_all(pairs, GROUP, 0, 0, tiled=True).astype(F32), axis=0)
    own = lax.axis_index(NARROW) * (rows // 8)
    part = lax.dynamic_slice_in_dim(image_unit, own, rows // 8, 0)
    part_norm = lax.dynamic_slice_in_dim(image_norm, own, rows // 8, 0)
    done = finish(image_sum, part, part_norm)
    grad_image = lax.all_to_all(jnp.broadcast_to(done[None], (8,) + done.shape), NARROW, 0, 0, tiled=True)

    text_sum = sum(returned).reshape(4, mine, width)
    text_sum = text_sum[0] + sum(fan_in(text_sum[d], Y, d) for d in (1, 2, 3))
    grad_text = finish(scale * text_sum, text_unit, text_norm)
    return grad_image.reshape(rows, width), grad_text


def solution(mesh):
    fine = Mesh(mesh.devices.reshape(4, 2, 4, 2, 4, 2), AXES)
    dp = ("yh", "yl", "w", "c")
    in_specs = (P(dp, None), P(AXES, None), P(AXES), P(), P())
    out_specs = (P(dp, None), P(AXES, None))
    return jax.shard_map(local, mesh=fine, in_specs=in_specs, out_specs=out_specs, check_vma=False)
```

time: 218 us -> 156 us (0.72)
  the two profiles are of different devices: /device:TPU:145 before, /device:TPU:10 now
where the time goes in v2:
time: 156 us; the launch traced here: 155 us
  starting transfers between devices  75.8 us (49%)
  waiting for transfers between devices  43.9 us (28%)
  other arithmetic  13.6 us (9%)
  matrix products  12.7 us (8%)
  local copies, waits for them, and re-layouts  6.41 us (4%)
  between operations  2.5 us (2%)
    ppermute x6, starting transfers between devices, fan_in(): return lax.ppermute(terms.astype(BF16), axes, back).astype(F32)  27.9 us
    ppermute x6, starting transfers between devices, fan_out(): return lax.ppermute(block, axes, route(axes, distance))  27.6 us
    ppermute x6, waiting for transfers between devices, fan_in(): return lax.ppermute(terms.astype(BF16), axes, back).astype(F32)  21.6 us
    ppermute x6, waiting for transfers between devices, fan_out(): return lax.ppermute(block, axes, route(axes, distance))  19.4 us
    ppermute x4, starting transfers between devices, swap(): return lax.ppermute(block, axis, [(0, 1), (1, 0)])  8.39 us
    dot_general x4, matrix products, local(): lax.dot_general(grad, images, (((0,), (0,)), ((), ())), preferred_element...  7.4 us
    all_to_all x1, starting transfers between devices, local(): lax.all_to_all(pairs, GROUP, 0, 0, tiled=True).astype(F32)  6.48 us
    all_to_all x1, starting transfers between devices, local(): lax.all_to_all(jnp.broadcast_to(done[None], (8,) + done.shape), NARROW, 0...  5.42 us
  transfers between devices with their start and end apart: 18, of which 8 were waited for; matrix products, arithmetic and copies ran while one was open for 8% of the time, Pallas kernels for 0%

profile of v2, /device:TPU:10, one launch (start us, length us, event | category | flops | bytes accessed | tf_op | source)
XLA Modules:
  0.0 154.9 jit_solution(17752825388242484677)
XLA Ops:
  0.6 1.0 fusion.39
  1.7 1.0 constant_dynamic-update-slice_fusion.6
  2.7 6.7 %collective-permute-start.5 = (bf16[32,1152]{1,0:T(8,128)(2,1)S(1)}, bf16[32,1152]{1,0:T(8,128)(2,1)S(1)}, u32[]{:S(2)}, u32[]{:S(2)}) collective-permute-start(bf16[32,1152]{1,0:T(8,128)(2,1)S(1)} %get-tuple-element.3), channel_id=1, source_target_pairs={{0,320},{64,256},{128,448},{192,384},{256,64},{320,0},{384,192},{4... | collective-permute-start | bytes 221192 | tf_op jit(solution)/shard_map/ppermute | solution.py:34
  9.4 2.2 %collective-permute-start.4 = (bf16[32,1152]{1,0:T(8,128)(2,1)S(1)}, bf16[32,1152]{1,0:T(8,128)(2,1)S(1)}, u32[]{:S(2)}, u32[]{:S(2)}) collective-permute-start(bf16[32,1152]{1,0:T(8,128)(2,1)S(1)} %get-tuple-element.3), channel_id=1, source_target_pairs={{0,128},{64,448},{128,256},{192,64},{256,384},{320,192},{384,0},{4... | collective-permute-start | bytes 221192 | tf_op jit(solution)/shard_map/ppermute | solution.py:34
  11.6 2.4 %collective-permute-start.3 = (bf16[32,1152]{1,0:T(8,128)(2,1)S(1)}, bf16[32,1152]{1,0:T(8,128)(2,1)S(1)}, u32[]{:S(2)}, u32[]{:S(2)}) collective-permute-start(bf16[32,1152]{1,0:T(8,128)(2,1)S(1)} %get-tuple-element.3), channel_id=1, source_target_pairs={{0,448},{64,128},{128,64},{192,256},{256,192},{320,384},{384,320},... | collective-permute-start | bytes 221192 | tf_op jit(solution)/shard_map/ppermute | solution.py:34
  14.0 1.3 fusion.29
  15.3 2.3 %convert_divide_fusion = (f32[256,1152]{1,0:T(8,128)}, bf16[256,1152]{1,0:T(8,128)(2,1)S(1)}) fusion(bf16[256,1152]{1,0:T(8,128)(2,1)} %param.5, f32[256]{0:T(256)S(1)} %add_sqrt_fusion), kind=kLoop, calls=%fused_computation.13 | loop fusion | flops 884736 | bytes 2360320 | tf_op jit(solution)/shard_map/div | solution.py:17
  17.6 2.6 %collective-permute-start.1 = (bf16[256,1152]{1,0:T(8,128)(2,1)S(1)}, bf16[256,1152]{1,0:T(8,128)(2,1)S(1)}, u32[]{:S(2)}, u32[]{:S(2)}) collective-permute-start(bf16[256,1152]{1,0:T(8,128)(2,1)S(1)} %get-tuple-element.5), channel_id=1, source_target_pairs={{0,64},{64,0},{1,65},{65,1},{2,66},{66,2},{3,67},{67,3},{4,68},{68... | collective-permute-start | bytes 1769480 | tf_op jit(solution)/shard_map/ppermute | solution.py:21
  20.2 1.9 %collective-permute-start = (bf16[256,1152]{1,0:T(8,128)(2,1)S(1)}, bf16[256,1152]{1,0:T(8,128)(2,1)S(1)}, u32[]{:S(2)}, u32[]{:S(2)}) collective-permute-start(bf16[256,1152]{1,0:T(8,128)(2,1)S(1)} %get-tuple-element.5), channel_id=1, source_target_pairs={{0,8},{8,0},{1,9},{9,1},{2,10},{10,2},{3,11},{11,3},{4,12},{12,4},... | collective-permute-start | bytes 1769480 | tf_op jit(solution)/shard_map/ppermute | solution.py:21
  23.7 6.1 %collective-permute-start.7 = (bf16[128,1152]{1,0:T(8,128)(2,1)S(1)}, bf16[128,1152]{1,0:T(8,128)(2,1)S(1)}, u32[]{:S(2)}, u32[]{:S(2)}) collective-permute-start(bf16[128,1152]{1,0:T(8,128)(2,1)S(1)} %pad_maximum_fusion.1), channel_id=1, source_target_pairs={{0,16},{1,49},{16,32},{17,1},{32,48},{33,17},{48,0},{49,33},{2,18}... | collective-permute-start | bytes 884744 | tf_op jit(solution)/shard_map/ppermute | solution.py:34
  29.8 7.3 %collective-permute-start.6 = (bf16[128,1152]{1,0:T(8,128)(2,1)S(1)}, bf16[128,1152]{1,0:T(8,128)(2,1)S(1)}, u32[]{:S(2)}, u32[]{:S(2)}) collective-permute-start(bf16[128,1152]{1,0:T(8,128)(2,1)S(1)} %pad_maximum_fusion.1), channel_id=1, source_target_pairs={{0,49},{1,16},{16,1},{17,32},{32,17},{33,48},{48,33},{49,0},{2,51}... | collective-permute-start | bytes 884744 | tf_op jit(solution)/shard_map/ppermute | solution.py:34
  37.1 2.8 %collective-permute-start.8 = (bf16[128,1152]{1,0:T(8,128)(2,1)S(1)}, bf16[128,1152]{1,0:T(8,128)(2,1)S(1)}, u32[]{:S(2)}, u32[]{:S(2)}) collective-permute-start(bf16[128,1152]{1,0:T(8,128)(2,1)S(1)} %pad_maximum_fusion.1), channel_id=1, source_target_pairs={{0,33},{1,32},{16,49},{17,48},{32,1},{33,0},{48,17},{49,16},{2,35}... | collective-permute-start | bytes 884744 | tf_op jit(solution)/shard_map/ppermute | solution.py:34
  40.0 1.9 %collective-permute-start.2 = (bf16[256,1152]{1,0:T(8,128)(2,1)S(1)}, bf16[256,1152]{1,0:T(8,128)(2,1)S(1)}, u32[]{:S(2)}, u32[]{:S(2)}) collective-permute-start(bf16[256,1152]{1,0:T(8,128)(2,1)S(1)} %collective-permute-done.1), channel_id=1, source_target_pairs={{0,8},{8,0},{1,9},{9,1},{2,10},{10,2},{3,11},{11,3},{4,12},{12,4},... | collective-permute-start | bytes 1769480 | tf_op jit(solution)/shard_map/ppermute | solution.py:21
  41.9 13.2 %collective-permute-done.6 = bf16[128,1152]{1,0:T(8,128)(2,1)S(1)} collective-permute-done((bf16[128,1152]{1,0:T(8,128)(2,1)S(1)}, bf16[128,1152]{1,0:T(8,128)(2,1)S(1)}, u32[]{:S(2)}, u32[]{:S(2)}) %collective-permute-start.6) | collective-permute-done | bytes 294944 | tf_op jit(solution)/shard_map/ppermute | solution.py:34
  55.2 6.2 %collective-permute-done.8 = bf16[128,1152]{1,0:T(8,128)(2,1)S(1)} collective-permute-done((bf16[128,1152]{1,0:T(8,128)(2,1)S(1)}, bf16[128,1152]{1,0:T(8,128)(2,1)S(1)}, u32[]{:S(2)}, u32[]{:S(2)}) %collective-permute-start.8) | collective-permute-done | bytes 294944 | tf_op jit(solution)/shard_map/ppermute | solution.py:34
  61.5 1.0 copy-done.19
  62.5 0.8 copy-done.4
  63.3 1.2 pad_maximum_fusion
  64.5 0.9 fusion.27
  65.5 0.9 fusion.26
  66.5 0.9 fusion.25
  67.5 0.9 fusion.28
  68.8 1.6 %fusion.31 = f32[1024,1152]{1,0:T(8,128)S(1)} fusion(bf16[512,1152]{1,0:T(8,128)(2,1)S(1)} %copy-done.20, bf16[1024,128]{0,1:T(8,128)(2,1)S(1)} %fusion.27, bf16[1024,128]{0,1:T(8,128)(2,1)S(1)} %fusion.26, bf16[1024,128]{0,1:T(8,128)(2,1)S(1)} %fusion.25, bf16[1024,128]{0,1:T(8,128)(2,1)S(1)} %fusion.28), kind=kOutput, calls=%fused_computation.46 | convolution fusion | flops 1212153856 | bytes 6946816 | tf_op jit(solution)/shard_map/dot_general | solution.py:77
  70.4 2.1 %copy-done = f32[1024,1152]{1,0:T(8,128)} copy-done((f32[1024,1152]{1,0:T(8,128)}, f32[1024,1152]{1,0:T(8,128)S(1)}, u32[]{:S(2)}) %copy-start) | copy-done | bytes 4718616
  72.6 2.0 %collective-permute-start.9 = (bf16[2,256,1152]{2,1,0:T(8,128)(2,1)S(1)}, bf16[2,256,1152]{2,1,0:T(8,128)(2,1)}, u32[]{:S(2)}, u32[]{:S(2)}) collective-permute-start(bf16[2,256,1152]{2,1,0:T(8,128)(2,1)S(1)} %fusion.30), channel_id=1, source_target_pairs={{0,8},{8,0},{1,9},{9,1},{2,10},{10,2},{3,11},{11,3},{4,12},{12,4},... | collective-permute-start | bytes 3538952 | tf_op jit(solution)/shard_map/ppermute | solution.py:21
  74.6 2.9 %collective-permute-done.9 = bf16[2,256,1152]{2,1,0:T(8,128)(2,1)} collective-permute-done((bf16[2,256,1152]{2,1,0:T(8,128)(2,1)S(1)}, bf16[2,256,1152]{2,1,0:T(8,128)(2,1)}, u32[]{:S(2)}, u32[]{:S(2)}) %collective-permute-start.9) | collective-permute-done | bytes 1179680 | tf_op jit(solution)/shard_map/ppermute | solution.py:21
  77.5 2.2 %fusion.3 = bf16[2,256,1152]{2,1,0:T(8,128)(2,1)S(1)} fusion(f32[2,2,256,1152]{3,2,1,0:T(8,128)} %bitcast.34, bf16[2,256,1152]{2,1,0:T(8,128)(2,1)} %collective-permute-done.9), kind=kLoop, calls=%fused_computation.10 | loop fusion | flops 1769472 | bytes 4718592 | tf_op jit(solution)/shard_map/add | solution.py:79
  79.7 1.2 fusion.2
  80.9 6.5 %all-to-all-start = ((bf16[16,32,1152]{2,1,0:T(8,128)(2,1)}), bf16[16,32,1152]{2,1,0:T(8,128)(2,1)S(1)}, u32[]{:S(2)}, u32[]{:S(2)}) async-start(bf16[16,32,1152]{2,1,0:T(8,128)(2,1)} %bitcast.5), calls=%async_computation | async-start | bytes 2359296 | tf_op jit(solution)/shard_map/all_to_all | solution.py:82
  87.4 2.2 %convolution_convert_fusion.2 = bf16[128,1152]{1,0:T(8,128)(2,1)} fusion(bf16[1024,128]{0,1:T(8,128)(2,1)} %copy-done.18, bf16[1024,1152]{1,0:T(8,128)(2,1)S(1)} %pad_maximum_fusion), kind=kOutput, calls=%fused_computation.6 | convolution fusion | flops 302137344 | bytes 2916352 | tf_op jit(solution)/shard_map/dot_general | solution.py:72
  89.7 1.2 convolution_convert_fusion.1
  90.9 1.2 convolution_convert_fusion
  92.1 7.6 %collective-permute-start.12 = (bf16[128,1152]{1,0:T(8,128)(2,1)}, bf16[128,1152]{1,0:T(8,128)(2,1)}, u32[]{:S(2)}, u32[]{:S(2)}) collective-permute-start(bf16[128,1152]{1,0:T(8,128)(2,1)} %convolution_convert_fusion), channel_id=1, source_target_pairs={{33,0},{32,1},{49,16},{48,17},{1,32},{0,33},{17,48},{16,49},{35,2}... | collective-permute-start | bytes 884744 | tf_op jit(solution)/shard_map/ppermute | solution.py:39
  99.7 1.9 %collective-permute-start.11 = (bf16[128,1152]{1,0:T(8,128)(2,1)}, bf16[128,1152]{1,0:T(8,128)(2,1)}, u32[]{:S(2)}, u32[]{:S(2)}) collective-permute-start(bf16[128,1152]{1,0:T(8,128)(2,1)} %convolution_convert_fusion.1), channel_id=1, source_target_pairs={{16,0},{49,1},{32,16},{1,17},{48,32},{17,33},{0,48},{33,49},{18,2}... | collective-permute-start | bytes 884744 | tf_op jit(solution)/shard_map/ppermute | solution.py:39
  101.6 5.1 %collective-permute-start.10 = (bf16[128,1152]{1,0:T(8,128)(2,1)}, bf16[128,1152]{1,0:T(8,128)(2,1)}, u32[]{:S(2)}, u32[]{:S(2)}) collective-permute-start(bf16[128,1152]{1,0:T(8,128)(2,1)} %convolution_convert_fusion.2), channel_id=1, source_target_pairs={{49,0},{16,1},{1,16},{32,17},{17,32},{48,33},{33,48},{0,49},{51,2}... | collective-permute-start | bytes 884744 | tf_op jit(solution)/shard_map/ppermute | solution.py:39
  106.9 7.0 %collective-permute-done.12 = bf16[128,1152]{1,0:T(8,128)(2,1)} collective-permute-done((bf16[128,1152]{1,0:T(8,128)(2,1)}, bf16[128,1152]{1,0:T(8,128)(2,1)}, u32[]{:S(2)}, u32[]{:S(2)}) %collective-permute-start.12) | collective-permute-done | bytes 294944 | tf_op jit(solution)/shard_map/ppermute | solution.py:39
  113.9 6.1 %collective-permute-done.11 = bf16[128,1152]{1,0:T(8,128)(2,1)} collective-permute-done((bf16[128,1152]{1,0:T(8,128)(2,1)}, bf16[128,1152]{1,0:T(8,128)(2,1)}, u32[]{:S(2)}, u32[]{:S(2)}) %collective-permute-start.11) | collective-permute-done | bytes 294944 | tf_op jit(solution)/shard_map/ppermute | solution.py:39
  120.0 4.6 %collective-permute-done.10 = bf16[128,1152]{1,0:T(8,128)(2,1)} collective-permute-done((bf16[128,1152]{1,0:T(8,128)(2,1)}, bf16[128,1152]{1,0:T(8,128)(2,1)}, u32[]{:S(2)}, u32[]{:S(2)}) %collective-permute-start.10) | collective-permute-done | bytes 294944 | tf_op jit(solution)/shard_map/ppermute | solution.py:39
  124.5 2.7 %fusion.46 = (bf16[128,1152]{1,0:T(8,128)(2,1)}, f32[128,1152]{1,0:T(8,128)}) fusion(bf16[128,1152]{1,0:T(8,128)(2,1)} %collective-permute-done.12, bf16[128,1152]{1,0:T(8,128)(2,1)} %collective-permute-done.11, bf16[128,1152]{1,0:T(8,128)(2,1)} %collective-permute-done.10, bf16[1024,128]{0,1:T(8,128)(2,1)} %copy-done.13, ...), kind=kOutput, calls=%fused_computation.79 | convolution fusion | flops 303022080 | bytes 4390912 | tf_op jit(solution)/shard_map/dot_general | solution.py:72
  127.4 1.1 multiply_reduce_fusion.1
  128.6 1.0 divide_convert_fusion.1
  129.6 0.9 broadcast_in_dim.2
  130.4 5.4 %all-to-all-start.1 = ((bf16[8,32,1152]{2,1,0:T(8,128)(2,1)}), bf16[8,32,1152]{2,1,0:T(8,128)(2,1)S(1)}, u32[]{:S(2)}, u32[]{:S(2)}) async-start(bf16[8,32,1152]{2,1,0:T(8,128)(2,1)} %broadcast_in_dim.2), calls=%async_computation.1 | async-start | bytes 1179648 | tf_op jit(solution)/shard_map/all_to_all | solution.py:87
  135.9 3.5 %collective-permute-start.13 = (bf16[32,1152]{1,0:T(8,128)(2,1)S(1)}, bf16[32,1152]{1,0:T(8,128)(2,1)S(1)}, u32[]{:S(2)}, u32[]{:S(2)}) collective-permute-start(bf16[32,1152]{1,0:T(8,128)(2,1)S(1)} %get-tuple-element.6), channel_id=1, source_target_pairs={{448,0},{128,64},{64,128},{256,192},{192,256},{384,320},{320,384},... | collective-permute-start | bytes 221192 | tf_op jit(solution)/shard_map/ppermute | solution.py:39
  139.4 5.4 %collective-permute-start.15 = (bf16[32,1152]{1,0:T(8,128)(2,1)S(1)}, bf16[32,1152]{1,0:T(8,128)(2,1)S(1)}, u32[]{:S(2)}, u32[]{:S(2)}) collective-permute-start(bf16[32,1152]{1,0:T(8,128)(2,1)S(1)} %get-tuple-element.7), channel_id=1, source_target_pairs={{320,0},{256,64},{448,128},{384,192},{64,256},{0,320},{192,384},{1... | collective-permute-start | bytes 221192 | tf_op jit(solution)/shard_map/ppermute | solution.py:39
  144.8 4.4 %collective-permute-start.14 = (bf16[32,1152]{1,0:T(8,128)(2,1)S(1)}, bf16[32,1152]{1,0:T(8,128)(2,1)S(1)}, u32[]{:S(2)}, u32[]{:S(2)}) collective-permute-start(bf16[32,1152]{1,0:T(8,128)(2,1)S(1)} %get-tuple-element.8), channel_id=1, source_target_pairs={{128,0},{448,64},{256,128},{64,192},{384,256},{192,320},{0,384},{3... | collective-permute-start | bytes 221192 | tf_op jit(solution)/shard_map/ppermute | solution.py:39
  149.5 3.7 %collective-permute-done.14 = bf16[32,1152]{1,0:T(8,128)(2,1)S(1)} collective-permute-done((bf16[32,1152]{1,0:T(8,128)(2,1)S(1)}, bf16[32,1152]{1,0:T(8,128)(2,1)S(1)}, u32[]{:S(2)}, u32[]{:S(2)}) %collective-permute-start.14) | collective-permute-done | bytes 73760 | tf_op jit(solution)/shard_map/ppermute | solution.py:39
  154.1 0.8 copy.20
  (69 shorter events, 2.3 us)
Async XLA Ops:
  0.6 21.5 %copy-start.21 = (s32[32]{0:T(128)S(1)}, s32[32]{0:T(128)}, u32[]{:S(2)}) copy-start(s32[32]{0:T(128)} %param.7) | copy-start | bytes 388
  2.6 52.5 %copy-start.5 = (bf16[32,1152]{1,0:T(8,128)(2,1)}, bf16[32,1152]{1,0:T(8,128)(2,1)S(1)}, u32[]{:S(2)}) copy-start(bf16[32,1152]{1,0:T(8,128)(2,1)S(1)} %get-tuple-element.3) | copy-start | bytes 221188
  2.7 20.9 %collective-permute-start.5 = (bf16[32,1152]{1,0:T(8,128)(2,1)S(1)}, bf16[32,1152]{1,0:T(8,128)(2,1)S(1)}, u32[]{:S(2)}, u32[]{:S(2)}) collective-permute-start(bf16[32,1152]{1,0:T(8,128)(2,1)S(1)} %get-tuple-element.3), channel_id=1, source_target_pairs={{0,320},{64,256},{128,448},{192,384},{256,64},{320,0},{384,192},{4... | collective-permute-start | bytes 221192 | tf_op jit(solution)/shard_map/ppermute | solution.py:34
  9.4 14.2 %collective-permute-start.4 = (bf16[32,1152]{1,0:T(8,128)(2,1)S(1)}, bf16[32,1152]{1,0:T(8,128)(2,1)S(1)}, u32[]{:S(2)}, u32[]{:S(2)}) collective-permute-start(bf16[32,1152]{1,0:T(8,128)(2,1)S(1)} %get-tuple-element.3), channel_id=1, source_target_pairs={{0,128},{64,448},{128,256},{192,64},{256,384},{320,192},{384,0},{4... | collective-permute-start | bytes 221192 | tf_op jit(solution)/shard_map/ppermute | solution.py:34
  11.6 12.0 %collective-permute-start.3 = (bf16[32,1152]{1,0:T(8,128)(2,1)S(1)}, bf16[32,1152]{1,0:T(8,128)(2,1)S(1)}, u32[]{:S(2)}, u32[]{:S(2)}) collective-permute-start(bf16[32,1152]{1,0:T(8,128)(2,1)S(1)} %get-tuple-element.3), channel_id=1, source_target_pairs={{0,448},{64,128},{128,64},{192,256},{256,192},{320,384},{384,320},... | collective-permute-start | bytes 221192 | tf_op jit(solution)/shard_map/ppermute | solution.py:34
  17.6 22.4 %collective-permute-start.1 = (bf16[256,1152]{1,0:T(8,128)(2,1)S(1)}, bf16[256,1152]{1,0:T(8,128)(2,1)S(1)}, u32[]{:S(2)}, u32[]{:S(2)}) collective-permute-start(bf16[256,1152]{1,0:T(8,128)(2,1)S(1)} %get-tuple-element.5), channel_id=1, source_target_pairs={{0,64},{64,0},{1,65},{65,1},{2,66},{66,2},{3,67},{67,3},{4,68},{68... | collective-permute-start | bytes 1769480 | tf_op jit(solution)/shard_map/ppermute | solution.py:21
  20.2 41.2 %collective-permute-start = (bf16[256,1152]{1,0:T(8,128)(2,1)S(1)}, bf16[256,1152]{1,0:T(8,128)(2,1)S(1)}, u32[]{:S(2)}, u32[]{:S(2)}) collective-permute-start(bf16[256,1152]{1,0:T(8,128)(2,1)S(1)} %get-tuple-element.5), channel_id=1, source_target_pairs={{0,8},{8,0},{1,9},{9,1},{2,10},{10,2},{3,11},{11,3},{4,12},{12,4},... | collective-permute-start | bytes 1769480 | tf_op jit(solution)/shard_map/ppermute | solution.py:21
  23.6 37.9 %copy-start.7 = (bf16[32,1152]{1,0:T(8,128)(2,1)}, bf16[32,1152]{1,0:T(8,128)(2,1)S(1)}, u32[]{:S(2)}) copy-start(bf16[32,1152]{1,0:T(8,128)(2,1)S(1)} %collective-permute-done.5) | copy-start | bytes 221188
  23.6 37.9 %copy-start.9 = (bf16[32,1152]{1,0:T(8,128)(2,1)}, bf16[32,1152]{1,0:T(8,128)(2,1)S(1)}, u32[]{:S(2)}) copy-start(bf16[32,1152]{1,0:T(8,128)(2,1)S(1)} %collective-permute-done.4) | copy-start | bytes 221188
  23.6 37.8 %copy-start.11 = (bf16[32,1152]{1,0:T(8,128)(2,1)}, bf16[32,1152]{1,0:T(8,128)(2,1)S(1)}, u32[]{:S(2)}) copy-start(bf16[32,1152]{1,0:T(8,128)(2,1)S(1)} %collective-permute-done.3) | copy-start | bytes 221188
  23.7 31.5 %collective-permute-start.7 = (bf16[128,1152]{1,0:T(8,128)(2,1)S(1)}, bf16[128,1152]{1,0:T(8,128)(2,1)S(1)}, u32[]{:S(2)}, u32[]{:S(2)}) collective-permute-start(bf16[128,1152]{1,0:T(8,128)(2,1)S(1)} %pad_maximum_fusion.1), channel_id=1, source_target_pairs={{0,16},{1,49},{16,32},{17,1},{32,48},{33,17},{48,0},{49,33},{2,18}... | collective-permute-start | bytes 884744 | tf_op jit(solution)/shard_map/ppermute | solution.py:34
  29.8 25.3 %collective-permute-start.6 = (bf16[128,1152]{1,0:T(8,128)(2,1)S(1)}, bf16[128,1152]{1,0:T(8,128)(2,1)S(1)}, u32[]{:S(2)}, u32[]{:S(2)}) collective-permute-start(bf16[128,1152]{1,0:T(8,128)(2,1)S(1)} %pad_maximum_fusion.1), channel_id=1, source_target_pairs={{0,49},{1,16},{16,1},{17,32},{32,17},{33,48},{48,33},{49,0},{2,51}... | collective-permute-start | bytes 884744 | tf_op jit(solution)/shard_map/ppermute | solution.py:34
  37.1 24.3 %collective-permute-start.8 = (bf16[128,1152]{1,0:T(8,128)(2,1)S(1)}, bf16[128,1152]{1,0:T(8,128)(2,1)S(1)}, u32[]{:S(2)}, u32[]{:S(2)}) collective-permute-start(bf16[128,1152]{1,0:T(8,128)(2,1)S(1)} %pad_maximum_fusion.1), channel_id=1, source_target_pairs={{0,33},{1,32},{16,49},{17,48},{32,1},{33,0},{48,17},{49,16},{2,35}... | collective-permute-start | bytes 884744 | tf_op jit(solution)/shard_map/ppermute | solution.py:34
  40.0 23.3 %collective-permute-start.2 = (bf16[256,1152]{1,0:T(8,128)(2,1)S(1)}, bf16[256,1152]{1,0:T(8,128)(2,1)S(1)}, u32[]{:S(2)}, u32[]{:S(2)}) collective-permute-start(bf16[256,1152]{1,0:T(8,128)(2,1)S(1)} %collective-permute-done.1), channel_id=1, source_target_pairs={{0,8},{8,0},{1,9},{9,1},{2,10},{10,2},{3,11},{11,3},{4,12},{12,4},... | collective-permute-start | bytes 1769480 | tf_op jit(solution)/shard_map/ppermute | solution.py:21
  61.4 1.0 copy-start.19
  62.5 0.8 copy-start.4
  65.5 3.0 %copy-start.14 = (bf16[1024,128]{0,1:T(8,128)(2,1)}, bf16[1024,128]{0,1:T(8,128)(2,1)S(1)}, u32[]{:S(2)}) copy-start(bf16[1024,128]{0,1:T(8,128)(2,1)S(1)} %fusion.27) | copy-start | bytes 786436
  66.4 2.1 %copy-start.16 = (bf16[1024,128]{0,1:T(8,128)(2,1)}, bf16[1024,128]{0,1:T(8,128)(2,1)S(1)}, u32[]{:S(2)}) copy-start(bf16[1024,128]{0,1:T(8,128)(2,1)S(1)} %fusion.26) | copy-start | bytes 786436
  66.4 1.0 copy-start.6
  66.4 1.0 copy-start.8
  66.4 1.0 copy-start.10
  66.5 1.1 copy-start.12
  67.4 1.1 copy-start.18
  67.5 1.3 copy-start.20
  68.8 3.9 %copy-start.13 = (bf16[1024,128]{0,1:T(8,128)(2,1)}, bf16[1024,128]{0,1:T(8,128)(2,1)S(1)}, u32[]{:S(2)}) copy-start(bf16[1024,128]{0,1:T(8,128)(2,1)S(1)} %fusion.28) | copy-start | bytes 786436
  70.4 2.2 %copy-start = (f32[1024,1152]{1,0:T(8,128)}, f32[1024,1152]{1,0:T(8,128)S(1)}, u32[]{:S(2)}) copy-start(f32[1024,1152]{1,0:T(8,128)S(1)} %fusion.31) | copy-start | bytes 14155780
  72.6 4.9 %collective-permute-start.9 = (bf16[2,256,1152]{2,1,0:T(8,128)(2,1)S(1)}, bf16[2,256,1152]{2,1,0:T(8,128)(2,1)}, u32[]{:S(2)}, u32[]{:S(2)}) collective-permute-start(bf16[2,256,1152]{2,1,0:T(8,128)(2,1)S(1)} %fusion.30), channel_id=1, source_target_pairs={{0,8},{8,0},{1,9},{9,1},{2,10},{10,2},{3,11},{11,3},{4,12},{12,4},... | collective-permute-start | bytes 3538952 | tf_op jit(solution)/shard_map/ppermute | solution.py:21
  80.9 46.3 %all-to-all-start = ((bf16[16,32,1152]{2,1,0:T(8,128)(2,1)}), bf16[16,32,1152]{2,1,0:T(8,128)(2,1)S(1)}, u32[]{:S(2)}, u32[]{:S(2)}) async-start(bf16[16,32,1152]{2,1,0:T(8,128)(2,1)} %bitcast.5), calls=%async_computation | async-start | bytes 2359296 | tf_op jit(solution)/shard_map/all_to_all | solution.py:82
  87.4 2.2 %copy-start.17 = (bf16[1024,128]{0,1:T(8,128)(2,1)S(1)}, bf16[1024,128]{0,1:T(8,128)(2,1)}, u32[]{:S(2)}) copy-start(bf16[1024,128]{0,1:T(8,128)(2,1)} %copy-done.16) | copy-start | bytes 786436
  89.7 1.3 copy-start.15
  92.1 21.8 %collective-permute-start.12 = (bf16[128,1152]{1,0:T(8,128)(2,1)}, bf16[128,1152]{1,0:T(8,128)(2,1)}, u32[]{:S(2)}, u32[]{:S(2)}) collective-permute-start(bf16[128,1152]{1,0:T(8,128)(2,1)} %convolution_convert_fusion), channel_id=1, source_target_pairs={{33,0},{32,1},{49,16},{48,17},{1,32},{0,33},{17,48},{16,49},{35,2}... | collective-permute-start | bytes 884744 | tf_op jit(solution)/shard_map/ppermute | solution.py:39
  99.7 20.3 %collective-permute-start.11 = (bf16[128,1152]{1,0:T(8,128)(2,1)}, bf16[128,1152]{1,0:T(8,128)(2,1)}, u32[]{:S(2)}, u32[]{:S(2)}) collective-permute-start(bf16[128,1152]{1,0:T(8,128)(2,1)} %convolution_convert_fusion.1), channel_id=1, source_target_pairs={{16,0},{49,1},{32,16},{1,17},{48,32},{17,33},{0,48},{33,49},{18,2}... | collective-permute-start | bytes 884744 | tf_op jit(solution)/shard_map/ppermute | solution.py:39
  101.6 22.9 %collective-permute-start.10 = (bf16[128,1152]{1,0:T(8,128)(2,1)}, bf16[128,1152]{1,0:T(8,128)(2,1)}, u32[]{:S(2)}, u32[]{:S(2)}) collective-permute-start(bf16[128,1152]{1,0:T(8,128)(2,1)} %convolution_convert_fusion.2), channel_id=1, source_target_pairs={{49,0},{16,1},{1,16},{32,17},{17,32},{48,33},{33,48},{0,49},{51,2}... | collective-permute-start | bytes 884744 | tf_op jit(solution)/shard_map/ppermute | solution.py:39
  127.2 8.6 %copy-start.3 = (bf16[128,1152]{1,0:T(8,128)(2,1)S(1)}, bf16[128,1152]{1,0:T(8,128)(2,1)}, u32[]{:S(2)}) copy-start(bf16[128,1152]{1,0:T(8,128)(2,1)} %get-tuple-element.9) | copy-start | bytes 884740
  127.2 25.9 %copy-start.1 = (f32[128,1152]{1,0:T(8,128)S(1)}, f32[128,1152]{1,0:T(8,128)}, u32[]{:S(2)}) copy-start(f32[128,1152]{1,0:T(8,128)} %get-tuple-element.10) | copy-start | bytes 1769476
  127.2 25.9 %copy-start.2 = (bf16[32,1152]{1,0:T(8,128)(2,1)S(1)}, bf16[32,1152]{1,0:T(8,128)(2,1)}, u32[]{:S(2)}) copy-start(bf16[32,1152]{1,0:T(8,128)(2,1)} %param.6) | copy-start | bytes 221188
  130.4 23.7 %all-to-all-start.1 = ((bf16[8,32,1152]{2,1,0:T(8,128)(2,1)}), bf16[8,32,1152]{2,1,0:T(8,128)(2,1)S(1)}, u32[]{:S(2)}, u32[]{:S(2)}) async-start(bf16[8,32,1152]{2,1,0:T(8,128)(2,1)} %broadcast_in_dim.2), calls=%async_computation.1 | async-start | bytes 1179648 | tf_op jit(solution)/shard_map/all_to_all | solution.py:87
  135.9 13.4 %collective-permute-start.13 = (bf16[32,1152]{1,0:T(8,128)(2,1)S(1)}, bf16[32,1152]{1,0:T(8,128)(2,1)S(1)}, u32[]{:S(2)}, u32[]{:S(2)}) collective-permute-start(bf16[32,1152]{1,0:T(8,128)(2,1)S(1)} %get-tuple-element.6), channel_id=1, source_target_pairs={{448,0},{128,64},{64,128},{256,192},{192,256},{384,320},{320,384},... | collective-permute-start | bytes 221192 | tf_op jit(solution)/shard_map/ppermute | solution.py:39
  139.4 10.1 %collective-permute-start.15 = (bf16[32,1152]{1,0:T(8,128)(2,1)S(1)}, bf16[32,1152]{1,0:T(8,128)(2,1)S(1)}, u32[]{:S(2)}, u32[]{:S(2)}) collective-permute-start(bf16[32,1152]{1,0:T(8,128)(2,1)S(1)} %get-tuple-element.7), channel_id=1, source_target_pairs={{320,0},{256,64},{448,128},{384,192},{64,256},{0,320},{192,384},{1... | collective-permute-start | bytes 221192 | tf_op jit(solution)/shard_map/ppermute | solution.py:39
  144.8 8.4 %collective-permute-start.14 = (bf16[32,1152]{1,0:T(8,128)(2,1)S(1)}, bf16[32,1152]{1,0:T(8,128)(2,1)S(1)}, u32[]{:S(2)}, u32[]{:S(2)}) collective-permute-start(bf16[32,1152]{1,0:T(8,128)(2,1)S(1)} %get-tuple-element.8), channel_id=1, source_target_pairs={{128,0},{448,64},{256,128},{64,192},{384,256},{192,320},{0,384},{3... | collective-permute-start | bytes 221192 | tf_op jit(solution)/shard_map/ppermute | solution.py:39

commit v3 on v2

v3 whole, which is shorter than its diff:
```python
import jax
import jax.numpy as jnp
from jax import lax
from jax.sharding import Mesh, PartitionSpec as P

epsilon = 1e-06
AXES = ("yh", "yl", "w", "c", "x", "l")
TEXT_GROUP = ("yh", "w")
NARROW = ("x", "l")
BF16, F32 = jnp.bfloat16, jnp.float32


def unit_rows(values):
    as_float = values.astype(F32)
    row_norm = jnp.sqrt(jnp.sum(as_float * as_float, axis=1, keepdims=True) + epsilon)
    return as_float / row_norm, row_norm


def swap(block, axis):
    return lax.ppermute(block, axis, [(0, 1), (1, 0)])


def spread(block, axes):
    count = lax.axis_size(axes)
    copies = jnp.broadcast_to(block[None], (count,) + block.shape)
    return lax.all_to_all(copies, axes, 0, 0, tiled=True).reshape((-1,) + block.shape[1:])


def collect(terms, axes):
    got = lax.all_to_all(terms.astype(BF16), axes, 0, 0, tiled=True)
    return jnp.sum(got.astype(F32), axis=0)


def finish(grad_unit, unit, norm):
    along = jnp.sum(unit * grad_unit, axis=1, keepdims=True)
    return ((grad_unit - unit * along) / norm).astype(BF16)


def local(image_emb, text_emb, positive, log_scale, bias):
    scale = jnp.exp(log_scale[0])
    rows, width = image_emb.shape
    mine = text_emb.shape[0]
    text_unit, text_norm = unit_rows(text_emb)
    texts = spread(text_unit.astype(BF16), TEXT_GROUP)

    image_unit, image_norm = unit_rows(image_emb)
    image_bf = image_unit.astype(BF16)
    beyond = swap(image_bf, "yl")
    images = jnp.concatenate([image_bf, swap(image_bf, "c"), beyond, swap(beyond, "c")], axis=0)

    wanted = positive - lax.axis_index(("yh", "yl", "w", "c")) * rows
    slot = lax.axis_index(TEXT_GROUP) * mine
    wanted = lax.dynamic_update_slice_in_dim(jnp.full((texts.shape[0],), -1, jnp.int32), wanted, slot, 0)
    hit = (jnp.arange(images.shape[0], dtype=jnp.int32)[:, None] == wanted[None, :]).astype(F32)

    cosine = lax.dot_general(images, texts, (((1,), (1,)), ((), ())), preferred_element_type=F32)
    grad = (jax.nn.sigmoid(scale * cosine + bias[0]) - hit).astype(BF16)
    image_terms = jnp.dot(grad, texts, preferred_element_type=F32).reshape(2, 2, rows, width)
    text_terms = lax.dot_general(grad, images, (((0,), (0,)), ((), ())), preferred_element_type=F32)

    pairs = image_terms[:, 0] + swap(image_terms[:, 1].astype(BF16), "c").astype(F32)
    pairs = pairs.reshape(2, 8, rows // 8, width).transpose(1, 0, 2, 3)
    part_terms = collect(pairs, NARROW)
    image_sum = scale * (part_terms[0] + swap(part_terms[1].astype(BF16), "yl").astype(F32))
    own = lax.axis_index(NARROW) * (rows // 8)
    part = lax.dynamic_slice_in_dim(image_unit, own, rows // 8, 0)
    part_norm = lax.dynamic_slice_in_dim(image_norm, own, rows // 8, 0)
    grad_image = spread(finish(image_sum, part, part_norm), NARROW)

    text_sum = collect(text_terms.reshape(16, mine, width), TEXT_GROUP)
    grad_text = finish(scale * text_sum, text_unit, text_norm)
    return grad_image, grad_text


def solution(mesh):
    fine = Mesh(mesh.devices.reshape(4, 2, 4, 2, 4, 2), AXES)
    dp = ("yh", "yl", "w", "c")
    in_specs = (P(dp, None), P(AXES, None), P(AXES), P(), P())
    out_specs = (P(dp, None), P(AXES, None))
    return jax.shard_map(local, mesh=fine, in_specs=in_specs, out_specs=out_specs, check_vma=False)
```

time: 156 us -> 160 us (1.026)
  the two profiles are of different devices: /device:TPU:10 before, /device:TPU:48 now
where the time goes in v3:
time: 160 us; the launch traced here: 159 us
  waiting for transfers between devices  91.5 us (57%)
  starting transfers between devices  45.7 us (29%)
  matrix products  9.09 us (6%)
  other arithmetic  6.11 us (4%)
  local copies, waits for them, and re-layouts  4.86 us (3%)
  between operations  2.18 us (1%)
    ppermute x5, waiting for transfers between devices, swap(): return lax.ppermute(block, axis, [(0, 1), (1, 0)])  63.2 us
    all_to_all x2, waiting for transfers between devices, collect(): got = lax.all_to_all(terms.astype(BF16), axes, 0, 0, tiled=True)  20.4 us
    all_to_all x2, starting transfers between devices, spread(): lax.all_to_all(copies, axes, 0, 0, tiled=True)  19.1 us
    all_to_all x2, starting transfers between devices, collect(): got = lax.all_to_all(terms.astype(BF16), axes, 0, 0, tiled=True)  15.3 us
    ppermute x5, starting transfers between devices, swap(): return lax.ppermute(block, axis, [(0, 1), (1, 0)])  11.2 us
    all_to_all x2, waiting for transfers between devices, spread(): lax.all_to_all(copies, axes, 0, 0, tiled=True)  7.85 us
    dot_general x1, matrix products, local(): lax.dot_general(grad, images, (((0,), (0,)), ((), ())), preferred_element...  4.2 us
    dot_general x1, matrix products, local(): lax.dot_general(images, texts, (((1,), (1,)), ((), ())), preferred_elemen...  3.37 us
  transfers between devices with their start and end apart: 9, of which 7 were waited for; matrix products, arithmetic and copies ran while one was open for 5% of the time, Pallas kernels for 0%

profile of v3, /device:TPU:48, one launch (start us, length us, event | category | flops | bytes accessed | tf_op | source)
XLA Modules:
  0.0 159.4 jit_solution(8844267853319226208)
XLA Ops:
  0.6 0.0 copy-start
  0.6 1.1 fusion.4
  1.7 1.0 fusion.10
  2.7 1.1 broadcast_in_dim.4
  3.8 15.6 %all-to-all-start = ((bf16[16,32,1152]{2,1,0:T(8,128)(2,1)}), bf16[16,32,1152]{2,1,0:T(8,128)(2,1)S(1)}, u32[]{:S(2)}, u32[]{:S(2)}) async-start(bf16[16,32,1152]{2,1,0:T(8,128)(2,1)} %broadcast_in_dim.4), calls=%async_computation | async-start | bytes 2359296 | tf_op jit(solution)/shard_map/all_to_all | solution.py:26
  19.4 0.0 copy-done
  19.4 0.2 fusion.2
  19.6 0.2 fusion.11
  19.8 0.0 copy-start.5
  19.8 2.6 %collective-permute-start.1 = (bf16[256,1152]{1,0:T(8,128)(2,1)S(1)}, bf16[256,1152]{1,0:T(8,128)(2,1)}, u32[]{:S(2)}, u32[]{:S(2)}) collective-permute-start(bf16[256,1152]{1,0:T(8,128)(2,1)S(1)} %get-tuple-element.2), channel_id=1, source_target_pairs={{0,64},{64,0},{1,65},{65,1},{2,66},{66,2},{3,67},{67,3},{4,68},{68... | collective-permute-start | bytes 1769480 | tf_op jit(solution)/shard_map/ppermute | solution.py:20
  22.4 1.9 %collective-permute-start = (bf16[256,1152]{1,0:T(8,128)(2,1)S(1)}, bf16[256,1152]{1,0:T(8,128)(2,1)}, u32[]{:S(2)}, u32[]{:S(2)}) collective-permute-start(bf16[256,1152]{1,0:T(8,128)(2,1)S(1)} %get-tuple-element.2), channel_id=1, source_target_pairs={{0,8},{8,0},{1,9},{9,1},{2,10},{10,2},{3,11},{11,3},{4,12},{12,4},... | collective-permute-start | bytes 1769480 | tf_op jit(solution)/shard_map/ppermute | solution.py:20
  24.4 35.9 %collective-permute-done.1 = bf16[256,1152]{1,0:T(8,128)(2,1)} collective-permute-done((bf16[256,1152]{1,0:T(8,128)(2,1)S(1)}, bf16[256,1152]{1,0:T(8,128)(2,1)}, u32[]{:S(2)}, u32[]{:S(2)}) %collective-permute-start.1) | collective-permute-done | bytes 589856 | tf_op jit(solution)/shard_map/ppermute | solution.py:20
  60.3 1.9 %collective-permute-start.2 = (bf16[256,1152]{1,0:T(8,128)(2,1)}, bf16[256,1152]{1,0:T(8,128)(2,1)}, u32[]{:S(2)}, u32[]{:S(2)}) collective-permute-start(bf16[256,1152]{1,0:T(8,128)(2,1)} %collective-permute-done.1), channel_id=1, source_target_pairs={{0,8},{8,0},{1,9},{9,1},{2,10},{10,2},{3,11},{11,3},{4,12},{12,4},... | collective-permute-start | bytes 1769480 | tf_op jit(solution)/shard_map/ppermute | solution.py:20
  63.5 0.0 copy-done.6
  63.6 0.1 subtract_dynamic-update-slice_fusion
  63.7 0.0 collective-permute-done
  63.7 0.8 collective-permute-done.2
  64.5 0.0 all-to-all-done
  64.5 3.4 %subtract_convert_fusion = bf16[1024,512]{1,0:T(8,128)(2,1)S(1)} fusion(bf16[512,1152]{1,0:T(8,128)(2,1)S(1)} %bitcast.41, s32[512]{0:T(512)S(1)} %subtract_dynamic-update-slice_fusion, f32[]{:T(128)} %bitcast.40, f32[]{:T(128)} %bitcast, bf16[256,1152]{1,0:T(8,128)(2,1)} %collective-permute-done.2, bf16[256,1152]{1,0:T(8,128)(2,1)} %collective-permute-done.1, ...), kind=kOutput, calls=%fused_computation.8 | convolution fusion | flops 1222115328 | bytes 4589576 | tf_op jit(solution)/shard_map/dot_general | solution.py:56
  67.9 0.0 copy-done.5
  67.9 0.0 copy-start.3
  67.9 1.5 fusion.12
  69.4 0.0 copy-done.3
  69.4 0.1 fusion.3
  69.6 2.0 %collective-permute-start.3 = (bf16[2,256,1152]{2,1,0:T(8,128)(2,1)S(1)}, bf16[2,256,1152]{2,1,0:T(8,128)(2,1)S(1)}, u32[]{:S(2)}, u32[]{:S(2)}) collective-permute-start(bf16[2,256,1152]{2,1,0:T(8,128)(2,1)S(1)} %fusion.3), channel_id=1, source_target_pairs={{0,8},{8,0},{1,9},{9,1},{2,10},{10,2},{3,11},{11,3},{4,12},{12,4},... | collective-permute-start | bytes 3538952 | tf_op jit(solution)/shard_map/ppermute | solution.py:20
  71.6 2.7 %collective-permute-done.3 = bf16[2,256,1152]{2,1,0:T(8,128)(2,1)S(1)} collective-permute-done((bf16[2,256,1152]{2,1,0:T(8,128)(2,1)S(1)}, bf16[2,256,1152]{2,1,0:T(8,128)(2,1)S(1)}, u32[]{:S(2)}, u32[]{:S(2)}) %collective-permute-start.3) | collective-permute-done | bytes 1179680 | tf_op jit(solution)/shard_map/ppermute | solution.py:20
  74.3 0.2 fusion.1
  74.5 1.1 copy.13
  75.7 4.3 %all-to-all-start.1 = ((bf16[8,2,32,1152]{3,2,1,0:T(8,128)(2,1)}), bf16[8,2,32,1152]{3,2,1,0:T(8,128)(2,1)S(1)}, u32[]{:S(2)}, u32[]{:S(2)}) async-start(bf16[8,2,32,1152]{3,2,1,0:T(8,128)(2,1)} %bitcast.39), calls=%async_computation.1 | async-start | bytes 2359296 | tf_op jit(solution)/shard_map/all_to_all | solution.py:30
  80.0 4.2 %convolution_convert_fusion = bf16[512,1152]{1,0:T(8,128)(2,1)} fusion(bf16[1024,512]{1,0:T(8,128)(2,1)S(1)} %copy-done.4, bf16[256,1152]{1,0:T(8,128)(2,1)} %collective-permute-done.2, bf16[256,1152]{1,0:T(8,128)(2,1)} %collective-permute-done.1, bf16[256,1152]{1,0:T(8,128)(2,1)} %collective-permute-done, bf16[256,1152]{1,0:T(8,128)(2,1)} %copy-done.5), kind=kOutput, calls=%fused_computation | convolution fusion | flops 1217986560 | bytes 4587520 | tf_op jit(solution)/shard_map/dot_general | solution.py:59
  84.2 13.2 %all-to-all-done.1 = bf16[8,2,32,1152]{3,2,1,0:T(8,128)(2,1)S(1)} async-done(((bf16[8,2,32,1152]{3,2,1,0:T(8,128)(2,1)}), bf16[8,2,32,1152]{3,2,1,0:T(8,128)(2,1)S(1)}, u32[]{:S(2)}, u32[]{:S(2)}) %all-to-all-start.1) | async-done | bytes 1179680 | tf_op jit(solution)/shard_map/all_to_all | solution.py:30
  97.4 11.0 %all-to-all-start.3 = ((bf16[16,32,1152]{2,1,0:T(8,128)(2,1)}), bf16[16,32,1152]{2,1,0:T(8,128)(2,1)S(1)}, u32[]{:S(2)}, u32[]{:S(2)}) async-start(bf16[16,32,1152]{2,1,0:T(8,128)(2,1)} %bitcast.45), calls=%async_computation.3 | async-start | bytes 2359296 | tf_op jit(solution)/shard_map/all_to_all | solution.py:30
  108.4 0.2 convert_reduce_fusion.1
  108.6 0.0 copy-start.1
  108.6 0.7 copy-done.1
  109.3 2.8 %collective-permute-start.4 = (bf16[32,1152]{1,0:T(8,128)(2,1)S(1)}, bf16[32,1152]{1,0:T(8,128)(2,1)S(1)}, u32[]{:S(2)}, u32[]{:S(2)}) collective-permute-start(bf16[32,1152]{1,0:T(8,128)(2,1)S(1)} %fusion.7), channel_id=1, source_target_pairs={{0,64},{64,0},{1,65},{65,1},{2,66},{66,2},{3,67},{67,3},{4,68},{68... | collective-permute-start | bytes 221192 | tf_op jit(solution)/shard_map/ppermute | solution.py:20
  112.1 0.1 dynamic-slice.3
  112.2 23.8 %collective-permute-done.4 = bf16[32,1152]{1,0:T(8,128)(2,1)S(1)} collective-permute-done((bf16[32,1152]{1,0:T(8,128)(2,1)S(1)}, bf16[32,1152]{1,0:T(8,128)(2,1)S(1)}, u32[]{:S(2)}, u32[]{:S(2)}) %collective-permute-start.4) | collective-permute-done | bytes 73760 | tf_op jit(solution)/shard_map/ppermute | solution.py:20
  135.9 1.0 multiply_reduce_fusion.1
  137.0 1.0 divide_convert_fusion.1
  138.0 7.2 %all-to-all-done.3 = bf16[16,32,1152]{2,1,0:T(8,128)(2,1)S(1)} async-done(((bf16[16,32,1152]{2,1,0:T(8,128)(2,1)}), bf16[16,32,1152]{2,1,0:T(8,128)(2,1)S(1)}, u32[]{:S(2)}, u32[]{:S(2)}) %all-to-all-start.3) | async-done | bytes 1179680 | tf_op jit(solution)/shard_map/all_to_all | solution.py:30
  145.2 0.9 broadcast_in_dim.5
  146.0 3.5 %all-to-all-start.2 = ((bf16[8,32,1152]{2,1,0:T(8,128)(2,1)}), bf16[8,32,1152]{2,1,0:T(8,128)(2,1)S(1)}, u32[]{:S(2)}, u32[]{:S(2)}) async-start(bf16[8,32,1152]{2,1,0:T(8,128)(2,1)} %broadcast_in_dim.5), calls=%async_computation.2 | async-start | bytes 1179648 | tf_op jit(solution)/shard_map/all_to_all | solution.py:26
  149.6 0.2 convert_reduce_fusion
  149.8 0.2 multiply_reduce_fusion
  150.0 0.7 divide_convert_fusion
  150.7 7.8 %all-to-all-done.2 = bf16[8,32,1152]{2,1,0:T(8,128)(2,1)S(1)} async-done(((bf16[8,32,1152]{2,1,0:T(8,128)(2,1)}), bf16[8,32,1152]{2,1,0:T(8,128)(2,1)S(1)}, u32[]{:S(2)}, u32[]{:S(2)}) %all-to-all-start.2) | async-done | bytes 589856 | tf_op jit(solution)/shard_map/all_to_all | solution.py:26
  158.6 0.8 copy.18
  (9 shorter events, 0.0 us)
Async XLA Ops:
  0.6 18.8 %copy-start = (bf16[256,1152]{1,0:T(8,128)(2,1)S(1)}, bf16[256,1152]{1,0:T(8,128)(2,1)}, u32[]{:S(2)}) copy-start(bf16[256,1152]{1,0:T(8,128)(2,1)} %param.5) | copy-start | bytes 1769476
  3.8 59.7 %copy-start.6 = (s32[32]{0:T(128)S(1)}, s32[32]{0:T(128)}, u32[]{:S(2)}) copy-start(s32[32]{0:T(128)} %param.7) | copy-start | bytes 388
  3.8 60.7 %all-to-all-start = ((bf16[16,32,1152]{2,1,0:T(8,128)(2,1)}), bf16[16,32,1152]{2,1,0:T(8,128)(2,1)S(1)}, u32[]{:S(2)}, u32[]{:S(2)}) async-start(bf16[16,32,1152]{2,1,0:T(8,128)(2,1)} %broadcast_in_dim.4), calls=%async_computation | async-start | bytes 2359296 | tf_op jit(solution)/shard_map/all_to_all | solution.py:26
  19.8 48.0 %copy-start.5 = (bf16[256,1152]{1,0:T(8,128)(2,1)}, bf16[256,1152]{1,0:T(8,128)(2,1)S(1)}, u32[]{:S(2)}) copy-start(bf16[256,1152]{1,0:T(8,128)(2,1)S(1)} %get-tuple-element.2) | copy-start | bytes 1769476
  19.8 40.4 %collective-permute-start.1 = (bf16[256,1152]{1,0:T(8,128)(2,1)S(1)}, bf16[256,1152]{1,0:T(8,128)(2,1)}, u32[]{:S(2)}, u32[]{:S(2)}) collective-permute-start(bf16[256,1152]{1,0:T(8,128)(2,1)S(1)} %get-tuple-element.2), channel_id=1, source_target_pairs={{0,64},{64,0},{1,65},{65,1},{2,66},{66,2},{3,67},{67,3},{4,68},{68... | collective-permute-start | bytes 1769480 | tf_op jit(solution)/shard_map/ppermute | solution.py:20
  22.4 41.2 %collective-permute-start = (bf16[256,1152]{1,0:T(8,128)(2,1)S(1)}, bf16[256,1152]{1,0:T(8,128)(2,1)}, u32[]{:S(2)}, u32[]{:S(2)}) collective-permute-start(bf16[256,1152]{1,0:T(8,128)(2,1)S(1)} %get-tuple-element.2), channel_id=1, source_target_pairs={{0,8},{8,0},{1,9},{9,1},{2,10},{10,2},{3,11},{11,3},{4,12},{12,4},... | collective-permute-start | bytes 1769480 | tf_op jit(solution)/shard_map/ppermute | solution.py:20
  60.3 4.2 %collective-permute-start.2 = (bf16[256,1152]{1,0:T(8,128)(2,1)}, bf16[256,1152]{1,0:T(8,128)(2,1)}, u32[]{:S(2)}, u32[]{:S(2)}) collective-permute-start(bf16[256,1152]{1,0:T(8,128)(2,1)} %collective-permute-done.1), channel_id=1, source_target_pairs={{0,8},{8,0},{1,9},{9,1},{2,10},{10,2},{3,11},{11,3},{4,12},{12,4},... | collective-permute-start | bytes 1769480 | tf_op jit(solution)/shard_map/ppermute | solution.py:20
  67.9 1.5 copy-start.3
  69.6 4.7 %collective-permute-start.3 = (bf16[2,256,1152]{2,1,0:T(8,128)(2,1)S(1)}, bf16[2,256,1152]{2,1,0:T(8,128)(2,1)S(1)}, u32[]{:S(2)}, u32[]{:S(2)}) collective-permute-start(bf16[2,256,1152]{2,1,0:T(8,128)(2,1)S(1)} %fusion.3), channel_id=1, source_target_pairs={{0,8},{8,0},{1,9},{9,1},{2,10},{10,2},{3,11},{11,3},{4,12},{12,4},... | collective-permute-start | bytes 3538952 | tf_op jit(solution)/shard_map/ppermute | solution.py:20
  74.5 5.5 %copy-start.4 = (bf16[1024,512]{1,0:T(8,128)(2,1)S(1)}, bf16[1024,512]{1,0:T(8,128)(2,1)}, u32[]{:S(2)}) copy-start(bf16[1024,512]{1,0:T(8,128)(2,1)} %copy-done.3) | copy-start | bytes 3145732
  75.7 21.8 %all-to-all-start.1 = ((bf16[8,2,32,1152]{3,2,1,0:T(8,128)(2,1)}), bf16[8,2,32,1152]{3,2,1,0:T(8,128)(2,1)S(1)}, u32[]{:S(2)}, u32[]{:S(2)}) async-start(bf16[8,2,32,1152]{3,2,1,0:T(8,128)(2,1)} %bitcast.39), calls=%async_computation.1 | async-start | bytes 2359296 | tf_op jit(solution)/shard_map/all_to_all | solution.py:30
  97.4 47.8 %all-to-all-start.3 = ((bf16[16,32,1152]{2,1,0:T(8,128)(2,1)}), bf16[16,32,1152]{2,1,0:T(8,128)(2,1)S(1)}, u32[]{:S(2)}, u32[]{:S(2)}) async-start(bf16[16,32,1152]{2,1,0:T(8,128)(2,1)} %bitcast.45), calls=%async_computation.3 | async-start | bytes 2359296 | tf_op jit(solution)/shard_map/all_to_all | solution.py:30
  108.6 0.7 copy-start.1
  109.3 40.5 %copy-start.2 = (bf16[32,1152]{1,0:T(8,128)(2,1)S(1)}, bf16[32,1152]{1,0:T(8,128)(2,1)}, u32[]{:S(2)}) copy-start(bf16[32,1152]{1,0:T(8,128)(2,1)} %param.6) | copy-start | bytes 221188
  109.3 26.6 %collective-permute-start.4 = (bf16[32,1152]{1,0:T(8,128)(2,1)S(1)}, bf16[32,1152]{1,0:T(8,128)(2,1)S(1)}, u32[]{:S(2)}, u32[]{:S(2)}) collective-permute-start(bf16[32,1152]{1,0:T(8,128)(2,1)S(1)} %fusion.7), channel_id=1, source_target_pairs={{0,64},{64,0},{1,65},{65,1},{2,66},{66,2},{3,67},{67,3},{4,68},{68... | collective-permute-start | bytes 221192 | tf_op jit(solution)/shard_map/ppermute | solution.py:20
  146.0 12.5 %all-to-all-start.2 = ((bf16[8,32,1152]{2,1,0:T(8,128)(2,1)}), bf16[8,32,1152]{2,1,0:T(8,128)(2,1)S(1)}, u32[]{:S(2)}, u32[]{:S(2)}) async-start(bf16[8,32,1152]{2,1,0:T(8,128)(2,1)} %broadcast_in_dim.5), calls=%async_computation.2 | async-start | bytes 1179648 | tf_op jit(solution)/shard_map/all_to_all | solution.py:26

commit v4 on v3

--- a/solution.py
+++ b/solution.py
@@ -5,7 +5,8 @@
 
 epsilon = 1e-06
 AXES = ("yh", "yl", "w", "c", "x", "l")
-TEXT_GROUP = ("yh", "w")
+Z = ("w", "l")
+DISTANCES = (3, 2, 1)
 NARROW = ("x", "l")
 BF16, F32 = jnp.bfloat16, jnp.float32
 
@@ -18,6 +19,24 @@
 
 def swap(block, axis):
     return lax.ppermute(block, axis, [(0, 1), (1, 0)])
+
+
+def route(axes, distance):
+    count = lax.axis_size(axes)
+    pairs = []
+    for i in range(count):
+        sign = 1 if (i + distance) % 2 == 0 else -1
+        pairs.append((i, (i + sign * distance) % count))
+    return pairs
+
+
+def fan_out(block, axes, distance):
+    return lax.ppermute(block, axes, route(axes, distance))
+
+
+def fan_in(terms, axes, distance):
+    back = [(target, source) for source, target in route(axes, distance)]
+    return lax.ppermute(terms, axes, back)
 
 
 def spread(block, axes):
@@ -41,7 +60,8 @@
     rows, width = image_emb.shape
     mine = text_emb.shape[0]
     text_unit, text_norm = unit_rows(text_emb)
-    texts = spread(text_unit.astype(BF16), TEXT_GROUP)
+    along_y = spread(text_unit.astype(BF16), "yh")
+    blocks = [along_y] + [fan_out(along_y, Z, d) for d in DISTANCES]
 
     image_unit, image_norm = unit_rows(image_emb)
     image_bf = image_unit.astype(BF16)
@@ -49,25 +69,33 @@
     images = jnp.concatenate([image_bf, swap(image_bf, "c"), beyond, swap(beyond, "c")], axis=0)
 
     wanted = positive - lax.axis_index(("yh", "yl", "w", "c")) * rows
-    slot = lax.axis_index(TEXT_GROUP) * mine
-    wanted = lax.dynamic_update_slice_in_dim(jnp.full((texts.shape[0],), -1, jnp.int32), wanted, slot, 0)
+    slot = lax.axis_index("yh") * mine
+    wanted = lax.dynamic_update_slice_in_dim(jnp.full((along_y.shape[0],), -1, jnp.int32), wanted, slot, 0)
     hit = (jnp.arange(images.shape[0], dtype=jnp.int32)[:, None] == wanted[None, :]).astype(F32)
 
-    cosine = lax.dot_general(images, texts, (((1,), (1,)), ((), ())), preferred_element_type=F32)
-    grad = (jax.nn.sigmoid(scale * cosine + bias[0]) - hit).astype(BF16)
-    image_terms = jnp.dot(grad, texts, preferred_element_type=F32).reshape(2, 2, rows, width)
-    text_terms = lax.dot_general(grad, images, (((0,), (0,)), ((), ())), preferred_element_type=F32)
+    grads, terms = [], []
+    for k, block in enumerate(blocks):
+        cosine = lax.dot_general(images, block, (((1,), (1,)), ((), ())), preferred_element_type=F32)
+        grad = jax.nn.sigmoid(scale * cosine + bias[0])
+        grad = (grad - hit if k == 0 else grad).astype(BF16)
+        term = lax.dot_general(grad, images, (((0,), (0,)), ((), ())), preferred_element_type=F32)
+        terms.append(term if k == 0 else fan_in(term.astype(BF16), Z, DISTANCES[k - 1]))
+        grads.append(grad)
+    image_terms = jnp.dot(jnp.concatenate(grads, axis=1), jnp.concatenate(blocks, axis=0), preferred_element_type=F32)
+    image_terms = image_terms.reshape(2, 2, rows, width)
 
     pairs = image_terms[:, 0] + swap(image_terms[:, 1].astype(BF16), "c").astype(F32)
     pairs = pairs.reshape(2, 8, rows // 8, width).transpose(1, 0, 2, 3)
     part_terms = collect(pairs, NARROW)
+    part_terms, terms = lax.optimization_barrier((part_terms, terms))
     image_sum = scale * (part_terms[0] + swap(part_terms[1].astype(BF16), "yl").astype(F32))
     own = lax.axis_index(NARROW) * (rows // 8)
     part = lax.dynamic_slice_in_dim(image_unit, own, rows // 8, 0)
     part_norm = lax.dynamic_slice_in_dim(image_norm, own, rows // 8, 0)
     grad_image = spread(finish(image_sum, part, part_norm), NARROW)
 
-    text_sum = collect(text_terms.reshape(16, mine, width), TEXT_GROUP)
+    text_sum = sum(term.astype(F32) for term in terms)
+    text_sum = collect(text_sum.reshape(4, mine, width), "yh")
     grad_text = finish(scale * text_sum, text_unit, text_norm)
     return grad_image, grad_text
 

time: 160 us -> 165 us (1.031)
  the two profiles are of different devices: /device:TPU:48 before, /device:TPU:56 now
where the time goes in v4:
time: 165 us; the launch traced here: 162 us
  starting transfers between devices  71.4 us (43%)
  waiting for transfers between devices  59 us (36%)
  matrix products  13.4 us (8%)
  other arithmetic  10.9 us (7%)
  local copies, waits for them, and re-layouts  4.62 us (3%)
  between operations  2.33 us (1%)
    ppermute x3, starting transfers between devices, fan_out(): return lax.ppermute(block, axes, route(axes, distance))  18 us
    all_to_all x2, starting transfers between devices, spread(): lax.all_to_all(copies, axes, 0, 0, tiled=True)  14.7 us
    ppermute x5, starting transfers between devices, swap(): return lax.ppermute(block, axis, [(0, 1), (1, 0)])  14.7 us
    ppermute x5, waiting for transfers between devices, swap(): return lax.ppermute(block, axis, [(0, 1), (1, 0)])  14.4 us
    all_to_all x2, waiting for transfers between devices, spread(): lax.all_to_all(copies, axes, 0, 0, tiled=True)  14.1 us
    ppermute x3, starting transfers between devices, fan_in(): return lax.ppermute(terms, axes, back)  12.6 us
    all_to_all x2, waiting for transfers between devices, collect(): got = lax.all_to_all(terms.astype(BF16), axes, 0, 0, tiled=True)  12.5 us
    all_to_all x2, starting transfers between devices, collect(): got = lax.all_to_all(terms.astype(BF16), axes, 0, 0, tiled=True)  11.4 us
  transfers between devices with their start and end apart: 15, of which 9 were waited for; matrix products, arithmetic and copies ran while one was open for 11% of the time, Pallas kernels for 0%

profile of v4, /device:TPU:56, one launch (start us, length us, event | category | flops | bytes accessed | tf_op | source)
XLA Modules:
  0.0 161.6 jit_solution(12417828236752323899)
XLA Ops:
  0.7 1.3 fusion.27
  2.0 2.3 %fusion.49 = (bf16[256,1152]{1,0:T(8,128)(2,1)S(1)}, f32[256,1152]{1,0:T(8,128)}) fusion(f32[256]{0:T(256)S(1)} %add_sqrt_fusion, bf16[256,1152]{1,0:T(8,128)(2,1)} %param.5), kind=kLoop, calls=%fused_computation.76 | loop fusion | flops 884736 | bytes 2360320 | tf_op jit(solution)/shard_map/convert_element_type | solution.py:67
  4.3 3.2 %collective-permute-start.1 = (bf16[256,1152]{1,0:T(8,128)(2,1)S(1)}, bf16[256,1152]{1,0:T(8,128)(2,1)S(1)}, u32[]{:S(2)}, u32[]{:S(2)}) collective-permute-start(bf16[256,1152]{1,0:T(8,128)(2,1)S(1)} %get-tuple-element.12), channel_id=1, source_target_pairs={{0,64},{64,0},{1,65},{65,1},{2,66},{66,2},{3,67},{67,3},{4,68},{68... | collective-permute-start | bytes 1769480 | tf_op jit(solution)/shard_map/ppermute | solution.py:21
  7.5 1.9 %collective-permute-start = (bf16[256,1152]{1,0:T(8,128)(2,1)S(1)}, bf16[256,1152]{1,0:T(8,128)(2,1)S(1)}, u32[]{:S(2)}, u32[]{:S(2)}) collective-permute-start(bf16[256,1152]{1,0:T(8,128)(2,1)S(1)} %get-tuple-element.12), channel_id=1, source_target_pairs={{0,8},{8,0},{1,9},{9,1},{2,10},{10,2},{3,11},{11,3},{4,12},{12,4},... | collective-permute-start | bytes 1769480 | tf_op jit(solution)/shard_map/ppermute | solution.py:21
  9.6 11.6 %collective-permute-done.1 = bf16[256,1152]{1,0:T(8,128)(2,1)S(1)} collective-permute-done((bf16[256,1152]{1,0:T(8,128)(2,1)S(1)}, bf16[256,1152]{1,0:T(8,128)(2,1)S(1)}, u32[]{:S(2)}, u32[]{:S(2)}) %collective-permute-start.1) | collective-permute-done | bytes 589856 | tf_op jit(solution)/shard_map/ppermute | solution.py:21
  21.2 1.9 %collective-permute-start.2 = (bf16[256,1152]{1,0:T(8,128)(2,1)S(1)}, bf16[256,1152]{1,0:T(8,128)(2,1)}, u32[]{:S(2)}, u32[]{:S(2)}) collective-permute-start(bf16[256,1152]{1,0:T(8,128)(2,1)S(1)} %collective-permute-done.1), channel_id=1, source_target_pairs={{0,8},{8,0},{1,9},{9,1},{2,10},{10,2},{3,11},{11,3},{4,12},{12,4},... | collective-permute-start | bytes 1769480 | tf_op jit(solution)/shard_map/ppermute | solution.py:21
  23.2 0.7 broadcast_in_dim.4
  24.0 7.0 %all-to-all-start = ((bf16[4,32,1152]{2,1,0:T(8,128)(2,1)}), bf16[4,32,1152]{2,1,0:T(8,128)(2,1)}, u32[]{:S(2)}, u32[]{:S(2)}) async-start(bf16[4,32,1152]{2,1,0:T(8,128)(2,1)} %broadcast_in_dim.4), calls=%async_computation | async-start | bytes 589824 | tf_op jit(solution)/shard_map/all_to_all | solution.py:45
  32.4 6.1 %all-to-all-done = bf16[4,32,1152]{2,1,0:T(8,128)(2,1)} async-done(((bf16[4,32,1152]{2,1,0:T(8,128)(2,1)}), bf16[4,32,1152]{2,1,0:T(8,128)(2,1)}, u32[]{:S(2)}, u32[]{:S(2)}) %all-to-all-start) | async-done | bytes 294944 | tf_op jit(solution)/shard_map/all_to_all | solution.py:45
  38.5 10.9 %collective-permute-start.5 = (bf16[128,1152]{1,0:T(8,128)(2,1)}, bf16[128,1152]{1,0:T(8,128)(2,1)S(1)}, u32[]{:S(2)}, u32[]{:S(2)}) collective-permute-start(bf16[128,1152]{1,0:T(8,128)(2,1)} %bitcast.1), channel_id=1, source_target_pairs={{0,49},{1,16},{16,1},{17,32},{32,17},{33,48},{48,33},{49,0},{2,51}... | collective-permute-start | bytes 884744 | tf_op jit(solution)/shard_map/ppermute | solution.py:34
  49.4 1.9 %collective-permute-start.4 = (bf16[128,1152]{1,0:T(8,128)(2,1)}, bf16[128,1152]{1,0:T(8,128)(2,1)S(1)}, u32[]{:S(2)}, u32[]{:S(2)}) collective-permute-start(bf16[128,1152]{1,0:T(8,128)(2,1)} %bitcast.1), channel_id=1, source_target_pairs={{0,16},{1,49},{16,32},{17,1},{32,48},{33,17},{48,0},{49,33},{2,18}... | collective-permute-start | bytes 884744 | tf_op jit(solution)/shard_map/ppermute | solution.py:34
  51.3 5.1 %collective-permute-start.3 = (bf16[128,1152]{1,0:T(8,128)(2,1)}, bf16[128,1152]{1,0:T(8,128)(2,1)S(1)}, u32[]{:S(2)}, u32[]{:S(2)}) collective-permute-start(bf16[128,1152]{1,0:T(8,128)(2,1)} %bitcast.1), channel_id=1, source_target_pairs={{0,33},{1,32},{16,49},{17,48},{32,1},{33,0},{48,17},{49,16},{2,35}... | collective-permute-start | bytes 884744 | tf_op jit(solution)/shard_map/ppermute | solution.py:34
  56.5 0.8 copy-done.2
  57.3 1.4 pad_maximum_fusion
  58.7 1.9 %fusion.26 = bf16[1024,128]{0,1:T(8,128)(2,1)S(1)} fusion(bf16[1024,1152]{1,0:T(8,128)(2,1)S(1)} %pad_maximum_fusion, bf16[128,1152]{1,0:T(8,128)(2,1)} %bitcast.1, s32[128]{0:T(128)S(1)} %subtract_dynamic-update-slice_fusion, f32[]{:T(128)} %bitcast.43, f32[]{:T(128)} %bitcast), kind=kOutput, calls=%fused_computation.39 | convolution fusion | flops 303169536 | bytes 2916872 | tf_op jit(solution)/shard_map/dot_general | solution.py:78
  60.6 9.2 %collective-permute-done.5 = bf16[128,1152]{1,0:T(8,128)(2,1)S(1)} collective-permute-done((bf16[128,1152]{1,0:T(8,128)(2,1)}, bf16[128,1152]{1,0:T(8,128)(2,1)S(1)}, u32[]{:S(2)}, u32[]{:S(2)}) %collective-permute-start.5) | collective-permute-done | bytes 294944 | tf_op jit(solution)/shard_map/ppermute | solution.py:34
  69.8 0.9 fusion.25
  70.8 0.9 fusion.24
  71.7 1.9 %collective-permute-done.3 = bf16[128,1152]{1,0:T(8,128)(2,1)S(1)} collective-permute-done((bf16[128,1152]{1,0:T(8,128)(2,1)}, bf16[128,1152]{1,0:T(8,128)(2,1)S(1)}, u32[]{:S(2)}, u32[]{:S(2)}) %collective-permute-start.3) | collective-permute-done | bytes 294944 | tf_op jit(solution)/shard_map/ppermute | solution.py:34
  73.6 0.9 fusion.23
  74.6 2.6 %fusion.29 = f32[1024,1152]{1,0:T(8,128)S(1)} fusion(bf16[128,1152]{1,0:T(8,128)(2,1)S(1)} %collective-permute-done.5, bf16[128,1152]{1,0:T(8,128)(2,1)S(1)} %collective-permute-done.4, bf16[128,1152]{1,0:T(8,128)(2,1)S(1)} %collective-permute-done.3, bf16[128,1152]{1,0:T(8,128)(2,1)} %bitcast.1, bf16[1024,128]{0,1:T(8,128)(2,1)S(1)} %fusion.25, ...), kind=kOutput, calls=%fused_computation.42 | convolution fusion | flops 1216872448 | bytes 6946816 | tf_op jit(solution)/shard_map/dot_general | solution.py:84
  77.4 1.9 %collective-permute-start.6 = (bf16[2,256,1152]{2,1,0:T(8,128)(2,1)S(1)}, bf16[2,256,1152]{2,1,0:T(8,128)(2,1)S(1)}, u32[]{:S(2)}, u32[]{:S(2)}) collective-permute-start(bf16[2,256,1152]{2,1,0:T(8,128)(2,1)S(1)} %fusion.28), channel_id=1, source_target_pairs={{0,8},{8,0},{1,9},{9,1},{2,10},{10,2},{3,11},{11,3},{4,12},{12,4},... | collective-permute-start | bytes 3538952 | tf_op jit(solution)/shard_map/ppermute | solution.py:21
  79.3 2.8 %collective-permute-done.6 = bf16[2,256,1152]{2,1,0:T(8,128)(2,1)S(1)} collective-permute-done((bf16[2,256,1152]{2,1,0:T(8,128)(2,1)S(1)}, bf16[2,256,1152]{2,1,0:T(8,128)(2,1)S(1)}, u32[]{:S(2)}, u32[]{:S(2)}) %collective-permute-start.6) | collective-permute-done | bytes 1179680 | tf_op jit(solution)/shard_map/ppermute | solution.py:21
  82.1 0.2 fusion.1
  82.4 1.1 copy.11
  83.5 4.9 %all-to-all-start.1 = ((bf16[8,2,32,1152]{3,2,1,0:T(8,128)(2,1)}), bf16[8,2,32,1152]{3,2,1,0:T(8,128)(2,1)S(1)}, u32[]{:S(2)}, u32[]{:S(2)}) async-start(bf16[8,2,32,1152]{3,2,1,0:T(8,128)(2,1)} %copy.11), calls=%async_computation.1 | async-start | bytes 2359296 | tf_op jit(solution)/shard_map/all_to_all | solution.py:49
  88.5 2.2 %convolution_convert_fusion = bf16[128,1152]{1,0:T(8,128)(2,1)} fusion(bf16[1024,128]{0,1:T(8,128)(2,1)} %copy-done.9, bf16[1024,1152]{1,0:T(8,128)(2,1)S(1)} %pad_maximum_fusion), kind=kOutput, calls=%fused_computation | convolution fusion | flops 302137344 | bytes 2916352 | tf_op jit(solution)/shard_map/dot_general | solution.py:81
  90.7 5.5 %collective-permute-start.9 = (bf16[128,1152]{1,0:T(8,128)(2,1)}, bf16[128,1152]{1,0:T(8,128)(2,1)}, u32[]{:S(2)}, u32[]{:S(2)}) collective-permute-start(bf16[128,1152]{1,0:T(8,128)(2,1)} %convolution_convert_fusion), channel_id=1, source_target_pairs={{49,0},{16,1},{1,16},{32,17},{17,32},{48,33},{33,48},{0,49},{51,2}... | collective-permute-start | bytes 884744 | tf_op jit(solution)/shard_map/ppermute | solution.py:39
  96.3 1.2 convolution_convert_fusion.1
  97.5 5.2 %collective-permute-start.8 = (bf16[128,1152]{1,0:T(8,128)(2,1)}, bf16[128,1152]{1,0:T(8,128)(2,1)}, u32[]{:S(2)}, u32[]{:S(2)}) collective-permute-start(bf16[128,1152]{1,0:T(8,128)(2,1)} %convolution_convert_fusion.1), channel_id=1, source_target_pairs={{16,0},{49,1},{32,16},{1,17},{48,32},{17,33},{0,48},{33,49},{18,2}... | collective-permute-start | bytes 884744 | tf_op jit(solution)/shard_map/ppermute | solution.py:39
  102.7 1.2 convolution_convert_fusion.2
  103.9 1.9 %collective-permute-start.7 = (bf16[128,1152]{1,0:T(8,128)(2,1)}, bf16[128,1152]{1,0:T(8,128)(2,1)}, u32[]{:S(2)}, u32[]{:S(2)}) collective-permute-start(bf16[128,1152]{1,0:T(8,128)(2,1)} %convolution_convert_fusion.2), channel_id=1, source_target_pairs={{33,0},{32,1},{49,16},{48,17},{1,32},{0,33},{17,48},{16,49},{35,2}... | collective-permute-start | bytes 884744 | tf_op jit(solution)/shard_map/ppermute | solution.py:39
  105.9 1.3 fusion.50
  107.2 7.3 %all-to-all-done.1 = bf16[8,2,32,1152]{3,2,1,0:T(8,128)(2,1)S(1)} async-done(((bf16[8,2,32,1152]{3,2,1,0:T(8,128)(2,1)}), bf16[8,2,32,1152]{3,2,1,0:T(8,128)(2,1)S(1)}, u32[]{:S(2)}, u32[]{:S(2)}) %all-to-all-start.1) | async-done | bytes 1179680 | tf_op jit(solution)/shard_map/all_to_all | solution.py:49
  114.5 0.2 convert_reduce_fusion
  114.7 6.8 %collective-permute-done.7 = bf16[128,1152]{1,0:T(8,128)(2,1)} collective-permute-done((bf16[128,1152]{1,0:T(8,128)(2,1)}, bf16[128,1152]{1,0:T(8,128)(2,1)}, u32[]{:S(2)}, u32[]{:S(2)}) %collective-permute-start.7) | collective-permute-done | bytes 294944 | tf_op jit(solution)/shard_map/ppermute | solution.py:39
  121.5 5.7 %collective-permute-start.10 = (bf16[32,1152]{1,0:T(8,128)(2,1)S(1)}, bf16[32,1152]{1,0:T(8,128)(2,1)S(1)}, u32[]{:S(2)}, u32[]{:S(2)}) collective-permute-start(bf16[32,1152]{1,0:T(8,128)(2,1)S(1)} %fusion.46), channel_id=1, source_target_pairs={{0,64},{64,0},{1,65},{65,1},{2,66},{66,2},{3,67},{67,3},{4,68},{68... | collective-permute-start | bytes 221192 | tf_op jit(solution)/shard_map/ppermute | solution.py:21
  127.2 2.2 %add_convert_fusion = bf16[128,1152]{1,0:T(8,128)(2,1)} fusion(bf16[128,1152]{1,0:T(8,128)(2,1)} %collective-permute-done.9, bf16[128,1152]{1,0:T(8,128)(2,1)} %collective-permute-done.8, f32[128,1152]{1,0:T(8,128)} %fusion.50, bf16[128,1152]{1,0:T(8,128)(2,1)} %collective-permute-done.7), kind=kLoop, calls=%fused_computation.58 | loop fusion | flops 1032192 | bytes 1769472 | tf_op jit(solution)/shard_map/convert_element_type | solution.py:49
  129.4 6.5 %all-to-all-start.3 = ((bf16[4,32,1152]{2,1,0:T(8,128)(2,1)}), bf16[4,32,1152]{2,1,0:T(8,128)(2,1)S(1)}, u32[]{:S(2)}, u32[]{:S(2)}) async-start(bf16[4,32,1152]{2,1,0:T(8,128)(2,1)} %bitcast.11), calls=%async_computation.3 | async-start | bytes 589824 | tf_op jit(solution)/shard_map/all_to_all | solution.py:49
  135.9 1.0 multiply_reduce_fusion.1
  137.0 1.0 divide_convert_fusion.1
  138.0 5.2 %all-to-all-done.3 = bf16[4,32,1152]{2,1,0:T(8,128)(2,1)S(1)} async-done(((bf16[4,32,1152]{2,1,0:T(8,128)(2,1)}), bf16[4,32,1152]{2,1,0:T(8,128)(2,1)S(1)}, u32[]{:S(2)}, u32[]{:S(2)}) %all-to-all-start.3) | async-done | bytes 294944 | tf_op jit(solution)/shard_map/all_to_all | solution.py:49
  143.2 0.9 broadcast_in_dim.5
  144.0 7.7 %all-to-all-start.2 = ((bf16[8,32,1152]{2,1,0:T(8,128)(2,1)}), bf16[8,32,1152]{2,1,0:T(8,128)(2,1)S(1)}, u32[]{:S(2)}, u32[]{:S(2)}) async-start(bf16[8,32,1152]{2,1,0:T(8,128)(2,1)} %broadcast_in_dim.5), calls=%async_computation.2 | async-start | bytes 1179648 | tf_op jit(solution)/shard_map/all_to_all | solution.py:45
  151.8 0.2 multiply_reduce_fusion
  152.0 0.7 divide_convert_fusion
  152.7 8.0 %all-to-all-done.2 = bf16[8,32,1152]{2,1,0:T(8,128)(2,1)S(1)} async-done(((bf16[8,32,1152]{2,1,0:T(8,128)(2,1)}), bf16[8,32,1152]{2,1,0:T(8,128)(2,1)S(1)}, u32[]{:S(2)}, u32[]{:S(2)}) %all-to-all-start.2) | async-done | bytes 589856 | tf_op jit(solution)/shard_map/all_to_all | solution.py:45
  160.8 0.8 copy.26
  (37 shorter events, 0.6 us)
Async XLA Ops:
  0.6 8.8 %copy-start = (bf16[32,1152]{1,0:T(8,128)(2,1)S(1)}, bf16[32,1152]{1,0:T(8,128)(2,1)}, u32[]{:S(2)}) copy-start(bf16[32,1152]{1,0:T(8,128)(2,1)} %param.6) | copy-start | bytes 221188
  0.6 31.6 %copy-start.10 = (s32[32]{0:T(128)S(1)}, s32[32]{0:T(128)}, u32[]{:S(2)}) copy-start(s32[32]{0:T(128)} %param.7) | copy-start | bytes 388
  4.3 16.9 %collective-permute-start.1 = (bf16[256,1152]{1,0:T(8,128)(2,1)S(1)}, bf16[256,1152]{1,0:T(8,128)(2,1)S(1)}, u32[]{:S(2)}, u32[]{:S(2)}) collective-permute-start(bf16[256,1152]{1,0:T(8,128)(2,1)S(1)} %get-tuple-element.12), channel_id=1, source_target_pairs={{0,64},{64,0},{1,65},{65,1},{2,66},{66,2},{3,67},{67,3},{4,68},{68... | collective-permute-start | bytes 1769480 | tf_op jit(solution)/shard_map/ppermute | solution.py:21
  7.5 48.9 %collective-permute-start = (bf16[256,1152]{1,0:T(8,128)(2,1)S(1)}, bf16[256,1152]{1,0:T(8,128)(2,1)S(1)}, u32[]{:S(2)}, u32[]{:S(2)}) collective-permute-start(bf16[256,1152]{1,0:T(8,128)(2,1)S(1)} %get-tuple-element.12), channel_id=1, source_target_pairs={{0,8},{8,0},{1,9},{9,1},{2,10},{10,2},{3,11},{11,3},{4,12},{12,4},... | collective-permute-start | bytes 1769480 | tf_op jit(solution)/shard_map/ppermute | solution.py:21
  21.2 36.1 %collective-permute-start.2 = (bf16[256,1152]{1,0:T(8,128)(2,1)S(1)}, bf16[256,1152]{1,0:T(8,128)(2,1)}, u32[]{:S(2)}, u32[]{:S(2)}) collective-permute-start(bf16[256,1152]{1,0:T(8,128)(2,1)S(1)} %collective-permute-done.1), channel_id=1, source_target_pairs={{0,8},{8,0},{1,9},{9,1},{2,10},{10,2},{3,11},{11,3},{4,12},{12,4},... | collective-permute-start | bytes 1769480 | tf_op jit(solution)/shard_map/ppermute | solution.py:21
  24.0 14.5 %all-to-all-start = ((bf16[4,32,1152]{2,1,0:T(8,128)(2,1)}), bf16[4,32,1152]{2,1,0:T(8,128)(2,1)}, u32[]{:S(2)}, u32[]{:S(2)}) async-start(bf16[4,32,1152]{2,1,0:T(8,128)(2,1)} %broadcast_in_dim.4), calls=%async_computation | async-start | bytes 589824 | tf_op jit(solution)/shard_map/all_to_all | solution.py:45
  38.5 31.3 %collective-permute-start.5 = (bf16[128,1152]{1,0:T(8,128)(2,1)}, bf16[128,1152]{1,0:T(8,128)(2,1)S(1)}, u32[]{:S(2)}, u32[]{:S(2)}) collective-permute-start(bf16[128,1152]{1,0:T(8,128)(2,1)} %bitcast.1), channel_id=1, source_target_pairs={{0,49},{1,16},{16,1},{17,32},{32,17},{33,48},{48,33},{49,0},{2,51}... | collective-permute-start | bytes 884744 | tf_op jit(solution)/shard_map/ppermute | solution.py:34
  49.4 21.4 %collective-permute-start.4 = (bf16[128,1152]{1,0:T(8,128)(2,1)}, bf16[128,1152]{1,0:T(8,128)(2,1)S(1)}, u32[]{:S(2)}, u32[]{:S(2)}) collective-permute-start(bf16[128,1152]{1,0:T(8,128)(2,1)} %bitcast.1), channel_id=1, source_target_pairs={{0,16},{1,49},{16,32},{17,1},{32,48},{33,17},{48,0},{49,33},{2,18}... | collective-permute-start | bytes 884744 | tf_op jit(solution)/shard_map/ppermute | solution.py:34
  51.3 22.3 %collective-permute-start.3 = (bf16[128,1152]{1,0:T(8,128)(2,1)}, bf16[128,1152]{1,0:T(8,128)(2,1)S(1)}, u32[]{:S(2)}, u32[]{:S(2)}) collective-permute-start(bf16[128,1152]{1,0:T(8,128)(2,1)} %bitcast.1), channel_id=1, source_target_pairs={{0,33},{1,32},{16,49},{17,48},{32,1},{33,0},{48,17},{49,16},{2,35}... | collective-permute-start | bytes 884744 | tf_op jit(solution)/shard_map/ppermute | solution.py:34
  56.4 0.8 copy-start.2
  60.6 14.0 %copy-start.3 = (bf16[1024,128]{0,1:T(8,128)(2,1)}, bf16[1024,128]{0,1:T(8,128)(2,1)S(1)}, u32[]{:S(2)}) copy-start(bf16[1024,128]{0,1:T(8,128)(2,1)S(1)} %fusion.26) | copy-start | bytes 786436
  70.7 3.8 %copy-start.9 = (bf16[1024,128]{0,1:T(8,128)(2,1)}, bf16[1024,128]{0,1:T(8,128)(2,1)S(1)}, u32[]{:S(2)}) copy-start(bf16[1024,128]{0,1:T(8,128)(2,1)S(1)} %fusion.25) | copy-start | bytes 786436
  71.7 2.9 %copy-start.7 = (bf16[1024,128]{0,1:T(8,128)(2,1)}, bf16[1024,128]{0,1:T(8,128)(2,1)S(1)}, u32[]{:S(2)}) copy-start(bf16[1024,128]{0,1:T(8,128)(2,1)S(1)} %fusion.24) | copy-start | bytes 786436
  74.6 2.7 %copy-start.5 = (bf16[1024,128]{0,1:T(8,128)(2,1)}, bf16[1024,128]{0,1:T(8,128)(2,1)S(1)}, u32[]{:S(2)}) copy-start(bf16[1024,128]{0,1:T(8,128)(2,1)S(1)} %fusion.23) | copy-start | bytes 786436
  77.4 4.7 %collective-permute-start.6 = (bf16[2,256,1152]{2,1,0:T(8,128)(2,1)S(1)}, bf16[2,256,1152]{2,1,0:T(8,128)(2,1)S(1)}, u32[]{:S(2)}, u32[]{:S(2)}) collective-permute-start(bf16[2,256,1152]{2,1,0:T(8,128)(2,1)S(1)} %fusion.28), channel_id=1, source_target_pairs={{0,8},{8,0},{1,9},{9,1},{2,10},{10,2},{3,11},{11,3},{4,12},{12,4},... | collective-permute-start | bytes 3538952 | tf_op jit(solution)/shard_map/ppermute | solution.py:21
  83.5 31.0 %all-to-all-start.1 = ((bf16[8,2,32,1152]{3,2,1,0:T(8,128)(2,1)}), bf16[8,2,32,1152]{3,2,1,0:T(8,128)(2,1)S(1)}, u32[]{:S(2)}, u32[]{:S(2)}) async-start(bf16[8,2,32,1152]{3,2,1,0:T(8,128)(2,1)} %copy.11), calls=%async_computation.1 | async-start | bytes 2359296 | tf_op jit(solution)/shard_map/all_to_all | solution.py:49
  88.4 7.8 %copy-start.8 = (bf16[1024,128]{0,1:T(8,128)(2,1)S(1)}, bf16[1024,128]{0,1:T(8,128)(2,1)}, u32[]{:S(2)}) copy-start(bf16[1024,128]{0,1:T(8,128)(2,1)} %copy-done.7) | copy-start | bytes 786436
  88.5 14.2 %copy-start.6 = (bf16[1024,128]{0,1:T(8,128)(2,1)S(1)}, bf16[1024,128]{0,1:T(8,128)(2,1)}, u32[]{:S(2)}) copy-start(bf16[1024,128]{0,1:T(8,128)(2,1)} %copy-done.5) | copy-start | bytes 786436
  90.7 15.1 %copy-start.4 = (bf16[1024,128]{0,1:T(8,128)(2,1)S(1)}, bf16[1024,128]{0,1:T(8,128)(2,1)}, u32[]{:S(2)}) copy-start(bf16[1024,128]{0,1:T(8,128)(2,1)} %copy-done.3) | copy-start | bytes 786436
  90.7 24.0 %collective-permute-start.9 = (bf16[128,1152]{1,0:T(8,128)(2,1)}, bf16[128,1152]{1,0:T(8,128)(2,1)}, u32[]{:S(2)}, u32[]{:S(2)}) collective-permute-start(bf16[128,1152]{1,0:T(8,128)(2,1)} %convolution_convert_fusion), channel_id=1, source_target_pairs={{49,0},{16,1},{1,16},{32,17},{17,32},{48,33},{33,48},{0,49},{51,2}... | collective-permute-start | bytes 884744 | tf_op jit(solution)/shard_map/ppermute | solution.py:39
  97.5 17.2 %collective-permute-start.8 = (bf16[128,1152]{1,0:T(8,128)(2,1)}, bf16[128,1152]{1,0:T(8,128)(2,1)}, u32[]{:S(2)}, u32[]{:S(2)}) collective-permute-start(bf16[128,1152]{1,0:T(8,128)(2,1)} %convolution_convert_fusion.1), channel_id=1, source_target_pairs={{16,0},{49,1},{32,16},{1,17},{48,32},{17,33},{0,48},{33,49},{18,2}... | collective-permute-start | bytes 884744 | tf_op jit(solution)/shard_map/ppermute | solution.py:39
  103.9 17.6 %collective-permute-start.7 = (bf16[128,1152]{1,0:T(8,128)(2,1)}, bf16[128,1152]{1,0:T(8,128)(2,1)}, u32[]{:S(2)}, u32[]{:S(2)}) collective-permute-start(bf16[128,1152]{1,0:T(8,128)(2,1)} %convolution_convert_fusion.2), channel_id=1, source_target_pairs={{33,0},{32,1},{49,16},{48,17},{1,32},{0,33},{17,48},{16,49},{35,2}... | collective-permute-start | bytes 884744 | tf_op jit(solution)/shard_map/ppermute | solution.py:39
  121.5 30.3 %copy-start.1 = (bf16[32,1152]{1,0:T(8,128)(2,1)S(1)}, bf16[32,1152]{1,0:T(8,128)(2,1)}, u32[]{:S(2)}) copy-start(bf16[32,1152]{1,0:T(8,128)(2,1)} %param.6) | copy-start | bytes 221188
  121.5 14.4 %collective-permute-start.10 = (bf16[32,1152]{1,0:T(8,128)(2,1)S(1)}, bf16[32,1152]{1,0:T(8,128)(2,1)S(1)}, u32[]{:S(2)}, u32[]{:S(2)}) collective-permute-start(bf16[32,1152]{1,0:T(8,128)(2,1)S(1)} %fusion.46), channel_id=1, source_target_pairs={{0,64},{64,0},{1,65},{65,1},{2,66},{66,2},{3,67},{67,3},{4,68},{68... | collective-permute-start | bytes 221192 | tf_op jit(solution)/shard_map/ppermute | solution.py:21
  129.4 13.8 %all-to-all-start.3 = ((bf16[4,32,1152]{2,1,0:T(8,128)(2,1)}), bf16[4,32,1152]{2,1,0:T(8,128)(2,1)S(1)}, u32[]{:S(2)}, u32[]{:S(2)}) async-start(bf16[4,32,1152]{2,1,0:T(8,128)(2,1)} %bitcast.11), calls=%async_computation.3 | async-start | bytes 589824 | tf_op jit(solution)/shard_map/all_to_all | solution.py:49
  144.0 16.8 %all-to-all-start.2 = ((bf16[8,32,1152]{2,1,0:T(8,128)(2,1)}), bf16[8,32,1152]{2,1,0:T(8,128)(2,1)S(1)}, u32[]{:S(2)}, u32[]{:S(2)}) async-start(bf16[8,32,1152]{2,1,0:T(8,128)(2,1)} %broadcast_in_dim.5), calls=%async_computation.2 | async-start | bytes 1179648 | tf_op jit(solution)/shard_map/all_to_all | solution.py:45

commit v5 on v3

v5 whole, which is shorter than its diff:
```python
import jax
import jax.numpy as jnp
from jax import lax
from jax.sharding import Mesh, PartitionSpec as P

epsilon = 1e-06
AXES = ("yh", "yl", "w", "c", "x", "l")
TEXT_GROUP = ("yh", "w")
NARROW = ("x", "l")
BF16, F32 = jnp.bfloat16, jnp.float32


def unit_rows(values):
    as_float = values.astype(F32)
    row_norm = jnp.sqrt(jnp.sum(as_float * as_float, axis=1, keepdims=True) + epsilon)
    return as_float / row_norm, row_norm


def swap(block, axis):
    return lax.ppermute(block, axis, [(0, 1), (1, 0)])


def shift(block, axis, distance):
    count = lax.axis_size(axis)
    return lax.ppermute(block, axis, [(i, (i + distance) % count) for i in range(count)])


def spread(block, axes):
    count = lax.axis_size(axes)
    copies = jnp.broadcast_to(block[None], (count,) + block.shape)
    return lax.all_to_all(copies, axes, 0, 0, tiled=True).reshape((-1,) + block.shape[1:])


def collect(terms, axes):
    got = lax.all_to_all(terms.astype(BF16), axes, 0, 0, tiled=True)
    return jnp.sum(got.astype(F32), axis=0)


def finish(grad_unit, unit, norm):
    along = jnp.sum(unit * grad_unit, axis=1, keepdims=True)
    return ((grad_unit - unit * along) / norm).astype(BF16)


def local(image_emb, text_emb, positive, log_scale, bias):
    scale = jnp.exp(log_scale[0])
    rows, width = image_emb.shape
    mine = text_emb.shape[0]
    n_x = lax.axis_size("x")
    x = lax.axis_index("x")
    quarter = rows // n_x

    part = swap(lax.dynamic_slice_in_dim(image_emb, x * quarter, quarter, 0), "yl")
    beyond = [part] + [shift(part, "x", d) for d in range(1, n_x)]
    chip = jnp.concatenate([image_emb] + beyond, axis=0)
    images = jnp.concatenate([chip, swap(chip, "c")], axis=0)
    image_bf = unit_rows(images)[0].astype(BF16)

    texts = spread(text_emb, TEXT_GROUP)
    text_bf = unit_rows(texts)[0].astype(BF16)

    wanted = positive - lax.axis_index(("yh", "yl", "w", "c")) * rows
    slot = lax.axis_index(TEXT_GROUP) * mine
    wanted = lax.dynamic_update_slice_in_dim(jnp.full((texts.shape[0],), -1, jnp.int32), wanted, slot, 0)
    hit = (jnp.arange(images.shape[0], dtype=jnp.int32)[:, None] == wanted[None, :]).astype(F32)

    cosine = lax.dot_general(image_bf, text_bf, (((1,), (1,)), ((), ())), preferred_element_type=F32)
    grad = (jax.nn.sigmoid(scale * cosine + bias[0]) - hit).astype(BF16)
    text_terms = lax.dot_general(grad, image_bf, (((0,), (0,)), ((), ())), preferred_element_type=F32).astype(BF16)
    text_terms, grad = lax.optimization_barrier((text_terms, grad))
    text_sum = collect(text_terms.reshape(-1, mine, width), TEXT_GROUP)

    image_terms = jnp.dot(grad, text_bf, preferred_element_type=F32).reshape(2, 2 * rows, width)
    both = image_terms[0] + swap(image_terms[1].astype(BF16), "c").astype(F32)
    own, other = both[:rows], both[rows:].reshape(n_x, quarter, width)
    own_sum, other_sum = lax.dynamic_slice_in_dim(own, x * quarter, quarter, 0), other[0]
    for d in range(1, n_x):
        sent = lax.dynamic_slice_in_dim(own, lax.rem(x + d, n_x) * quarter, quarter, 0)
        got = shift(jnp.concatenate([sent, other[n_x - d]], axis=0).astype(BF16), "x", d).astype(F32)
        own_sum, other_sum = own_sum + got[:quarter], other_sum + got[quarter:]
    lower = lax.axis_index("yl") == 0
    pair = jnp.stack([jnp.where(lower, own_sum, other_sum), jnp.where(lower, other_sum, own_sum)])
    image_sum = scale * collect(pair.reshape(4, rows // 8, width), ("yl", "l"))

    first = lax.axis_index(NARROW) * (rows // 8)
    part_unit, part_norm = unit_rows(lax.dynamic_slice_in_dim(image_emb, first, rows // 8, 0))
    grad_image = spread(finish(image_sum, part_unit, part_norm), NARROW)

    text_unit, text_norm = unit_rows(text_emb)
    grad_text = finish(scale * text_sum, text_unit, text_norm)
    return grad_image, grad_text


def solution(mesh):
    fine = Mesh(mesh.devices.reshape(4, 2, 4, 2, 4, 2), AXES)
    dp = ("yh", "yl", "w", "c")
    in_specs = (P(dp, None), P(AXES, None), P(AXES), P(), P())
    out_specs = (P(dp, None), P(AXES, None))
    return jax.shard_map(local, mesh=fine, in_specs=in_specs, out_specs=out_specs, check_vma=False)
```

time: 160 us -> 170 us (1.062)
  the two profiles are of different devices: /device:TPU:48 before, /device:TPU:1 now
where the time goes in v5:
time: 170 us; the launch traced here: 169 us
  starting transfers between devices  60.9 us (36%)
  waiting for transfers between devices  53.5 us (31%)
  blocking collectives  17.9 us (11%)
  local copies, waits for them, and re-layouts  14.9 us (9%)
  other arithmetic  13 us (8%)
  matrix products  6.88 us (4%)
  between operations  2.27 us (1%)
    all_to_all x1, waiting for transfers between devices, collect(): got = lax.all_to_all(terms.astype(BF16), axes, 0, 0, tiled=True)  31.3 us
    all_to_all x2, starting transfers between devices, spread(): lax.all_to_all(copies, axes, 0, 0, tiled=True)  23.5 us
    ppermute x6, starting transfers between devices, shift(): lax.ppermute(block, axis, [(i, (i + distance) % count) for i in range(cou...  21 us
    all_to_all x1, blocking collectives, collect(): got = lax.all_to_all(terms.astype(BF16), axes, 0, 0, tiled=True)  17.9 us
    ppermute x3, starting transfers between devices, swap(): return lax.ppermute(block, axis, [(0, 1), (1, 0)])  12.3 us
    all_to_all x2, waiting for transfers between devices, spread(): lax.all_to_all(copies, axes, 0, 0, tiled=True)  11.2 us
    unnamed x13, local copies, waits for them, and re-layouts  7.88 us
    ppermute x6, waiting for transfers between devices, shift(): lax.ppermute(block, axis, [(i, (i + distance) % count) for i in range(cou...  7.16 us
  transfers between devices with their start and end apart: 12, of which 8 were waited for; matrix products, arithmetic and copies ran while one was open for 10% of the time, Pallas kernels for 0%

profile of v5, /device:TPU:1, one launch (start us, length us, event | category | flops | bytes accessed | tf_op | source)
XLA Modules:
  0.0 169.3 jit_solution(9719048606918488211)
XLA Ops:
  0.6 1.6 constant_dynamic-slice_fusion
  2.2 4.0 %collective-permute-start = (bf16[64,1152]{1,0:T(8,128)(2,1)}, bf16[64,1152]{1,0:T(8,128)(2,1)}, u32[]{:S(2)}, u32[]{:S(2)}) collective-permute-start(bf16[64,1152]{1,0:T(8,128)(2,1)} %constant_dynamic-slice_fusion), channel_id=1, source_target_pairs={{0,64},{64,0},{1,65},{65,1},{2,66},{66,2},{3,67},{67,3},{4,68},{68... | collective-permute-start | bytes 442376 | tf_op jit(solution)/shard_map/ppermute | solution.py:20
  6.3 2.0 %broadcast_in_dim.4 = bf16[16,32,1152]{2,1,0:T(8,128)(2,1)} broadcast(bf16[32,1152]{1,0:T(8,128)(2,1)} %param.6), dimensions={1,2} | broadcast | bytes 1253376 | tf_op jit(solution)/shard_map/broadcast_in_dim | solution.py:30
  8.2 14.5 %all-to-all-start = ((bf16[16,32,1152]{2,1,0:T(8,128)(2,1)}), bf16[16,32,1152]{2,1,0:T(8,128)(2,1)S(1)}, u32[]{:S(2)}, u32[]{:S(2)}) async-start(bf16[16,32,1152]{2,1,0:T(8,128)(2,1)} %broadcast_in_dim.4), calls=%async_computation | async-start | bytes 2359296 | tf_op jit(solution)/shard_map/all_to_all | solution.py:31
  22.8 2.0 %constant_dynamic-update-slice_fusion.4 = (bf16[512,1152]{1,0:T(8,128)(2,1)}, bf16[1024,1152]{1,0:T(8,128)(2,1)S(1)}) fusion(bf16[256,1152]{1,0:T(8,128)(2,1)} %param.5), kind=kLoop, calls=%fused_computation.45 | loop fusion | bytes 1769472
  24.7 3.1 %collective-permute-start.1 = (bf16[64,1152]{1,0:T(8,128)(2,1)}, bf16[64,1152]{1,0:T(8,128)(2,1)S(1)}, u32[]{:S(2)}, u32[]{:S(2)}) collective-permute-start(bf16[64,1152]{1,0:T(8,128)(2,1)} %collective-permute-done), channel_id=1, source_target_pairs={{0,2},{2,4},{4,6},{6,0},{1,3},{3,5},{5,7},{7,1},{8,10},{10,12},{12... | collective-permute-start | bytes 442376 | tf_op jit(solution)/shard_map/ppermute | solution.py:25
  27.8 4.4 %collective-permute-start.2 = (bf16[64,1152]{1,0:T(8,128)(2,1)}, bf16[64,1152]{1,0:T(8,128)(2,1)S(1)}, u32[]{:S(2)}, u32[]{:S(2)}) collective-permute-start(bf16[64,1152]{1,0:T(8,128)(2,1)} %collective-permute-done), channel_id=1, source_target_pairs={{0,4},{2,6},{4,0},{6,2},{1,5},{3,7},{5,1},{7,3},{8,12},{10,14},{12... | collective-permute-start | bytes 442376 | tf_op jit(solution)/shard_map/ppermute | solution.py:25
  32.2 3.1 %collective-permute-start.3 = (bf16[64,1152]{1,0:T(8,128)(2,1)}, bf16[64,1152]{1,0:T(8,128)(2,1)S(1)}, u32[]{:S(2)}, u32[]{:S(2)}) collective-permute-start(bf16[64,1152]{1,0:T(8,128)(2,1)} %collective-permute-done), channel_id=1, source_target_pairs={{0,6},{2,0},{4,2},{6,4},{1,7},{3,1},{5,3},{7,5},{8,14},{10,8},{12,... | collective-permute-start | bytes 442376 | tf_op jit(solution)/shard_map/ppermute | solution.py:25
  35.3 1.6 constant_dynamic-update-slice_fusion.3
  36.9 0.7 constant_dynamic-update-slice_fusion.2
  37.6 0.7 constant_dynamic-update-slice_fusion.1
  38.2 0.3 collective-permute-done.3
  38.6 0.7 constant_dynamic-update-slice_fusion
  39.3 4.5 %collective-permute-start.4 = (bf16[512,1152]{1,0:T(8,128)(2,1)}, bf16[512,1152]{1,0:T(8,128)(2,1)}, u32[]{:S(2)}, u32[]{:S(2)}) collective-permute-start(bf16[512,1152]{1,0:T(8,128)(2,1)} %get-tuple-element.19), channel_id=1, source_target_pairs={{0,8},{8,0},{1,9},{9,1},{2,10},{10,2},{3,11},{11,3},{4,12},{12,4},... | collective-permute-start | bytes 3538952 | tf_op jit(solution)/shard_map/ppermute | solution.py:20
  45.3 1.3 collective-permute-done.4
  46.6 1.4 constant_dynamic-update-slice_fusion.5
  48.1 0.5 fusion
  48.6 3.0 %all-to-all-done = bf16[16,32,1152]{2,1,0:T(8,128)(2,1)S(1)} async-done(((bf16[16,32,1152]{2,1,0:T(8,128)(2,1)}), bf16[16,32,1152]{2,1,0:T(8,128)(2,1)S(1)}, u32[]{:S(2)}, u32[]{:S(2)}) %all-to-all-start) | async-done | bytes 1179680 | tf_op jit(solution)/shard_map/all_to_all | solution.py:31
  52.1 0.4 fusion.2
  52.4 2.7 %subtract_convert_fusion = bf16[1024,512]{1,0:T(8,128)(2,1)S(1)} fusion(bf16[512,1152]{1,0:T(8,128)(2,1)S(1)} %fusion.2, s32[512]{0:T(512)} %copy-done.2, f32[]{:T(128)} %bitcast.17, f32[]{:T(128)} %bitcast, bf16[1024,1152]{1,0:T(8,128)(2,1)S(1)} %constant_dynamic-update-slice_fusion.5, f32[1024]{0:T(1024)S(1)} %add_sqrt_fusion.1), kind=kOutput, calls=%fused_computation.11 | convolution fusion | flops 1216217088 | bytes 4593672 | tf_op jit(solution)/shard_map/dot_general | solution.py:66
  55.1 2.7 %convolution_convert_fusion = bf16[512,1152]{1,0:T(8,128)(2,1)} fusion(bf16[1024,512]{1,0:T(8,128)(2,1)S(1)} %subtract_convert_fusion, bf16[1024,1152]{1,0:T(8,128)(2,1)S(1)} %constant_dynamic-update-slice_fusion.5, f32[1024]{0:T(1024)S(1)} %add_sqrt_fusion.1), kind=kOutput, calls=%fused_computation.4 | convolution fusion | flops 1212088320 | bytes 4591616 | tf_op jit(solution)/shard_map/dot_general | solution.py:68
  57.8 1.5 fusion.11
  59.3 2.1 %copy-done = f32[1024,1152]{1,0:T(8,128)} copy-done((f32[1024,1152]{1,0:T(8,128)}, f32[1024,1152]{1,0:T(8,128)S(1)}, u32[]{:S(2)}) %copy-start) | copy-done | bytes 4718616
  61.6 3.7 %collective-permute-start.5 = (bf16[512,1152]{1,0:T(8,128)(2,1)S(1)}, bf16[512,1152]{1,0:T(8,128)(2,1)S(1)}, u32[]{:S(2)}, u32[]{:S(2)}) collective-permute-start(bf16[512,1152]{1,0:T(8,128)(2,1)S(1)} %slice.97), channel_id=1, source_target_pairs={{0,8},{8,0},{1,9},{9,1},{2,10},{10,2},{3,11},{11,3},{4,12},{12,4},... | collective-permute-start | bytes 3538952 | tf_op jit(solution)/shard_map/ppermute | solution.py:20
  65.3 2.4 %collective-permute-done.5 = bf16[512,1152]{1,0:T(8,128)(2,1)S(1)} collective-permute-done((bf16[512,1152]{1,0:T(8,128)(2,1)S(1)}, bf16[512,1152]{1,0:T(8,128)(2,1)S(1)}, u32[]{:S(2)}, u32[]{:S(2)}) %collective-permute-start.5) | collective-permute-done | bytes 1179680 | tf_op jit(solution)/shard_map/ppermute | solution.py:20
  67.7 1.9 %fusion.9 = (bf16[512,1152]{1,0:T(8,128)(2,1)S(1)}, f32[512,1152]{1,0:T(8,128)S(1)}) fusion(bf16[512,1152]{1,0:T(8,128)(2,1)S(1)} %collective-permute-done.5, f32[1024,1152]{1,0:T(8,128)} %copy-done), kind=kLoop, calls=%fused_computation.58 | loop fusion | flops 1769472 | bytes 7077888 | tf_op jit(solution)/shard_map/convert.13
  69.9 0.7 pad_maximum_fusion
  70.6 3.1 %collective-permute-start.6 = (bf16[128,1152]{1,0:T(8,128)(2,1)}, bf16[128,1152]{1,0:T(8,128)(2,1)}, u32[]{:S(2)}, u32[]{:S(2)}) collective-permute-start(bf16[128,1152]{1,0:T(8,128)(2,1)} %pad_maximum_fusion), channel_id=1, source_target_pairs={{0,2},{2,4},{4,6},{6,0},{1,3},{3,5},{5,7},{7,1},{8,10},{10,12},{12... | collective-permute-start | bytes 884744 | tf_op jit(solution)/shard_map/ppermute | solution.py:25
  73.7 0.7 pad_maximum_fusion.1
  74.5 4.3 %collective-permute-start.7 = (bf16[128,1152]{1,0:T(8,128)(2,1)}, bf16[128,1152]{1,0:T(8,128)(2,1)}, u32[]{:S(2)}, u32[]{:S(2)}) collective-permute-start(bf16[128,1152]{1,0:T(8,128)(2,1)} %pad_maximum_fusion.1), channel_id=1, source_target_pairs={{0,4},{2,6},{4,0},{6,2},{1,5},{3,7},{5,1},{7,3},{8,12},{10,14},{12... | collective-permute-start | bytes 884744 | tf_op jit(solution)/shard_map/ppermute | solution.py:25
  78.8 0.7 pad_maximum_fusion.2
  79.5 3.0 %collective-permute-start.8 = (bf16[128,1152]{1,0:T(8,128)(2,1)}, bf16[128,1152]{1,0:T(8,128)(2,1)}, u32[]{:S(2)}, u32[]{:S(2)}) collective-permute-start(bf16[128,1152]{1,0:T(8,128)(2,1)} %pad_maximum_fusion.2), channel_id=1, source_target_pairs={{0,6},{2,0},{4,2},{6,4},{1,7},{3,1},{5,3},{7,5},{8,14},{10,8},{12,... | collective-permute-start | bytes 884744 | tf_op jit(solution)/shard_map/ppermute | solution.py:25
  82.6 1.0 convert_element_type.75
  83.6 5.9 %collective-permute-done.7 = bf16[128,1152]{1,0:T(8,128)(2,1)} collective-permute-done((bf16[128,1152]{1,0:T(8,128)(2,1)}, bf16[128,1152]{1,0:T(8,128)(2,1)}, u32[]{:S(2)}, u32[]{:S(2)}) %collective-permute-start.7) | collective-permute-done | bytes 294944 | tf_op jit(solution)/shard_map/ppermute | solution.py:25
  89.5 1.0 convert_element_type.76
  90.5 0.9 collective-permute-done.8
  91.4 1.0 convert_element_type.77
  92.6 17.9 %all_to_all.20 = bf16[4,32,1152]{2,1,0:T(8,128)(2,1)S(1)} all-to-all(bf16[4,32,1152]{2,1,0:T(8,128)(2,1)S(1)} %bitcast.20), channel_id=1, replica_groups=mesh['yh'=4,'yl'=2,'w'=4,'c'=2,'x'=4,'l'=2] {'yl','l'}, dimensions={0} | all-to-all | bytes 589824 | tf_op jit(solution)/shard_map/all_to_all | solution.py:35
  110.6 4.1 %all-to-all-start.3 = ((bf16[16,32,1152]{2,1,0:T(8,128)(2,1)}), bf16[16,32,1152]{2,1,0:T(8,128)(2,1)S(1)}, u32[]{:S(2)}, u32[]{:S(2)}) async-start(bf16[16,32,1152]{2,1,0:T(8,128)(2,1)} %bitcast.19), calls=%async_computation.3 | async-start | bytes 2359296 | tf_op jit(solution)/shard_map/all_to_all | solution.py:35
  114.7 1.0 fusion.3
  115.8 1.1 multiply_reduce_fusion.2
  116.8 1.0 divide_convert_fusion.1
  117.8 31.3 %all-to-all-done.3 = bf16[16,32,1152]{2,1,0:T(8,128)(2,1)S(1)} async-done(((bf16[16,32,1152]{2,1,0:T(8,128)(2,1)}), bf16[16,32,1152]{2,1,0:T(8,128)(2,1)S(1)}, u32[]{:S(2)}, u32[]{:S(2)}) %all-to-all-start.3) | async-done | bytes 1179680 | tf_op jit(solution)/shard_map/all_to_all | solution.py:35
  149.2 0.9 broadcast_in_dim.5
  150.0 9.0 %all-to-all-start.2 = ((bf16[8,32,1152]{2,1,0:T(8,128)(2,1)}), bf16[8,32,1152]{2,1,0:T(8,128)(2,1)S(1)}, u32[]{:S(2)}, u32[]{:S(2)}) async-start(bf16[8,32,1152]{2,1,0:T(8,128)(2,1)} %broadcast_in_dim.5), calls=%async_computation.2 | async-start | bytes 1179648 | tf_op jit(solution)/shard_map/all_to_all | solution.py:31
  159.6 0.7 divide_convert_fusion
  160.3 8.2 %all-to-all-done.2 = bf16[8,32,1152]{2,1,0:T(8,128)(2,1)S(1)} async-done(((bf16[8,32,1152]{2,1,0:T(8,128)(2,1)}), bf16[8,32,1152]{2,1,0:T(8,128)(2,1)S(1)}, u32[]{:S(2)}, u32[]{:S(2)}) %all-to-all-start.2) | async-done | bytes 589856 | tf_op jit(solution)/shard_map/all_to_all | solution.py:31
  168.5 0.8 copy.20
  (29 shorter events, 1.6 us)
Async XLA Ops:
  2.2 22.5 %collective-permute-start = (bf16[64,1152]{1,0:T(8,128)(2,1)}, bf16[64,1152]{1,0:T(8,128)(2,1)}, u32[]{:S(2)}, u32[]{:S(2)}) collective-permute-start(bf16[64,1152]{1,0:T(8,128)(2,1)} %constant_dynamic-slice_fusion), channel_id=1, source_target_pairs={{0,64},{64,0},{1,65},{65,1},{2,66},{66,2},{3,67},{67,3},{4,68},{68... | collective-permute-start | bytes 442376 | tf_op jit(solution)/shard_map/ppermute | solution.py:20
  8.2 43.4 %all-to-all-start = ((bf16[16,32,1152]{2,1,0:T(8,128)(2,1)}), bf16[16,32,1152]{2,1,0:T(8,128)(2,1)S(1)}, u32[]{:S(2)}, u32[]{:S(2)}) async-start(bf16[16,32,1152]{2,1,0:T(8,128)(2,1)} %broadcast_in_dim.4), calls=%async_computation | async-start | bytes 2359296 | tf_op jit(solution)/shard_map/all_to_all | solution.py:31
  22.7 22.5 %copy-start.3 = (s32[32]{0:T(128)S(1)}, s32[32]{0:T(128)}, u32[]{:S(2)}) copy-start(s32[32]{0:T(128)} %param.7) | copy-start | bytes 388
  24.7 12.2 %collective-permute-start.1 = (bf16[64,1152]{1,0:T(8,128)(2,1)}, bf16[64,1152]{1,0:T(8,128)(2,1)S(1)}, u32[]{:S(2)}, u32[]{:S(2)}) collective-permute-start(bf16[64,1152]{1,0:T(8,128)(2,1)} %collective-permute-done), channel_id=1, source_target_pairs={{0,2},{2,4},{4,6},{6,0},{1,3},{3,5},{5,7},{7,1},{8,10},{10,12},{12... | collective-permute-start | bytes 442376 | tf_op jit(solution)/shard_map/ppermute | solution.py:25
  27.8 9.7 %collective-permute-start.2 = (bf16[64,1152]{1,0:T(8,128)(2,1)}, bf16[64,1152]{1,0:T(8,128)(2,1)S(1)}, u32[]{:S(2)}, u32[]{:S(2)}) collective-permute-start(bf16[64,1152]{1,0:T(8,128)(2,1)} %collective-permute-done), channel_id=1, source_target_pairs={{0,4},{2,6},{4,0},{6,2},{1,5},{3,7},{5,1},{7,3},{8,12},{10,14},{12... | collective-permute-start | bytes 442376 | tf_op jit(solution)/shard_map/ppermute | solution.py:25
  32.2 6.4 %collective-permute-start.3 = (bf16[64,1152]{1,0:T(8,128)(2,1)}, bf16[64,1152]{1,0:T(8,128)(2,1)S(1)}, u32[]{:S(2)}, u32[]{:S(2)}) collective-permute-start(bf16[64,1152]{1,0:T(8,128)(2,1)} %collective-permute-done), channel_id=1, source_target_pairs={{0,6},{2,0},{4,2},{6,4},{1,7},{3,1},{5,3},{7,5},{8,14},{10,8},{12,... | collective-permute-start | bytes 442376 | tf_op jit(solution)/shard_map/ppermute | solution.py:25
  39.3 7.3 %collective-permute-start.4 = (bf16[512,1152]{1,0:T(8,128)(2,1)}, bf16[512,1152]{1,0:T(8,128)(2,1)}, u32[]{:S(2)}, u32[]{:S(2)}) collective-permute-start(bf16[512,1152]{1,0:T(8,128)(2,1)} %get-tuple-element.19), channel_id=1, source_target_pairs={{0,8},{8,0},{1,9},{9,1},{2,10},{10,2},{3,11},{11,3},{4,12},{12,4},... | collective-permute-start | bytes 3538952 | tf_op jit(solution)/shard_map/ppermute | solution.py:20
  45.3 1.3 copy-start.2
  59.3 2.1 %copy-start = (f32[1024,1152]{1,0:T(8,128)}, f32[1024,1152]{1,0:T(8,128)S(1)}, u32[]{:S(2)}) copy-start(f32[1024,1152]{1,0:T(8,128)S(1)} %fusion.11) | copy-start | bytes 14155780
  61.6 6.2 %collective-permute-start.5 = (bf16[512,1152]{1,0:T(8,128)(2,1)S(1)}, bf16[512,1152]{1,0:T(8,128)(2,1)S(1)}, u32[]{:S(2)}, u32[]{:S(2)}) collective-permute-start(bf16[512,1152]{1,0:T(8,128)(2,1)S(1)} %slice.97), channel_id=1, source_target_pairs={{0,8},{8,0},{1,9},{9,1},{2,10},{10,2},{3,11},{11,3},{4,12},{12,4},... | collective-permute-start | bytes 3538952 | tf_op jit(solution)/shard_map/ppermute | solution.py:20
  70.6 12.0 %collective-permute-start.6 = (bf16[128,1152]{1,0:T(8,128)(2,1)}, bf16[128,1152]{1,0:T(8,128)(2,1)}, u32[]{:S(2)}, u32[]{:S(2)}) collective-permute-start(bf16[128,1152]{1,0:T(8,128)(2,1)} %pad_maximum_fusion), channel_id=1, source_target_pairs={{0,2},{2,4},{4,6},{6,0},{1,3},{3,5},{5,7},{7,1},{8,10},{10,12},{12... | collective-permute-start | bytes 884744 | tf_op jit(solution)/shard_map/ppermute | solution.py:25
  74.5 15.1 %collective-permute-start.7 = (bf16[128,1152]{1,0:T(8,128)(2,1)}, bf16[128,1152]{1,0:T(8,128)(2,1)}, u32[]{:S(2)}, u32[]{:S(2)}) collective-permute-start(bf16[128,1152]{1,0:T(8,128)(2,1)} %pad_maximum_fusion.1), channel_id=1, source_target_pairs={{0,4},{2,6},{4,0},{6,2},{1,5},{3,7},{5,1},{7,3},{8,12},{10,14},{12... | collective-permute-start | bytes 884744 | tf_op jit(solution)/shard_map/ppermute | solution.py:25
  79.5 11.9 %collective-permute-start.8 = (bf16[128,1152]{1,0:T(8,128)(2,1)}, bf16[128,1152]{1,0:T(8,128)(2,1)}, u32[]{:S(2)}, u32[]{:S(2)}) collective-permute-start(bf16[128,1152]{1,0:T(8,128)(2,1)} %pad_maximum_fusion.2), channel_id=1, source_target_pairs={{0,6},{2,0},{4,2},{6,4},{1,7},{3,1},{5,3},{7,5},{8,14},{10,8},{12,... | collective-permute-start | bytes 884744 | tf_op jit(solution)/shard_map/ppermute | solution.py:25
  110.6 48.5 %copy-start.1 = (bf16[32,1152]{1,0:T(8,128)(2,1)S(1)}, bf16[32,1152]{1,0:T(8,128)(2,1)}, u32[]{:S(2)}) copy-start(bf16[32,1152]{1,0:T(8,128)(2,1)} %param.6) | copy-start | bytes 221188
  110.6 38.6 %all-to-all-start.3 = ((bf16[16,32,1152]{2,1,0:T(8,128)(2,1)}), bf16[16,32,1152]{2,1,0:T(8,128)(2,1)S(1)}, u32[]{:S(2)}, u32[]{:S(2)}) async-start(bf16[16,32,1152]{2,1,0:T(8,128)(2,1)} %bitcast.19), calls=%async_computation.3 | async-start | bytes 2359296 | tf_op jit(solution)/shard_map/all_to_all | solution.py:35
  150.0 18.5 %all-to-all-start.2 = ((bf16[8,32,1152]{2,1,0:T(8,128)(2,1)}), bf16[8,32,1152]{2,1,0:T(8,128)(2,1)S(1)}, u32[]{:S(2)}, u32[]{:S(2)}) async-start(bf16[8,32,1152]{2,1,0:T(8,128)(2,1)} %broadcast_in_dim.5), calls=%async_computation.2 | async-start | bytes 1179648 | tf_op jit(solution)/shard_map/all_to_all | solution.py:31

commit v6 on v5

--- a/solution.py
+++ b/solution.py
@@ -79,6 +79,7 @@
         own_sum, other_sum = own_sum + got[:quarter], other_sum + got[quarter:]
     lower = lax.axis_index("yl") == 0
     pair = jnp.stack([jnp.where(lower, own_sum, other_sum), jnp.where(lower, other_sum, own_sum)])
+    pair, text_sum = lax.optimization_barrier((pair, text_sum))
     image_sum = scale * collect(pair.reshape(4, rows // 8, width), ("yl", "l"))
 
     first = lax.axis_index(NARROW) * (rows // 8)

time: 170 us -> 148 us (0.87)
  the two profiles are of different devices: /device:TPU:1 before, /device:TPU:56 now
where the time goes in v6:
time: 148 us; the launch traced here: 147 us
  starting transfers between devices  56.8 us (38%)
  waiting for transfers between devices  48.3 us (33%)
  local copies, waits for them, and re-layouts  16.4 us (11%)
  other arithmetic  16.3 us (11%)
  matrix products  6.89 us (5%)
  between operations  2.23 us (2%)
    ppermute x6, starting transfers between devices, shift(): lax.ppermute(block, axis, [(i, (i + distance) % count) for i in range(cou...  20.9 us
    all_to_all x2, starting transfers between devices, spread(): lax.all_to_all(copies, axes, 0, 0, tiled=True)  19.2 us
    all_to_all x2, waiting for transfers between devices, spread(): lax.all_to_all(copies, axes, 0, 0, tiled=True)  18.9 us
    all_to_all x2, waiting for transfers between devices, collect(): got = lax.all_to_all(terms.astype(BF16), axes, 0, 0, tiled=True)  17.6 us
    ppermute x6, waiting for transfers between devices, shift(): lax.ppermute(block, axis, [(i, (i + distance) % count) for i in range(cou...  11.8 us
    all_to_all x2, starting transfers between devices, collect(): got = lax.all_to_all(terms.astype(BF16), axes, 0, 0, tiled=True)  9.61 us
    unnamed x13, local copies, waits for them, and re-layouts  8.89 us
    ppermute x3, starting transfers between devices, swap(): return lax.ppermute(block, axis, [(0, 1), (1, 0)])  7.08 us
  transfers between devices with their start and end apart: 13, of which 8 were waited for; matrix products, arithmetic and copies ran while one was open for 16% of the time, Pallas kernels for 0%

profile of v6, /device:TPU:56, one launch (start us, length us, event | category | flops | bytes accessed | tf_op | source)
XLA Modules:
  0.0 146.9 jit_solution(10642298906858016616)
XLA Ops:
  0.6 1.6 %constant_dynamic-slice_fusion = bf16[64,1152]{1,0:T(8,128)(2,1)} fusion(bf16[256,1152]{1,0:T(8,128)(2,1)} %param.5, s32[]{:T(128)S(6)} %select_n.32), kind=kLoop, calls=%fused_computation.52 | loop fusion | bytes 294916 | tf_op jit(solution)/shard_map/dynamic_slice | solution.py:52
  2.2 3.2 %collective-permute-start = (bf16[64,1152]{1,0:T(8,128)(2,1)}, bf16[64,1152]{1,0:T(8,128)(2,1)}, u32[]{:S(2)}, u32[]{:S(2)}) collective-permute-start(bf16[64,1152]{1,0:T(8,128)(2,1)} %constant_dynamic-slice_fusion), channel_id=1, source_target_pairs={{0,64},{64,0},{1,65},{65,1},{2,66},{66,2},{3,67},{67,3},{4,68},{68... | collective-permute-start | bytes 442376 | tf_op jit(solution)/shard_map/ppermute | solution.py:20
  5.5 2.0 %broadcast_in_dim.4 = bf16[16,32,1152]{2,1,0:T(8,128)(2,1)} broadcast(bf16[32,1152]{1,0:T(8,128)(2,1)} %param.6), dimensions={1,2} | broadcast | bytes 1253376 | tf_op jit(solution)/shard_map/broadcast_in_dim | solution.py:30
  7.5 15.5 %all-to-all-start = ((bf16[16,32,1152]{2,1,0:T(8,128)(2,1)}), bf16[16,32,1152]{2,1,0:T(8,128)(2,1)S(1)}, u32[]{:S(2)}, u32[]{:S(2)}) async-start(bf16[16,32,1152]{2,1,0:T(8,128)(2,1)} %broadcast_in_dim.4), calls=%async_computation | async-start | bytes 2359296 | tf_op jit(solution)/shard_map/all_to_all | solution.py:31
  22.9 2.0 %constant_dynamic-update-slice_fusion.4 = (bf16[512,1152]{1,0:T(8,128)(2,1)}, bf16[1024,1152]{1,0:T(8,128)(2,1)S(1)}) fusion(bf16[256,1152]{1,0:T(8,128)(2,1)} %param.5), kind=kLoop, calls=%fused_computation.43 | loop fusion | bytes 1769472
  24.9 4.7 %collective-permute-start.3 = (bf16[64,1152]{1,0:T(8,128)(2,1)}, bf16[64,1152]{1,0:T(8,128)(2,1)S(1)}, u32[]{:S(2)}, u32[]{:S(2)}) collective-permute-start(bf16[64,1152]{1,0:T(8,128)(2,1)} %collective-permute-done), channel_id=1, source_target_pairs={{0,6},{2,0},{4,2},{6,4},{1,7},{3,1},{5,3},{7,5},{8,14},{10,8},{12,... | collective-permute-start | bytes 442376 | tf_op jit(solution)/shard_map/ppermute | solution.py:25
  29.6 2.7 %collective-permute-start.2 = (bf16[64,1152]{1,0:T(8,128)(2,1)}, bf16[64,1152]{1,0:T(8,128)(2,1)S(1)}, u32[]{:S(2)}, u32[]{:S(2)}) collective-permute-start(bf16[64,1152]{1,0:T(8,128)(2,1)} %collective-permute-done), channel_id=1, source_target_pairs={{0,4},{2,6},{4,0},{6,2},{1,5},{3,7},{5,1},{7,3},{8,12},{10,14},{12... | collective-permute-start | bytes 442376 | tf_op jit(solution)/shard_map/ppermute | solution.py:25
  32.3 2.8 %collective-permute-start.1 = (bf16[64,1152]{1,0:T(8,128)(2,1)}, bf16[64,1152]{1,0:T(8,128)(2,1)S(1)}, u32[]{:S(2)}, u32[]{:S(2)}) collective-permute-start(bf16[64,1152]{1,0:T(8,128)(2,1)} %collective-permute-done), channel_id=1, source_target_pairs={{0,2},{2,4},{4,6},{6,0},{1,3},{3,5},{5,7},{7,1},{8,10},{10,12},{12... | collective-permute-start | bytes 442376 | tf_op jit(solution)/shard_map/ppermute | solution.py:25
  35.1 1.6 %constant_dynamic-update-slice_fusion.3 = (bf16[512,1152]{1,0:T(8,128)(2,1)}, bf16[1024,1152]{1,0:T(8,128)(2,1)S(1)}) fusion(bf16[512,1152]{1,0:T(8,128)(2,1)} %get-tuple-element.21, bf16[64,1152]{1,0:T(8,128)(2,1)} %collective-permute-done, bf16[1024,1152]{1,0:T(8,128)(2,1)S(1)} %get-tuple-element.22), kind=kLoop, calls=%fused_computation.42 | loop fusion | bytes 442368
  36.7 4.7 %collective-permute-done.1 = bf16[64,1152]{1,0:T(8,128)(2,1)S(1)} collective-permute-done((bf16[64,1152]{1,0:T(8,128)(2,1)}, bf16[64,1152]{1,0:T(8,128)(2,1)S(1)}, u32[]{:S(2)}, u32[]{:S(2)}) %collective-permute-start.1) | collective-permute-done | bytes 147488 | tf_op jit(solution)/shard_map/ppermute | solution.py:25
  41.4 0.7 constant_dynamic-update-slice_fusion.2
  42.1 0.7 constant_dynamic-update-slice_fusion.1
  43.4 1.9 %collective-permute-start.4 = (bf16[512,1152]{1,0:T(8,128)(2,1)}, bf16[512,1152]{1,0:T(8,128)(2,1)}, u32[]{:S(2)}, u32[]{:S(2)}) collective-permute-start(bf16[512,1152]{1,0:T(8,128)(2,1)} %get-tuple-element.23), channel_id=1, source_target_pairs={{0,8},{8,0},{1,9},{9,1},{2,10},{10,2},{3,11},{11,3},{4,12},{12,4},... | collective-permute-start | bytes 3538952 | tf_op jit(solution)/shard_map/ppermute | solution.py:20
  47.3 1.3 subtract_dynamic-update-slice_fusion
  48.6 1.4 constant_dynamic-update-slice_fusion.5
  50.6 10.0 %all-to-all-done = bf16[16,32,1152]{2,1,0:T(8,128)(2,1)S(1)} async-done(((bf16[16,32,1152]{2,1,0:T(8,128)(2,1)}), bf16[16,32,1152]{2,1,0:T(8,128)(2,1)S(1)}, u32[]{:S(2)}, u32[]{:S(2)}) %all-to-all-start) | async-done | bytes 1179680 | tf_op jit(solution)/shard_map/all_to_all | solution.py:31
  61.4 2.7 %subtract_convert_fusion = bf16[1024,512]{1,0:T(8,128)(2,1)S(1)} fusion(bf16[512,1152]{1,0:T(8,128)(2,1)S(1)} %fusion.2, s32[512]{0:T(512)} %subtract_dynamic-update-slice_fusion, f32[]{:T(128)} %bitcast.17, f32[]{:T(128)} %bitcast, bf16[1024,1152]{1,0:T(8,128)(2,1)S(1)} %constant_dynamic-update-slice_fusion.5, f32[1024]{0:T(1024)S(1)} %add_sqrt_fusion.1), kind=kOutput, calls=%fused_computation.11 | convolution fusion | flops 1216217088 | bytes 4593672 | tf_op jit(solution)/shard_map/dot_general | solution.py:66
  64.0 2.7 %convolution_convert_fusion = bf16[512,1152]{1,0:T(8,128)(2,1)} fusion(bf16[1024,512]{1,0:T(8,128)(2,1)S(1)} %subtract_convert_fusion, bf16[1024,1152]{1,0:T(8,128)(2,1)S(1)} %constant_dynamic-update-slice_fusion.5, f32[1024]{0:T(1024)S(1)} %add_sqrt_fusion.1), kind=kOutput, calls=%fused_computation.4 | convolution fusion | flops 1212088320 | bytes 4591616 | tf_op jit(solution)/shard_map/dot_general | solution.py:68
  66.7 1.5 %fusion.9 = f32[1024,1152]{1,0:T(8,128)S(1)} fusion(bf16[1024,512]{1,0:T(8,128)(2,1)S(1)} %subtract_convert_fusion, bf16[512,1152]{1,0:T(8,128)(2,1)S(1)} %fusion.2), kind=kOutput, calls=%fused_computation.58 | convolution fusion | flops 1207959552 | bytes 6946816 | tf_op jit(solution)/shard_map/dot_general | solution.py:72
  68.3 2.1 %copy-done = f32[1024,1152]{1,0:T(8,128)} copy-done((f32[1024,1152]{1,0:T(8,128)}, f32[1024,1152]{1,0:T(8,128)S(1)}, u32[]{:S(2)}) %copy-start) | copy-done | bytes 4718616
  70.5 1.9 %collective-permute-start.5 = (bf16[512,1152]{1,0:T(8,128)(2,1)S(1)}, bf16[512,1152]{1,0:T(8,128)(2,1)}, u32[]{:S(2)}, u32[]{:S(2)}) collective-permute-start(bf16[512,1152]{1,0:T(8,128)(2,1)S(1)} %slice.97), channel_id=1, source_target_pairs={{0,8},{8,0},{1,9},{9,1},{2,10},{10,2},{3,11},{11,3},{4,12},{12,4},... | collective-permute-start | bytes 3538952 | tf_op jit(solution)/shard_map/ppermute | solution.py:20
  72.5 6.2 %all-to-all-start.1 = ((bf16[16,32,1152]{2,1,0:T(8,128)(2,1)}), bf16[16,32,1152]{2,1,0:T(8,128)(2,1)S(1)}, u32[]{:S(2)}, u32[]{:S(2)}) async-start(bf16[16,32,1152]{2,1,0:T(8,128)(2,1)} %bitcast.5), calls=%async_computation.1 | async-start | bytes 2359296 | tf_op jit(solution)/shard_map/all_to_all | solution.py:35
  78.6 2.3 %fusion.7 = (bf16[512,1152]{1,0:T(8,128)(2,1)S(1)}, f32[512,1152]{1,0:T(8,128)S(1)}) fusion(bf16[512,1152]{1,0:T(8,128)(2,1)} %collective-permute-done.5, f32[1024,1152]{1,0:T(8,128)} %copy-done), kind=kLoop, calls=%fused_computation.56 | loop fusion | flops 1769472 | bytes 7077888 | tf_op jit(solution)/shard_map/convert.9
  81.0 1.0 copy-done.1
  82.1 0.7 pad_maximum_fusion.2
  82.9 4.9 %collective-permute-start.7 = (bf16[128,1152]{1,0:T(8,128)(2,1)}, bf16[128,1152]{1,0:T(8,128)(2,1)}, u32[]{:S(2)}, u32[]{:S(2)}) collective-permute-start(bf16[128,1152]{1,0:T(8,128)(2,1)} %pad_maximum_fusion.2), channel_id=1, source_target_pairs={{0,4},{2,6},{4,0},{6,2},{1,5},{3,7},{5,1},{7,3},{8,12},{10,14},{12... | collective-permute-start | bytes 884744 | tf_op jit(solution)/shard_map/ppermute | solution.py:25
  87.8 0.7 pad_maximum_fusion.3
  88.5 3.0 %collective-permute-start.8 = (bf16[128,1152]{1,0:T(8,128)(2,1)}, bf16[128,1152]{1,0:T(8,128)(2,1)}, u32[]{:S(2)}, u32[]{:S(2)}) collective-permute-start(bf16[128,1152]{1,0:T(8,128)(2,1)} %pad_maximum_fusion.3), channel_id=1, source_target_pairs={{0,6},{2,0},{4,2},{6,4},{1,7},{3,1},{5,3},{7,5},{8,14},{10,8},{12,... | collective-permute-start | bytes 884744 | tf_op jit(solution)/shard_map/ppermute | solution.py:25
  91.6 0.7 pad_maximum_fusion.1
  92.3 2.8 %collective-permute-start.6 = (bf16[128,1152]{1,0:T(8,128)(2,1)}, bf16[128,1152]{1,0:T(8,128)(2,1)}, u32[]{:S(2)}, u32[]{:S(2)}) collective-permute-start(bf16[128,1152]{1,0:T(8,128)(2,1)} %pad_maximum_fusion.1), channel_id=1, source_target_pairs={{0,2},{2,4},{4,6},{6,0},{1,3},{3,5},{5,7},{7,1},{8,10},{10,12},{12... | collective-permute-start | bytes 884744 | tf_op jit(solution)/shard_map/ppermute | solution.py:25
  95.7 1.0 convert_element_type.78
  96.7 5.4 %collective-permute-done.8 = bf16[128,1152]{1,0:T(8,128)(2,1)} collective-permute-done((bf16[128,1152]{1,0:T(8,128)(2,1)}, bf16[128,1152]{1,0:T(8,128)(2,1)}, u32[]{:S(2)}, u32[]{:S(2)}) %collective-permute-start.8) | collective-permute-done | bytes 294944 | tf_op jit(solution)/shard_map/ppermute | solution.py:25
  102.2 1.0 convert_element_type.79
  103.2 1.1 collective-permute-done.6
  104.3 1.0 convert_element_type.77
  105.3 1.1 select_bitcast_fusion.1
  106.4 0.7 pad_maximum_fusion
  107.2 14.0 %all-to-all-done.1 = bf16[16,32,1152]{2,1,0:T(8,128)(2,1)S(1)} async-done(((bf16[16,32,1152]{2,1,0:T(8,128)(2,1)}), bf16[16,32,1152]{2,1,0:T(8,128)(2,1)S(1)}, u32[]{:S(2)}, u32[]{:S(2)}) %all-to-all-start.1) | async-done | bytes 1179680 | tf_op jit(solution)/shard_map/all_to_all | solution.py:35
  121.3 3.5 %all-to-all-start.2 = ((bf16[4,32,1152]{2,1,0:T(8,128)(2,1)}), bf16[4,32,1152]{2,1,0:T(8,128)(2,1)S(1)}, u32[]{:S(2)}, u32[]{:S(2)}) async-start(bf16[4,32,1152]{2,1,0:T(8,128)(2,1)} %bitcast.6), calls=%async_computation.2 | async-start | bytes 589824 | tf_op jit(solution)/shard_map/all_to_all | solution.py:35
  124.8 1.0 fusion.3
  125.8 3.6 %all-to-all-done.2 = bf16[4,32,1152]{2,1,0:T(8,128)(2,1)S(1)} async-done(((bf16[4,32,1152]{2,1,0:T(8,128)(2,1)}), bf16[4,32,1152]{2,1,0:T(8,128)(2,1)S(1)}, u32[]{:S(2)}, u32[]{:S(2)}) %all-to-all-start.2) | async-done | bytes 294944 | tf_op jit(solution)/shard_map/all_to_all | solution.py:35
  129.5 1.1 multiply_reduce_fusion.2
  130.5 1.0 divide_convert_fusion.1
  131.5 0.9 broadcast_in_dim.5
  132.4 3.7 %all-to-all-start.3 = ((bf16[8,32,1152]{2,1,0:T(8,128)(2,1)}), bf16[8,32,1152]{2,1,0:T(8,128)(2,1)S(1)}, u32[]{:S(2)}, u32[]{:S(2)}) async-start(bf16[8,32,1152]{2,1,0:T(8,128)(2,1)} %broadcast_in_dim.5), calls=%async_computation.3 | async-start | bytes 1179648 | tf_op jit(solution)/shard_map/all_to_all | solution.py:31
  136.5 0.7 divide_convert_fusion
  137.2 8.9 %all-to-all-done.3 = bf16[8,32,1152]{2,1,0:T(8,128)(2,1)S(1)} async-done(((bf16[8,32,1152]{2,1,0:T(8,128)(2,1)}), bf16[8,32,1152]{2,1,0:T(8,128)(2,1)S(1)}, u32[]{:S(2)}, u32[]{:S(2)}) %all-to-all-start.3) | async-done | bytes 589856 | tf_op jit(solution)/shard_map/all_to_all | solution.py:31
  146.1 0.8 copy.20
  (30 shorter events, 4.0 us)
Async XLA Ops:
  2.2 22.7 %collective-permute-start = (bf16[64,1152]{1,0:T(8,128)(2,1)}, bf16[64,1152]{1,0:T(8,128)(2,1)}, u32[]{:S(2)}, u32[]{:S(2)}) collective-permute-start(bf16[64,1152]{1,0:T(8,128)(2,1)} %constant_dynamic-slice_fusion), channel_id=1, source_target_pairs={{0,64},{64,0},{1,65},{65,1},{2,66},{66,2},{3,67},{67,3},{4,68},{68... | collective-permute-start | bytes 442376 | tf_op jit(solution)/shard_map/ppermute | solution.py:20
  7.5 53.1 %all-to-all-start = ((bf16[16,32,1152]{2,1,0:T(8,128)(2,1)}), bf16[16,32,1152]{2,1,0:T(8,128)(2,1)S(1)}, u32[]{:S(2)}, u32[]{:S(2)}) async-start(bf16[16,32,1152]{2,1,0:T(8,128)(2,1)} %broadcast_in_dim.4), calls=%async_computation | async-start | bytes 2359296 | tf_op jit(solution)/shard_map/all_to_all | solution.py:31
  22.9 24.3 %copy-start.3 = (s32[32]{0:T(128)S(1)}, s32[32]{0:T(128)}, u32[]{:S(2)}) copy-start(s32[32]{0:T(128)} %param.7) | copy-start | bytes 388
  24.9 17.8 %collective-permute-start.3 = (bf16[64,1152]{1,0:T(8,128)(2,1)}, bf16[64,1152]{1,0:T(8,128)(2,1)S(1)}, u32[]{:S(2)}, u32[]{:S(2)}) collective-permute-start(bf16[64,1152]{1,0:T(8,128)(2,1)} %collective-permute-done), channel_id=1, source_target_pairs={{0,6},{2,0},{4,2},{6,4},{1,7},{3,1},{5,3},{7,5},{8,14},{10,8},{12,... | collective-permute-start | bytes 442376 | tf_op jit(solution)/shard_map/ppermute | solution.py:25
  29.6 12.5 %collective-permute-start.2 = (bf16[64,1152]{1,0:T(8,128)(2,1)}, bf16[64,1152]{1,0:T(8,128)(2,1)S(1)}, u32[]{:S(2)}, u32[]{:S(2)}) collective-permute-start(bf16[64,1152]{1,0:T(8,128)(2,1)} %collective-permute-done), channel_id=1, source_target_pairs={{0,4},{2,6},{4,0},{6,2},{1,5},{3,7},{5,1},{7,3},{8,12},{10,14},{12... | collective-permute-start | bytes 442376 | tf_op jit(solution)/shard_map/ppermute | solution.py:25
  32.3 9.1 %collective-permute-start.1 = (bf16[64,1152]{1,0:T(8,128)(2,1)}, bf16[64,1152]{1,0:T(8,128)(2,1)S(1)}, u32[]{:S(2)}, u32[]{:S(2)}) collective-permute-start(bf16[64,1152]{1,0:T(8,128)(2,1)} %collective-permute-done), channel_id=1, source_target_pairs={{0,2},{2,4},{4,6},{6,0},{1,3},{3,5},{5,7},{7,1},{8,10},{10,12},{12... | collective-permute-start | bytes 442376 | tf_op jit(solution)/shard_map/ppermute | solution.py:25
  43.4 5.2 %collective-permute-start.4 = (bf16[512,1152]{1,0:T(8,128)(2,1)}, bf16[512,1152]{1,0:T(8,128)(2,1)}, u32[]{:S(2)}, u32[]{:S(2)}) collective-permute-start(bf16[512,1152]{1,0:T(8,128)(2,1)} %get-tuple-element.23), channel_id=1, source_target_pairs={{0,8},{8,0},{1,9},{9,1},{2,10},{10,2},{3,11},{11,3},{4,12},{12,4},... | collective-permute-start | bytes 3538952 | tf_op jit(solution)/shard_map/ppermute | solution.py:20
  68.3 2.1 %copy-start = (f32[1024,1152]{1,0:T(8,128)}, f32[1024,1152]{1,0:T(8,128)S(1)}, u32[]{:S(2)}) copy-start(f32[1024,1152]{1,0:T(8,128)S(1)} %fusion.9) | copy-start | bytes 14155780
  70.5 8.1 %collective-permute-start.5 = (bf16[512,1152]{1,0:T(8,128)(2,1)S(1)}, bf16[512,1152]{1,0:T(8,128)(2,1)}, u32[]{:S(2)}, u32[]{:S(2)}) collective-permute-start(bf16[512,1152]{1,0:T(8,128)(2,1)S(1)} %slice.97), channel_id=1, source_target_pairs={{0,8},{8,0},{1,9},{9,1},{2,10},{10,2},{3,11},{11,3},{4,12},{12,4},... | collective-permute-start | bytes 3538952 | tf_op jit(solution)/shard_map/ppermute | solution.py:20
  72.5 48.7 %all-to-all-start.1 = ((bf16[16,32,1152]{2,1,0:T(8,128)(2,1)}), bf16[16,32,1152]{2,1,0:T(8,128)(2,1)S(1)}, u32[]{:S(2)}, u32[]{:S(2)}) async-start(bf16[16,32,1152]{2,1,0:T(8,128)(2,1)} %bitcast.5), calls=%async_computation.1 | async-start | bytes 2359296 | tf_op jit(solution)/shard_map/all_to_all | solution.py:35
  81.0 1.0 copy-start.1
  82.9 12.8 %collective-permute-start.7 = (bf16[128,1152]{1,0:T(8,128)(2,1)}, bf16[128,1152]{1,0:T(8,128)(2,1)}, u32[]{:S(2)}, u32[]{:S(2)}) collective-permute-start(bf16[128,1152]{1,0:T(8,128)(2,1)} %pad_maximum_fusion.2), channel_id=1, source_target_pairs={{0,4},{2,6},{4,0},{6,2},{1,5},{3,7},{5,1},{7,3},{8,12},{10,14},{12... | collective-permute-start | bytes 884744 | tf_op jit(solution)/shard_map/ppermute | solution.py:25
  88.5 13.6 %collective-permute-start.8 = (bf16[128,1152]{1,0:T(8,128)(2,1)}, bf16[128,1152]{1,0:T(8,128)(2,1)}, u32[]{:S(2)}, u32[]{:S(2)}) collective-permute-start(bf16[128,1152]{1,0:T(8,128)(2,1)} %pad_maximum_fusion.3), channel_id=1, source_target_pairs={{0,6},{2,0},{4,2},{6,4},{1,7},{3,1},{5,3},{7,5},{8,14},{10,8},{12,... | collective-permute-start | bytes 884744 | tf_op jit(solution)/shard_map/ppermute | solution.py:25
  92.3 12.0 %collective-permute-start.6 = (bf16[128,1152]{1,0:T(8,128)(2,1)}, bf16[128,1152]{1,0:T(8,128)(2,1)}, u32[]{:S(2)}, u32[]{:S(2)}) collective-permute-start(bf16[128,1152]{1,0:T(8,128)(2,1)} %pad_maximum_fusion.1), channel_id=1, source_target_pairs={{0,2},{2,4},{4,6},{6,0},{1,3},{3,5},{5,7},{7,1},{8,10},{10,12},{12... | collective-permute-start | bytes 884744 | tf_op jit(solution)/shard_map/ppermute | solution.py:25
  107.2 28.9 %copy-start.2 = (bf16[32,1152]{1,0:T(8,128)(2,1)S(1)}, bf16[32,1152]{1,0:T(8,128)(2,1)}, u32[]{:S(2)}) copy-start(bf16[32,1152]{1,0:T(8,128)(2,1)} %param.6) | copy-start | bytes 221188
  121.3 8.1 %all-to-all-start.2 = ((bf16[4,32,1152]{2,1,0:T(8,128)(2,1)}), bf16[4,32,1152]{2,1,0:T(8,128)(2,1)S(1)}, u32[]{:S(2)}, u32[]{:S(2)}) async-start(bf16[4,32,1152]{2,1,0:T(8,128)(2,1)} %bitcast.6), calls=%async_computation.2 | async-start | bytes 589824 | tf_op jit(solution)/shard_map/all_to_all | solution.py:35
  132.4 13.7 %all-to-all-start.3 = ((bf16[8,32,1152]{2,1,0:T(8,128)(2,1)}), bf16[8,32,1152]{2,1,0:T(8,128)(2,1)S(1)}, u32[]{:S(2)}, u32[]{:S(2)}) async-start(bf16[8,32,1152]{2,1,0:T(8,128)(2,1)} %broadcast_in_dim.5), calls=%async_computation.3 | async-start | bytes 1179648 | tf_op jit(solution)/shard_map/all_to_all | solution.py:31

commit v7 on v5

v7 whole, which is shorter than its diff:
```python
import jax
import jax.numpy as jnp
from jax import lax
from jax.experimental import pallas as pl
from jax.experimental.pallas import tpu as pltpu
from jax.sharding import Mesh, PartitionSpec as P

epsilon = 1e-06
AXES = ("yh", "yl", "w", "c", "x", "l")
CLASSES = ((0, 3, 5, 6), (1, 2, 4, 7))
RINGS = ("yh", "yl", "w", "l")
TEXT_GROUPS = [[y * 8 + z for y in of_y for z in of_z] for of_y in CLASSES for of_z in CLASSES]
NARROW = ("x", "l")
BF16, F32 = jnp.bfloat16, jnp.float32


def unit_rows(values):
    as_float = values.astype(F32)
    row_norm = jnp.sqrt(jnp.sum(as_float * as_float, axis=1, keepdims=True) + epsilon)
    return as_float / row_norm, row_norm


def swap(block, axis):
    return lax.ppermute(block, axis, [(0, 1), (1, 0)])


def shift(block, axis, distance):
    count = lax.axis_size(axis)
    return lax.ppermute(block, axis, [(i, (i + distance) % count) for i in range(count)])


def exchange(blocks, axes, groups=None):
    return lax.all_to_all(blocks, axes, 0, 0, axis_index_groups=groups, tiled=True)


def first_copies(x, image_emb, text_emb, quarter, peers):
    mine, width = text_emb.shape

    def body(x_ref, image_ref, text_ref, quarter_ref, copies_ref):
        start = pl.multiple_of(x_ref[0] * quarter, quarter)
        quarter_ref[...] = image_ref[pl.ds(start, quarter), :]
        for k in range(peers):
            copies_ref[k] = text_ref[...]

    whole = pl.BlockSpec(memory_space=pltpu.VMEM)
    return pl.pallas_call(
        body,
        out_shape=(
            jax.ShapeDtypeStruct((quarter, width), BF16),
            jax.ShapeDtypeStruct((peers, mine, width), BF16),
        ),
        in_specs=[pl.BlockSpec(memory_space=pltpu.SMEM), whole, whole],
        out_specs=(whole, whole),
        name="first_copies",
    )(x, image_emb, text_emb)


def finish(terms, rows, scale):
    count, height, width = terms.shape

    def body(scale_ref, terms_ref, rows_ref, out_ref):
        unit, norm = unit_rows(rows_ref[...])
        total = terms_ref[0].astype(F32)
        for k in range(1, count):
            total = total + terms_ref[k].astype(F32)
        total = scale_ref[0] * total
        along = jnp.sum(unit * total, axis=1, keepdims=True)
        out_ref[...] = ((total - unit * along) / norm).astype(BF16)

    whole = pl.BlockSpec(memory_space=pltpu.VMEM)
    return pl.pallas_call(
        body,
        out_shape=jax.ShapeDtypeStruct((height, width), BF16),
        in_specs=[pl.BlockSpec(memory_space=pltpu.SMEM), whole, whole],
        out_specs=whole,
        name="finish",
    )(scale.reshape(1), terms, rows)


def local(image_emb, text_emb, positive, log_scale, bias):
    scale = jnp.exp(log_scale[0])
    rows, width = image_emb.shape
    mine = text_emb.shape[0]
    peers = len(TEXT_GROUPS[0])
    n_x = lax.axis_size("x")
    x = lax.axis_index("x")
    upper = lax.axis_index("yl") == 1
    quarter = rows // n_x

    part, copies = first_copies(x.astype(jnp.int32).reshape(1), image_emb, text_emb, quarter, peers)
    part = swap(part, "yl")
    texts = exchange(copies, RINGS, TEXT_GROUPS).reshape(-1, width)
    around = [part] + [shift(part, "x", n_x - d) for d in range(1, n_x)]
    beyond = lax.dynamic_slice_in_dim(jnp.concatenate(around * 2, axis=0), lax.rem(n_x - x, n_x) * quarter, rows, 0)
    chip = jnp.concatenate([jnp.where(upper, beyond, image_emb), jnp.where(upper, image_emb, beyond)], axis=0)
    near = unit_rows(chip)[0].astype(BF16)
    far = swap(near, "c")
    text_bf = unit_rows(texts)[0].astype(BF16)

    wanted = positive - lax.axis_index(("yh", "yl", "w", "c")) * rows + lax.axis_index("yl") * rows
    slot = lax.axis_index(("yh", "w")) * mine
    wanted = lax.dynamic_update_slice_in_dim(jnp.full((texts.shape[0],), -1, jnp.int32), wanted, slot, 0)
    hit = (jnp.arange(near.shape[0], dtype=jnp.int32)[:, None] == wanted[None, :]).astype(F32)

    def pair_grad(images):
        cosine = lax.dot_general(images, text_bf, (((1,), (1,)), ((), ())), preferred_element_type=F32)
        return jax.nn.sigmoid(scale * cosine + bias[0])

    far_grad = pair_grad(far).astype(BF16)
    far_terms = swap(jnp.dot(far_grad, text_bf, preferred_element_type=F32).astype(BF16), "c")
    near_grad = (pair_grad(near) - hit).astype(BF16)
    near_terms = jnp.dot(near_grad, text_bf, preferred_element_type=F32) + far_terms.astype(F32)
    near_terms = near_terms.astype(BF16).reshape(peers, rows // 8, width)
    first = lax.axis_index(NARROW) * (rows // 8)
    image_rows = lax.dynamic_slice_in_dim(image_emb, first, rows // 8, 0)
    done = finish(exchange(near_terms, ("yl", "x", "l")), image_rows, scale)

    over_images = (((0,), (0,)), ((), ()))
    text_terms = lax.dot_general(near_grad, near, over_images, preferred_element_type=F32)
    text_terms = text_terms + lax.dot_general(far_grad, far, over_images, preferred_element_type=F32)
    text_terms, done = lax.optimization_barrier((text_terms.astype(BF16), done))
    grad_image = lax.all_gather(done, NARROW, axis=0, tiled=True)
    grad_text = finish(exchange(text_terms.reshape(peers, mine, width), RINGS, TEXT_GROUPS), text_emb, scale)
    return grad_image, grad_text


def solution(mesh):
    fine = Mesh(mesh.devices.reshape(4, 2, 4, 2, 4, 2), AXES)
    dp = ("yh", "yl", "w", "c")
    in_specs = (P(dp, None), P(AXES, None), P(AXES), P(), P())
    out_specs = (P(dp, None), P(AXES, None))
    return jax.shard_map(local, mesh=fine, in_specs=in_specs, out_specs=out_specs, check_vma=False)
```

time: 170 us -> 154 us (0.906)
  the two profiles are of different devices: /device:TPU:1 before, /device:TPU:56 now
where the time goes in v7:
time: 154 us; the launch traced here: 152 us
  starting transfers between devices  51.8 us (34%)
  blocking collectives  46.8 us (30%)
  waiting for transfers between devices  24.8 us (16%)
  matrix products  14.2 us (9%)
  Pallas kernels  6.55 us (4%)
  local copies, waits for them, and re-layouts  3.96 us (3%)
  between operations  2.22 us (1%)
  other arithmetic  1.71 us (1%)
    all_gather x1, blocking collectives, local(): grad_image = lax.all_gather(done, NARROW, axis=0, tiled=True)  46.8 us
    all_to_all x3, starting transfers between devices, exchange(): lax.all_to_all(blocks, axes, 0, 0, axis_index_groups=groups, tiled=True)  34.4 us
    all_to_all x3, waiting for transfers between devices, exchange(): lax.all_to_all(blocks, axes, 0, 0, axis_index_groups=groups, tiled=True)  18.2 us
    ppermute x3, starting transfers between devices, shift(): lax.ppermute(block, axis, [(i, (i + distance) % count) for i in range(cou...  10.3 us
    ppermute x3, starting transfers between devices, swap(): return lax.ppermute(block, axis, [(0, 1), (1, 0)])  7.08 us
    ppermute x3, waiting for transfers between devices, shift(): lax.ppermute(block, axis, [(i, (i + distance) % count) for i in range(cou...  6 us
    dot_general x2, matrix products, pair_grad(): lax.dot_general(images, text_bf, (((1,), (1,)), ((), ())), preferred_elem...  5.15 us
    pallas_call x2, Pallas kernels, finish(): pl.pallas_call(body, out_shape=jax.ShapeDtypeStruct((height, width), BF16...  4.37 us
  transfers between devices with their start and end apart: 9, of which 5 were waited for; matrix products, arithmetic and copies ran while one was open for 6% of the time, Pallas kernels for 0%

profile of v7, /device:TPU:56, one launch (start us, length us, event | category | flops | bytes accessed | tf_op | source)
XLA Modules:
  0.0 152.1 jit_solution(2784570375546034687)
XLA Ops:
  0.6 2.2 %first_copies.1 = (bf16[64,1152]{1,0:T(8,128)(2,1)}, bf16[16,32,1152]{2,1,0:T(8,128)(2,1)}) custom-call(s32[1]{0:T(128)} %bitcast.1.x_ref, bf16[256,1152]{1,0:T(8,128)(2,1)} %image_ref.1, bf16[32,1152]{1,0:T(8,128)(2,1)} %rows_ref.1), custom_call_target="tpu_custom_call" | custom-call | tf_op jit(solution)/shard_map/first_copies/pallas_call | solution.py:46
  2.8 3.2 %collective-permute-start = (bf16[64,1152]{1,0:T(8,128)(2,1)}, bf16[64,1152]{1,0:T(8,128)(2,1)S(1)}, u32[]{:S(2)}, u32[]{:S(2)}) collective-permute-start(bf16[64,1152]{1,0:T(8,128)(2,1)} %get-tuple-element.6), channel_id=1, source_target_pairs={{0,64},{64,0},{1,65},{65,1},{2,66},{66,2},{3,67},{67,3},{4,68},{68... | collective-permute-start | bytes 442376 | tf_op jit(solution)/shard_map/ppermute | solution.py:24
  6.1 14.7 %all-to-all-start = ((bf16[16,32,1152]{2,1,0:T(8,128)(2,1)}), bf16[16,32,1152]{2,1,0:T(8,128)(2,1)S(1)}, u32[]{:S(2)}, u32[]{:S(2)}) async-start(bf16[16,32,1152]{2,1,0:T(8,128)(2,1)} %get-tuple-element.7), calls=%async_computation | async-start | bytes 2359296 | tf_op jit(solution)/shard_map/all_to_all | solution.py:33
  20.8 0.0 collective-permute-done
  20.8 4.8 %collective-permute-start.1 = (bf16[64,1152]{1,0:T(8,128)(2,1)S(1)}, bf16[64,1152]{1,0:T(8,128)(2,1)S(1)}, u32[]{:S(2)}, u32[]{:S(2)}) collective-permute-start(bf16[64,1152]{1,0:T(8,128)(2,1)S(1)} %collective-permute-done), channel_id=1, source_target_pairs={{0,6},{2,0},{4,2},{6,4},{1,7},{3,1},{5,3},{7,5},{8,14},{10,8},{12,... | collective-permute-start | bytes 442376 | tf_op jit(solution)/shard_map/ppermute | solution.py:29
  25.6 2.7 %collective-permute-start.2 = (bf16[64,1152]{1,0:T(8,128)(2,1)S(1)}, bf16[64,1152]{1,0:T(8,128)(2,1)S(1)}, u32[]{:S(2)}, u32[]{:S(2)}) collective-permute-start(bf16[64,1152]{1,0:T(8,128)(2,1)S(1)} %collective-permute-done), channel_id=1, source_target_pairs={{0,4},{2,6},{4,0},{6,2},{1,5},{3,7},{5,1},{7,3},{8,12},{10,14},{12... | collective-permute-start | bytes 442376 | tf_op jit(solution)/shard_map/ppermute | solution.py:29
  28.3 2.8 %collective-permute-start.3 = (bf16[64,1152]{1,0:T(8,128)(2,1)S(1)}, bf16[64,1152]{1,0:T(8,128)(2,1)S(1)}, u32[]{:S(2)}, u32[]{:S(2)}) collective-permute-start(bf16[64,1152]{1,0:T(8,128)(2,1)S(1)} %collective-permute-done), channel_id=1, source_target_pairs={{0,2},{2,4},{4,6},{6,0},{1,3},{3,5},{5,7},{7,1},{8,10},{10,12},{12... | collective-permute-start | bytes 442376 | tf_op jit(solution)/shard_map/ppermute | solution.py:29
  31.1 0.0 collective-permute-done.1
  31.2 4.3 %collective-permute-done.2 = bf16[64,1152]{1,0:T(8,128)(2,1)S(1)} collective-permute-done((bf16[64,1152]{1,0:T(8,128)(2,1)S(1)}, bf16[64,1152]{1,0:T(8,128)(2,1)S(1)}, u32[]{:S(2)}, u32[]{:S(2)}) %collective-permute-start.2) | collective-permute-done | bytes 147488 | tf_op jit(solution)/shard_map/ppermute | solution.py:29
  35.5 1.7 %collective-permute-done.3 = bf16[64,1152]{1,0:T(8,128)(2,1)S(1)} collective-permute-done((bf16[64,1152]{1,0:T(8,128)(2,1)S(1)}, bf16[64,1152]{1,0:T(8,128)(2,1)S(1)}, u32[]{:S(2)}, u32[]{:S(2)}) %collective-permute-start.3) | collective-permute-done | bytes 147488 | tf_op jit(solution)/shard_map/ppermute | solution.py:29
  37.3 0.0 copy-done.2
  37.3 0.2 broadcast_select_fusion.1
  37.6 0.3 fusion.1
  37.9 0.4 fusion.2
  38.2 1.9 %collective-permute-start.4 = (bf16[512,1152]{1,0:T(8,128)(2,1)S(1)}, bf16[512,1152]{1,0:T(8,128)(2,1)}, u32[]{:S(2)}, u32[]{:S(2)}) collective-permute-start(bf16[512,1152]{1,0:T(8,128)(2,1)S(1)} %fusion.2), channel_id=1, source_target_pairs={{0,8},{8,0},{1,9},{9,1},{2,10},{10,2},{3,11},{11,3},{4,12},{12,4},... | collective-permute-start | bytes 3538952 | tf_op jit(solution)/shard_map/ppermute | solution.py:24
  41.5 7.0 %all-to-all-done = bf16[16,32,1152]{2,1,0:T(8,128)(2,1)S(1)} async-done(((bf16[16,32,1152]{2,1,0:T(8,128)(2,1)}), bf16[16,32,1152]{2,1,0:T(8,128)(2,1)S(1)}, u32[]{:S(2)}, u32[]{:S(2)}) %all-to-all-start) | async-done | bytes 1179680 | tf_op jit(solution)/shard_map/all_to_all | solution.py:33
  48.6 0.3 multiply_reduce_fusion
  48.9 0.1 sqrt.21
  49.0 0.4 fusion.3
  49.3 0.0 copy-start.3
  49.3 0.0 collective-permute-done.4
  49.3 2.7 %fusion.16 = bf16[512,512]{1,0:T(8,128)(2,1)S(1)} fusion(bf16[512,1152]{1,0:T(8,128)(2,1)} %collective-permute-done.4, bf16[512,1152]{1,0:T(8,128)(2,1)S(1)} %fusion.3, f32[]{:T(128)} %bitcast.22, f32[]{:T(128)} %bitcast), kind=kOutput, calls=%fused_computation.25 | convolution fusion | flops 605552640 | bytes 2883592 | tf_op jit(solution)/shard_map/dot_general | solution.py:106
  52.1 0.0 copy-done.3
  52.1 0.0 copy-start.5
  52.1 0.0 copy-start.8
  52.1 1.9 %convolution_convert_fusion = bf16[512,1152]{1,0:T(8,128)(2,1)} fusion(bf16[512,512]{1,0:T(8,128)(2,1)S(1)} %fusion.16, bf16[512,1152]{1,0:T(8,128)(2,1)S(1)} %fusion.3), kind=kOutput, calls=%fused_computation.2 | convolution fusion | flops 604569600 | bytes 2883584 | tf_op jit(solution)/shard_map/dot_general | solution.py:110
  54.0 0.0 copy-done.5
  54.0 1.9 %collective-permute-start.5 = (bf16[512,1152]{1,0:T(8,128)(2,1)}, bf16[512,1152]{1,0:T(8,128)(2,1)}, u32[]{:S(2)}, u32[]{:S(2)}) collective-permute-start(bf16[512,1152]{1,0:T(8,128)(2,1)} %convolution_convert_fusion), channel_id=1, source_target_pairs={{0,8},{8,0},{1,9},{9,1},{2,10},{10,2},{3,11},{11,3},{4,12},{12,4},... | collective-permute-start | bytes 3538952 | tf_op jit(solution)/shard_map/ppermute | solution.py:24
  55.9 0.0 copy-done.8
  55.9 0.1 add_dynamic-update-slice_fusion
  56.0 2.4 %fusion.15 = bf16[512,512]{1,0:T(8,128)(2,1)S(1)} fusion(bf16[512,1152]{1,0:T(8,128)(2,1)S(1)} %fusion.2, bf16[512,1152]{1,0:T(8,128)(2,1)} %copy-done.3, s32[512]{0:T(512)S(1)} %add_dynamic-update-slice_fusion, f32[]{:T(128)} %bitcast.21, f32[]{:T(128)} %bitcast), kind=kOutput, calls=%fused_computation.24 | convolution fusion | flops 606339072 | bytes 2885640 | tf_op jit(solution)/shard_map/dot_general | solution.py:106
  58.5 0.6 collective-permute-done.5
  59.0 0.0 copy-done.4
  59.0 3.2 %add_convert_fusion = bf16[512,1152]{1,0:T(8,128)(2,1)} fusion(bf16[512,1152]{1,0:T(8,128)(2,1)} %collective-permute-done.5, bf16[512,512]{1,0:T(8,128)(2,1)S(1)} %fusion.15, bf16[512,1152]{1,0:T(8,128)(2,1)S(1)} %copy-done.4), kind=kOutput, calls=%fused_computation.9 | convolution fusion | flops 605749248 | bytes 4063232 | tf_op jit(solution)/shard_map/dot_general | solution.py:112
  62.2 12.5 %all-to-all-start.1 = ((bf16[16,32,1152]{2,1,0:T(8,128)(2,1)}), bf16[16,32,1152]{2,1,0:T(8,128)(2,1)S(1)}, u32[]{:S(2)}, u32[]{:S(2)}) async-start(bf16[16,32,1152]{2,1,0:T(8,128)(2,1)} %bitcast.23), calls=%async_computation.1 | async-start | bytes 2359296 | tf_op jit(solution)/shard_map/all_to_all | solution.py:33
  74.7 0.6 constant_dynamic-slice_fusion.rows_ref
  75.3 0.9 fusion.17
  76.2 0.2 copy-done.6
  76.4 3.2 %fusion = bf16[512,1152]{1,0:T(8,128)(2,1)} fusion(f32[512,1152]{1,0:T(8,128)S(1)} %fusion.17, bf16[512,512]{1,0:T(8,128)(2,1)S(1)} %copy-done.6, bf16[512,1152]{1,0:T(8,128)(2,1)} %collective-permute-done.4), kind=kOutput, calls=%fused_computation.1 | convolution fusion | flops 605159424 | bytes 5242880 | tf_op jit(solution)/shard_map/dot_general | solution.py:120
  79.5 11.2 %all-to-all-done.1.terms_ref = bf16[16,32,1152]{2,1,0:T(8,128)(2,1)S(1)} async-done(((bf16[16,32,1152]{2,1,0:T(8,128)(2,1)}), bf16[16,32,1152]{2,1,0:T(8,128)(2,1)S(1)}, u32[]{:S(2)}, u32[]{:S(2)}) %all-to-all-start.1) | async-done | bytes 1179680 | tf_op jit(solution)/shard_map/all_to_all | solution.py:33
  90.7 1.0 copy-done
  91.7 2.2 %finish.2 = bf16[32,1152]{1,0:T(8,128)(2,1)} custom-call(f32[1]{0:T(128)} %exp.12.scale_ref, bf16[16,32,1152]{2,1,0:T(8,128)(2,1)} %copy-done, bf16[32,1152]{1,0:T(8,128)(2,1)} %constant_dynamic-slice_fusion.rows_ref), custom_call_target="tpu_custom_call" | custom-call | tf_op jit(solution)/shard_map/finish/pallas_call | solution.py:71
  93.9 7.3 %all-to-all-start.2 = ((bf16[16,32,1152]{2,1,0:T(8,128)(2,1)}), bf16[16,32,1152]{2,1,0:T(8,128)(2,1)S(1)}, u32[]{:S(2)}, u32[]{:S(2)}) async-start(bf16[16,32,1152]{2,1,0:T(8,128)(2,1)} %bitcast.5), calls=%async_computation.2 | async-start | bytes 2359296 | tf_op jit(solution)/shard_map/all_to_all | solution.py:33
  101.2 46.8 %all_gather.3 = bf16[256,1152]{1,0:T(8,128)(2,1)S(1)} all-gather(bf16[32,1152]{1,0:T(8,128)(2,1)S(1)} %copy-done.7), channel_id=1, replica_groups=mesh['yh'=4,'yl'=2,'w'=4,'c'=2,'x'=4,'l'=2] {'x','l'}, dimensions={0}, use_global_device_ids=true | all-gather | bytes 663552 | tf_op jit(solution)/shard_map/all_gather | solution.py:122
  148.0 0.0 all-to-all-done.2.terms_ref
  148.0 1.0 copy-done.1
  149.1 2.2 %finish.3 = bf16[32,1152]{1,0:T(8,128)(2,1)} custom-call(f32[1]{0:T(128)} %exp.12.scale_ref, bf16[16,32,1152]{2,1,0:T(8,128)(2,1)} %copy-done.1, bf16[32,1152]{1,0:T(8,128)(2,1)} %rows_ref.1), custom_call_target="tpu_custom_call" | custom-call | tf_op jit(solution)/shard_map/finish/pallas_call | solution.py:71
  151.2 0.8 copy.18
  (18 shorter events, 0.2 us)
Async XLA Ops:
  2.8 18.0 %collective-permute-start = (bf16[64,1152]{1,0:T(8,128)(2,1)}, bf16[64,1152]{1,0:T(8,128)(2,1)S(1)}, u32[]{:S(2)}, u32[]{:S(2)}) collective-permute-start(bf16[64,1152]{1,0:T(8,128)(2,1)} %get-tuple-element.6), channel_id=1, source_target_pairs={{0,64},{64,0},{1,65},{65,1},{2,66},{66,2},{3,67},{67,3},{4,68},{68... | collective-permute-start | bytes 442376 | tf_op jit(solution)/shard_map/ppermute | solution.py:24
  6.1 42.5 %all-to-all-start = ((bf16[16,32,1152]{2,1,0:T(8,128)(2,1)}), bf16[16,32,1152]{2,1,0:T(8,128)(2,1)S(1)}, u32[]{:S(2)}, u32[]{:S(2)}) async-start(bf16[16,32,1152]{2,1,0:T(8,128)(2,1)} %get-tuple-element.7), calls=%async_computation | async-start | bytes 2359296 | tf_op jit(solution)/shard_map/all_to_all | solution.py:33
  20.8 16.5 %copy-start.2 = (bf16[256,1152]{1,0:T(8,128)(2,1)S(1)}, bf16[256,1152]{1,0:T(8,128)(2,1)}, u32[]{:S(2)}) copy-start(bf16[256,1152]{1,0:T(8,128)(2,1)} %image_ref.1) | copy-start | bytes 1769476
  20.8 10.3 %collective-permute-start.1 = (bf16[64,1152]{1,0:T(8,128)(2,1)S(1)}, bf16[64,1152]{1,0:T(8,128)(2,1)S(1)}, u32[]{:S(2)}, u32[]{:S(2)}) collective-permute-start(bf16[64,1152]{1,0:T(8,128)(2,1)S(1)} %collective-permute-done), channel_id=1, source_target_pairs={{0,6},{2,0},{4,2},{6,4},{1,7},{3,1},{5,3},{7,5},{8,14},{10,8},{12,... | collective-permute-start | bytes 442376 | tf_op jit(solution)/shard_map/ppermute | solution.py:29
  25.6 9.9 %collective-permute-start.2 = (bf16[64,1152]{1,0:T(8,128)(2,1)S(1)}, bf16[64,1152]{1,0:T(8,128)(2,1)S(1)}, u32[]{:S(2)}, u32[]{:S(2)}) collective-permute-start(bf16[64,1152]{1,0:T(8,128)(2,1)S(1)} %collective-permute-done), channel_id=1, source_target_pairs={{0,4},{2,6},{4,0},{6,2},{1,5},{3,7},{5,1},{7,3},{8,12},{10,14},{12... | collective-permute-start | bytes 442376 | tf_op jit(solution)/shard_map/ppermute | solution.py:29
  28.3 8.9 %collective-permute-start.3 = (bf16[64,1152]{1,0:T(8,128)(2,1)S(1)}, bf16[64,1152]{1,0:T(8,128)(2,1)S(1)}, u32[]{:S(2)}, u32[]{:S(2)}) collective-permute-start(bf16[64,1152]{1,0:T(8,128)(2,1)S(1)} %collective-permute-done), channel_id=1, source_target_pairs={{0,2},{2,4},{4,6},{6,0},{1,3},{3,5},{5,7},{7,1},{8,10},{10,12},{12... | collective-permute-start | bytes 442376 | tf_op jit(solution)/shard_map/ppermute | solution.py:29
  38.2 11.1 %collective-permute-start.4 = (bf16[512,1152]{1,0:T(8,128)(2,1)S(1)}, bf16[512,1152]{1,0:T(8,128)(2,1)}, u32[]{:S(2)}, u32[]{:S(2)}) collective-permute-start(bf16[512,1152]{1,0:T(8,128)(2,1)S(1)} %fusion.2), channel_id=1, source_target_pairs={{0,8},{8,0},{1,9},{9,1},{2,10},{10,2},{3,11},{11,3},{4,12},{12,4},... | collective-permute-start | bytes 3538952 | tf_op jit(solution)/shard_map/ppermute | solution.py:24
  49.3 2.7 %copy-start.3 = (bf16[512,1152]{1,0:T(8,128)(2,1)}, bf16[512,1152]{1,0:T(8,128)(2,1)S(1)}, u32[]{:S(2)}) copy-start(bf16[512,1152]{1,0:T(8,128)(2,1)S(1)} %fusion.3) | copy-start | bytes 3538948
  52.1 1.9 %copy-start.5 = (bf16[512,512]{1,0:T(8,128)(2,1)}, bf16[512,512]{1,0:T(8,128)(2,1)S(1)}, u32[]{:S(2)}) copy-start(bf16[512,512]{1,0:T(8,128)(2,1)S(1)} %fusion.16) | copy-start | bytes 1572868
  52.1 3.8 %copy-start.8 = (s32[32]{0:T(128)S(1)}, s32[32]{0:T(128)}, u32[]{:S(2)}) copy-start(s32[32]{0:T(128)} %param.7) | copy-start | bytes 388
  54.0 5.1 %collective-permute-start.5 = (bf16[512,1152]{1,0:T(8,128)(2,1)}, bf16[512,1152]{1,0:T(8,128)(2,1)}, u32[]{:S(2)}, u32[]{:S(2)}) collective-permute-start(bf16[512,1152]{1,0:T(8,128)(2,1)} %convolution_convert_fusion), channel_id=1, source_target_pairs={{0,8},{8,0},{1,9},{9,1},{2,10},{10,2},{3,11},{11,3},{4,12},{12,4},... | collective-permute-start | bytes 3538952 | tf_op jit(solution)/shard_map/ppermute | solution.py:24
  56.0 3.0 %copy-start.4 = (bf16[512,1152]{1,0:T(8,128)(2,1)S(1)}, bf16[512,1152]{1,0:T(8,128)(2,1)}, u32[]{:S(2)}) copy-start(bf16[512,1152]{1,0:T(8,128)(2,1)} %copy-done.3) | copy-start | bytes 3538948
  62.2 28.5 %all-to-all-start.1 = ((bf16[16,32,1152]{2,1,0:T(8,128)(2,1)}), bf16[16,32,1152]{2,1,0:T(8,128)(2,1)S(1)}, u32[]{:S(2)}, u32[]{:S(2)}) async-start(bf16[16,32,1152]{2,1,0:T(8,128)(2,1)} %bitcast.23), calls=%async_computation.1 | async-start | bytes 2359296 | tf_op jit(solution)/shard_map/all_to_all | solution.py:33
  75.3 1.0 copy-start.6
  90.7 1.0 copy-start
  93.9 7.3 %copy-start.7 = (bf16[32,1152]{1,0:T(8,128)(2,1)S(1)}, bf16[32,1152]{1,0:T(8,128)(2,1)}, u32[]{:S(2)}) copy-start(bf16[32,1152]{1,0:T(8,128)(2,1)} %finish.2) | copy-start | bytes 221188
  93.9 54.1 %all-to-all-start.2 = ((bf16[16,32,1152]{2,1,0:T(8,128)(2,1)}), bf16[16,32,1152]{2,1,0:T(8,128)(2,1)S(1)}, u32[]{:S(2)}, u32[]{:S(2)}) async-start(bf16[16,32,1152]{2,1,0:T(8,128)(2,1)} %bitcast.5), calls=%async_computation.2 | async-start | bytes 2359296 | tf_op jit(solution)/shard_map/all_to_all | solution.py:33
  148.0 1.0 copy-start.1

commit v8 on v7

v8 whole, which is shorter than its diff:
```python
import jax
import jax.numpy as jnp
from jax import lax
from jax.experimental import pallas as pl
from jax.experimental.pallas import tpu as pltpu
from jax.sharding import Mesh, PartitionSpec as P

epsilon = 1e-06
AXES = ("yh", "yl", "wh", "wl", "c", "x", "l")
SIZES = (4, 2, 2, 2, 2, 4, 2)
Y_GROUPS = ((0, 3, 5, 6), (1, 2, 4, 7))
Z_GROUPS = ((0, 7), (1, 6), (2, 5), (3, 4))
RINGS = ("yh", "yl", "wh", "wl", "l")
TEXT_GROUPS = [[y * 8 + z for y in of_y for z in of_z] for of_y in Y_GROUPS for of_z in Z_GROUPS]
NARROW = ("x", "l")
BF16, F32 = jnp.bfloat16, jnp.float32


def unit_rows(values):
    as_float = values.astype(F32)
    row_norm = jnp.sqrt(jnp.sum(as_float * as_float, axis=1, keepdims=True) + epsilon)
    return as_float / row_norm, row_norm


def swap(block, axes):
    count = lax.axis_size(axes)
    return lax.ppermute(block, axes, [(i, count - 1 - i) for i in range(count)])


def shift(block, axis, distance):
    count = lax.axis_size(axis)
    return lax.ppermute(block, axis, [(i, (i + distance) % count) for i in range(count)])


def exchange(blocks, axes, groups=None):
    return lax.all_to_all(blocks, axes, 0, 0, axis_index_groups=groups, tiled=True)


def first_copies(x, image_emb, text_emb, quarter, peers):
    mine, width = text_emb.shape

    def body(x_ref, image_ref, text_ref, quarter_ref, copies_ref):
        start = pl.multiple_of(x_ref[0] * quarter, quarter)
        quarter_ref[...] = image_ref[pl.ds(start, quarter), :]
        for k in range(peers):
            copies_ref[k] = text_ref[...]

    whole = pl.BlockSpec(memory_space=pltpu.VMEM)
    return pl.pallas_call(
        body,
        out_shape=(
            jax.ShapeDtypeStruct((quarter, width), BF16),
            jax.ShapeDtypeStruct((peers, mine, width), BF16),
        ),
        in_specs=[pl.BlockSpec(memory_space=pltpu.SMEM), whole, whole],
        out_specs=(whole, whole),
        name="first_copies",
    )(x, image_emb, text_emb)


def finish(terms, rows, scale, peers):
    count, height, width = terms.shape

    def body(scale_ref, terms_ref, rows_ref, out_ref):
        unit, norm = unit_rows(rows_ref[...])
        total = terms_ref[0].astype(F32)
        for k in range(1, count):
            total = total + terms_ref[k].astype(F32)
        total = scale_ref[0] * total
        along = jnp.sum(unit * total, axis=1, keepdims=True)
        grad = ((total - unit * along) / norm).astype(BF16)
        for k in range(peers):
            out_ref[k] = grad

    whole = pl.BlockSpec(memory_space=pltpu.VMEM)
    return pl.pallas_call(
        body,
        out_shape=jax.ShapeDtypeStruct((peers, height, width), BF16),
        in_specs=[pl.BlockSpec(memory_space=pltpu.SMEM), whole, whole],
        out_specs=whole,
        name="finish",
    )(scale.reshape(1), terms, rows)


def local(image_emb, text_emb, positive, log_scale, bias):
    scale = jnp.exp(log_scale[0])
    rows, width = image_emb.shape
    mine = text_emb.shape[0]
    peers = len(TEXT_GROUPS[0])
    n_x = lax.axis_size("x")
    x = lax.axis_index("x")
    quarter = rows // n_x

    part, copies = first_copies(x.astype(jnp.int32).reshape(1), image_emb, text_emb, quarter, peers)
    parts = [swap(part, axes) for axes in ("wl", "yl", ("yl", "wl"))]
    parts = jnp.concatenate(parts, axis=0)
    texts = exchange(copies, RINGS, TEXT_GROUPS).reshape(-1, width)

    twice = jnp.concatenate([image_emb, image_emb], axis=0)
    near, far = [], []
    for d in range(n_x):
        own = lax.dynamic_slice_in_dim(twice, (x + d) * quarter, quarter, 0)
        raw = jnp.concatenate([own, parts if d == 0 else shift(parts, "x", n_x - d)], axis=0)
        near.append(unit_rows(raw)[0].astype(BF16))
        far.append(swap(near[d], "c"))
    near, far = jnp.concatenate(near, axis=0), jnp.concatenate(far, axis=0)
    text_bf = unit_rows(texts)[0].astype(BF16)

    wanted = positive - lax.axis_index(("yh", "yl", "wh", "wl", "c")) * rows
    place = lax.rem(wanted // quarter + n_x - x, n_x) * (4 * quarter) + lax.rem(wanted, quarter)
    slot = lax.axis_index(("yh", "wh")) * mine
    place = lax.dynamic_update_slice_in_dim(jnp.full((texts.shape[0],), -1, jnp.int32), place, slot, 0)
    hit = (jnp.arange(near.shape[0], dtype=jnp.int32)[:, None] == place[None, :]).astype(F32)

    def pair_grad(images):
        cosine = lax.dot_general(images, text_bf, (((1,), (1,)), ((), ())), preferred_element_type=F32)
        return jax.nn.sigmoid(scale * cosine + bias[0])

    near_grad = (pair_grad(near) - hit).astype(BF16)
    far_grad = pair_grad(far).astype(BF16)
    near_terms = jnp.dot(near_grad, text_bf, preferred_element_type=F32).reshape(n_x, -1, width)
    far_terms = jnp.dot(far_grad, text_bf, preferred_element_type=F32).astype(BF16).reshape(n_x, -1, width)
    over_images = (((0,), (0,)), ((), ()))
    text_terms = lax.dot_general(near_grad, near, over_images, preferred_element_type=F32)
    text_terms = text_terms + lax.dot_general(far_grad, far, over_images, preferred_element_type=F32)
    text_terms = exchange(text_terms.astype(BF16).reshape(peers, mine, width), RINGS, TEXT_GROUPS)

    total = None
    for d in (2, 1, 3, 0):
        terms = near_terms[d] + swap(far_terms[d], "c").astype(F32)
        terms = shift(terms.astype(BF16), "x", d).astype(F32) if d else terms
        total = terms if total is None else total + terms
    total = total.astype(BF16).reshape(2, 2, 2, rows // 8, width)
    total = jnp.where(lax.axis_index("yl") == 1, total[::-1], total)
    total = jnp.where(lax.axis_index("wl") == 1, total[:, ::-1], total)
    total, text_terms = lax.optimization_barrier((total, text_terms))
    image_terms = exchange(total.reshape(8, rows // 8, width), ("yl", "wl", "l"))

    first = lax.axis_index(NARROW) * (rows // 8)
    image_rows = lax.dynamic_slice_in_dim(image_emb, first, rows // 8, 0)
    grad_image = exchange(finish(image_terms, image_rows, scale, 8), NARROW).reshape(rows, width)
    grad_text = finish(text_terms, text_emb, scale, 1).reshape(mine, width)
    return grad_image, grad_text


def solution(mesh):
    fine = Mesh(mesh.devices.reshape(SIZES), AXES)
    dp = ("yh", "yl", "wh", "wl", "c")
    in_specs = (P(dp, None), P(AXES, None), P(AXES), P(), P())
    out_specs = (P(dp, None), P(AXES, None))
    return jax.shard_map(local, mesh=fine, in_specs=in_specs, out_specs=out_specs, check_vma=False)
```

time: 154 us -> 163 us (1.058)
  the two profiles are of different devices: /device:TPU:56 before, /device:TPU:8 now
where the time goes in v8:
time: 163 us; the launch traced here: 162 us
  starting transfers between devices  79.9 us (49%)
  waiting for transfers between devices  48.1 us (30%)
  other arithmetic  9.4 us (6%)
  matrix products  9.03 us (6%)
  local copies, waits for them, and re-layouts  7.05 us (4%)
  Pallas kernels  6.05 us (4%)
  between operations  2.45 us (2%)
    ppermute x11, starting transfers between devices, swap(): return lax.ppermute(block, axes, [(i, count - 1 - i) for i in range(count)])  30.7 us
    all_to_all x4, starting transfers between devices, exchange(): lax.all_to_all(blocks, axes, 0, 0, axis_index_groups=groups, tiled=True)  28.8 us
    all_to_all x4, waiting for transfers between devices, exchange(): lax.all_to_all(blocks, axes, 0, 0, axis_index_groups=groups, tiled=True)  27.5 us
    ppermute x6, waiting for transfers between devices, shift(): lax.ppermute(block, axis, [(i, (i + distance) % count) for i in range(cou...  20.5 us
    ppermute x6, starting transfers between devices, shift(): lax.ppermute(block, axis, [(i, (i + distance) % count) for i in range(cou...  20.5 us
    unnamed x21, local copies, waits for them, and re-layouts  4.05 us
    pallas_call x2, Pallas kernels, finish(): pl.pallas_call(body, out_shape=jax.ShapeDtypeStruct((peers, height, width...  4.04 us
    convert_element_type x4, other arithmetic, local(): near.append(unit_rows(raw)[0].astype(BF16))  3.39 us
  transfers between devices with their start and end apart: 21, of which 6 were waited for; matrix products, arithmetic and copies ran while one was open for 12% of the time, Pallas kernels for 1%

profile of v8, /device:TPU:8, one launch (start us, length us, event | category | flops | bytes accessed | tf_op | source)
XLA Modules:
  0.0 162.0 jit_solution(9825581265474745583)
XLA Ops:
  0.6 2.0 %first_copies.1 = (bf16[64,1152]{1,0:T(8,128)(2,1)}, bf16[8,32,1152]{2,1,0:T(8,128)(2,1)}) custom-call(s32[1]{0:T(128)} %bitcast.1.x_ref, bf16[256,1152]{1,0:T(8,128)(2,1)} %image_ref.1, bf16[32,1152]{1,0:T(8,128)(2,1)} %rows_ref.1), custom_call_target="tpu_custom_call" | custom-call | tf_op jit(solution)/shard_map/first_copies/pallas_call | solution.py:49
  2.6 6.1 %collective-permute-start = (bf16[64,1152]{1,0:T(8,128)(2,1)}, bf16[64,1152]{1,0:T(8,128)(2,1)S(1)}, u32[]{:S(2)}, u32[]{:S(2)}) collective-permute-start(bf16[64,1152]{1,0:T(8,128)(2,1)} %get-tuple-element.6), channel_id=1, source_target_pairs={{0,16},{16,0},{1,17},{17,1},{2,18},{18,2},{3,19},{19,3},{4,20},{20... | collective-permute-start | bytes 442376 | tf_op jit(solution)/shard_map/ppermute | solution.py:27
  8.7 3.6 %collective-permute-start.1 = (bf16[64,1152]{1,0:T(8,128)(2,1)}, bf16[64,1152]{1,0:T(8,128)(2,1)S(1)}, u32[]{:S(2)}, u32[]{:S(2)}) collective-permute-start(bf16[64,1152]{1,0:T(8,128)(2,1)} %get-tuple-element.6), channel_id=1, source_target_pairs={{0,64},{64,0},{1,65},{65,1},{2,66},{66,2},{3,67},{67,3},{4,68},{68... | collective-permute-start | bytes 442376 | tf_op jit(solution)/shard_map/ppermute | solution.py:27
  12.3 4.3 %collective-permute-start.2 = (bf16[64,1152]{1,0:T(8,128)(2,1)}, bf16[64,1152]{1,0:T(8,128)(2,1)S(1)}, u32[]{:S(2)}, u32[]{:S(2)}) collective-permute-start(bf16[64,1152]{1,0:T(8,128)(2,1)} %get-tuple-element.6), channel_id=1, source_target_pairs={{0,80},{16,64},{64,16},{80,0},{1,81},{17,65},{65,17},{81,1},{2,82}... | collective-permute-start | bytes 442376 | tf_op jit(solution)/shard_map/ppermute | solution.py:27
  16.6 10.8 %all-to-all-start = ((bf16[8,32,1152]{2,1,0:T(8,128)(2,1)}), bf16[8,32,1152]{2,1,0:T(8,128)(2,1)S(1)}, u32[]{:S(2)}, u32[]{:S(2)}) async-start(bf16[8,32,1152]{2,1,0:T(8,128)(2,1)} %get-tuple-element.7), calls=%async_computation | async-start | bytes 1179648 | tf_op jit(solution)/shard_map/all_to_all | solution.py:36
  29.2 4.7 %collective-permute-start.3 = (bf16[192,1152]{1,0:T(8,128)(2,1)S(1)}, bf16[192,1152]{1,0:T(8,128)(2,1)S(1)}, u32[]{:S(2)}, u32[]{:S(2)}) collective-permute-start(bf16[192,1152]{1,0:T(8,128)(2,1)S(1)} %constant_dynamic-update-slice_fusion.2), channel_id=1, source_target_pairs={{0,6},{2,0},{4,2},{6,4},{1,7},{3,1},{5,3},{7,5},{8,14},{10,8},{12,... | collective-permute-start | bytes 1327112 | tf_op jit(solution)/shard_map/ppermute | solution.py:32
  33.8 2.7 %collective-permute-start.4 = (bf16[192,1152]{1,0:T(8,128)(2,1)S(1)}, bf16[192,1152]{1,0:T(8,128)(2,1)S(1)}, u32[]{:S(2)}, u32[]{:S(2)}) collective-permute-start(bf16[192,1152]{1,0:T(8,128)(2,1)S(1)} %constant_dynamic-update-slice_fusion.2), channel_id=1, source_target_pairs={{0,4},{2,6},{4,0},{6,2},{1,5},{3,7},{5,1},{7,3},{8,12},{10,14},{12... | collective-permute-start | bytes 1327112 | tf_op jit(solution)/shard_map/ppermute | solution.py:32
  36.5 2.8 %collective-permute-start.5 = (bf16[192,1152]{1,0:T(8,128)(2,1)S(1)}, bf16[192,1152]{1,0:T(8,128)(2,1)S(1)}, u32[]{:S(2)}, u32[]{:S(2)}) collective-permute-start(bf16[192,1152]{1,0:T(8,128)(2,1)S(1)} %constant_dynamic-update-slice_fusion.2), channel_id=1, source_target_pairs={{0,2},{2,4},{4,6},{6,0},{1,3},{3,5},{5,7},{7,1},{8,10},{10,12},{12... | collective-permute-start | bytes 1327112 | tf_op jit(solution)/shard_map/ppermute | solution.py:32
  39.8 1.9 %collective-permute-start.6 = (bf16[256,1152]{1,0:T(8,128)(2,1)S(1)}, bf16[256,1152]{1,0:T(8,128)(2,1)S(1)}, u32[]{:S(2)}, u32[]{:S(2)}) collective-permute-start(bf16[256,1152]{1,0:T(8,128)(2,1)S(1)} %fusion.15), channel_id=1, source_target_pairs={{0,8},{8,0},{1,9},{9,1},{2,10},{10,2},{3,11},{11,3},{4,12},{12,4},... | collective-permute-start | bytes 1769480 | tf_op jit(solution)/shard_map/ppermute | solution.py:27
  41.7 9.9 %collective-permute-done.3 = bf16[192,1152]{1,0:T(8,128)(2,1)S(1)} collective-permute-done((bf16[192,1152]{1,0:T(8,128)(2,1)S(1)}, bf16[192,1152]{1,0:T(8,128)(2,1)S(1)}, u32[]{:S(2)}, u32[]{:S(2)}) %collective-permute-start.3) | collective-permute-done | bytes 442400 | tf_op jit(solution)/shard_map/ppermute | solution.py:32
  52.0 1.1 fusion.17
  53.1 1.9 %collective-permute-start.7 = (bf16[256,1152]{1,0:T(8,128)(2,1)}, bf16[256,1152]{1,0:T(8,128)(2,1)}, u32[]{:S(2)}, u32[]{:S(2)}) collective-permute-start(bf16[256,1152]{1,0:T(8,128)(2,1)} %fusion.17), channel_id=1, source_target_pairs={{0,8},{8,0},{1,9},{9,1},{2,10},{10,2},{3,11},{11,3},{4,12},{12,4},... | collective-permute-start | bytes 1769480 | tf_op jit(solution)/shard_map/ppermute | solution.py:27
  55.0 1.1 fusion.19
  56.1 2.4 %collective-permute-start.8 = (bf16[256,1152]{1,0:T(8,128)(2,1)}, bf16[256,1152]{1,0:T(8,128)(2,1)}, u32[]{:S(2)}, u32[]{:S(2)}) collective-permute-start(bf16[256,1152]{1,0:T(8,128)(2,1)} %fusion.19), channel_id=1, source_target_pairs={{0,8},{8,0},{1,9},{9,1},{2,10},{10,2},{3,11},{11,3},{4,12},{12,4},... | collective-permute-start | bytes 1769480 | tf_op jit(solution)/shard_map/ppermute | solution.py:27
  58.7 1.1 fusion.21
  59.8 1.9 %collective-permute-start.9 = (bf16[256,1152]{1,0:T(8,128)(2,1)}, bf16[256,1152]{1,0:T(8,128)(2,1)}, u32[]{:S(2)}, u32[]{:S(2)}) collective-permute-start(bf16[256,1152]{1,0:T(8,128)(2,1)} %fusion.21), channel_id=1, source_target_pairs={{0,8},{8,0},{1,9},{9,1},{2,10},{10,2},{3,11},{11,3},{4,12},{12,4},... | collective-permute-start | bytes 1769480 | tf_op jit(solution)/shard_map/ppermute | solution.py:27
  62.3 1.1 constant_dynamic-update-slice_fusion.7
  63.4 1.1 constant_dynamic-update-slice_fusion.6
  64.6 1.1 constant_dynamic-update-slice_fusion.5
  65.7 0.9 fusion.12
  66.6 0.9 convolution_convert_fusion
  67.5 1.0 fusion.35
  68.5 2.4 %collective-permute-start.10 = (bf16[256,1152]{1,0:T(8,128)(2,1)S(1)}, bf16[256,1152]{1,0:T(8,128)(2,1)S(1)}, u32[]{:S(2)}, u32[]{:S(2)}) collective-permute-start(bf16[256,1152]{1,0:T(8,128)(2,1)S(1)} %get-tuple-element.13), channel_id=1, source_target_pairs={{0,8},{8,0},{1,9},{9,1},{2,10},{10,2},{3,11},{11,3},{4,12},{12,4},... | collective-permute-start | bytes 1769480 | tf_op jit(solution)/shard_map/ppermute | solution.py:27
  70.9 1.9 %collective-permute-start.12 = (bf16[256,1152]{1,0:T(8,128)(2,1)S(1)}, bf16[256,1152]{1,0:T(8,128)(2,1)S(1)}, u32[]{:S(2)}, u32[]{:S(2)}) collective-permute-start(bf16[256,1152]{1,0:T(8,128)(2,1)S(1)} %get-tuple-element.16), channel_id=1, source_target_pairs={{0,8},{8,0},{1,9},{9,1},{2,10},{10,2},{3,11},{11,3},{4,12},{12,4},... | collective-permute-start | bytes 1769480 | tf_op jit(solution)/shard_map/ppermute | solution.py:27
  72.8 2.4 %collective-permute-start.14 = (bf16[256,1152]{1,0:T(8,128)(2,1)S(1)}, bf16[256,1152]{1,0:T(8,128)(2,1)S(1)}, u32[]{:S(2)}, u32[]{:S(2)}) collective-permute-start(bf16[256,1152]{1,0:T(8,128)(2,1)S(1)} %get-tuple-element.15), channel_id=1, source_target_pairs={{0,8},{8,0},{1,9},{9,1},{2,10},{10,2},{3,11},{11,3},{4,12},{12,4},... | collective-permute-start | bytes 1769480 | tf_op jit(solution)/shard_map/ppermute | solution.py:27
  75.2 2.4 %fusion.13 = bf16[1024,256]{1,0:T(8,128)(2,1)S(1)} fusion(bf16[256,1152]{1,0:T(8,128)(2,1)S(1)} %fusion.27, s32[256]{0:T(256)S(1)} %fusion.32, f32[]{:T(128)} %bitcast.22, f32[]{:T(128)} %bitcast, bf16[256,1152]{1,0:T(8,128)(2,1)} %fusion.21, bf16[256,1152]{1,0:T(8,128)(2,1)} %fusion.19, bf16[256,1152]{1,0:T(8,128)(2,1)} %fusion.17, ...), kind=kOutput, calls=%fused_computation.26 | convolution fusion | flops 615776256 | bytes 3474440 | tf_op jit(solution)/shard_map/dot_general | solution.py:116
  77.6 0.9 fusion.36
  78.5 1.9 %collective-permute-start.16 = (bf16[256,1152]{1,0:T(8,128)(2,1)}, bf16[256,1152]{1,0:T(8,128)(2,1)}, u32[]{:S(2)}, u32[]{:S(2)}) collective-permute-start(bf16[256,1152]{1,0:T(8,128)(2,1)} %get-tuple-element.14), channel_id=1, source_target_pairs={{0,8},{8,0},{1,9},{9,1},{2,10},{10,2},{3,11},{11,3},{4,12},{12,4},... | collective-permute-start | bytes 1769480 | tf_op jit(solution)/shard_map/ppermute | solution.py:27
  80.5 1.3 fusion.26
  81.8 1.9 %collective-permute-start.11 = (bf16[256,1152]{1,0:T(8,128)(2,1)}, bf16[256,1152]{1,0:T(8,128)(2,1)}, u32[]{:S(2)}, u32[]{:S(2)}) collective-permute-start(bf16[256,1152]{1,0:T(8,128)(2,1)} %get-tuple-element.10), channel_id=1, source_target_pairs={{0,4},{2,6},{4,0},{6,2},{1,5},{3,7},{5,1},{7,3},{8,12},{10,14},{12... | collective-permute-start | bytes 1769480 | tf_op jit(solution)/shard_map/ppermute | solution.py:32
  83.7 6.4 %collective-permute-start.13 = (bf16[256,1152]{1,0:T(8,128)(2,1)}, bf16[256,1152]{1,0:T(8,128)(2,1)}, u32[]{:S(2)}, u32[]{:S(2)}) collective-permute-start(bf16[256,1152]{1,0:T(8,128)(2,1)} %get-tuple-element.12), channel_id=1, source_target_pairs={{0,2},{2,4},{4,6},{6,0},{1,3},{3,5},{5,7},{7,1},{8,10},{10,12},{12... | collective-permute-start | bytes 1769480 | tf_op jit(solution)/shard_map/ppermute | solution.py:32
  90.2 2.0 %collective-permute-start.15 = (bf16[256,1152]{1,0:T(8,128)(2,1)}, bf16[256,1152]{1,0:T(8,128)(2,1)}, u32[]{:S(2)}, u32[]{:S(2)}) collective-permute-start(bf16[256,1152]{1,0:T(8,128)(2,1)} %get-tuple-element.11), channel_id=1, source_target_pairs={{0,6},{2,0},{4,2},{6,4},{1,7},{3,1},{5,3},{7,5},{8,14},{10,8},{12,... | collective-permute-start | bytes 1769480 | tf_op jit(solution)/shard_map/ppermute | solution.py:32
  92.1 2.3 %fusion.28 = f32[256,1152]{1,0:T(8,128)S(1)} fusion(bf16[1024,256]{1,0:T(8,128)(2,1)S(1)} %fusion.13, bf16[256,1152]{1,0:T(8,128)(2,1)} %fusion.21, bf16[256,1152]{1,0:T(8,128)(2,1)} %fusion.19, bf16[256,1152]{1,0:T(8,128)(2,1)} %fusion.17, bf16[256,1152]{1,0:T(8,128)(2,1)S(1)} %copy-done.5), kind=kOutput, calls=%fused_computation.54 | convolution fusion | flops 613416960 | bytes 4063232 | tf_op jit(solution)/shard_map/dot_general | solution.py:124
  94.4 1.7 %fusion = bf16[256,1152]{1,0:T(8,128)(2,1)} fusion(f32[256,1152]{1,0:T(8,128)S(1)} %fusion.28, bf16[1024,256]{1,0:T(8,128)(2,1)S(1)} %fusion.12, bf16[1024,1152]{1,0:T(8,128)(2,1)S(1)} %constant_dynamic-update-slice_fusion.5), kind=kOutput, calls=%fused_computation.2 | convolution fusion | flops 604569600 | bytes 4653056 | tf_op jit(solution)/shard_map/dot_general | solution.py:125
  96.2 8.1 %all-to-all-start.1 = ((bf16[8,32,1152]{2,1,0:T(8,128)(2,1)}), bf16[8,32,1152]{2,1,0:T(8,128)(2,1)S(1)}, u32[]{:S(2)}, u32[]{:S(2)}) async-start(bf16[8,32,1152]{2,1,0:T(8,128)(2,1)} %bitcast.5), calls=%async_computation.1 | async-start | bytes 1179648 | tf_op jit(solution)/shard_map/all_to_all | solution.py:36
  104.3 9.6 %collective-permute-done.13 = bf16[256,1152]{1,0:T(8,128)(2,1)} collective-permute-done((bf16[256,1152]{1,0:T(8,128)(2,1)}, bf16[256,1152]{1,0:T(8,128)(2,1)}, u32[]{:S(2)}, u32[]{:S(2)}) %collective-permute-start.13) | collective-permute-done | bytes 589856 | tf_op jit(solution)/shard_map/ppermute | solution.py:32
  113.9 1.0 collective-permute-done.15
  114.9 2.3 %fusion.23 = bf16[256,1152]{1,0:T(8,128)(2,1)S(1)} fusion(f32[1024,1152]{1,0:T(8,128)} %copy-done, bf16[256,1152]{1,0:T(8,128)(2,1)} %collective-permute-done.16, bf16[256,1152]{1,0:T(8,128)(2,1)} %collective-permute-done.15, bf16[256,1152]{1,0:T(8,128)(2,1)} %collective-permute-done.13, bf16[256,1152]{1,0:T(8,128)(2,1)} %collective-permute-done.11), kind=kLoop, calls=%fused_computation.37 | loop fusion | flops 2654208 | bytes 4128768 | tf_op jit(solution)/shard_map/convert_element_type | solution.py:133
  117.3 0.9 reverse_select_fusion
  118.2 4.0 %all-to-all-done.1.terms_ref = bf16[8,32,1152]{2,1,0:T(8,128)(2,1)S(1)} async-done(((bf16[8,32,1152]{2,1,0:T(8,128)(2,1)}), bf16[8,32,1152]{2,1,0:T(8,128)(2,1)S(1)}, u32[]{:S(2)}, u32[]{:S(2)}) %all-to-all-start.1) | async-done | bytes 589856 | tf_op jit(solution)/shard_map/all_to_all | solution.py:36
  122.2 6.4 %all-to-all-start.2 = ((bf16[8,32,1152]{2,1,0:T(8,128)(2,1)}), bf16[8,32,1152]{2,1,0:T(8,128)(2,1)S(1)}, u32[]{:S(2)}, u32[]{:S(2)}) async-start(bf16[8,32,1152]{2,1,0:T(8,128)(2,1)} %bitcast.6), calls=%async_computation.2 | async-start | bytes 1179648 | tf_op jit(solution)/shard_map/all_to_all | solution.py:36
  129.2 14.4 %all-to-all-done.2.terms_ref = bf16[8,32,1152]{2,1,0:T(8,128)(2,1)S(1)} async-done(((bf16[8,32,1152]{2,1,0:T(8,128)(2,1)}), bf16[8,32,1152]{2,1,0:T(8,128)(2,1)S(1)}, u32[]{:S(2)}, u32[]{:S(2)}) %all-to-all-start.2) | async-done | bytes 589856 | tf_op jit(solution)/shard_map/all_to_all | solution.py:36
  143.6 0.8 copy-done.3
  144.4 2.1 %finish.2 = bf16[8,32,1152]{2,1,0:T(8,128)(2,1)} custom-call(f32[1]{0:T(128)} %exp.12.scale_ref, bf16[8,32,1152]{2,1,0:T(8,128)(2,1)} %copy-done.3, bf16[32,1152]{1,0:T(8,128)(2,1)} %constant_dynamic-slice_fusion.rows_ref), custom_call_target="tpu_custom_call" | custom-call | tf_op jit(solution)/shard_map/finish/pallas_call | solution.py:76
  146.5 3.5 %all-to-all-start.3 = ((bf16[8,32,1152]{2,1,0:T(8,128)(2,1)}), bf16[8,32,1152]{2,1,0:T(8,128)(2,1)S(1)}, u32[]{:S(2)}, u32[]{:S(2)}) async-start(bf16[8,32,1152]{2,1,0:T(8,128)(2,1)} %finish.2), calls=%async_computation.3 | async-start | bytes 1179648 | tf_op jit(solution)/shard_map/all_to_all | solution.py:36
  150.1 1.9 %finish.3 = bf16[1,32,1152]{2,1,0:T(8,128)(2,1)} custom-call(f32[1]{0:T(128)} %exp.12.scale_ref, bf16[8,32,1152]{2,1,0:T(8,128)(2,1)} %copy-done.2, bf16[32,1152]{1,0:T(8,128)(2,1)} %rows_ref.1), custom_call_target="tpu_custom_call" | custom-call | tf_op jit(solution)/shard_map/finish/pallas_call | solution.py:76
  152.0 9.2 %all-to-all-done.3 = bf16[8,32,1152]{2,1,0:T(8,128)(2,1)S(1)} async-done(((bf16[8,32,1152]{2,1,0:T(8,128)(2,1)}), bf16[8,32,1152]{2,1,0:T(8,128)(2,1)S(1)}, u32[]{:S(2)}, u32[]{:S(2)}) %all-to-all-start.3) | async-done | bytes 589856 | tf_op jit(solution)/shard_map/all_to_all | solution.py:36
  161.2 0.8 copy.17
  (52 shorter events, 2.8 us)
Async XLA Ops:
  0.6 26.7 %copy-start.1 = (bf16[256,1152]{1,0:T(8,128)(2,1)S(1)}, bf16[256,1152]{1,0:T(8,128)(2,1)}, u32[]{:S(2)}) copy-start(bf16[256,1152]{1,0:T(8,128)(2,1)} %image_ref.1) | copy-start | bytes 1769476
  2.6 26.4 %collective-permute-start = (bf16[64,1152]{1,0:T(8,128)(2,1)}, bf16[64,1152]{1,0:T(8,128)(2,1)S(1)}, u32[]{:S(2)}, u32[]{:S(2)}) collective-permute-start(bf16[64,1152]{1,0:T(8,128)(2,1)} %get-tuple-element.6), channel_id=1, source_target_pairs={{0,16},{16,0},{1,17},{17,1},{2,18},{18,2},{3,19},{19,3},{4,20},{20... | collective-permute-start | bytes 442376 | tf_op jit(solution)/shard_map/ppermute | solution.py:27
  8.7 20.4 %collective-permute-start.1 = (bf16[64,1152]{1,0:T(8,128)(2,1)}, bf16[64,1152]{1,0:T(8,128)(2,1)S(1)}, u32[]{:S(2)}, u32[]{:S(2)}) collective-permute-start(bf16[64,1152]{1,0:T(8,128)(2,1)} %get-tuple-element.6), channel_id=1, source_target_pairs={{0,64},{64,0},{1,65},{65,1},{2,66},{66,2},{3,67},{67,3},{4,68},{68... | collective-permute-start | bytes 442376 | tf_op jit(solution)/shard_map/ppermute | solution.py:27
  12.3 16.8 %collective-permute-start.2 = (bf16[64,1152]{1,0:T(8,128)(2,1)}, bf16[64,1152]{1,0:T(8,128)(2,1)S(1)}, u32[]{:S(2)}, u32[]{:S(2)}) collective-permute-start(bf16[64,1152]{1,0:T(8,128)(2,1)} %get-tuple-element.6), channel_id=1, source_target_pairs={{0,80},{16,64},{64,16},{80,0},{1,81},{17,65},{65,17},{81,1},{2,82}... | collective-permute-start | bytes 442376 | tf_op jit(solution)/shard_map/ppermute | solution.py:27
  16.6 45.2 %all-to-all-start = ((bf16[8,32,1152]{2,1,0:T(8,128)(2,1)}), bf16[8,32,1152]{2,1,0:T(8,128)(2,1)S(1)}, u32[]{:S(2)}, u32[]{:S(2)}) async-start(bf16[8,32,1152]{2,1,0:T(8,128)(2,1)} %get-tuple-element.7), calls=%async_computation | async-start | bytes 1179648 | tf_op jit(solution)/shard_map/all_to_all | solution.py:36
  27.4 1.5 copy-start.6
  29.2 22.5 %collective-permute-start.3 = (bf16[192,1152]{1,0:T(8,128)(2,1)S(1)}, bf16[192,1152]{1,0:T(8,128)(2,1)S(1)}, u32[]{:S(2)}, u32[]{:S(2)}) collective-permute-start(bf16[192,1152]{1,0:T(8,128)(2,1)S(1)} %constant_dynamic-update-slice_fusion.2), channel_id=1, source_target_pairs={{0,6},{2,0},{4,2},{6,4},{1,7},{3,1},{5,3},{7,5},{8,14},{10,8},{12,... | collective-permute-start | bytes 1327112 | tf_op jit(solution)/shard_map/ppermute | solution.py:32
  33.8 18.0 %collective-permute-start.4 = (bf16[192,1152]{1,0:T(8,128)(2,1)S(1)}, bf16[192,1152]{1,0:T(8,128)(2,1)S(1)}, u32[]{:S(2)}, u32[]{:S(2)}) collective-permute-start(bf16[192,1152]{1,0:T(8,128)(2,1)S(1)} %constant_dynamic-update-slice_fusion.2), channel_id=1, source_target_pairs={{0,4},{2,6},{4,0},{6,2},{1,5},{3,7},{5,1},{7,3},{8,12},{10,14},{12... | collective-permute-start | bytes 1327112 | tf_op jit(solution)/shard_map/ppermute | solution.py:32
  36.5 21.9 %collective-permute-start.5 = (bf16[192,1152]{1,0:T(8,128)(2,1)S(1)}, bf16[192,1152]{1,0:T(8,128)(2,1)S(1)}, u32[]{:S(2)}, u32[]{:S(2)}) collective-permute-start(bf16[192,1152]{1,0:T(8,128)(2,1)S(1)} %constant_dynamic-update-slice_fusion.2), channel_id=1, source_target_pairs={{0,2},{2,4},{4,6},{6,0},{1,3},{3,5},{5,7},{7,1},{8,10},{10,12},{12... | collective-permute-start | bytes 1327112 | tf_op jit(solution)/shard_map/ppermute | solution.py:32
  39.8 13.3 %copy-start.4 = (bf16[256,1152]{1,0:T(8,128)(2,1)}, bf16[256,1152]{1,0:T(8,128)(2,1)S(1)}, u32[]{:S(2)}) copy-start(bf16[256,1152]{1,0:T(8,128)(2,1)S(1)} %fusion.15) | copy-start | bytes 1769476
  39.8 21.9 %collective-permute-start.6 = (bf16[256,1152]{1,0:T(8,128)(2,1)S(1)}, bf16[256,1152]{1,0:T(8,128)(2,1)S(1)}, u32[]{:S(2)}, u32[]{:S(2)}) collective-permute-start(bf16[256,1152]{1,0:T(8,128)(2,1)S(1)} %fusion.15), channel_id=1, source_target_pairs={{0,8},{8,0},{1,9},{9,1},{2,10},{10,2},{3,11},{11,3},{4,12},{12,4},... | collective-permute-start | bytes 1769480 | tf_op jit(solution)/shard_map/ppermute | solution.py:27
  53.1 9.2 %collective-permute-start.7 = (bf16[256,1152]{1,0:T(8,128)(2,1)}, bf16[256,1152]{1,0:T(8,128)(2,1)}, u32[]{:S(2)}, u32[]{:S(2)}) collective-permute-start(bf16[256,1152]{1,0:T(8,128)(2,1)} %fusion.17), channel_id=1, source_target_pairs={{0,8},{8,0},{1,9},{9,1},{2,10},{10,2},{3,11},{11,3},{4,12},{12,4},... | collective-permute-start | bytes 1769480 | tf_op jit(solution)/shard_map/ppermute | solution.py:27
  56.1 7.3 %collective-permute-start.8 = (bf16[256,1152]{1,0:T(8,128)(2,1)}, bf16[256,1152]{1,0:T(8,128)(2,1)}, u32[]{:S(2)}, u32[]{:S(2)}) collective-permute-start(bf16[256,1152]{1,0:T(8,128)(2,1)} %fusion.19), channel_id=1, source_target_pairs={{0,8},{8,0},{1,9},{9,1},{2,10},{10,2},{3,11},{11,3},{4,12},{12,4},... | collective-permute-start | bytes 1769480 | tf_op jit(solution)/shard_map/ppermute | solution.py:27
  59.8 4.8 %collective-permute-start.9 = (bf16[256,1152]{1,0:T(8,128)(2,1)}, bf16[256,1152]{1,0:T(8,128)(2,1)}, u32[]{:S(2)}, u32[]{:S(2)}) collective-permute-start(bf16[256,1152]{1,0:T(8,128)(2,1)} %fusion.21), channel_id=1, source_target_pairs={{0,8},{8,0},{1,9},{9,1},{2,10},{10,2},{3,11},{11,3},{4,12},{12,4},... | collective-permute-start | bytes 1769480 | tf_op jit(solution)/shard_map/ppermute | solution.py:27
  67.5 7.8 %copy-start.5 = (bf16[256,1152]{1,0:T(8,128)(2,1)S(1)}, bf16[256,1152]{1,0:T(8,128)(2,1)}, u32[]{:S(2)}) copy-start(bf16[256,1152]{1,0:T(8,128)(2,1)} %copy-done.4) | copy-start | bytes 1769476
  68.5 12.0 %collective-permute-start.10 = (bf16[256,1152]{1,0:T(8,128)(2,1)S(1)}, bf16[256,1152]{1,0:T(8,128)(2,1)S(1)}, u32[]{:S(2)}, u32[]{:S(2)}) collective-permute-start(bf16[256,1152]{1,0:T(8,128)(2,1)S(1)} %get-tuple-element.13), channel_id=1, source_target_pairs={{0,8},{8,0},{1,9},{9,1},{2,10},{10,2},{3,11},{11,3},{4,12},{12,4},... | collective-permute-start | bytes 1769480 | tf_op jit(solution)/shard_map/ppermute | solution.py:27
  70.9 9.6 %collective-permute-start.12 = (bf16[256,1152]{1,0:T(8,128)(2,1)S(1)}, bf16[256,1152]{1,0:T(8,128)(2,1)S(1)}, u32[]{:S(2)}, u32[]{:S(2)}) collective-permute-start(bf16[256,1152]{1,0:T(8,128)(2,1)S(1)} %get-tuple-element.16), channel_id=1, source_target_pairs={{0,8},{8,0},{1,9},{9,1},{2,10},{10,2},{3,11},{11,3},{4,12},{12,4},... | collective-permute-start | bytes 1769480 | tf_op jit(solution)/shard_map/ppermute | solution.py:27
  72.8 7.7 %collective-permute-start.14 = (bf16[256,1152]{1,0:T(8,128)(2,1)S(1)}, bf16[256,1152]{1,0:T(8,128)(2,1)S(1)}, u32[]{:S(2)}, u32[]{:S(2)}) collective-permute-start(bf16[256,1152]{1,0:T(8,128)(2,1)S(1)} %get-tuple-element.15), channel_id=1, source_target_pairs={{0,8},{8,0},{1,9},{9,1},{2,10},{10,2},{3,11},{11,3},{4,12},{12,4},... | collective-permute-start | bytes 1769480 | tf_op jit(solution)/shard_map/ppermute | solution.py:27
  78.5 3.3 %copy-start = (f32[1024,1152]{1,0:T(8,128)}, f32[1024,1152]{1,0:T(8,128)S(1)}, u32[]{:S(2)}) copy-start(f32[1024,1152]{1,0:T(8,128)S(1)} %fusion.36) | copy-start | bytes 14155780
  78.5 25.8 %collective-permute-start.16 = (bf16[256,1152]{1,0:T(8,128)(2,1)}, bf16[256,1152]{1,0:T(8,128)(2,1)}, u32[]{:S(2)}, u32[]{:S(2)}) collective-permute-start(bf16[256,1152]{1,0:T(8,128)(2,1)} %get-tuple-element.14), channel_id=1, source_target_pairs={{0,8},{8,0},{1,9},{9,1},{2,10},{10,2},{3,11},{11,3},{4,12},{12,4},... | collective-permute-start | bytes 1769480 | tf_op jit(solution)/shard_map/ppermute | solution.py:27
  81.8 22.5 %collective-permute-start.11 = (bf16[256,1152]{1,0:T(8,128)(2,1)}, bf16[256,1152]{1,0:T(8,128)(2,1)}, u32[]{:S(2)}, u32[]{:S(2)}) collective-permute-start(bf16[256,1152]{1,0:T(8,128)(2,1)} %get-tuple-element.10), channel_id=1, source_target_pairs={{0,4},{2,6},{4,0},{6,2},{1,5},{3,7},{5,1},{7,3},{8,12},{10,14},{12... | collective-permute-start | bytes 1769480 | tf_op jit(solution)/shard_map/ppermute | solution.py:32
  83.7 30.2 %collective-permute-start.13 = (bf16[256,1152]{1,0:T(8,128)(2,1)}, bf16[256,1152]{1,0:T(8,128)(2,1)}, u32[]{:S(2)}, u32[]{:S(2)}) collective-permute-start(bf16[256,1152]{1,0:T(8,128)(2,1)} %get-tuple-element.12), channel_id=1, source_target_pairs={{0,2},{2,4},{4,6},{6,0},{1,3},{3,5},{5,7},{7,1},{8,10},{10,12},{12... | collective-permute-start | bytes 1769480 | tf_op jit(solution)/shard_map/ppermute | solution.py:32
  90.2 24.8 %collective-permute-start.15 = (bf16[256,1152]{1,0:T(8,128)(2,1)}, bf16[256,1152]{1,0:T(8,128)(2,1)}, u32[]{:S(2)}, u32[]{:S(2)}) collective-permute-start(bf16[256,1152]{1,0:T(8,128)(2,1)} %get-tuple-element.11), channel_id=1, source_target_pairs={{0,6},{2,0},{4,2},{6,4},{1,7},{3,1},{5,3},{7,5},{8,14},{10,8},{12,... | collective-permute-start | bytes 1769480 | tf_op jit(solution)/shard_map/ppermute | solution.py:32
  96.2 26.0 %all-to-all-start.1 = ((bf16[8,32,1152]{2,1,0:T(8,128)(2,1)}), bf16[8,32,1152]{2,1,0:T(8,128)(2,1)S(1)}, u32[]{:S(2)}, u32[]{:S(2)}) async-start(bf16[8,32,1152]{2,1,0:T(8,128)(2,1)} %bitcast.5), calls=%async_computation.1 | async-start | bytes 1179648 | tf_op jit(solution)/shard_map/all_to_all | solution.py:36
  122.2 24.3 %copy-start.2 = (bf16[8,32,1152]{2,1,0:T(8,128)(2,1)}, bf16[8,32,1152]{2,1,0:T(8,128)(2,1)S(1)}, u32[]{:S(2)}) copy-start(bf16[8,32,1152]{2,1,0:T(8,128)(2,1)S(1)} %all-to-all-done.1.terms_ref) | copy-start | bytes 1769476
  122.2 21.4 %all-to-all-start.2 = ((bf16[8,32,1152]{2,1,0:T(8,128)(2,1)}), bf16[8,32,1152]{2,1,0:T(8,128)(2,1)S(1)}, u32[]{:S(2)}, u32[]{:S(2)}) async-start(bf16[8,32,1152]{2,1,0:T(8,128)(2,1)} %bitcast.6), calls=%async_computation.2 | async-start | bytes 1179648 | tf_op jit(solution)/shard_map/all_to_all | solution.py:36
  143.6 0.8 copy-start.3
  146.5 14.7 %all-to-all-start.3 = ((bf16[8,32,1152]{2,1,0:T(8,128)(2,1)}), bf16[8,32,1152]{2,1,0:T(8,128)(2,1)S(1)}, u32[]{:S(2)}, u32[]{:S(2)}) async-start(bf16[8,32,1152]{2,1,0:T(8,128)(2,1)} %finish.2), calls=%async_computation.3 | async-start | bytes 1179648 | tf_op jit(solution)/shard_map/all_to_all | solution.py:36

commit v9 on v7

--- a/solution.py
+++ b/solution.py
@@ -55,26 +55,10 @@
     )(x, image_emb, text_emb)
 
 
-def finish(terms, rows, scale):
-    count, height, width = terms.shape
-
-    def body(scale_ref, terms_ref, rows_ref, out_ref):
-        unit, norm = unit_rows(rows_ref[...])
-        total = terms_ref[0].astype(F32)
-        for k in range(1, count):
-            total = total + terms_ref[k].astype(F32)
-        total = scale_ref[0] * total
-        along = jnp.sum(unit * total, axis=1, keepdims=True)
-        out_ref[...] = ((total - unit * along) / norm).astype(BF16)
-
-    whole = pl.BlockSpec(memory_space=pltpu.VMEM)
-    return pl.pallas_call(
-        body,
-        out_shape=jax.ShapeDtypeStruct((height, width), BF16),
-        in_specs=[pl.BlockSpec(memory_space=pltpu.SMEM), whole, whole],
-        out_specs=whole,
-        name="finish",
-    )(scale.reshape(1), terms, rows)
+def finish(terms, unit, norm, scale):
+    total = scale * jnp.sum(terms.astype(F32), axis=0)
+    along = jnp.sum(unit * total, axis=1, keepdims=True)
+    return ((total - unit * along) / norm).astype(BF16)
 
 
 def local(image_emb, text_emb, positive, log_scale, bias):
@@ -100,27 +84,41 @@
     wanted = positive - lax.axis_index(("yh", "yl", "w", "c")) * rows + lax.axis_index("yl") * rows
     slot = lax.axis_index(("yh", "w")) * mine
     wanted = lax.dynamic_update_slice_in_dim(jnp.full((texts.shape[0],), -1, jnp.int32), wanted, slot, 0)
-    hit = (jnp.arange(near.shape[0], dtype=jnp.int32)[:, None] == wanted[None, :]).astype(F32)
+    hit = (wanted[:, None] == jnp.arange(2 * near.shape[0], dtype=jnp.int32)[None, :]).astype(F32)
 
-    def pair_grad(images):
-        cosine = lax.dot_general(images, text_bf, (((1,), (1,)), ((), ())), preferred_element_type=F32)
-        return jax.nn.sigmoid(scale * cosine + bias[0])
+    first = lax.axis_index(NARROW) * (rows // 8)
+    image_unit, image_norm = unit_rows(lax.dynamic_slice_in_dim(image_emb, first, rows // 8, 0))
+    text_unit, text_norm = unit_rows(text_emb)
+    image_unit, image_norm, text_unit, text_norm = lax.optimization_barrier(
+        (image_unit, image_norm, text_unit, text_norm)
+    )
 
-    far_grad = pair_grad(far).astype(BF16)
-    far_terms = swap(jnp.dot(far_grad, text_bf, preferred_element_type=F32).astype(BF16), "c")
-    near_grad = (pair_grad(near) - hit).astype(BF16)
-    near_terms = jnp.dot(near_grad, text_bf, preferred_element_type=F32) + far_terms.astype(F32)
-    near_terms = near_terms.astype(BF16).reshape(peers, rows // 8, width)
-    first = lax.axis_index(NARROW) * (rows // 8)
-    image_rows = lax.dynamic_slice_in_dim(image_emb, first, rows // 8, 0)
-    done = finish(exchange(near_terms, ("yl", "x", "l")), image_rows, scale)
+    images = jnp.concatenate([near, far], axis=0)
+    cosine = lax.dot_general(text_bf, images, (((1,), (1,)), ((), ())), preferred_element_type=F32)
+    grad = (jax.nn.sigmoid(scale * cosine + bias[0]) - hit).astype(BF16)
+    text_terms = jnp.dot(grad, images, preferred_element_type=F32).astype(BF16)
+    text_terms, grad = lax.optimization_barrier((text_terms, grad))
+    text_sum = exchange(text_terms.reshape(peers, mine, width), RINGS, TEXT_GROUPS)
 
-    over_images = (((0,), (0,)), ((), ()))
-    text_terms = lax.dot_general(near_grad, near, over_images, preferred_element_type=F32)
-    text_terms = text_terms + lax.dot_general(far_grad, far, over_images, preferred_element_type=F32)
-    text_terms, done = lax.optimization_barrier((text_terms.astype(BF16), done))
-    grad_image = lax.all_gather(done, NARROW, axis=0, tiled=True)
-    grad_text = finish(exchange(text_terms.reshape(peers, mine, width), RINGS, TEXT_GROUPS), text_emb, scale)
+    def image_product(columns):
+        return lax.dot_general(columns, text_bf, (((0,), (0,)), ((), ())), preferred_element_type=F32)
+
+    half = near.shape[0]
+    far_terms = swap(image_product(grad[:, half:]).astype(BF16), "c")
+    both = (image_product(grad[:, :half]) + far_terms.astype(F32)).reshape(2, n_x, quarter, width)
+
+    def of_position(k):
+        return lax.dynamic_index_in_dim(both, lax.rem(x + k, n_x), axis=1, keepdims=False)
+
+    total = of_position(0)
+    for d in (2, 1, 3):
+        sent = of_position(d).astype(BF16).reshape(2 * quarter, width)
+        total = total + shift(sent, "x", d).astype(F32).reshape(2, quarter, width)
+    total, text_sum = lax.optimization_barrier((total.astype(BF16), text_sum))
+    image_sum = exchange(total.reshape(4, rows // 8, width), ("yl", "l"))
+    done = finish(image_sum, image_unit, image_norm, scale)
+    grad_image = exchange(jnp.broadcast_to(done[None], (8,) + done.shape), NARROW).reshape(rows, width)
+    grad_text = finish(text_sum, text_unit, text_norm, scale)
     return grad_image, grad_text
 
 

time: 154 us -> 137 us (0.89)
  blocking collectives: 46.8 us -> 0 us
  starting transfers between devices: 51.8 us -> 71.9 us
  waiting for transfers between devices: 24.8 us -> 37.4 us
  other arithmetic: 1.71 us -> 8.45 us
  Pallas kernels: 6.55 us -> 2.18 us
  matrix products: 14.2 us -> 10.6 us
  local copies, waits for them, and re-layouts: 3.96 us -> 2.06 us
    all_gather x1 -> x0, blocking collectives: 46.8 us -> none  [local(): grad_image = lax.all_gather(done, NARROW, axis=0, tiled=True)]
    ppermute x3 -> x6, starting transfers between devices: 10.3 us -> 22.3 us  [shift(): lax.ppermute(block, axis, [(i, (i + distance) % count) for i in range(cou...]
    all_to_all x3 -> x4, starting transfers between devices: 34.4 us -> 42.5 us  [exchange(): lax.all_to_all(blocks, axes, 0, 0, axis_index_groups=groups, tiled=True)]
    all_to_all x3 -> x4, waiting for transfers between devices: 18.2 us -> 25.8 us  [exchange(): lax.all_to_all(blocks, axes, 0, 0, axis_index_groups=groups, tiled=True)]
    ppermute x3 -> x6, waiting for transfers between devices: 6 us -> 11.6 us  [shift(): lax.ppermute(block, axis, [(i, (i + distance) % count) for i in range(cou...]
    pallas_call x2 -> x0, Pallas kernels: 4.37 us -> none  [finish(): pl.pallas_call(body, out_shape=jax.ShapeDtypeStruct((height, width), BF16...]
    dot_general x6 -> x4, matrix products: 14.2 us -> 10.6 us  [the longest x1 4.2 us: local(): text_terms = jnp.dot(grad, images, preferred_element_type=F32).astype(BF16)]
    convert_element_type x0 -> x3, other arithmetic: none -> 2.81 us  [the longest x1 1.98 us: local(): total, text_sum = lax.optimization_barrier((total.astype(BF16), text_sum))]
  transfers between devices with their start and end apart: 9 -> 13, of which waited for: 5 -> 9; matrix products, arithmetic and copies ran while one was open for 6% -> 8% of each run, Pallas kernels for 0% -> 0%
where the time goes in v9:
time: 137 us; the launch traced here: 135 us
  starting transfers between devices  71.9 us (52%)
  waiting for transfers between devices  37.4 us (27%)
  matrix products  10.6 us (8%)
  other arithmetic  8.45 us (6%)
  between operations  2.29 us (2%)
  Pallas kernels  2.18 us (2%)
  local copies, waits for them, and re-layouts  2.06 us (2%)
    all_to_all x4, starting transfers between devices, exchange(): lax.all_to_all(blocks, axes, 0, 0, axis_index_groups=groups, tiled=True)  42.5 us
    all_to_all x4, waiting for transfers between devices, exchange(): lax.all_to_all(blocks, axes, 0, 0, axis_index_groups=groups, tiled=True)  25.8 us
    ppermute x6, starting transfers between devices, shift(): lax.ppermute(block, axis, [(i, (i + distance) % count) for i in range(cou...  22.3 us
    ppermute x6, waiting for transfers between devices, shift(): lax.ppermute(block, axis, [(i, (i + distance) % count) for i in range(cou...  11.6 us
    ppermute x3, starting transfers between devices, swap(): return lax.ppermute(block, axis, [(0, 1), (1, 0)])  7.09 us
    dot_general x1, matrix products, local(): text_terms = jnp.dot(grad, images, preferred_element_type=F32).astype(BF16)  4.2 us
    dot_general x2, matrix products, image_product(): lax.dot_general(columns, text_bf, (((0,), (0,)), ((), ())), preferred_ele...  3.19 us
    dot_general x1, matrix products, local(): lax.dot_general(text_bf, images, (((1,), (1,)), ((), ())), preferred_elem...  3.17 us
  transfers between devices with their start and end apart: 13, of which 9 were waited for; matrix products, arithmetic and copies ran while one was open for 8% of the time, Pallas kernels for 0%

profile of v9, /device:TPU:56, one launch (start us, length us, event | category | flops | bytes accessed | tf_op | source)
XLA Modules:
  0.0 134.9 jit_solution(10599685018419568612)
XLA Ops:
  0.6 2.2 %first_copies.1 = (bf16[64,1152]{1,0:T(8,128)(2,1)}, bf16[16,32,1152]{2,1,0:T(8,128)(2,1)}) custom-call(s32[1]{0:T(128)} %bitcast.1.x_ref, bf16[256,1152]{1,0:T(8,128)(2,1)} %image_ref.1, bf16[32,1152]{1,0:T(8,128)(2,1)} %text_ref.1), custom_call_target="tpu_custom_call" | custom-call | tf_op jit(solution)/shard_map/first_copies/pallas_call | solution.py:46
  2.8 3.2 %collective-permute-start = (bf16[64,1152]{1,0:T(8,128)(2,1)}, bf16[64,1152]{1,0:T(8,128)(2,1)S(1)}, u32[]{:S(2)}, u32[]{:S(2)}) collective-permute-start(bf16[64,1152]{1,0:T(8,128)(2,1)} %get-tuple-element.13), channel_id=1, source_target_pairs={{0,64},{64,0},{1,65},{65,1},{2,66},{66,2},{3,67},{67,3},{4,68},{68... | collective-permute-start | bytes 442376 | tf_op jit(solution)/shard_map/ppermute | solution.py:24
  6.1 14.7 %all-to-all-start = ((bf16[16,32,1152]{2,1,0:T(8,128)(2,1)}), bf16[16,32,1152]{2,1,0:T(8,128)(2,1)S(1)}, u32[]{:S(2)}, u32[]{:S(2)}) async-start(bf16[16,32,1152]{2,1,0:T(8,128)(2,1)} %get-tuple-element.12), calls=%async_computation | async-start | bytes 2359296 | tf_op jit(solution)/shard_map/all_to_all | solution.py:33
  22.1 0.0 copy-start
  22.1 4.8 %collective-permute-start.1 = (bf16[64,1152]{1,0:T(8,128)(2,1)S(1)}, bf16[64,1152]{1,0:T(8,128)(2,1)S(1)}, u32[]{:S(2)}, u32[]{:S(2)}) collective-permute-start(bf16[64,1152]{1,0:T(8,128)(2,1)S(1)} %collective-permute-done), channel_id=1, source_target_pairs={{0,6},{2,0},{4,2},{6,4},{1,7},{3,1},{5,3},{7,5},{8,14},{10,8},{12,... | collective-permute-start | bytes 442376 | tf_op jit(solution)/shard_map/ppermute | solution.py:29
  26.9 2.7 %collective-permute-start.2 = (bf16[64,1152]{1,0:T(8,128)(2,1)S(1)}, bf16[64,1152]{1,0:T(8,128)(2,1)S(1)}, u32[]{:S(2)}, u32[]{:S(2)}) collective-permute-start(bf16[64,1152]{1,0:T(8,128)(2,1)S(1)} %collective-permute-done), channel_id=1, source_target_pairs={{0,4},{2,6},{4,0},{6,2},{1,5},{3,7},{5,1},{7,3},{8,12},{10,14},{12... | collective-permute-start | bytes 442376 | tf_op jit(solution)/shard_map/ppermute | solution.py:29
  29.6 2.8 %collective-permute-start.3 = (bf16[64,1152]{1,0:T(8,128)(2,1)S(1)}, bf16[64,1152]{1,0:T(8,128)(2,1)S(1)}, u32[]{:S(2)}, u32[]{:S(2)}) collective-permute-start(bf16[64,1152]{1,0:T(8,128)(2,1)S(1)} %collective-permute-done), channel_id=1, source_target_pairs={{0,2},{2,4},{4,6},{6,0},{1,3},{3,5},{5,7},{7,1},{8,10},{10,12},{12... | collective-permute-start | bytes 442376 | tf_op jit(solution)/shard_map/ppermute | solution.py:29
  32.5 4.3 %collective-permute-done.2 = bf16[64,1152]{1,0:T(8,128)(2,1)S(1)} collective-permute-done((bf16[64,1152]{1,0:T(8,128)(2,1)S(1)}, bf16[64,1152]{1,0:T(8,128)(2,1)S(1)}, u32[]{:S(2)}, u32[]{:S(2)}) %collective-permute-start.2) | collective-permute-done | bytes 147488 | tf_op jit(solution)/shard_map/ppermute | solution.py:29
  36.9 1.7 %collective-permute-done.3 = bf16[64,1152]{1,0:T(8,128)(2,1)S(1)} collective-permute-done((bf16[64,1152]{1,0:T(8,128)(2,1)S(1)}, bf16[64,1152]{1,0:T(8,128)(2,1)S(1)}, u32[]{:S(2)}, u32[]{:S(2)}) %collective-permute-start.3) | collective-permute-done | bytes 147488 | tf_op jit(solution)/shard_map/ppermute | solution.py:29
  38.6 0.2 broadcast_select_fusion.1
  38.9 0.3 fusion
  39.2 0.4 fusion.1
  39.6 1.9 %collective-permute-start.4 = (bf16[512,1152]{1,0:T(8,128)(2,1)S(1)}, bf16[512,1152]{1,0:T(8,128)(2,1)}, u32[]{:S(2)}, u32[]{:S(2)}) collective-permute-start(bf16[512,1152]{1,0:T(8,128)(2,1)S(1)} %fusion.1), channel_id=1, source_target_pairs={{0,8},{8,0},{1,9},{9,1},{2,10},{10,2},{3,11},{11,3},{4,12},{12,4},... | collective-permute-start | bytes 3538952 | tf_op jit(solution)/shard_map/ppermute | solution.py:24
  41.5 0.1 add_dynamic-update-slice_fusion
  41.7 6.9 %all-to-all-done = bf16[16,32,1152]{2,1,0:T(8,128)(2,1)S(1)} async-done(((bf16[16,32,1152]{2,1,0:T(8,128)(2,1)}), bf16[16,32,1152]{2,1,0:T(8,128)(2,1)S(1)}, u32[]{:S(2)}, u32[]{:S(2)}) %all-to-all-start) | async-done | bytes 1179680 | tf_op jit(solution)/shard_map/all_to_all | solution.py:33
  48.6 0.3 multiply_reduce_fusion
  48.9 0.1 sqrt.50
  49.0 0.4 fusion.2
  49.3 3.2 %subtract_convert_fusion = bf16[512,1024]{1,0:T(8,128)(2,1)S(1)} fusion(bf16[512,1152]{1,0:T(8,128)(2,1)S(1)} %fusion.2, bf16[512,1152]{1,0:T(8,128)(2,1)} %collective-permute-done.4, bf16[512,1152]{1,0:T(8,128)(2,1)S(1)} %fusion.1, s32[512]{0:T(512)S(1)} %add_dynamic-update-slice_fusion, f32[]{:T(128)} %bitcast.32, f32[]{:T(128)} %bitcast), kind=kOutput, calls=%fused_computation.12 | convolution fusion | flops 1217396736 | bytes 4589576 | tf_op jit(solution)/shard_map/dot_general | solution.py:97
  52.5 4.2 %convolution_convert_fusion.1 = bf16[512,1152]{1,0:T(8,128)(2,1)} fusion(bf16[512,1024]{1,0:T(8,128)(2,1)S(1)} %subtract_convert_fusion, bf16[512,1152]{1,0:T(8,128)(2,1)} %collective-permute-done.4, bf16[512,1152]{1,0:T(8,128)(2,1)S(1)} %fusion.1), kind=kOutput, calls=%fused_computation.1 | convolution fusion | flops 1213267968 | bytes 4587520 | tf_op jit(solution)/shard_map/dot_general | solution.py:99
  56.7 0.9 convolution_convert_fusion
  57.6 1.9 %collective-permute-start.5 = (bf16[512,1152]{1,0:T(8,128)(2,1)S(1)}, bf16[512,1152]{1,0:T(8,128)(2,1)}, u32[]{:S(2)}, u32[]{:S(2)}) collective-permute-start(bf16[512,1152]{1,0:T(8,128)(2,1)S(1)} %convolution_convert_fusion), channel_id=1, source_target_pairs={{0,8},{8,0},{1,9},{9,1},{2,10},{10,2},{3,11},{11,3},{4,12},{12,4},... | collective-permute-start | bytes 3538952 | tf_op jit(solution)/shard_map/ppermute | solution.py:24
  59.6 10.2 %all-to-all-start.1 = ((bf16[16,32,1152]{2,1,0:T(8,128)(2,1)}), bf16[16,32,1152]{2,1,0:T(8,128)(2,1)}, u32[]{:S(2)}, u32[]{:S(2)}) async-start(bf16[16,32,1152]{2,1,0:T(8,128)(2,1)} %bitcast.12), calls=%async_computation.1 | async-start | bytes 2359296 | tf_op jit(solution)/shard_map/all_to_all | solution.py:33
  69.7 0.1 fusion.10
  69.9 2.3 %convert_add_fusion = f32[512,1152]{1,0:T(8,128)S(1)} fusion(bf16[512,1152]{1,0:T(8,128)(2,1)} %collective-permute-done.5, bf16[512,1152]{1,0:T(8,128)(2,1)S(1)} %fusion.2, bf16[512,1024]{1,0:T(8,128)(2,1)} %copy-done.3), kind=kOutput, calls=%fused_computation.10 | convolution fusion | flops 605159424 | bytes 5242880 | tf_op jit(solution)/shard_map/dot_general | solution.py:104
  72.2 0.1 dynamic-slice_convert_fusion.2
  72.3 4.9 %collective-permute-start.6 = (bf16[128,1152]{1,0:T(8,128)(2,1)S(1)}, bf16[128,1152]{1,0:T(8,128)(2,1)}, u32[]{:S(2)}, u32[]{:S(2)}) collective-permute-start(bf16[128,1152]{1,0:T(8,128)(2,1)S(1)} %bitcast.38), channel_id=1, source_target_pairs={{0,4},{2,6},{4,0},{6,2},{1,5},{3,7},{5,1},{7,3},{8,12},{10,14},{12... | collective-permute-start | bytes 884744 | tf_op jit(solution)/shard_map/ppermute | solution.py:29
  77.3 2.5 %collective-permute-start.7 = (bf16[128,1152]{1,0:T(8,128)(2,1)S(1)}, bf16[128,1152]{1,0:T(8,128)(2,1)}, u32[]{:S(2)}, u32[]{:S(2)}) collective-permute-start(bf16[128,1152]{1,0:T(8,128)(2,1)S(1)} %bitcast.37), channel_id=1, source_target_pairs={{0,2},{2,4},{4,6},{6,0},{1,3},{3,5},{5,7},{7,1},{8,10},{10,12},{12... | collective-permute-start | bytes 884744 | tf_op jit(solution)/shard_map/ppermute | solution.py:29
  79.8 4.6 %collective-permute-start.8 = (bf16[128,1152]{1,0:T(8,128)(2,1)S(1)}, bf16[128,1152]{1,0:T(8,128)(2,1)}, u32[]{:S(2)}, u32[]{:S(2)}) collective-permute-start(bf16[128,1152]{1,0:T(8,128)(2,1)S(1)} %bitcast.36), channel_id=1, source_target_pairs={{0,6},{2,0},{4,2},{6,4},{1,7},{3,1},{5,3},{7,5},{8,14},{10,8},{12,... | collective-permute-start | bytes 884744 | tf_op jit(solution)/shard_map/ppermute | solution.py:29
  84.4 0.1 convert_divide_fusion.1
  84.5 1.0 fusion.9
  85.5 0.2 collective-permute-done.6
  85.7 5.3 %collective-permute-done.7 = bf16[128,1152]{1,0:T(8,128)(2,1)} collective-permute-done((bf16[128,1152]{1,0:T(8,128)(2,1)S(1)}, bf16[128,1152]{1,0:T(8,128)(2,1)}, u32[]{:S(2)}, u32[]{:S(2)}) %collective-permute-start.7) | collective-permute-done | bytes 294944 | tf_op jit(solution)/shard_map/ppermute | solution.py:29
  91.0 0.1 collective-permute-done.8
  91.1 2.0 %fusion.3 = bf16[2,64,1152]{2,1,0:T(8,128)(2,1)} fusion(bf16[2,64,1152]{2,1,0:T(8,128)(2,1)} %bitcast.21, bf16[2,64,1152]{2,1,0:T(8,128)(2,1)} %bitcast.20, bf16[2,64,1152]{2,1,0:T(8,128)(2,1)} %bitcast.19, f32[2,4,64,1152]{3,2,1,0:T(8,128)S(1)} %bitcast.34, s32[]{:T(128)S(6)} %select_n.39), kind=kLoop, calls=%fused_computation.16 | loop fusion | flops 1032192 | bytes 1769476 | tf_op jit(solution)/shard_map/convert_element_type | solution.py:117
  93.1 7.2 %all-to-all-done.1 = bf16[16,32,1152]{2,1,0:T(8,128)(2,1)} async-done(((bf16[16,32,1152]{2,1,0:T(8,128)(2,1)}), bf16[16,32,1152]{2,1,0:T(8,128)(2,1)}, u32[]{:S(2)}, u32[]{:S(2)}) %all-to-all-start.1) | async-done | bytes 1179680 | tf_op jit(solution)/shard_map/all_to_all | solution.py:33
  100.3 12.8 %all-to-all-start.2 = ((bf16[4,32,1152]{2,1,0:T(8,128)(2,1)}), bf16[4,32,1152]{2,1,0:T(8,128)(2,1)S(1)}, u32[]{:S(2)}, u32[]{:S(2)}) async-start(bf16[4,32,1152]{2,1,0:T(8,128)(2,1)} %bitcast.13), calls=%async_computation.2 | async-start | bytes 589824 | tf_op jit(solution)/shard_map/all_to_all | solution.py:33
  113.1 1.0 convert_divide_fusion.2
  114.1 3.9 %all-to-all-done.2 = bf16[4,32,1152]{2,1,0:T(8,128)(2,1)S(1)} async-done(((bf16[4,32,1152]{2,1,0:T(8,128)(2,1)}), bf16[4,32,1152]{2,1,0:T(8,128)(2,1)S(1)}, u32[]{:S(2)}, u32[]{:S(2)}) %all-to-all-start.2) | async-done | bytes 294944 | tf_op jit(solution)/shard_map/all_to_all | solution.py:33
  118.0 0.1 multiply_reduce_fusion.2
  118.1 0.1 divide_convert_fusion.1
  118.2 0.9 broadcast_in_dim.2
  119.1 4.9 %all-to-all-start.3 = ((bf16[8,32,1152]{2,1,0:T(8,128)(2,1)}), bf16[8,32,1152]{2,1,0:T(8,128)(2,1)S(1)}, u32[]{:S(2)}, u32[]{:S(2)}) async-start(bf16[8,32,1152]{2,1,0:T(8,128)(2,1)} %broadcast_in_dim.2), calls=%async_computation.3 | async-start | bytes 1179648 | tf_op jit(solution)/shard_map/all_to_all | solution.py:33
  124.0 1.4 %convert_reduce_fusion = f32[32,1152]{1,0:T(8,128)S(1)} fusion(bf16[16,32,1152]{2,1,0:T(8,128)(2,1)} %all-to-all-done.1), kind=kLoop, calls=%fused_computation.9 | loop fusion | flops 1142784 | bytes 1327104 | tf_op jit(solution)/shard_map/reduce_sum | solution.py:59
  125.4 0.1 multiply_reduce_fusion.1
  125.6 0.7 divide_convert_fusion
  126.3 7.8 %all-to-all-done.3 = bf16[8,32,1152]{2,1,0:T(8,128)(2,1)S(1)} async-done(((bf16[8,32,1152]{2,1,0:T(8,128)(2,1)}), bf16[8,32,1152]{2,1,0:T(8,128)(2,1)S(1)}, u32[]{:S(2)}, u32[]{:S(2)}) %all-to-all-start.3) | async-done | bytes 589856 | tf_op jit(solution)/shard_map/all_to_all | solution.py:33
  134.1 0.8 copy.18
  (27 shorter events, 0.3 us)
Async XLA Ops:
  2.8 19.3 %collective-permute-start = (bf16[64,1152]{1,0:T(8,128)(2,1)}, bf16[64,1152]{1,0:T(8,128)(2,1)S(1)}, u32[]{:S(2)}, u32[]{:S(2)}) collective-permute-start(bf16[64,1152]{1,0:T(8,128)(2,1)} %get-tuple-element.13), channel_id=1, source_target_pairs={{0,64},{64,0},{1,65},{65,1},{2,66},{66,2},{3,67},{67,3},{4,68},{68... | collective-permute-start | bytes 442376 | tf_op jit(solution)/shard_map/ppermute | solution.py:24
  6.1 42.5 %all-to-all-start = ((bf16[16,32,1152]{2,1,0:T(8,128)(2,1)}), bf16[16,32,1152]{2,1,0:T(8,128)(2,1)S(1)}, u32[]{:S(2)}, u32[]{:S(2)}) async-start(bf16[16,32,1152]{2,1,0:T(8,128)(2,1)} %get-tuple-element.12), calls=%async_computation | async-start | bytes 2359296 | tf_op jit(solution)/shard_map/all_to_all | solution.py:33
  22.1 16.5 %copy-start = (bf16[256,1152]{1,0:T(8,128)(2,1)S(1)}, bf16[256,1152]{1,0:T(8,128)(2,1)}, u32[]{:S(2)}) copy-start(bf16[256,1152]{1,0:T(8,128)(2,1)} %image_ref.1) | copy-start | bytes 1769476
  22.1 10.3 %collective-permute-start.1 = (bf16[64,1152]{1,0:T(8,128)(2,1)S(1)}, bf16[64,1152]{1,0:T(8,128)(2,1)S(1)}, u32[]{:S(2)}, u32[]{:S(2)}) collective-permute-start(bf16[64,1152]{1,0:T(8,128)(2,1)S(1)} %collective-permute-done), channel_id=1, source_target_pairs={{0,6},{2,0},{4,2},{6,4},{1,7},{3,1},{5,3},{7,5},{8,14},{10,8},{12,... | collective-permute-start | bytes 442376 | tf_op jit(solution)/shard_map/ppermute | solution.py:29
  26.9 9.9 %collective-permute-start.2 = (bf16[64,1152]{1,0:T(8,128)(2,1)S(1)}, bf16[64,1152]{1,0:T(8,128)(2,1)S(1)}, u32[]{:S(2)}, u32[]{:S(2)}) collective-permute-start(bf16[64,1152]{1,0:T(8,128)(2,1)S(1)} %collective-permute-done), channel_id=1, source_target_pairs={{0,4},{2,6},{4,0},{6,2},{1,5},{3,7},{5,1},{7,3},{8,12},{10,14},{12... | collective-permute-start | bytes 442376 | tf_op jit(solution)/shard_map/ppermute | solution.py:29
  29.6 8.9 %collective-permute-start.3 = (bf16[64,1152]{1,0:T(8,128)(2,1)S(1)}, bf16[64,1152]{1,0:T(8,128)(2,1)S(1)}, u32[]{:S(2)}, u32[]{:S(2)}) collective-permute-start(bf16[64,1152]{1,0:T(8,128)(2,1)S(1)} %collective-permute-done), channel_id=1, source_target_pairs={{0,2},{2,4},{4,6},{6,0},{1,3},{3,5},{5,7},{7,1},{8,10},{10,12},{12... | collective-permute-start | bytes 442376 | tf_op jit(solution)/shard_map/ppermute | solution.py:29
  39.2 2.3 %copy-start.4 = (s32[32]{0:T(128)S(1)}, s32[32]{0:T(128)}, u32[]{:S(2)}) copy-start(s32[32]{0:T(128)} %param.7) | copy-start | bytes 388
  39.6 9.7 %collective-permute-start.4 = (bf16[512,1152]{1,0:T(8,128)(2,1)S(1)}, bf16[512,1152]{1,0:T(8,128)(2,1)}, u32[]{:S(2)}, u32[]{:S(2)}) collective-permute-start(bf16[512,1152]{1,0:T(8,128)(2,1)S(1)} %fusion.1), channel_id=1, source_target_pairs={{0,8},{8,0},{1,9},{9,1},{2,10},{10,2},{3,11},{11,3},{4,12},{12,4},... | collective-permute-start | bytes 3538952 | tf_op jit(solution)/shard_map/ppermute | solution.py:24
  52.5 4.2 %copy-start.3 = (bf16[512,1024]{1,0:T(8,128)(2,1)}, bf16[512,1024]{1,0:T(8,128)(2,1)S(1)}, u32[]{:S(2)}) copy-start(bf16[512,1024]{1,0:T(8,128)(2,1)S(1)} %subtract_convert_fusion) | copy-start | bytes 3145732
  57.6 12.2 %collective-permute-start.5 = (bf16[512,1152]{1,0:T(8,128)(2,1)S(1)}, bf16[512,1152]{1,0:T(8,128)(2,1)}, u32[]{:S(2)}, u32[]{:S(2)}) collective-permute-start(bf16[512,1152]{1,0:T(8,128)(2,1)S(1)} %convolution_convert_fusion), channel_id=1, source_target_pairs={{0,8},{8,0},{1,9},{9,1},{2,10},{10,2},{3,11},{11,3},{4,12},{12,4},... | collective-permute-start | bytes 3538952 | tf_op jit(solution)/shard_map/ppermute | solution.py:24
  59.5 10.2 %copy-start.1 = (bf16[32,1152]{1,0:T(8,128)(2,1)S(1)}, bf16[32,1152]{1,0:T(8,128)(2,1)}, u32[]{:S(2)}) copy-start(bf16[32,1152]{1,0:T(8,128)(2,1)} %text_ref.1) | copy-start | bytes 221188
  59.6 40.7 %all-to-all-start.1 = ((bf16[16,32,1152]{2,1,0:T(8,128)(2,1)}), bf16[16,32,1152]{2,1,0:T(8,128)(2,1)}, u32[]{:S(2)}, u32[]{:S(2)}) async-start(bf16[16,32,1152]{2,1,0:T(8,128)(2,1)} %bitcast.12), calls=%async_computation.1 | async-start | bytes 2359296 | tf_op jit(solution)/shard_map/all_to_all | solution.py:33
  72.2 12.2 %copy-start.2 = (bf16[32,1152]{1,0:T(8,128)(2,1)S(1)}, bf16[32,1152]{1,0:T(8,128)(2,1)}, u32[]{:S(2)}) copy-start(bf16[32,1152]{1,0:T(8,128)(2,1)} %text_ref.1) | copy-start | bytes 221188
  72.3 13.4 %collective-permute-start.6 = (bf16[128,1152]{1,0:T(8,128)(2,1)S(1)}, bf16[128,1152]{1,0:T(8,128)(2,1)}, u32[]{:S(2)}, u32[]{:S(2)}) collective-permute-start(bf16[128,1152]{1,0:T(8,128)(2,1)S(1)} %bitcast.38), channel_id=1, source_target_pairs={{0,4},{2,6},{4,0},{6,2},{1,5},{3,7},{5,1},{7,3},{8,12},{10,14},{12... | collective-permute-start | bytes 884744 | tf_op jit(solution)/shard_map/ppermute | solution.py:29
  77.3 13.7 %collective-permute-start.7 = (bf16[128,1152]{1,0:T(8,128)(2,1)S(1)}, bf16[128,1152]{1,0:T(8,128)(2,1)}, u32[]{:S(2)}, u32[]{:S(2)}) collective-permute-start(bf16[128,1152]{1,0:T(8,128)(2,1)S(1)} %bitcast.37), channel_id=1, source_target_pairs={{0,2},{2,4},{4,6},{6,0},{1,3},{3,5},{5,7},{7,1},{8,10},{10,12},{12... | collective-permute-start | bytes 884744 | tf_op jit(solution)/shard_map/ppermute | solution.py:29
  79.8 11.3 %collective-permute-start.8 = (bf16[128,1152]{1,0:T(8,128)(2,1)S(1)}, bf16[128,1152]{1,0:T(8,128)(2,1)}, u32[]{:S(2)}, u32[]{:S(2)}) collective-permute-start(bf16[128,1152]{1,0:T(8,128)(2,1)S(1)} %bitcast.36), channel_id=1, source_target_pairs={{0,6},{2,0},{4,2},{6,4},{1,7},{3,1},{5,3},{7,5},{8,14},{10,8},{12,... | collective-permute-start | bytes 884744 | tf_op jit(solution)/shard_map/ppermute | solution.py:29
  100.3 17.7 %all-to-all-start.2 = ((bf16[4,32,1152]{2,1,0:T(8,128)(2,1)}), bf16[4,32,1152]{2,1,0:T(8,128)(2,1)S(1)}, u32[]{:S(2)}, u32[]{:S(2)}) async-start(bf16[4,32,1152]{2,1,0:T(8,128)(2,1)} %bitcast.13), calls=%async_computation.2 | async-start | bytes 589824 | tf_op jit(solution)/shard_map/all_to_all | solution.py:33
  119.1 15.0 %all-to-all-start.3 = ((bf16[8,32,1152]{2,1,0:T(8,128)(2,1)}), bf16[8,32,1152]{2,1,0:T(8,128)(2,1)S(1)}, u32[]{:S(2)}, u32[]{:S(2)}) async-start(bf16[8,32,1152]{2,1,0:T(8,128)(2,1)} %broadcast_in_dim.2), calls=%async_computation.3 | async-start | bytes 1179648 | tf_op jit(solution)/shard_map/all_to_all | solution.py:33

commit v10 on v9

v10 whole, which is shorter than its diff:
```python
import jax
import jax.numpy as jnp
from jax import lax
from jax.experimental import pallas as pl
from jax.experimental.pallas import tpu as pltpu
from jax.sharding import Mesh, PartitionSpec as P

epsilon = 1e-06
AXES = ("yh", "yl", "w", "c", "x", "l")
CLASSES = ((0, 3, 5, 6), (1, 2, 4, 7))
RINGS = ("yh", "yl", "w", "l")
TEXT_GROUPS = [[y * 8 + z for y in of_y for z in of_z] for of_y in CLASSES for of_z in CLASSES]
NARROW = ("x", "l")
BF16, F32 = jnp.bfloat16, jnp.float32


def unit_rows(values):
    as_float = values.astype(F32)
    row_norm = jnp.sqrt(jnp.sum(as_float * as_float, axis=1, keepdims=True) + epsilon)
    return as_float / row_norm, row_norm


def swap(block, axes):
    count = lax.axis_size(axes)
    return lax.ppermute(block, axes, [(i, count - 1 - i) for i in range(count)])


def shift(block, axis, distance):
    count = lax.axis_size(axis)
    return lax.ppermute(block, axis, [(i, (i + distance) % count) for i in range(count)])


def exchange(blocks, axes, groups=None):
    return lax.all_to_all(blocks, axes, 0, 0, axis_index_groups=groups, tiled=True)


def in_order(around, x):
    count, height = len(around), around[0].shape[0]
    start = lax.rem(count - x, count) * height
    return lax.dynamic_slice_in_dim(jnp.concatenate(around * 2, axis=0), start, count * height, 0)


def first_copies(x, image_emb, text_emb, quarter, peers):
    mine, width = text_emb.shape

    def body(x_ref, image_ref, text_ref, quarter_ref, copies_ref, sems):
        start = pl.multiple_of(x_ref[0] * quarter, quarter)
        copies = [pltpu.make_async_copy(image_ref.at[pl.ds(start, quarter)], quarter_ref, sems.at[peers])]
        copies += [pltpu.make_async_copy(text_ref, copies_ref.at[k], sems.at[k]) for k in range(peers)]
        for copy in copies:
            copy.start()
        for copy in copies:
            copy.wait()

    anywhere = pl.BlockSpec(memory_space=pl.ANY)
    return pl.pallas_call(
        body,
        out_shape=(
            jax.ShapeDtypeStruct((quarter, width), BF16),
            jax.ShapeDtypeStruct((peers, mine, width), BF16),
        ),
        in_specs=[pl.BlockSpec(memory_space=pltpu.SMEM), anywhere, anywhere],
        out_specs=(anywhere, anywhere),
        scratch_shapes=[pltpu.SemaphoreType.DMA((peers + 1,))],
        name="first_copies",
    )(x, image_emb, text_emb)


def finish(terms, unit, norm, scale):
    total = scale * jnp.sum(terms.astype(F32), axis=0)
    along = jnp.sum(unit * total, axis=1, keepdims=True)
    return ((total - unit * along) / norm).astype(BF16)


def local(image_emb, text_emb, positive, log_scale, bias):
    scale = jnp.exp(log_scale[0])
    rows, width = image_emb.shape
    mine = text_emb.shape[0]
    peers = len(TEXT_GROUPS[0])
    n_x = lax.axis_size("x")
    x = lax.axis_index("x")
    upper = lax.axis_index("yl") == 1
    quarter = rows // n_x

    part, copies = first_copies(x.astype(jnp.int32).reshape(1), image_emb, text_emb, quarter, peers)
    part = swap(part, "yl")
    texts = exchange(copies, RINGS, TEXT_GROUPS).reshape(-1, width)
    around = [part] + [shift(part, "x", n_x - d) for d in range(1, n_x)]
    beyond = in_order(around, x)
    chip = jnp.concatenate([jnp.where(upper, beyond, image_emb), jnp.where(upper, image_emb, beyond)], axis=0)
    near = unit_rows(chip)[0].astype(BF16)
    far = swap(near, "c")
    text_bf = unit_rows(texts)[0].astype(BF16)

    wanted = positive - lax.axis_index(("yh", "yl", "w", "c")) * rows + lax.axis_index("yl") * rows
    slot = lax.axis_index(("yh", "w")) * mine
    wanted = lax.dynamic_update_slice_in_dim(jnp.full((texts.shape[0],), -1, jnp.int32), wanted, slot, 0)
    hit = (jnp.arange(2 * near.shape[0], dtype=jnp.int32)[:, None] == wanted[None, :]).astype(F32)

    image_unit, image_norm = unit_rows(lax.dynamic_slice_in_dim(image_emb, x * quarter, quarter, 0))
    text_unit, text_norm = unit_rows(text_emb)
    image_unit, image_norm, text_unit, text_norm = lax.optimization_barrier(
        (image_unit, image_norm, text_unit, text_norm)
    )

    images = jnp.concatenate([near, far], axis=0)
    cosine = lax.dot_general(images, text_bf, (((1,), (1,)), ((), ())), preferred_element_type=F32)
    grad = (jax.nn.sigmoid(scale * cosine + bias[0]) - hit).astype(BF16)
    text_terms = lax.dot_general(grad, images, (((0,), (0,)), ((), ())), preferred_element_type=F32).astype(BF16)
    text_terms, grad = lax.optimization_barrier((text_terms, grad))
    text_sum = exchange(text_terms.reshape(peers, mine, width), RINGS, TEXT_GROUPS)

    half = near.shape[0]
    far_terms = jnp.dot(grad[half:], text_bf, preferred_element_type=F32).astype(BF16)
    far_terms = swap(far_terms, "c").astype(F32)
    both = jnp.dot(grad[:half], text_bf, preferred_element_type=F32) + far_terms
    both = both.reshape(2, n_x, quarter, width)

    def of_position(k):
        return lax.dynamic_index_in_dim(both, lax.rem(x + k, n_x), axis=1, keepdims=False)

    total = of_position(0)
    for d in (2, 1, 3):
        sent = of_position(d).astype(BF16).reshape(2 * quarter, width)
        total = total + shift(sent, "x", d).astype(F32).reshape(2, quarter, width)
    total = total.astype(BF16)
    own, other = jnp.where(upper, total[1], total[0]), jnp.where(upper, total[0], total[1])
    beside, across, corner = swap(own, "l"), swap(other, "yl"), swap(other, ("yl", "l"))
    image_sum = (own.astype(F32) + beside.astype(F32)) + (across.astype(F32) + corner.astype(F32))
    image_sum, text_sum = lax.optimization_barrier((image_sum, text_sum))
    done = finish(image_sum[None], image_unit, image_norm, scale)
    around = [done] + [shift(done, "x", n_x - d) for d in range(1, n_x)]
    grad_image = in_order(around, x)
    grad_text = finish(text_sum, text_unit, text_norm, scale)
    return grad_image, grad_text


def solution(mesh):
    fine = Mesh(mesh.devices.reshape(4, 2, 4, 2, 4, 2), AXES)
    dp = ("yh", "yl", "w", "c")
    in_specs = (P(dp, None), P(AXES, None), P(AXES), P(), P())
    out_specs = (P(dp, None), P(AXES, None))
    return jax.shard_map(local, mesh=fine, in_specs=in_specs, out_specs=out_specs, check_vma=False)
```

time: 137 us -> 172 us (1.26)
  Pallas kernels: 2.18 us -> 41.5 us
  waiting for transfers between devices: 37.4 us -> 29.9 us
  starting transfers between devices: 71.9 us -> 76 us
  other arithmetic: 8.45 us -> 4.74 us
    pallas_call x1, Pallas kernels: 2.18 us -> 41.5 us  [first_copies(): pl.pallas_call(body, out_shape=(jax.ShapeDtypeStruct((quarter, width), BF...]
    all_to_all x4 -> x2, waiting for transfers between devices: 25.8 us -> 5.89 us  [exchange(): lax.all_to_all(blocks, axes, 0, 0, axis_index_groups=groups, tiled=True)]
    all_to_all x4 -> x2, starting transfers between devices: 42.5 us -> 24.7 us  [exchange(): lax.all_to_all(blocks, axes, 0, 0, axis_index_groups=groups, tiled=True)]
    ppermute x3 -> x6, starting transfers between devices: 7.09 us -> 18.7 us  [swap(): return lax.ppermute(block, axes, [(i, count - 1 - i) for i in range(count)])]
    ppermute x6 -> x9, starting transfers between devices: 22.3 us -> 32.6 us  [shift(): lax.ppermute(block, axis, [(i, (i + distance) % count) for i in range(cou...]
    ppermute x3 -> x6, waiting for transfers between devices: 0.01 us -> 6.67 us  [swap(): return lax.ppermute(block, axes, [(i, count - 1 - i) for i in range(count)])]
    ppermute x6 -> x9, waiting for transfers between devices: 11.6 us -> 17.3 us  [shift(): lax.ppermute(block, axis, [(i, (i + distance) % count) for i in range(cou...]
    convert_element_type x1, other arithmetic: 1.98 us -> 0.15 us  [local(): total = total.astype(BF16)]
  transfers between devices with their start and end apart: 13 -> 17, of which waited for: 9 -> 10; matrix products, arithmetic and copies ran while one was open for 8% -> 4% of each run, Pallas kernels for 0% -> 0%
where the time goes in v10:
time: 172 us; the launch traced here: 168 us
  starting transfers between devices  76 us (44%)
  Pallas kernels  41.5 us (24%)
  waiting for transfers between devices  29.9 us (17%)
  matrix products  12.3 us (7%)
  other arithmetic  4.74 us (3%)
  between operations  2.38 us (1%)
    pallas_call x1, Pallas kernels, first_copies(): pl.pallas_call(body, out_shape=(jax.ShapeDtypeStruct((quarter, width), BF...  41.5 us
    ppermute x9, starting transfers between devices, shift(): lax.ppermute(block, axis, [(i, (i + distance) % count) for i in range(cou...  32.6 us
    all_to_all x2, starting transfers between devices, exchange(): lax.all_to_all(blocks, axes, 0, 0, axis_index_groups=groups, tiled=True)  24.7 us
    ppermute x6, starting transfers between devices, swap(): return lax.ppermute(block, axes, [(i, count - 1 - i) for i in range(count)])  18.7 us
    ppermute x9, waiting for transfers between devices, shift(): lax.ppermute(block, axis, [(i, (i + distance) % count) for i in range(cou...  17.3 us
    ppermute x6, waiting for transfers between devices, swap(): return lax.ppermute(block, axes, [(i, count - 1 - i) for i in range(count)])  6.67 us
    all_to_all x2, waiting for transfers between devices, exchange(): lax.all_to_all(blocks, axes, 0, 0, axis_index_groups=groups, tiled=True)  5.89 us
    dot_general x1, matrix products, local(): lax.dot_general(grad, images, (((0,), (0,)), ((), ())), preferred_element...  4.59 us
  transfers between devices with their start and end apart: 17, of which 10 were waited for; matrix products, arithmetic and copies ran while one was open for 4% of the time, Pallas kernels for 0%

profile of v10, /device:TPU:56, one launch (start us, length us, event | category | flops | bytes accessed | tf_op | source)
XLA Modules:
  0.0 168.2 jit_solution(12474670015673601180)
XLA Ops:
  0.6 41.5 %first_copies.1 = (bf16[64,1152]{1,0:T(8,128)(2,1)}, bf16[16,32,1152]{2,1,0:T(8,128)(2,1)}) custom-call(s32[1]{0:T(128)} %bitcast.1.x_ref, bf16[256,1152]{1,0:T(8,128)(2,1)} %image_ref.1, bf16[32,1152]{1,0:T(8,128)(2,1)} %text_ref.1), custom_call_target="tpu_custom_call" | custom-call | tf_op jit(solution)/shard_map/first_copies/pallas_call | solution.py:56
  42.1 3.3 %collective-permute-start = (bf16[64,1152]{1,0:T(8,128)(2,1)}, bf16[64,1152]{1,0:T(8,128)(2,1)S(1)}, u32[]{:S(2)}, u32[]{:S(2)}) collective-permute-start(bf16[64,1152]{1,0:T(8,128)(2,1)} %get-tuple-element.12), channel_id=1, source_target_pairs={{0,64},{64,0},{1,65},{65,1},{2,66},{66,2},{3,67},{67,3},{4,68},{68... | collective-permute-start | bytes 442376 | tf_op jit(solution)/shard_map/ppermute | solution.py:25
  45.4 14.7 %all-to-all-start = ((bf16[16,32,1152]{2,1,0:T(8,128)(2,1)}), bf16[16,32,1152]{2,1,0:T(8,128)(2,1)S(1)}, u32[]{:S(2)}, u32[]{:S(2)}) async-start(bf16[16,32,1152]{2,1,0:T(8,128)(2,1)} %get-tuple-element.13), calls=%async_computation | async-start | bytes 2359296 | tf_op jit(solution)/shard_map/all_to_all | solution.py:34
  61.4 4.8 %collective-permute-start.1 = (bf16[64,1152]{1,0:T(8,128)(2,1)S(1)}, bf16[64,1152]{1,0:T(8,128)(2,1)S(1)}, u32[]{:S(2)}, u32[]{:S(2)}) collective-permute-start(bf16[64,1152]{1,0:T(8,128)(2,1)S(1)} %collective-permute-done), channel_id=1, source_target_pairs={{0,6},{2,0},{4,2},{6,4},{1,7},{3,1},{5,3},{7,5},{8,14},{10,8},{12,... | collective-permute-start | bytes 442376 | tf_op jit(solution)/shard_map/ppermute | solution.py:30
  66.2 2.7 %collective-permute-start.2 = (bf16[64,1152]{1,0:T(8,128)(2,1)S(1)}, bf16[64,1152]{1,0:T(8,128)(2,1)S(1)}, u32[]{:S(2)}, u32[]{:S(2)}) collective-permute-start(bf16[64,1152]{1,0:T(8,128)(2,1)S(1)} %collective-permute-done), channel_id=1, source_target_pairs={{0,4},{2,6},{4,0},{6,2},{1,5},{3,7},{5,1},{7,3},{8,12},{10,14},{12... | collective-permute-start | bytes 442376 | tf_op jit(solution)/shard_map/ppermute | solution.py:30
  68.9 2.8 %collective-permute-start.3 = (bf16[64,1152]{1,0:T(8,128)(2,1)S(1)}, bf16[64,1152]{1,0:T(8,128)(2,1)S(1)}, u32[]{:S(2)}, u32[]{:S(2)}) collective-permute-start(bf16[64,1152]{1,0:T(8,128)(2,1)S(1)} %collective-permute-done), channel_id=1, source_target_pairs={{0,2},{2,4},{4,6},{6,0},{1,3},{3,5},{5,7},{7,1},{8,10},{10,12},{12... | collective-permute-start | bytes 442376 | tf_op jit(solution)/shard_map/ppermute | solution.py:30
  71.8 4.3 %collective-permute-done.2 = bf16[64,1152]{1,0:T(8,128)(2,1)S(1)} collective-permute-done((bf16[64,1152]{1,0:T(8,128)(2,1)S(1)}, bf16[64,1152]{1,0:T(8,128)(2,1)S(1)}, u32[]{:S(2)}, u32[]{:S(2)}) %collective-permute-start.2) | collective-permute-done | bytes 147488 | tf_op jit(solution)/shard_map/ppermute | solution.py:30
  76.2 1.7 collective-permute-done.3
  77.9 0.2 broadcast_select_fusion.1
  78.2 0.3 fusion
  78.5 1.4 fusion.1
  79.9 1.9 %collective-permute-start.4 = (bf16[512,1152]{1,0:T(8,128)(2,1)}, bf16[512,1152]{1,0:T(8,128)(2,1)}, u32[]{:S(2)}, u32[]{:S(2)}) collective-permute-start(bf16[512,1152]{1,0:T(8,128)(2,1)} %fusion.1), channel_id=1, source_target_pairs={{0,8},{8,0},{1,9},{9,1},{2,10},{10,2},{3,11},{11,3},{4,12},{12,4},... | collective-permute-start | bytes 3538952 | tf_op jit(solution)/shard_map/ppermute | solution.py:25
  81.9 0.1 add_dynamic-update-slice_fusion
  82.0 5.9 %all-to-all-done = bf16[16,32,1152]{2,1,0:T(8,128)(2,1)S(1)} async-done(((bf16[16,32,1152]{2,1,0:T(8,128)(2,1)}), bf16[16,32,1152]{2,1,0:T(8,128)(2,1)S(1)}, u32[]{:S(2)}, u32[]{:S(2)}) %all-to-all-start) | async-done | bytes 1179680 | tf_op jit(solution)/shard_map/all_to_all | solution.py:34
  87.9 0.3 multiply_reduce_fusion
  88.3 0.4 fusion.2
  88.6 3.6 %subtract_convert_fusion = bf16[1024,512]{1,0:T(8,128)(2,1)S(1)} fusion(bf16[512,1152]{1,0:T(8,128)(2,1)S(1)} %fusion.2, bf16[512,1152]{1,0:T(8,128)(2,1)} %collective-permute-done.4, bf16[512,1152]{1,0:T(8,128)(2,1)} %fusion.1, s32[512]{0:T(512)S(1)} %add_dynamic-update-slice_fusion, f32[]{:T(128)} %bitcast.34, f32[]{:T(128)} %bitcast), kind=kOutput, calls=%fused_computation.12 | convolution fusion | flops 1217396736 | bytes 4589576 | tf_op jit(solution)/shard_map/dot_general | solution.py:107
  92.2 4.6 %convolution_convert_fusion.1 = bf16[512,1152]{1,0:T(8,128)(2,1)} fusion(bf16[1024,512]{1,0:T(8,128)(2,1)S(1)} %subtract_convert_fusion, bf16[512,1152]{1,0:T(8,128)(2,1)} %collective-permute-done.4, bf16[512,1152]{1,0:T(8,128)(2,1)} %fusion.1), kind=kOutput, calls=%fused_computation.1 | convolution fusion | flops 1213267968 | bytes 4587520 | tf_op jit(solution)/shard_map/dot_general | solution.py:109
  96.8 1.9 %convolution_convert_fusion = bf16[512,1152]{1,0:T(8,128)(2,1)} fusion(bf16[512,1152]{1,0:T(8,128)(2,1)S(1)} %fusion.2, bf16[1024,512]{1,0:T(8,128)(2,1)S(1)} %subtract_convert_fusion), kind=kOutput, calls=%fused_computation | convolution fusion | flops 604569600 | bytes 2883584 | tf_op jit(solution)/shard_map/dot_general | solution.py:114
  98.7 1.9 %collective-permute-start.5 = (bf16[512,1152]{1,0:T(8,128)(2,1)}, bf16[512,1152]{1,0:T(8,128)(2,1)}, u32[]{:S(2)}, u32[]{:S(2)}) collective-permute-start(bf16[512,1152]{1,0:T(8,128)(2,1)} %convolution_convert_fusion), channel_id=1, source_target_pairs={{0,8},{8,0},{1,9},{9,1},{2,10},{10,2},{3,11},{11,3},{4,12},{12,4},... | collective-permute-start | bytes 3538952 | tf_op jit(solution)/shard_map/ppermute | solution.py:25
  100.6 0.1 fusion.9
  100.8 0.1 convert_divide_fusion.1
  100.9 10.0 %all-to-all-start.1 = ((bf16[16,32,1152]{2,1,0:T(8,128)(2,1)}), bf16[16,32,1152]{2,1,0:T(8,128)(2,1)S(1)}, u32[]{:S(2)}, u32[]{:S(2)}) async-start(bf16[16,32,1152]{2,1,0:T(8,128)(2,1)} %bitcast.37), calls=%async_computation.1 | async-start | bytes 2359296 | tf_op jit(solution)/shard_map/all_to_all | solution.py:34
  110.9 2.3 %convert_add_fusion = f32[512,1152]{1,0:T(8,128)S(1)} fusion(bf16[512,1152]{1,0:T(8,128)(2,1)} %collective-permute-done.5, bf16[512,1152]{1,0:T(8,128)(2,1)S(1)} %fusion.2, bf16[1024,512]{1,0:T(8,128)(2,1)} %copy-done.2), kind=kOutput, calls=%fused_computation.10 | convolution fusion | flops 605159424 | bytes 5242880 | tf_op jit(solution)/shard_map/dot_general | solution.py:116
  113.2 0.1 dynamic-slice_convert_fusion.2
  113.4 4.9 %collective-permute-start.6 = (bf16[128,1152]{1,0:T(8,128)(2,1)S(1)}, bf16[128,1152]{1,0:T(8,128)(2,1)S(1)}, u32[]{:S(2)}, u32[]{:S(2)}) collective-permute-start(bf16[128,1152]{1,0:T(8,128)(2,1)S(1)} %bitcast.40), channel_id=1, source_target_pairs={{0,4},{2,6},{4,0},{6,2},{1,5},{3,7},{5,1},{7,3},{8,12},{10,14},{12... | collective-permute-start | bytes 884744 | tf_op jit(solution)/shard_map/ppermute | solution.py:30
  118.3 2.5 %collective-permute-start.7 = (bf16[128,1152]{1,0:T(8,128)(2,1)S(1)}, bf16[128,1152]{1,0:T(8,128)(2,1)S(1)}, u32[]{:S(2)}, u32[]{:S(2)}) collective-permute-start(bf16[128,1152]{1,0:T(8,128)(2,1)S(1)} %bitcast.39), channel_id=1, source_target_pairs={{0,2},{2,4},{4,6},{6,0},{1,3},{3,5},{5,7},{7,1},{8,10},{10,12},{12... | collective-permute-start | bytes 884744 | tf_op jit(solution)/shard_map/ppermute | solution.py:30
  120.8 4.6 %collective-permute-start.8 = (bf16[128,1152]{1,0:T(8,128)(2,1)S(1)}, bf16[128,1152]{1,0:T(8,128)(2,1)S(1)}, u32[]{:S(2)}, u32[]{:S(2)}) collective-permute-start(bf16[128,1152]{1,0:T(8,128)(2,1)S(1)} %bitcast.38), channel_id=1, source_target_pairs={{0,6},{2,0},{4,2},{6,4},{1,7},{3,1},{5,3},{7,5},{8,14},{10,8},{12,... | collective-permute-start | bytes 884744 | tf_op jit(solution)/shard_map/ppermute | solution.py:30
  125.4 0.1 fusion.10
  125.5 1.1 collective-permute-done.6
  126.6 5.3 %collective-permute-done.7 = bf16[128,1152]{1,0:T(8,128)(2,1)S(1)} collective-permute-done((bf16[128,1152]{1,0:T(8,128)(2,1)S(1)}, bf16[128,1152]{1,0:T(8,128)(2,1)S(1)}, u32[]{:S(2)}, u32[]{:S(2)}) %collective-permute-start.7) | collective-permute-done | bytes 294944 | tf_op jit(solution)/shard_map/ppermute | solution.py:30
  132.0 0.1 fusion.3
  132.2 6.3 %collective-permute-start.10 = (bf16[64,1152]{1,0:T(8,128)(2,1)S(1)}, bf16[64,1152]{1,0:T(8,128)(2,1)S(1)}, u32[]{:S(2)}, u32[]{:S(2)}) collective-permute-start(bf16[64,1152]{1,0:T(8,128)(2,1)S(1)} %get-tuple-element.30), channel_id=1, source_target_pairs={{0,64},{64,0},{1,65},{65,1},{2,66},{66,2},{3,67},{67,3},{4,68},{68... | collective-permute-start | bytes 442376 | tf_op jit(solution)/shard_map/ppermute | solution.py:25
  138.5 1.9 %collective-permute-start.11 = (bf16[64,1152]{1,0:T(8,128)(2,1)S(1)}, bf16[64,1152]{1,0:T(8,128)(2,1)S(1)}, u32[]{:S(2)}, u32[]{:S(2)}) collective-permute-start(bf16[64,1152]{1,0:T(8,128)(2,1)S(1)} %get-tuple-element.30), channel_id=1, source_target_pairs={{0,65},{1,64},{64,1},{65,0},{2,67},{3,66},{66,3},{67,2},{4,69},{5,... | collective-permute-start | bytes 442376 | tf_op jit(solution)/shard_map/ppermute | solution.py:25
  140.4 3.4 %collective-permute-start.9 = (bf16[64,1152]{1,0:T(8,128)(2,1)S(1)}, bf16[64,1152]{1,0:T(8,128)(2,1)S(1)}, u32[]{:S(2)}, u32[]{:S(2)}) collective-permute-start(bf16[64,1152]{1,0:T(8,128)(2,1)S(1)} %get-tuple-element.29), channel_id=1, source_target_pairs={{0,1},{1,0},{2,3},{3,2},{4,5},{5,4},{6,7},{7,6},{8,9},{9,8},{10,11... | collective-permute-start | bytes 442376 | tf_op jit(solution)/shard_map/ppermute | solution.py:25
  143.9 4.1 %collective-permute-done.11 = bf16[64,1152]{1,0:T(8,128)(2,1)S(1)} collective-permute-done((bf16[64,1152]{1,0:T(8,128)(2,1)S(1)}, bf16[64,1152]{1,0:T(8,128)(2,1)S(1)}, u32[]{:S(2)}, u32[]{:S(2)}) %collective-permute-start.11) | collective-permute-done | bytes 147488 | tf_op jit(solution)/shard_map/ppermute | solution.py:25
  148.0 2.6 %collective-permute-done.9 = bf16[64,1152]{1,0:T(8,128)(2,1)S(1)} collective-permute-done((bf16[64,1152]{1,0:T(8,128)(2,1)S(1)}, bf16[64,1152]{1,0:T(8,128)(2,1)S(1)}, u32[]{:S(2)}, u32[]{:S(2)}) %collective-permute-start.9) | collective-permute-done | bytes 147488 | tf_op jit(solution)/shard_map/ppermute | solution.py:25
  150.7 0.1 multiply_reduce_fusion.1
  150.8 0.1 constant_dynamic-update-slice_fusion.15
  150.9 4.2 %collective-permute-start.12 = (bf16[64,1152]{1,0:T(8,128)(2,1)S(1)}, bf16[64,1152]{1,0:T(8,128)(2,1)S(1)}, u32[]{:S(2)}, u32[]{:S(2)}) collective-permute-start(bf16[64,1152]{1,0:T(8,128)(2,1)S(1)} %get-tuple-element.23), channel_id=1, source_target_pairs={{0,6},{2,0},{4,2},{6,4},{1,7},{3,1},{5,3},{7,5},{8,14},{10,8},{12,... | collective-permute-start | bytes 442376 | tf_op jit(solution)/shard_map/ppermute | solution.py:30
  155.1 3.4 %collective-permute-start.13 = (bf16[64,1152]{1,0:T(8,128)(2,1)S(1)}, bf16[64,1152]{1,0:T(8,128)(2,1)S(1)}, u32[]{:S(2)}, u32[]{:S(2)}) collective-permute-start(bf16[64,1152]{1,0:T(8,128)(2,1)S(1)} %get-tuple-element.23), channel_id=1, source_target_pairs={{0,4},{2,6},{4,0},{6,2},{1,5},{3,7},{5,1},{7,3},{8,12},{10,14},{12... | collective-permute-start | bytes 442376 | tf_op jit(solution)/shard_map/ppermute | solution.py:30
  158.5 2.8 %collective-permute-start.14 = (bf16[64,1152]{1,0:T(8,128)(2,1)S(1)}, bf16[64,1152]{1,0:T(8,128)(2,1)S(1)}, u32[]{:S(2)}, u32[]{:S(2)}) collective-permute-start(bf16[64,1152]{1,0:T(8,128)(2,1)S(1)} %get-tuple-element.23), channel_id=1, source_target_pairs={{0,2},{2,4},{4,6},{6,0},{1,3},{3,5},{5,7},{7,1},{8,10},{10,12},{12... | collective-permute-start | bytes 442376 | tf_op jit(solution)/shard_map/ppermute | solution.py:30
  161.3 0.2 convert_reduce_fusion
  161.5 0.1 multiply_reduce_fusion.2
  161.6 0.7 divide_convert_fusion.1
  162.3 2.6 %collective-permute-done.13 = bf16[64,1152]{1,0:T(8,128)(2,1)S(1)} collective-permute-done((bf16[64,1152]{1,0:T(8,128)(2,1)S(1)}, bf16[64,1152]{1,0:T(8,128)(2,1)S(1)}, u32[]{:S(2)}, u32[]{:S(2)}) %collective-permute-start.13) | collective-permute-done | bytes 147488 | tf_op jit(solution)/shard_map/ppermute | solution.py:30
  164.9 2.3 %collective-permute-done.14 = bf16[64,1152]{1,0:T(8,128)(2,1)S(1)} collective-permute-done((bf16[64,1152]{1,0:T(8,128)(2,1)S(1)}, bf16[64,1152]{1,0:T(8,128)(2,1)S(1)}, u32[]{:S(2)}, u32[]{:S(2)}) %collective-permute-start.14) | collective-permute-done | bytes 147488 | tf_op jit(solution)/shard_map/ppermute | solution.py:30
  167.3 0.9 constant_dynamic-slice_fusion
  (40 shorter events, 0.7 us)
Async XLA Ops:
  42.1 19.3 %collective-permute-start = (bf16[64,1152]{1,0:T(8,128)(2,1)}, bf16[64,1152]{1,0:T(8,128)(2,1)S(1)}, u32[]{:S(2)}, u32[]{:S(2)}) collective-permute-start(bf16[64,1152]{1,0:T(8,128)(2,1)} %get-tuple-element.12), channel_id=1, source_target_pairs={{0,64},{64,0},{1,65},{65,1},{2,66},{66,2},{3,67},{67,3},{4,68},{68... | collective-permute-start | bytes 442376 | tf_op jit(solution)/shard_map/ppermute | solution.py:25
  45.4 42.5 %all-to-all-start = ((bf16[16,32,1152]{2,1,0:T(8,128)(2,1)}), bf16[16,32,1152]{2,1,0:T(8,128)(2,1)S(1)}, u32[]{:S(2)}, u32[]{:S(2)}) async-start(bf16[16,32,1152]{2,1,0:T(8,128)(2,1)} %get-tuple-element.13), calls=%async_computation | async-start | bytes 2359296 | tf_op jit(solution)/shard_map/all_to_all | solution.py:34
  61.4 16.5 %copy-start = (bf16[256,1152]{1,0:T(8,128)(2,1)S(1)}, bf16[256,1152]{1,0:T(8,128)(2,1)}, u32[]{:S(2)}) copy-start(bf16[256,1152]{1,0:T(8,128)(2,1)} %image_ref.1) | copy-start | bytes 1769476
  61.4 10.3 %collective-permute-start.1 = (bf16[64,1152]{1,0:T(8,128)(2,1)S(1)}, bf16[64,1152]{1,0:T(8,128)(2,1)S(1)}, u32[]{:S(2)}, u32[]{:S(2)}) collective-permute-start(bf16[64,1152]{1,0:T(8,128)(2,1)S(1)} %collective-permute-done), channel_id=1, source_target_pairs={{0,6},{2,0},{4,2},{6,4},{1,7},{3,1},{5,3},{7,5},{8,14},{10,8},{12,... | collective-permute-start | bytes 442376 | tf_op jit(solution)/shard_map/ppermute | solution.py:30
  66.2 9.9 %collective-permute-start.2 = (bf16[64,1152]{1,0:T(8,128)(2,1)S(1)}, bf16[64,1152]{1,0:T(8,128)(2,1)S(1)}, u32[]{:S(2)}, u32[]{:S(2)}) collective-permute-start(bf16[64,1152]{1,0:T(8,128)(2,1)S(1)} %collective-permute-done), channel_id=1, source_target_pairs={{0,4},{2,6},{4,0},{6,2},{1,5},{3,7},{5,1},{7,3},{8,12},{10,14},{12... | collective-permute-start | bytes 442376 | tf_op jit(solution)/shard_map/ppermute | solution.py:30
  68.9 8.9 %collective-permute-start.3 = (bf16[64,1152]{1,0:T(8,128)(2,1)S(1)}, bf16[64,1152]{1,0:T(8,128)(2,1)S(1)}, u32[]{:S(2)}, u32[]{:S(2)}) collective-permute-start(bf16[64,1152]{1,0:T(8,128)(2,1)S(1)} %collective-permute-done), channel_id=1, source_target_pairs={{0,2},{2,4},{4,6},{6,0},{1,3},{3,5},{5,7},{7,1},{8,10},{10,12},{12... | collective-permute-start | bytes 442376 | tf_op jit(solution)/shard_map/ppermute | solution.py:30
  78.5 3.3 %copy-start.3 = (s32[32]{0:T(128)S(1)}, s32[32]{0:T(128)}, u32[]{:S(2)}) copy-start(s32[32]{0:T(128)} %param.7) | copy-start | bytes 388
  79.9 8.7 %collective-permute-start.4 = (bf16[512,1152]{1,0:T(8,128)(2,1)}, bf16[512,1152]{1,0:T(8,128)(2,1)}, u32[]{:S(2)}, u32[]{:S(2)}) collective-permute-start(bf16[512,1152]{1,0:T(8,128)(2,1)} %fusion.1), channel_id=1, source_target_pairs={{0,8},{8,0},{1,9},{9,1},{2,10},{10,2},{3,11},{11,3},{4,12},{12,4},... | collective-permute-start | bytes 3538952 | tf_op jit(solution)/shard_map/ppermute | solution.py:25
  92.2 4.6 %copy-start.2 = (bf16[1024,512]{1,0:T(8,128)(2,1)}, bf16[1024,512]{1,0:T(8,128)(2,1)S(1)}, u32[]{:S(2)}) copy-start(bf16[1024,512]{1,0:T(8,128)(2,1)S(1)} %subtract_convert_fusion) | copy-start | bytes 3145732
  98.7 12.2 %collective-permute-start.5 = (bf16[512,1152]{1,0:T(8,128)(2,1)}, bf16[512,1152]{1,0:T(8,128)(2,1)}, u32[]{:S(2)}, u32[]{:S(2)}) collective-permute-start(bf16[512,1152]{1,0:T(8,128)(2,1)} %convolution_convert_fusion), channel_id=1, source_target_pairs={{0,8},{8,0},{1,9},{9,1},{2,10},{10,2},{3,11},{11,3},{4,12},{12,4},... | collective-permute-start | bytes 3538952 | tf_op jit(solution)/shard_map/ppermute | solution.py:25
  100.9 49.8 %all-to-all-start.1 = ((bf16[16,32,1152]{2,1,0:T(8,128)(2,1)}), bf16[16,32,1152]{2,1,0:T(8,128)(2,1)S(1)}, u32[]{:S(2)}, u32[]{:S(2)}) async-start(bf16[16,32,1152]{2,1,0:T(8,128)(2,1)} %bitcast.37), calls=%async_computation.1 | async-start | bytes 2359296 | tf_op jit(solution)/shard_map/all_to_all | solution.py:34
  113.2 12.2 %copy-start.1 = (bf16[32,1152]{1,0:T(8,128)(2,1)S(1)}, bf16[32,1152]{1,0:T(8,128)(2,1)}, u32[]{:S(2)}) copy-start(bf16[32,1152]{1,0:T(8,128)(2,1)} %text_ref.1) | copy-start | bytes 221188
  113.4 13.3 %collective-permute-start.6 = (bf16[128,1152]{1,0:T(8,128)(2,1)S(1)}, bf16[128,1152]{1,0:T(8,128)(2,1)S(1)}, u32[]{:S(2)}, u32[]{:S(2)}) collective-permute-start(bf16[128,1152]{1,0:T(8,128)(2,1)S(1)} %bitcast.40), channel_id=1, source_target_pairs={{0,4},{2,6},{4,0},{6,2},{1,5},{3,7},{5,1},{7,3},{8,12},{10,14},{12... | collective-permute-start | bytes 884744 | tf_op jit(solution)/shard_map/ppermute | solution.py:30
  118.3 13.6 %collective-permute-start.7 = (bf16[128,1152]{1,0:T(8,128)(2,1)S(1)}, bf16[128,1152]{1,0:T(8,128)(2,1)S(1)}, u32[]{:S(2)}, u32[]{:S(2)}) collective-permute-start(bf16[128,1152]{1,0:T(8,128)(2,1)S(1)} %bitcast.39), channel_id=1, source_target_pairs={{0,2},{2,4},{4,6},{6,0},{1,3},{3,5},{5,7},{7,1},{8,10},{10,12},{12... | collective-permute-start | bytes 884744 | tf_op jit(solution)/shard_map/ppermute | solution.py:30
  120.8 11.2 %collective-permute-start.8 = (bf16[128,1152]{1,0:T(8,128)(2,1)S(1)}, bf16[128,1152]{1,0:T(8,128)(2,1)S(1)}, u32[]{:S(2)}, u32[]{:S(2)}) collective-permute-start(bf16[128,1152]{1,0:T(8,128)(2,1)S(1)} %bitcast.38), channel_id=1, source_target_pairs={{0,6},{2,0},{4,2},{6,4},{1,7},{3,1},{5,3},{7,5},{8,14},{10,8},{12,... | collective-permute-start | bytes 884744 | tf_op jit(solution)/shard_map/ppermute | solution.py:30
  132.2 11.7 %collective-permute-start.10 = (bf16[64,1152]{1,0:T(8,128)(2,1)S(1)}, bf16[64,1152]{1,0:T(8,128)(2,1)S(1)}, u32[]{:S(2)}, u32[]{:S(2)}) collective-permute-start(bf16[64,1152]{1,0:T(8,128)(2,1)S(1)} %get-tuple-element.30), channel_id=1, source_target_pairs={{0,64},{64,0},{1,65},{65,1},{2,66},{66,2},{3,67},{67,3},{4,68},{68... | collective-permute-start | bytes 442376 | tf_op jit(solution)/shard_map/ppermute | solution.py:25
  138.5 9.5 %collective-permute-start.11 = (bf16[64,1152]{1,0:T(8,128)(2,1)S(1)}, bf16[64,1152]{1,0:T(8,128)(2,1)S(1)}, u32[]{:S(2)}, u32[]{:S(2)}) collective-permute-start(bf16[64,1152]{1,0:T(8,128)(2,1)S(1)} %get-tuple-element.30), channel_id=1, source_target_pairs={{0,65},{1,64},{64,1},{65,0},{2,67},{3,66},{66,3},{67,2},{4,69},{5,... | collective-permute-start | bytes 442376 | tf_op jit(solution)/shard_map/ppermute | solution.py:25
  140.4 10.1 %collective-permute-start.9 = (bf16[64,1152]{1,0:T(8,128)(2,1)S(1)}, bf16[64,1152]{1,0:T(8,128)(2,1)S(1)}, u32[]{:S(2)}, u32[]{:S(2)}) collective-permute-start(bf16[64,1152]{1,0:T(8,128)(2,1)S(1)} %get-tuple-element.29), channel_id=1, source_target_pairs={{0,1},{1,0},{2,3},{3,2},{4,5},{5,4},{6,7},{7,6},{8,9},{9,8},{10,11... | collective-permute-start | bytes 442376 | tf_op jit(solution)/shard_map/ppermute | solution.py:25
  150.9 11.4 %collective-permute-start.12 = (bf16[64,1152]{1,0:T(8,128)(2,1)S(1)}, bf16[64,1152]{1,0:T(8,128)(2,1)S(1)}, u32[]{:S(2)}, u32[]{:S(2)}) collective-permute-start(bf16[64,1152]{1,0:T(8,128)(2,1)S(1)} %get-tuple-element.23), channel_id=1, source_target_pairs={{0,6},{2,0},{4,2},{6,4},{1,7},{3,1},{5,3},{7,5},{8,14},{10,8},{12,... | collective-permute-start | bytes 442376 | tf_op jit(solution)/shard_map/ppermute | solution.py:30
  155.1 9.8 %collective-permute-start.13 = (bf16[64,1152]{1,0:T(8,128)(2,1)S(1)}, bf16[64,1152]{1,0:T(8,128)(2,1)S(1)}, u32[]{:S(2)}, u32[]{:S(2)}) collective-permute-start(bf16[64,1152]{1,0:T(8,128)(2,1)S(1)} %get-tuple-element.23), channel_id=1, source_target_pairs={{0,4},{2,6},{4,0},{6,2},{1,5},{3,7},{5,1},{7,3},{8,12},{10,14},{12... | collective-permute-start | bytes 442376 | tf_op jit(solution)/shard_map/ppermute | solution.py:30
  158.5 8.7 %collective-permute-start.14 = (bf16[64,1152]{1,0:T(8,128)(2,1)S(1)}, bf16[64,1152]{1,0:T(8,128)(2,1)S(1)}, u32[]{:S(2)}, u32[]{:S(2)}) collective-permute-start(bf16[64,1152]{1,0:T(8,128)(2,1)S(1)} %get-tuple-element.23), channel_id=1, source_target_pairs={{0,2},{2,4},{4,6},{6,0},{1,3},{3,5},{5,7},{7,1},{8,10},{10,12},{12... | collective-permute-start | bytes 442376 | tf_op jit(solution)/shard_map/ppermute | solution.py:30

commit v11 on v10

--- a/solution.py
+++ b/solution.py
@@ -52,15 +52,15 @@
         for copy in copies:
             copy.wait()
 
-    anywhere = pl.BlockSpec(memory_space=pl.ANY)
+    anywhere, whole = pl.BlockSpec(memory_space=pl.ANY), pl.BlockSpec(memory_space=pltpu.VMEM)
     return pl.pallas_call(
         body,
         out_shape=(
             jax.ShapeDtypeStruct((quarter, width), BF16),
             jax.ShapeDtypeStruct((peers, mine, width), BF16),
         ),
-        in_specs=[pl.BlockSpec(memory_space=pltpu.SMEM), anywhere, anywhere],
-        out_specs=(anywhere, anywhere),
+        in_specs=[pl.BlockSpec(memory_space=pltpu.SMEM), anywhere, whole],
+        out_specs=(whole, anywhere),
         scratch_shapes=[pltpu.SemaphoreType.DMA((peers + 1,))],
         name="first_copies",
     )(x, image_emb, text_emb)
@@ -103,18 +103,17 @@
         (image_unit, image_norm, text_unit, text_norm)
     )
 
-    images = jnp.concatenate([near, far], axis=0)
+    images = lax.optimization_barrier(jnp.concatenate([near, far], axis=0))
     cosine = lax.dot_general(images, text_bf, (((1,), (1,)), ((), ())), preferred_element_type=F32)
     grad = (jax.nn.sigmoid(scale * cosine + bias[0]) - hit).astype(BF16)
     text_terms = lax.dot_general(grad, images, (((0,), (0,)), ((), ())), preferred_element_type=F32).astype(BF16)
-    text_terms, grad = lax.optimization_barrier((text_terms, grad))
-    text_sum = exchange(text_terms.reshape(peers, mine, width), RINGS, TEXT_GROUPS)
-
     half = near.shape[0]
     far_terms = jnp.dot(grad[half:], text_bf, preferred_element_type=F32).astype(BF16)
     far_terms = swap(far_terms, "c").astype(F32)
     both = jnp.dot(grad[:half], text_bf, preferred_element_type=F32) + far_terms
     both = both.reshape(2, n_x, quarter, width)
+    text_terms, both = lax.optimization_barrier((text_terms, both))
+    text_sum = exchange(text_terms.reshape(peers, mine, width), RINGS, TEXT_GROUPS)
 
     def of_position(k):
         return lax.dynamic_index_in_dim(both, lax.rem(x + k, n_x), axis=1, keepdims=False)
@@ -127,7 +126,6 @@
     own, other = jnp.where(upper, total[1], total[0]), jnp.where(upper, total[0], total[1])
     beside, across, corner = swap(own, "l"), swap(other, "yl"), swap(other, ("yl", "l"))
     image_sum = (own.astype(F32) + beside.astype(F32)) + (across.astype(F32) + corner.astype(F32))
-    image_sum, text_sum = lax.optimization_barrier((image_sum, text_sum))
     done = finish(image_sum[None], image_unit, image_norm, scale)
     around = [done] + [shift(done, "x", n_x - d) for d in range(1, n_x)]
     grad_image = in_order(around, x)

time: 172 us -> 144 us (0.84)
  the two profiles are of different devices: /device:TPU:56 before, /device:TPU:48 now
where the time goes in v11:
time: 144 us; the launch traced here: 143 us
  starting transfers between devices  66.2 us (46%)
  waiting for transfers between devices  54 us (38%)
  matrix products  9.9 us (7%)
  other arithmetic  6.2 us (4%)
  Pallas kernels  2.77 us (2%)
  between operations  2.45 us (2%)
    ppermute x9, starting transfers between devices, shift(): lax.ppermute(block, axis, [(i, (i + distance) % count) for i in range(cou...  28.8 us
    all_to_all x2, waiting for transfers between devices, exchange(): lax.all_to_all(blocks, axes, 0, 0, axis_index_groups=groups, tiled=True)  28.5 us
    ppermute x9, waiting for transfers between devices, shift(): lax.ppermute(block, axis, [(i, (i + distance) % count) for i in range(cou...  24 us
    all_to_all x2, starting transfers between devices, exchange(): lax.all_to_all(blocks, axes, 0, 0, axis_index_groups=groups, tiled=True)  21.8 us
    ppermute x6, starting transfers between devices, swap(): return lax.ppermute(block, axes, [(i, count - 1 - i) for i in range(count)])  15.6 us
    dot_general x1, matrix products, local(): lax.dot_general(grad, images, (((0,), (0,)), ((), ())), preferred_element...  3.96 us
  transfers between devices with their start and end apart: 17, of which 9 were waited for; matrix products, arithmetic and copies ran while one was open for 7% of the time, Pallas kernels for 0%

profile of v11, /device:TPU:48, one launch (start us, length us, event | category | flops | bytes accessed | tf_op | source)
XLA Modules:
  0.0 142.9 jit_solution(11532444979490215561)
XLA Ops:
  0.6 2.8 %first_copies.1 = (bf16[64,1152]{1,0:T(8,128)(2,1)}, bf16[16,32,1152]{2,1,0:T(8,128)(2,1)}) custom-call(s32[1]{0:T(128)} %bitcast.1.x_ref, bf16[256,1152]{1,0:T(8,128)(2,1)} %image_ref.1, bf16[32,1152]{1,0:T(8,128)(2,1)} %text_ref.1), custom_call_target="tpu_custom_call" | custom-call | tf_op jit(solution)/shard_map/first_copies/pallas_call | solution.py:56
  3.4 2.6 %collective-permute-start = (bf16[64,1152]{1,0:T(8,128)(2,1)}, bf16[64,1152]{1,0:T(8,128)(2,1)S(1)}, u32[]{:S(2)}, u32[]{:S(2)}) collective-permute-start(bf16[64,1152]{1,0:T(8,128)(2,1)} %get-tuple-element.10), channel_id=1, source_target_pairs={{0,64},{64,0},{1,65},{65,1},{2,66},{66,2},{3,67},{67,3},{4,68},{68... | collective-permute-start | bytes 442376 | tf_op jit(solution)/shard_map/ppermute | solution.py:25
  6.0 15.4 %all-to-all-start = ((bf16[16,32,1152]{2,1,0:T(8,128)(2,1)}), bf16[16,32,1152]{2,1,0:T(8,128)(2,1)S(1)}, u32[]{:S(2)}, u32[]{:S(2)}) async-start(bf16[16,32,1152]{2,1,0:T(8,128)(2,1)} %get-tuple-element.11), calls=%async_computation | async-start | bytes 2359296 | tf_op jit(solution)/shard_map/all_to_all | solution.py:34
  21.4 4.8 %collective-permute-start.1 = (bf16[64,1152]{1,0:T(8,128)(2,1)S(1)}, bf16[64,1152]{1,0:T(8,128)(2,1)S(1)}, u32[]{:S(2)}, u32[]{:S(2)}) collective-permute-start(bf16[64,1152]{1,0:T(8,128)(2,1)S(1)} %collective-permute-done), channel_id=1, source_target_pairs={{0,6},{2,0},{4,2},{6,4},{1,7},{3,1},{5,3},{7,5},{8,14},{10,8},{12,... | collective-permute-start | bytes 442376 | tf_op jit(solution)/shard_map/ppermute | solution.py:30
  26.2 2.7 %collective-permute-start.2 = (bf16[64,1152]{1,0:T(8,128)(2,1)S(1)}, bf16[64,1152]{1,0:T(8,128)(2,1)S(1)}, u32[]{:S(2)}, u32[]{:S(2)}) collective-permute-start(bf16[64,1152]{1,0:T(8,128)(2,1)S(1)} %collective-permute-done), channel_id=1, source_target_pairs={{0,4},{2,6},{4,0},{6,2},{1,5},{3,7},{5,1},{7,3},{8,12},{10,14},{12... | collective-permute-start | bytes 442376 | tf_op jit(solution)/shard_map/ppermute | solution.py:30
  28.9 2.8 %collective-permute-start.3 = (bf16[64,1152]{1,0:T(8,128)(2,1)S(1)}, bf16[64,1152]{1,0:T(8,128)(2,1)S(1)}, u32[]{:S(2)}, u32[]{:S(2)}) collective-permute-start(bf16[64,1152]{1,0:T(8,128)(2,1)S(1)} %collective-permute-done), channel_id=1, source_target_pairs={{0,2},{2,4},{4,6},{6,0},{1,3},{3,5},{5,7},{7,1},{8,10},{10,12},{12... | collective-permute-start | bytes 442376 | tf_op jit(solution)/shard_map/ppermute | solution.py:30
  31.8 4.3 %collective-permute-done.2 = bf16[64,1152]{1,0:T(8,128)(2,1)S(1)} collective-permute-done((bf16[64,1152]{1,0:T(8,128)(2,1)S(1)}, bf16[64,1152]{1,0:T(8,128)(2,1)S(1)}, u32[]{:S(2)}, u32[]{:S(2)}) %collective-permute-start.2) | collective-permute-done | bytes 147488 | tf_op jit(solution)/shard_map/ppermute | solution.py:30
  36.1 1.7 %collective-permute-done.3 = bf16[64,1152]{1,0:T(8,128)(2,1)S(1)} collective-permute-done((bf16[64,1152]{1,0:T(8,128)(2,1)S(1)}, bf16[64,1152]{1,0:T(8,128)(2,1)S(1)}, u32[]{:S(2)}, u32[]{:S(2)}) %collective-permute-start.3) | collective-permute-done | bytes 147488 | tf_op jit(solution)/shard_map/ppermute | solution.py:30
  37.9 0.2 broadcast_select_fusion.1
  38.2 0.3 fusion
  38.5 0.4 fusion.1
  38.9 1.9 %collective-permute-start.4 = (bf16[512,1152]{1,0:T(8,128)(2,1)S(1)}, bf16[512,1152]{1,0:T(8,128)(2,1)}, u32[]{:S(2)}, u32[]{:S(2)}) collective-permute-start(bf16[512,1152]{1,0:T(8,128)(2,1)S(1)} %fusion.1), channel_id=1, source_target_pairs={{0,8},{8,0},{1,9},{9,1},{2,10},{10,2},{3,11},{11,3},{4,12},{12,4},... | collective-permute-start | bytes 3538952 | tf_op jit(solution)/shard_map/ppermute | solution.py:25
  42.3 1.5 %collective-permute-done.4 = bf16[512,1152]{1,0:T(8,128)(2,1)} collective-permute-done((bf16[512,1152]{1,0:T(8,128)(2,1)S(1)}, bf16[512,1152]{1,0:T(8,128)(2,1)}, u32[]{:S(2)}, u32[]{:S(2)}) %collective-permute-start.4) | collective-permute-done | bytes 1179680 | tf_op jit(solution)/shard_map/ppermute | solution.py:25
  43.7 1.8 %pad_maximum_fusion = bf16[1024,1152]{1,0:T(8,128)(2,1)S(1)} fusion(bf16[512,1152]{1,0:T(8,128)(2,1)} %collective-permute-done.4, bf16[512,1152]{1,0:T(8,128)(2,1)} %copy-done.2), kind=kLoop, calls=%fused_computation.6 | loop fusion | flops 4718592 | bytes 4718592 | tf_op jit(solution)/shard_map/concatenate | solution.py:106
  45.6 10.4 %all-to-all-done = bf16[16,32,1152]{2,1,0:T(8,128)(2,1)S(1)} async-done(((bf16[16,32,1152]{2,1,0:T(8,128)(2,1)}), bf16[16,32,1152]{2,1,0:T(8,128)(2,1)S(1)}, u32[]{:S(2)}, u32[]{:S(2)}) %all-to-all-start) | async-done | bytes 1179680 | tf_op jit(solution)/shard_map/all_to_all | solution.py:34
  56.0 0.3 multiply_reduce_fusion
  56.4 0.4 fusion.2
  56.7 1.9 %subtract_convert_fusion = bf16[1024,512]{1,0:T(8,128)(2,1)S(1)} fusion(bf16[1024,1152]{1,0:T(8,128)(2,1)S(1)} %pad_maximum_fusion, bf16[512,1152]{1,0:T(8,128)(2,1)S(1)} %fusion.2, s32[512]{0:T(512)S(1)} %add_dynamic-update-slice_fusion, f32[]{:T(128)} %bitcast.36, f32[]{:T(128)} %bitcast), kind=kOutput, calls=%fused_computation.12 | convolution fusion | flops 1212678144 | bytes 4589576 | tf_op jit(solution)/shard_map/dot_general | solution.py:107
  58.7 1.9 %convolution_convert_fusion = bf16[512,1152]{1,0:T(8,128)(2,1)} fusion(bf16[512,1152]{1,0:T(8,128)(2,1)S(1)} %fusion.2, bf16[1024,512]{1,0:T(8,128)(2,1)S(1)} %subtract_convert_fusion), kind=kOutput, calls=%fused_computation | convolution fusion | flops 604569600 | bytes 2883584 | tf_op jit(solution)/shard_map/dot_general | solution.py:111
  60.6 1.9 %collective-permute-start.5 = (bf16[512,1152]{1,0:T(8,128)(2,1)}, bf16[512,1152]{1,0:T(8,128)(2,1)}, u32[]{:S(2)}, u32[]{:S(2)}) collective-permute-start(bf16[512,1152]{1,0:T(8,128)(2,1)} %convolution_convert_fusion), channel_id=1, source_target_pairs={{0,8},{8,0},{1,9},{9,1},{2,10},{10,2},{3,11},{11,3},{4,12},{12,4},... | collective-permute-start | bytes 3538952 | tf_op jit(solution)/shard_map/ppermute | solution.py:25
  62.5 0.1 fusion.9
  62.7 0.8 convert_divide_fusion.1
  63.5 4.0 %convolution_convert_fusion.1 = bf16[512,1152]{1,0:T(8,128)(2,1)} fusion(bf16[1024,512]{1,0:T(8,128)(2,1)} %copy-done.6, bf16[1024,1152]{1,0:T(8,128)(2,1)S(1)} %pad_maximum_fusion), kind=kOutput, calls=%fused_computation.1 | convolution fusion | flops 1208549376 | bytes 4587520 | tf_op jit(solution)/shard_map/dot_general | solution.py:109
  67.5 2.1 %convert_add_fusion = f32[512,1152]{1,0:T(8,128)S(1)} fusion(bf16[512,1152]{1,0:T(8,128)(2,1)} %collective-permute-done.5, bf16[512,1152]{1,0:T(8,128)(2,1)S(1)} %copy-done.1, bf16[1024,512]{1,0:T(8,128)(2,1)S(1)} %copy-done.7), kind=kOutput, calls=%fused_computation.10 | convolution fusion | flops 605159424 | bytes 5242880 | tf_op jit(solution)/shard_map/dot_general | solution.py:113
  69.6 0.1 dynamic-slice_convert_fusion.2
  69.8 4.7 %collective-permute-start.8 = (bf16[128,1152]{1,0:T(8,128)(2,1)S(1)}, bf16[128,1152]{1,0:T(8,128)(2,1)S(1)}, u32[]{:S(2)}, u32[]{:S(2)}) collective-permute-start(bf16[128,1152]{1,0:T(8,128)(2,1)S(1)} %bitcast.41), channel_id=1, source_target_pairs={{0,6},{2,0},{4,2},{6,4},{1,7},{3,1},{5,3},{7,5},{8,14},{10,8},{12,... | collective-permute-start | bytes 884744 | tf_op jit(solution)/shard_map/ppermute | solution.py:30
  74.4 1.9 %collective-permute-start.7 = (bf16[128,1152]{1,0:T(8,128)(2,1)S(1)}, bf16[128,1152]{1,0:T(8,128)(2,1)S(1)}, u32[]{:S(2)}, u32[]{:S(2)}) collective-permute-start(bf16[128,1152]{1,0:T(8,128)(2,1)S(1)} %bitcast.40), channel_id=1, source_target_pairs={{0,2},{2,4},{4,6},{6,0},{1,3},{3,5},{5,7},{7,1},{8,10},{10,12},{12... | collective-permute-start | bytes 884744 | tf_op jit(solution)/shard_map/ppermute | solution.py:30
  76.4 4.2 %collective-permute-start.6 = (bf16[128,1152]{1,0:T(8,128)(2,1)S(1)}, bf16[128,1152]{1,0:T(8,128)(2,1)S(1)}, u32[]{:S(2)}, u32[]{:S(2)}) collective-permute-start(bf16[128,1152]{1,0:T(8,128)(2,1)S(1)} %bitcast.39), channel_id=1, source_target_pairs={{0,4},{2,6},{4,0},{6,2},{1,5},{3,7},{5,1},{7,3},{8,12},{10,14},{12... | collective-permute-start | bytes 884744 | tf_op jit(solution)/shard_map/ppermute | solution.py:30
  80.6 0.1 fusion.10
  80.7 0.6 collective-permute-done.8
  81.4 11.6 %collective-permute-done.7 = bf16[128,1152]{1,0:T(8,128)(2,1)S(1)} collective-permute-done((bf16[128,1152]{1,0:T(8,128)(2,1)S(1)}, bf16[128,1152]{1,0:T(8,128)(2,1)S(1)}, u32[]{:S(2)}, u32[]{:S(2)}) %collective-permute-start.7) | collective-permute-done | bytes 294944 | tf_op jit(solution)/shard_map/ppermute | solution.py:30
  93.0 0.1 fusion.3
  93.2 1.9 %collective-permute-start.11 = (bf16[64,1152]{1,0:T(8,128)(2,1)S(1)}, bf16[64,1152]{1,0:T(8,128)(2,1)S(1)}, u32[]{:S(2)}, u32[]{:S(2)}) collective-permute-start(bf16[64,1152]{1,0:T(8,128)(2,1)S(1)} %get-tuple-element.26), channel_id=1, source_target_pairs={{0,65},{1,64},{64,1},{65,0},{2,67},{3,66},{66,3},{67,2},{4,69},{5,... | collective-permute-start | bytes 442376 | tf_op jit(solution)/shard_map/ppermute | solution.py:25
  95.1 3.2 %collective-permute-start.10 = (bf16[64,1152]{1,0:T(8,128)(2,1)S(1)}, bf16[64,1152]{1,0:T(8,128)(2,1)S(1)}, u32[]{:S(2)}, u32[]{:S(2)}) collective-permute-start(bf16[64,1152]{1,0:T(8,128)(2,1)S(1)} %get-tuple-element.26), channel_id=1, source_target_pairs={{0,64},{64,0},{1,65},{65,1},{2,66},{66,2},{3,67},{67,3},{4,68},{68... | collective-permute-start | bytes 442376 | tf_op jit(solution)/shard_map/ppermute | solution.py:25
  98.4 4.1 %collective-permute-start.9 = (bf16[64,1152]{1,0:T(8,128)(2,1)S(1)}, bf16[64,1152]{1,0:T(8,128)(2,1)S(1)}, u32[]{:S(2)}, u32[]{:S(2)}) collective-permute-start(bf16[64,1152]{1,0:T(8,128)(2,1)S(1)} %get-tuple-element.25), channel_id=1, source_target_pairs={{0,1},{1,0},{2,3},{3,2},{4,5},{5,4},{6,7},{7,6},{8,9},{9,8},{10,11... | collective-permute-start | bytes 442376 | tf_op jit(solution)/shard_map/ppermute | solution.py:25
  102.5 6.4 %all-to-all-start.1 = ((bf16[16,32,1152]{2,1,0:T(8,128)(2,1)}), bf16[16,32,1152]{2,1,0:T(8,128)(2,1)S(1)}, u32[]{:S(2)}, u32[]{:S(2)}) async-start(bf16[16,32,1152]{2,1,0:T(8,128)(2,1)} %bitcast.17), calls=%async_computation.1 | async-start | bytes 2359296 | tf_op jit(solution)/shard_map/all_to_all | solution.py:34
  109.0 0.2 multiply_reduce_fusion.1
  109.2 0.1 constant_dynamic-update-slice_fusion.15
  109.3 1.9 %collective-permute-start.12 = (bf16[64,1152]{1,0:T(8,128)(2,1)S(1)}, bf16[64,1152]{1,0:T(8,128)(2,1)S(1)}, u32[]{:S(2)}, u32[]{:S(2)}) collective-permute-start(bf16[64,1152]{1,0:T(8,128)(2,1)S(1)} %get-tuple-element.19), channel_id=1, source_target_pairs={{0,6},{2,0},{4,2},{6,4},{1,7},{3,1},{5,3},{7,5},{8,14},{10,8},{12,... | collective-permute-start | bytes 442376 | tf_op jit(solution)/shard_map/ppermute | solution.py:30
  111.2 2.5 %collective-permute-start.13 = (bf16[64,1152]{1,0:T(8,128)(2,1)S(1)}, bf16[64,1152]{1,0:T(8,128)(2,1)S(1)}, u32[]{:S(2)}, u32[]{:S(2)}) collective-permute-start(bf16[64,1152]{1,0:T(8,128)(2,1)S(1)} %get-tuple-element.19), channel_id=1, source_target_pairs={{0,4},{2,6},{4,0},{6,2},{1,5},{3,7},{5,1},{7,3},{8,12},{10,14},{12... | collective-permute-start | bytes 442376 | tf_op jit(solution)/shard_map/ppermute | solution.py:30
  113.7 3.4 %collective-permute-start.14 = (bf16[64,1152]{1,0:T(8,128)(2,1)S(1)}, bf16[64,1152]{1,0:T(8,128)(2,1)S(1)}, u32[]{:S(2)}, u32[]{:S(2)}) collective-permute-start(bf16[64,1152]{1,0:T(8,128)(2,1)S(1)} %get-tuple-element.19), channel_id=1, source_target_pairs={{0,2},{2,4},{4,6},{6,0},{1,3},{3,5},{5,7},{7,1},{8,10},{10,12},{12... | collective-permute-start | bytes 442376 | tf_op jit(solution)/shard_map/ppermute | solution.py:30
  117.1 3.3 %collective-permute-done.13 = bf16[64,1152]{1,0:T(8,128)(2,1)S(1)} collective-permute-done((bf16[64,1152]{1,0:T(8,128)(2,1)S(1)}, bf16[64,1152]{1,0:T(8,128)(2,1)S(1)}, u32[]{:S(2)}, u32[]{:S(2)}) %collective-permute-start.13) | collective-permute-done | bytes 147488 | tf_op jit(solution)/shard_map/ppermute | solution.py:30
  120.4 2.4 %collective-permute-done.14 = bf16[64,1152]{1,0:T(8,128)(2,1)S(1)} collective-permute-done((bf16[64,1152]{1,0:T(8,128)(2,1)S(1)}, bf16[64,1152]{1,0:T(8,128)(2,1)S(1)}, u32[]{:S(2)}, u32[]{:S(2)}) %collective-permute-start.14) | collective-permute-done | bytes 147488 | tf_op jit(solution)/shard_map/ppermute | solution.py:30
  123.0 0.9 constant_dynamic-slice_fusion
  123.8 18.1 %all-to-all-done.1 = bf16[16,32,1152]{2,1,0:T(8,128)(2,1)S(1)} async-done(((bf16[16,32,1152]{2,1,0:T(8,128)(2,1)}), bf16[16,32,1152]{2,1,0:T(8,128)(2,1)S(1)}, u32[]{:S(2)}, u32[]{:S(2)}) %all-to-all-start.1) | async-done | bytes 1179680 | tf_op jit(solution)/shard_map/all_to_all | solution.py:34
  141.9 0.2 convert_reduce_fusion
  142.1 0.1 multiply_reduce_fusion.2
  142.2 0.7 divide_convert_fusion.1
  (52 shorter events, 0.7 us)
Async XLA Ops:
  3.4 18.0 %collective-permute-start = (bf16[64,1152]{1,0:T(8,128)(2,1)}, bf16[64,1152]{1,0:T(8,128)(2,1)S(1)}, u32[]{:S(2)}, u32[]{:S(2)}) collective-permute-start(bf16[64,1152]{1,0:T(8,128)(2,1)} %get-tuple-element.10), channel_id=1, source_target_pairs={{0,64},{64,0},{1,65},{65,1},{2,66},{66,2},{3,67},{67,3},{4,68},{68... | collective-permute-start | bytes 442376 | tf_op jit(solution)/shard_map/ppermute | solution.py:25
  6.0 49.9 %all-to-all-start = ((bf16[16,32,1152]{2,1,0:T(8,128)(2,1)}), bf16[16,32,1152]{2,1,0:T(8,128)(2,1)S(1)}, u32[]{:S(2)}, u32[]{:S(2)}) async-start(bf16[16,32,1152]{2,1,0:T(8,128)(2,1)} %get-tuple-element.11), calls=%async_computation | async-start | bytes 2359296 | tf_op jit(solution)/shard_map/all_to_all | solution.py:34
  21.4 16.5 %copy-start.3 = (bf16[256,1152]{1,0:T(8,128)(2,1)S(1)}, bf16[256,1152]{1,0:T(8,128)(2,1)}, u32[]{:S(2)}) copy-start(bf16[256,1152]{1,0:T(8,128)(2,1)} %image_ref.1) | copy-start | bytes 1769476
  21.4 10.3 %collective-permute-start.1 = (bf16[64,1152]{1,0:T(8,128)(2,1)S(1)}, bf16[64,1152]{1,0:T(8,128)(2,1)S(1)}, u32[]{:S(2)}, u32[]{:S(2)}) collective-permute-start(bf16[64,1152]{1,0:T(8,128)(2,1)S(1)} %collective-permute-done), channel_id=1, source_target_pairs={{0,6},{2,0},{4,2},{6,4},{1,7},{3,1},{5,3},{7,5},{8,14},{10,8},{12,... | collective-permute-start | bytes 442376 | tf_op jit(solution)/shard_map/ppermute | solution.py:30
  26.2 9.9 %collective-permute-start.2 = (bf16[64,1152]{1,0:T(8,128)(2,1)S(1)}, bf16[64,1152]{1,0:T(8,128)(2,1)S(1)}, u32[]{:S(2)}, u32[]{:S(2)}) collective-permute-start(bf16[64,1152]{1,0:T(8,128)(2,1)S(1)} %collective-permute-done), channel_id=1, source_target_pairs={{0,4},{2,6},{4,0},{6,2},{1,5},{3,7},{5,1},{7,3},{8,12},{10,14},{12... | collective-permute-start | bytes 442376 | tf_op jit(solution)/shard_map/ppermute | solution.py:30
  28.9 8.9 %collective-permute-start.3 = (bf16[64,1152]{1,0:T(8,128)(2,1)S(1)}, bf16[64,1152]{1,0:T(8,128)(2,1)S(1)}, u32[]{:S(2)}, u32[]{:S(2)}) collective-permute-start(bf16[64,1152]{1,0:T(8,128)(2,1)S(1)} %collective-permute-done), channel_id=1, source_target_pairs={{0,2},{2,4},{4,6},{6,0},{1,3},{3,5},{5,7},{7,1},{8,10},{10,12},{12... | collective-permute-start | bytes 442376 | tf_op jit(solution)/shard_map/ppermute | solution.py:30
  38.5 3.7 %copy-start.9 = (s32[32]{0:T(128)S(1)}, s32[32]{0:T(128)}, u32[]{:S(2)}) copy-start(s32[32]{0:T(128)} %param.7) | copy-start | bytes 388
  38.9 3.4 %copy-start.2 = (bf16[512,1152]{1,0:T(8,128)(2,1)}, bf16[512,1152]{1,0:T(8,128)(2,1)S(1)}, u32[]{:S(2)}) copy-start(bf16[512,1152]{1,0:T(8,128)(2,1)S(1)} %fusion.1) | copy-start | bytes 3538948
  38.9 4.9 %collective-permute-start.4 = (bf16[512,1152]{1,0:T(8,128)(2,1)S(1)}, bf16[512,1152]{1,0:T(8,128)(2,1)}, u32[]{:S(2)}, u32[]{:S(2)}) collective-permute-start(bf16[512,1152]{1,0:T(8,128)(2,1)S(1)} %fusion.1), channel_id=1, source_target_pairs={{0,8},{8,0},{1,9},{9,1},{2,10},{10,2},{3,11},{11,3},{4,12},{12,4},... | collective-permute-start | bytes 3538952 | tf_op jit(solution)/shard_map/ppermute | solution.py:25
  56.7 2.0 %copy-start = (bf16[512,1152]{1,0:T(8,128)(2,1)}, bf16[512,1152]{1,0:T(8,128)(2,1)S(1)}, u32[]{:S(2)}) copy-start(bf16[512,1152]{1,0:T(8,128)(2,1)S(1)} %fusion.2) | copy-start | bytes 3538948
  58.7 1.9 %copy-start.6 = (bf16[1024,512]{1,0:T(8,128)(2,1)}, bf16[1024,512]{1,0:T(8,128)(2,1)S(1)}, u32[]{:S(2)}) copy-start(bf16[1024,512]{1,0:T(8,128)(2,1)S(1)} %subtract_convert_fusion) | copy-start | bytes 3145732
  58.7 3.8 %copy-start.4 = (bf16[256,1152]{1,0:T(8,128)(2,1)S(1)}, bf16[256,1152]{1,0:T(8,128)(2,1)}, u32[]{:S(2)}) copy-start(bf16[256,1152]{1,0:T(8,128)(2,1)} %image_ref.1) | copy-start | bytes 1769476
  60.6 6.9 %collective-permute-start.5 = (bf16[512,1152]{1,0:T(8,128)(2,1)}, bf16[512,1152]{1,0:T(8,128)(2,1)}, u32[]{:S(2)}, u32[]{:S(2)}) collective-permute-start(bf16[512,1152]{1,0:T(8,128)(2,1)} %convolution_convert_fusion), channel_id=1, source_target_pairs={{0,8},{8,0},{1,9},{9,1},{2,10},{10,2},{3,11},{11,3},{4,12},{12,4},... | collective-permute-start | bytes 3538952 | tf_op jit(solution)/shard_map/ppermute | solution.py:25
  63.5 4.0 %copy-start.1 = (bf16[512,1152]{1,0:T(8,128)(2,1)S(1)}, bf16[512,1152]{1,0:T(8,128)(2,1)}, u32[]{:S(2)}) copy-start(bf16[512,1152]{1,0:T(8,128)(2,1)} %copy-done) | copy-start | bytes 3538948
  63.5 4.0 %copy-start.7 = (bf16[1024,512]{1,0:T(8,128)(2,1)S(1)}, bf16[1024,512]{1,0:T(8,128)(2,1)}, u32[]{:S(2)}) copy-start(bf16[1024,512]{1,0:T(8,128)(2,1)} %copy-done.6) | copy-start | bytes 3145732
  69.6 11.0 %copy-start.8 = (bf16[32,1152]{1,0:T(8,128)(2,1)S(1)}, bf16[32,1152]{1,0:T(8,128)(2,1)}, u32[]{:S(2)}) copy-start(bf16[32,1152]{1,0:T(8,128)(2,1)} %text_ref.1) | copy-start | bytes 221188
  69.8 11.6 %collective-permute-start.8 = (bf16[128,1152]{1,0:T(8,128)(2,1)S(1)}, bf16[128,1152]{1,0:T(8,128)(2,1)S(1)}, u32[]{:S(2)}, u32[]{:S(2)}) collective-permute-start(bf16[128,1152]{1,0:T(8,128)(2,1)S(1)} %bitcast.41), channel_id=1, source_target_pairs={{0,6},{2,0},{4,2},{6,4},{1,7},{3,1},{5,3},{7,5},{8,14},{10,8},{12,... | collective-permute-start | bytes 884744 | tf_op jit(solution)/shard_map/ppermute | solution.py:30
  74.4 18.6 %collective-permute-start.7 = (bf16[128,1152]{1,0:T(8,128)(2,1)S(1)}, bf16[128,1152]{1,0:T(8,128)(2,1)S(1)}, u32[]{:S(2)}, u32[]{:S(2)}) collective-permute-start(bf16[128,1152]{1,0:T(8,128)(2,1)S(1)} %bitcast.40), channel_id=1, source_target_pairs={{0,2},{2,4},{4,6},{6,0},{1,3},{3,5},{5,7},{7,1},{8,10},{10,12},{12... | collective-permute-start | bytes 884744 | tf_op jit(solution)/shard_map/ppermute | solution.py:30
  76.4 16.6 %collective-permute-start.6 = (bf16[128,1152]{1,0:T(8,128)(2,1)S(1)}, bf16[128,1152]{1,0:T(8,128)(2,1)S(1)}, u32[]{:S(2)}, u32[]{:S(2)}) collective-permute-start(bf16[128,1152]{1,0:T(8,128)(2,1)S(1)} %bitcast.39), channel_id=1, source_target_pairs={{0,4},{2,6},{4,0},{6,2},{1,5},{3,7},{5,1},{7,3},{8,12},{10,14},{12... | collective-permute-start | bytes 884744 | tf_op jit(solution)/shard_map/ppermute | solution.py:30
  93.2 15.8 %collective-permute-start.11 = (bf16[64,1152]{1,0:T(8,128)(2,1)S(1)}, bf16[64,1152]{1,0:T(8,128)(2,1)S(1)}, u32[]{:S(2)}, u32[]{:S(2)}) collective-permute-start(bf16[64,1152]{1,0:T(8,128)(2,1)S(1)} %get-tuple-element.26), channel_id=1, source_target_pairs={{0,65},{1,64},{64,1},{65,0},{2,67},{3,66},{66,3},{67,2},{4,69},{5,... | collective-permute-start | bytes 442376 | tf_op jit(solution)/shard_map/ppermute | solution.py:25
  95.1 13.8 %collective-permute-start.10 = (bf16[64,1152]{1,0:T(8,128)(2,1)S(1)}, bf16[64,1152]{1,0:T(8,128)(2,1)S(1)}, u32[]{:S(2)}, u32[]{:S(2)}) collective-permute-start(bf16[64,1152]{1,0:T(8,128)(2,1)S(1)} %get-tuple-element.26), channel_id=1, source_target_pairs={{0,64},{64,0},{1,65},{65,1},{2,66},{66,2},{3,67},{67,3},{4,68},{68... | collective-permute-start | bytes 442376 | tf_op jit(solution)/shard_map/ppermute | solution.py:25
  98.4 10.6 %collective-permute-start.9 = (bf16[64,1152]{1,0:T(8,128)(2,1)S(1)}, bf16[64,1152]{1,0:T(8,128)(2,1)S(1)}, u32[]{:S(2)}, u32[]{:S(2)}) collective-permute-start(bf16[64,1152]{1,0:T(8,128)(2,1)S(1)} %get-tuple-element.25), channel_id=1, source_target_pairs={{0,1},{1,0},{2,3},{3,2},{4,5},{5,4},{6,7},{7,6},{8,9},{9,8},{10,11... | collective-permute-start | bytes 442376 | tf_op jit(solution)/shard_map/ppermute | solution.py:25
  102.5 6.4 %copy-start.5 = (f32[64,1152]{1,0:T(8,128)S(1)}, f32[64,1152]{1,0:T(8,128)}, u32[]{:S(2)}) copy-start(f32[64,1152]{1,0:T(8,128)} %convert_divide_fusion.1) | copy-start | bytes 884740
  102.5 39.4 %all-to-all-start.1 = ((bf16[16,32,1152]{2,1,0:T(8,128)(2,1)}), bf16[16,32,1152]{2,1,0:T(8,128)(2,1)S(1)}, u32[]{:S(2)}, u32[]{:S(2)}) async-start(bf16[16,32,1152]{2,1,0:T(8,128)(2,1)} %bitcast.17), calls=%async_computation.1 | async-start | bytes 2359296 | tf_op jit(solution)/shard_map/all_to_all | solution.py:34
  109.3 7.8 %collective-permute-start.12 = (bf16[64,1152]{1,0:T(8,128)(2,1)S(1)}, bf16[64,1152]{1,0:T(8,128)(2,1)S(1)}, u32[]{:S(2)}, u32[]{:S(2)}) collective-permute-start(bf16[64,1152]{1,0:T(8,128)(2,1)S(1)} %get-tuple-element.19), channel_id=1, source_target_pairs={{0,6},{2,0},{4,2},{6,4},{1,7},{3,1},{5,3},{7,5},{8,14},{10,8},{12,... | collective-permute-start | bytes 442376 | tf_op jit(solution)/shard_map/ppermute | solution.py:30
  111.2 9.2 %collective-permute-start.13 = (bf16[64,1152]{1,0:T(8,128)(2,1)S(1)}, bf16[64,1152]{1,0:T(8,128)(2,1)S(1)}, u32[]{:S(2)}, u32[]{:S(2)}) collective-permute-start(bf16[64,1152]{1,0:T(8,128)(2,1)S(1)} %get-tuple-element.19), channel_id=1, source_target_pairs={{0,4},{2,6},{4,0},{6,2},{1,5},{3,7},{5,1},{7,3},{8,12},{10,14},{12... | collective-permute-start | bytes 442376 | tf_op jit(solution)/shard_map/ppermute | solution.py:30
  113.7 9.1 %collective-permute-start.14 = (bf16[64,1152]{1,0:T(8,128)(2,1)S(1)}, bf16[64,1152]{1,0:T(8,128)(2,1)S(1)}, u32[]{:S(2)}, u32[]{:S(2)}) collective-permute-start(bf16[64,1152]{1,0:T(8,128)(2,1)S(1)} %get-tuple-element.19), channel_id=1, source_target_pairs={{0,2},{2,4},{4,6},{6,0},{1,3},{3,5},{5,7},{7,1},{8,10},{10,12},{12... | collective-permute-start | bytes 442376 | tf_op jit(solution)/shard_map/ppermute | solution.py:30

commit v12 on v11

--- a/solution.py
+++ b/solution.py
@@ -107,13 +107,14 @@
     cosine = lax.dot_general(images, text_bf, (((1,), (1,)), ((), ())), preferred_element_type=F32)
     grad = (jax.nn.sigmoid(scale * cosine + bias[0]) - hit).astype(BF16)
     text_terms = lax.dot_general(grad, images, (((0,), (0,)), ((), ())), preferred_element_type=F32).astype(BF16)
+    text_terms, grad = lax.optimization_barrier((text_terms, grad))
+    text_sum = exchange(text_terms.reshape(peers, mine, width), RINGS, TEXT_GROUPS)
+
     half = near.shape[0]
     far_terms = jnp.dot(grad[half:], text_bf, preferred_element_type=F32).astype(BF16)
     far_terms = swap(far_terms, "c").astype(F32)
     both = jnp.dot(grad[:half], text_bf, preferred_element_type=F32) + far_terms
     both = both.reshape(2, n_x, quarter, width)
-    text_terms, both = lax.optimization_barrier((text_terms, both))
-    text_sum = exchange(text_terms.reshape(peers, mine, width), RINGS, TEXT_GROUPS)
 
     def of_position(k):
         return lax.dynamic_index_in_dim(both, lax.rem(x + k, n_x), axis=1, keepdims=False)
@@ -126,9 +127,9 @@
     own, other = jnp.where(upper, total[1], total[0]), jnp.where(upper, total[0], total[1])
     beside, across, corner = swap(own, "l"), swap(other, "yl"), swap(other, ("yl", "l"))
     image_sum = (own.astype(F32) + beside.astype(F32)) + (across.astype(F32) + corner.astype(F32))
+    image_sum, text_sum = lax.optimization_barrier((image_sum, text_sum))
     done = finish(image_sum[None], image_unit, image_norm, scale)
-    around = [done] + [shift(done, "x", n_x - d) for d in range(1, n_x)]
-    grad_image = in_order(around, x)
+    grad_image = exchange(jnp.broadcast_to(done[None], (n_x,) + done.shape), "x").reshape(rows, width)
     grad_text = finish(text_sum, text_unit, text_norm, scale)
     return grad_image, grad_text
 

time: 144 us -> 128 us (0.89)
  the two profiles are of different devices: /device:TPU:48 before, /device:TPU:1 now
where the time goes in v12:
time: 128 us; the launch traced here: 127 us
  starting transfers between devices  67.9 us (53%)
  waiting for transfers between devices  37.7 us (29%)
  matrix products  8.69 us (7%)
  other arithmetic  5.48 us (4%)
  Pallas kernels  2.77 us (2%)
  between operations  2.43 us (2%)
  local copies, waits for them, and re-layouts  2.05 us (2%)
    all_to_all x3, starting transfers between devices, exchange(): lax.all_to_all(blocks, axes, 0, 0, axis_index_groups=groups, tiled=True)  25.4 us
    ppermute x6, starting transfers between devices, swap(): return lax.ppermute(block, axes, [(i, count - 1 - i) for i in range(count)])  21.9 us
    ppermute x6, starting transfers between devices, shift(): lax.ppermute(block, axis, [(i, (i + distance) % count) for i in range(cou...  20.6 us
    all_to_all x3, waiting for transfers between devices, exchange(): lax.all_to_all(blocks, axes, 0, 0, axis_index_groups=groups, tiled=True)  14.2 us
    ppermute x6, waiting for transfers between devices, shift(): lax.ppermute(block, axis, [(i, (i + distance) % count) for i in range(cou...  14 us
    ppermute x6, waiting for transfers between devices, swap(): return lax.ppermute(block, axes, [(i, count - 1 - i) for i in range(count)])  9.43 us
    pallas_call x1, Pallas kernels, first_copies(): pl.pallas_call(body, out_shape=(jax.ShapeDtypeStruct((quarter, width), BF...  2.77 us
    dot_general x1, matrix products, local(): lax.dot_general(grad, images, (((0,), (0,)), ((), ())), preferred_element...  2.58 us
  transfers between devices with their start and end apart: 15, of which 9 were waited for; matrix products, arithmetic and copies ran while one was open for 5% of the time, Pallas kernels for 0%

profile of v12, /device:TPU:1, one launch (start us, length us, event | category | flops | bytes accessed | tf_op | source)
XLA Modules:
  0.0 127.0 jit_solution(12081370755879246440)
XLA Ops:
  0.6 2.8 %first_copies.1 = (bf16[64,1152]{1,0:T(8,128)(2,1)}, bf16[16,32,1152]{2,1,0:T(8,128)(2,1)}) custom-call(s32[1]{0:T(128)} %bitcast.1.x_ref, bf16[256,1152]{1,0:T(8,128)(2,1)} %image_ref.1, bf16[32,1152]{1,0:T(8,128)(2,1)} %text_ref.1), custom_call_target="tpu_custom_call" | custom-call | tf_op jit(solution)/shard_map/first_copies/pallas_call | solution.py:56
  3.4 4.0 %collective-permute-start = (bf16[64,1152]{1,0:T(8,128)(2,1)}, bf16[64,1152]{1,0:T(8,128)(2,1)S(1)}, u32[]{:S(2)}, u32[]{:S(2)}) collective-permute-start(bf16[64,1152]{1,0:T(8,128)(2,1)} %get-tuple-element.12), channel_id=1, source_target_pairs={{0,64},{64,0},{1,65},{65,1},{2,66},{66,2},{3,67},{67,3},{4,68},{68... | collective-permute-start | bytes 442376 | tf_op jit(solution)/shard_map/ppermute | solution.py:25
  7.5 14.4 %all-to-all-start = ((bf16[16,32,1152]{2,1,0:T(8,128)(2,1)}), bf16[16,32,1152]{2,1,0:T(8,128)(2,1)S(1)}, u32[]{:S(2)}, u32[]{:S(2)}) async-start(bf16[16,32,1152]{2,1,0:T(8,128)(2,1)} %get-tuple-element.13), calls=%async_computation | async-start | bytes 2359296 | tf_op jit(solution)/shard_map/all_to_all | solution.py:34
  21.9 4.5 %collective-permute-start.1 = (bf16[64,1152]{1,0:T(8,128)(2,1)S(1)}, bf16[64,1152]{1,0:T(8,128)(2,1)S(1)}, u32[]{:S(2)}, u32[]{:S(2)}) collective-permute-start(bf16[64,1152]{1,0:T(8,128)(2,1)S(1)} %collective-permute-done), channel_id=1, source_target_pairs={{0,6},{2,0},{4,2},{6,4},{1,7},{3,1},{5,3},{7,5},{8,14},{10,8},{12,... | collective-permute-start | bytes 442376 | tf_op jit(solution)/shard_map/ppermute | solution.py:30
  26.4 2.4 %collective-permute-start.2 = (bf16[64,1152]{1,0:T(8,128)(2,1)S(1)}, bf16[64,1152]{1,0:T(8,128)(2,1)S(1)}, u32[]{:S(2)}, u32[]{:S(2)}) collective-permute-start(bf16[64,1152]{1,0:T(8,128)(2,1)S(1)} %collective-permute-done), channel_id=1, source_target_pairs={{0,4},{2,6},{4,0},{6,2},{1,5},{3,7},{5,1},{7,3},{8,12},{10,14},{12... | collective-permute-start | bytes 442376 | tf_op jit(solution)/shard_map/ppermute | solution.py:30
  28.9 2.5 %collective-permute-start.3 = (bf16[64,1152]{1,0:T(8,128)(2,1)S(1)}, bf16[64,1152]{1,0:T(8,128)(2,1)S(1)}, u32[]{:S(2)}, u32[]{:S(2)}) collective-permute-start(bf16[64,1152]{1,0:T(8,128)(2,1)S(1)} %collective-permute-done), channel_id=1, source_target_pairs={{0,2},{2,4},{4,6},{6,0},{1,3},{3,5},{5,7},{7,1},{8,10},{10,12},{12... | collective-permute-start | bytes 442376 | tf_op jit(solution)/shard_map/ppermute | solution.py:30
  31.4 2.7 %collective-permute-done.2 = bf16[64,1152]{1,0:T(8,128)(2,1)S(1)} collective-permute-done((bf16[64,1152]{1,0:T(8,128)(2,1)S(1)}, bf16[64,1152]{1,0:T(8,128)(2,1)S(1)}, u32[]{:S(2)}, u32[]{:S(2)}) %collective-permute-start.2) | collective-permute-done | bytes 147488 | tf_op jit(solution)/shard_map/ppermute | solution.py:30
  34.1 4.0 %collective-permute-done.3 = bf16[64,1152]{1,0:T(8,128)(2,1)S(1)} collective-permute-done((bf16[64,1152]{1,0:T(8,128)(2,1)S(1)}, bf16[64,1152]{1,0:T(8,128)(2,1)S(1)}, u32[]{:S(2)}, u32[]{:S(2)}) %collective-permute-start.3) | collective-permute-done | bytes 147488 | tf_op jit(solution)/shard_map/ppermute | solution.py:30
  38.3 0.2 broadcast_select_fusion.1
  38.5 0.3 fusion
  38.8 0.4 fusion.1
  39.2 3.5 %collective-permute-start.4 = (bf16[512,1152]{1,0:T(8,128)(2,1)S(1)}, bf16[512,1152]{1,0:T(8,128)(2,1)}, u32[]{:S(2)}, u32[]{:S(2)}) collective-permute-start(bf16[512,1152]{1,0:T(8,128)(2,1)S(1)} %fusion.1), channel_id=1, source_target_pairs={{0,8},{8,0},{1,9},{9,1},{2,10},{10,2},{3,11},{11,3},{4,12},{12,4},... | collective-permute-start | bytes 3538952 | tf_op jit(solution)/shard_map/ppermute | solution.py:25
  44.1 0.1 add_dynamic-update-slice_fusion
  44.2 1.1 collective-permute-done.4
  45.3 1.8 %pad_maximum_fusion = bf16[1024,1152]{1,0:T(8,128)(2,1)S(1)} fusion(bf16[512,1152]{1,0:T(8,128)(2,1)} %collective-permute-done.4, bf16[512,1152]{1,0:T(8,128)(2,1)} %copy-done.2), kind=kLoop, calls=%fused_computation.6 | loop fusion | flops 4718592 | bytes 4718592 | tf_op jit(solution)/shard_map/concatenate | solution.py:106
  47.1 5.6 %all-to-all-done = bf16[16,32,1152]{2,1,0:T(8,128)(2,1)S(1)} async-done(((bf16[16,32,1152]{2,1,0:T(8,128)(2,1)}), bf16[16,32,1152]{2,1,0:T(8,128)(2,1)S(1)}, u32[]{:S(2)}, u32[]{:S(2)}) %all-to-all-start) | async-done | bytes 1179680 | tf_op jit(solution)/shard_map/all_to_all | solution.py:34
  52.7 0.3 multiply_reduce_fusion
  53.1 0.4 fusion.2
  53.5 1.9 %subtract_convert_fusion = bf16[1024,512]{1,0:T(8,128)(2,1)S(1)} fusion(bf16[1024,1152]{1,0:T(8,128)(2,1)S(1)} %pad_maximum_fusion, bf16[512,1152]{1,0:T(8,128)(2,1)S(1)} %fusion.2, s32[512]{0:T(512)S(1)} %add_dynamic-update-slice_fusion, f32[]{:T(128)} %bitcast.37, f32[]{:T(128)} %bitcast), kind=kOutput, calls=%fused_computation.12 | convolution fusion | flops 1212678144 | bytes 4589576 | tf_op jit(solution)/shard_map/dot_general | solution.py:107
  55.5 2.6 %convolution_convert_fusion.1 = bf16[512,1152]{1,0:T(8,128)(2,1)} fusion(bf16[1024,512]{1,0:T(8,128)(2,1)S(1)} %subtract_convert_fusion, bf16[1024,1152]{1,0:T(8,128)(2,1)S(1)} %pad_maximum_fusion), kind=kOutput, calls=%fused_computation.1 | convolution fusion | flops 1208549376 | bytes 4587520 | tf_op jit(solution)/shard_map/dot_general | solution.py:109
  58.1 1.9 %convolution_convert_fusion = bf16[512,1152]{1,0:T(8,128)(2,1)} fusion(bf16[512,1152]{1,0:T(8,128)(2,1)S(1)} %fusion.2, bf16[1024,512]{1,0:T(8,128)(2,1)S(1)} %subtract_convert_fusion), kind=kOutput, calls=%fused_computation | convolution fusion | flops 604569600 | bytes 2883584 | tf_op jit(solution)/shard_map/dot_general | solution.py:114
  59.9 6.0 %collective-permute-start.5 = (bf16[512,1152]{1,0:T(8,128)(2,1)}, bf16[512,1152]{1,0:T(8,128)(2,1)}, u32[]{:S(2)}, u32[]{:S(2)}) collective-permute-start(bf16[512,1152]{1,0:T(8,128)(2,1)} %convolution_convert_fusion), channel_id=1, source_target_pairs={{0,8},{8,0},{1,9},{9,1},{2,10},{10,2},{3,11},{11,3},{4,12},{12,4},... | collective-permute-start | bytes 3538952 | tf_op jit(solution)/shard_map/ppermute | solution.py:25
  66.0 0.1 fusion.9
  66.1 0.1 convert_divide_fusion.1
  66.2 7.0 %all-to-all-start.1 = ((bf16[16,32,1152]{2,1,0:T(8,128)(2,1)}), bf16[16,32,1152]{2,1,0:T(8,128)(2,1)S(1)}, u32[]{:S(2)}, u32[]{:S(2)}) async-start(bf16[16,32,1152]{2,1,0:T(8,128)(2,1)} %bitcast.14), calls=%async_computation.1 | async-start | bytes 2359296 | tf_op jit(solution)/shard_map/all_to_all | solution.py:34
  73.2 2.3 %convert_add_fusion = f32[512,1152]{1,0:T(8,128)S(1)} fusion(bf16[512,1152]{1,0:T(8,128)(2,1)} %collective-permute-done.5, bf16[512,1152]{1,0:T(8,128)(2,1)S(1)} %copy-done.1, bf16[1024,512]{1,0:T(8,128)(2,1)} %copy-done.5), kind=kOutput, calls=%fused_computation.10 | convolution fusion | flops 605159424 | bytes 5242880 | tf_op jit(solution)/shard_map/dot_general | solution.py:116
  75.5 0.1 dynamic-slice_convert_fusion.2
  75.7 4.7 %collective-permute-start.6 = (bf16[128,1152]{1,0:T(8,128)(2,1)S(1)}, bf16[128,1152]{1,0:T(8,128)(2,1)S(1)}, u32[]{:S(2)}, u32[]{:S(2)}) collective-permute-start(bf16[128,1152]{1,0:T(8,128)(2,1)S(1)} %bitcast.43), channel_id=1, source_target_pairs={{0,4},{2,6},{4,0},{6,2},{1,5},{3,7},{5,1},{7,3},{8,12},{10,14},{12... | collective-permute-start | bytes 884744 | tf_op jit(solution)/shard_map/ppermute | solution.py:30
  80.3 2.2 %collective-permute-start.7 = (bf16[128,1152]{1,0:T(8,128)(2,1)S(1)}, bf16[128,1152]{1,0:T(8,128)(2,1)S(1)}, u32[]{:S(2)}, u32[]{:S(2)}) collective-permute-start(bf16[128,1152]{1,0:T(8,128)(2,1)S(1)} %bitcast.42), channel_id=1, source_target_pairs={{0,2},{2,4},{4,6},{6,0},{1,3},{3,5},{5,7},{7,1},{8,10},{10,12},{12... | collective-permute-start | bytes 884744 | tf_op jit(solution)/shard_map/ppermute | solution.py:30
  82.5 4.3 %collective-permute-start.8 = (bf16[128,1152]{1,0:T(8,128)(2,1)S(1)}, bf16[128,1152]{1,0:T(8,128)(2,1)S(1)}, u32[]{:S(2)}, u32[]{:S(2)}) collective-permute-start(bf16[128,1152]{1,0:T(8,128)(2,1)S(1)} %bitcast.41), channel_id=1, source_target_pairs={{0,6},{2,0},{4,2},{6,4},{1,7},{3,1},{5,3},{7,5},{8,14},{10,8},{12,... | collective-permute-start | bytes 884744 | tf_op jit(solution)/shard_map/ppermute | solution.py:30
  86.8 0.1 fusion.10
  87.0 0.4 collective-permute-done.6
  87.4 6.9 %collective-permute-done.7 = bf16[128,1152]{1,0:T(8,128)(2,1)S(1)} collective-permute-done((bf16[128,1152]{1,0:T(8,128)(2,1)S(1)}, bf16[128,1152]{1,0:T(8,128)(2,1)S(1)}, u32[]{:S(2)}, u32[]{:S(2)}) %collective-permute-start.7) | collective-permute-done | bytes 294944 | tf_op jit(solution)/shard_map/ppermute | solution.py:30
  94.3 0.1 fusion.3
  94.5 1.9 %collective-permute-start.10 = (bf16[64,1152]{1,0:T(8,128)(2,1)S(1)}, bf16[64,1152]{1,0:T(8,128)(2,1)S(1)}, u32[]{:S(2)}, u32[]{:S(2)}) collective-permute-start(bf16[64,1152]{1,0:T(8,128)(2,1)S(1)} %get-tuple-element.28), channel_id=1, source_target_pairs={{0,64},{64,0},{1,65},{65,1},{2,66},{66,2},{3,67},{67,3},{4,68},{68... | collective-permute-start | bytes 442376 | tf_op jit(solution)/shard_map/ppermute | solution.py:25
  96.4 2.7 %collective-permute-start.11 = (bf16[64,1152]{1,0:T(8,128)(2,1)S(1)}, bf16[64,1152]{1,0:T(8,128)(2,1)S(1)}, u32[]{:S(2)}, u32[]{:S(2)}) collective-permute-start(bf16[64,1152]{1,0:T(8,128)(2,1)S(1)} %get-tuple-element.28), channel_id=1, source_target_pairs={{0,65},{1,64},{64,1},{65,0},{2,67},{3,66},{66,3},{67,2},{4,69},{5,... | collective-permute-start | bytes 442376 | tf_op jit(solution)/shard_map/ppermute | solution.py:25
  99.2 3.7 %collective-permute-start.9 = (bf16[64,1152]{1,0:T(8,128)(2,1)S(1)}, bf16[64,1152]{1,0:T(8,128)(2,1)S(1)}, u32[]{:S(2)}, u32[]{:S(2)}) collective-permute-start(bf16[64,1152]{1,0:T(8,128)(2,1)S(1)} %get-tuple-element.27), channel_id=1, source_target_pairs={{0,1},{1,0},{2,3},{3,2},{4,5},{5,4},{6,7},{7,6},{8,9},{9,8},{10,11... | collective-permute-start | bytes 442376 | tf_op jit(solution)/shard_map/ppermute | solution.py:25
  103.0 3.6 %collective-permute-done.11 = bf16[64,1152]{1,0:T(8,128)(2,1)S(1)} collective-permute-done((bf16[64,1152]{1,0:T(8,128)(2,1)S(1)}, bf16[64,1152]{1,0:T(8,128)(2,1)S(1)}, u32[]{:S(2)}, u32[]{:S(2)}) %collective-permute-start.11) | collective-permute-done | bytes 147488 | tf_op jit(solution)/shard_map/ppermute | solution.py:25
  106.6 4.7 %collective-permute-done.9 = bf16[64,1152]{1,0:T(8,128)(2,1)S(1)} collective-permute-done((bf16[64,1152]{1,0:T(8,128)(2,1)S(1)}, bf16[64,1152]{1,0:T(8,128)(2,1)S(1)}, u32[]{:S(2)}, u32[]{:S(2)}) %collective-permute-start.9) | collective-permute-done | bytes 147488 | tf_op jit(solution)/shard_map/ppermute | solution.py:25
  111.4 0.2 convert_reduce_fusion
  111.5 0.1 multiply_reduce_fusion.1
  111.7 0.1 divide_convert_fusion
  111.8 0.9 broadcast_in_dim.2
  112.7 4.0 %all-to-all-start.2 = ((bf16[4,64,1152]{2,1,0:T(8,128)(2,1)}), bf16[4,64,1152]{2,1,0:T(8,128)(2,1)S(1)}, u32[]{:S(2)}, u32[]{:S(2)}) async-start(bf16[4,64,1152]{2,1,0:T(8,128)(2,1)} %broadcast_in_dim.2), calls=%async_computation.2 | async-start | bytes 1179648 | tf_op jit(solution)/shard_map/all_to_all | solution.py:34
  116.7 0.1 multiply_reduce_fusion.2
  116.8 0.7 divide_convert_fusion.1
  117.6 8.6 %all-to-all-done.2 = bf16[4,64,1152]{2,1,0:T(8,128)(2,1)S(1)} async-done(((bf16[4,64,1152]{2,1,0:T(8,128)(2,1)}), bf16[4,64,1152]{2,1,0:T(8,128)(2,1)S(1)}, u32[]{:S(2)}, u32[]{:S(2)}) %all-to-all-start.2) | async-done | bytes 589856 | tf_op jit(solution)/shard_map/all_to_all | solution.py:34
  126.2 0.8 copy.18
  (39 shorter events, 0.5 us)
Async XLA Ops:
  3.4 18.5 %collective-permute-start = (bf16[64,1152]{1,0:T(8,128)(2,1)}, bf16[64,1152]{1,0:T(8,128)(2,1)S(1)}, u32[]{:S(2)}, u32[]{:S(2)}) collective-permute-start(bf16[64,1152]{1,0:T(8,128)(2,1)} %get-tuple-element.12), channel_id=1, source_target_pairs={{0,64},{64,0},{1,65},{65,1},{2,66},{66,2},{3,67},{67,3},{4,68},{68... | collective-permute-start | bytes 442376 | tf_op jit(solution)/shard_map/ppermute | solution.py:25
  7.5 45.3 %all-to-all-start = ((bf16[16,32,1152]{2,1,0:T(8,128)(2,1)}), bf16[16,32,1152]{2,1,0:T(8,128)(2,1)S(1)}, u32[]{:S(2)}, u32[]{:S(2)}) async-start(bf16[16,32,1152]{2,1,0:T(8,128)(2,1)} %get-tuple-element.13), calls=%async_computation | async-start | bytes 2359296 | tf_op jit(solution)/shard_map/all_to_all | solution.py:34
  21.9 16.4 %copy-start.3 = (bf16[256,1152]{1,0:T(8,128)(2,1)S(1)}, bf16[256,1152]{1,0:T(8,128)(2,1)}, u32[]{:S(2)}) copy-start(bf16[256,1152]{1,0:T(8,128)(2,1)} %image_ref.1) | copy-start | bytes 1769476
  21.9 9.5 %collective-permute-start.1 = (bf16[64,1152]{1,0:T(8,128)(2,1)S(1)}, bf16[64,1152]{1,0:T(8,128)(2,1)S(1)}, u32[]{:S(2)}, u32[]{:S(2)}) collective-permute-start(bf16[64,1152]{1,0:T(8,128)(2,1)S(1)} %collective-permute-done), channel_id=1, source_target_pairs={{0,6},{2,0},{4,2},{6,4},{1,7},{3,1},{5,3},{7,5},{8,14},{10,8},{12,... | collective-permute-start | bytes 442376 | tf_op jit(solution)/shard_map/ppermute | solution.py:30
  26.4 7.7 %collective-permute-start.2 = (bf16[64,1152]{1,0:T(8,128)(2,1)S(1)}, bf16[64,1152]{1,0:T(8,128)(2,1)S(1)}, u32[]{:S(2)}, u32[]{:S(2)}) collective-permute-start(bf16[64,1152]{1,0:T(8,128)(2,1)S(1)} %collective-permute-done), channel_id=1, source_target_pairs={{0,4},{2,6},{4,0},{6,2},{1,5},{3,7},{5,1},{7,3},{8,12},{10,14},{12... | collective-permute-start | bytes 442376 | tf_op jit(solution)/shard_map/ppermute | solution.py:30
  28.9 9.3 %collective-permute-start.3 = (bf16[64,1152]{1,0:T(8,128)(2,1)S(1)}, bf16[64,1152]{1,0:T(8,128)(2,1)S(1)}, u32[]{:S(2)}, u32[]{:S(2)}) collective-permute-start(bf16[64,1152]{1,0:T(8,128)(2,1)S(1)} %collective-permute-done), channel_id=1, source_target_pairs={{0,2},{2,4},{4,6},{6,0},{1,3},{3,5},{5,7},{7,1},{8,10},{10,12},{12... | collective-permute-start | bytes 442376 | tf_op jit(solution)/shard_map/ppermute | solution.py:30
  38.8 5.3 %copy-start.7 = (s32[32]{0:T(128)S(1)}, s32[32]{0:T(128)}, u32[]{:S(2)}) copy-start(s32[32]{0:T(128)} %param.7) | copy-start | bytes 388
  39.2 5.0 %copy-start.2 = (bf16[512,1152]{1,0:T(8,128)(2,1)}, bf16[512,1152]{1,0:T(8,128)(2,1)S(1)}, u32[]{:S(2)}) copy-start(bf16[512,1152]{1,0:T(8,128)(2,1)S(1)} %fusion.1) | copy-start | bytes 3538948
  39.2 6.1 %collective-permute-start.4 = (bf16[512,1152]{1,0:T(8,128)(2,1)S(1)}, bf16[512,1152]{1,0:T(8,128)(2,1)}, u32[]{:S(2)}, u32[]{:S(2)}) collective-permute-start(bf16[512,1152]{1,0:T(8,128)(2,1)S(1)} %fusion.1), channel_id=1, source_target_pairs={{0,8},{8,0},{1,9},{9,1},{2,10},{10,2},{3,11},{11,3},{4,12},{12,4},... | collective-permute-start | bytes 3538952 | tf_op jit(solution)/shard_map/ppermute | solution.py:25
  53.5 4.6 %copy-start = (bf16[512,1152]{1,0:T(8,128)(2,1)}, bf16[512,1152]{1,0:T(8,128)(2,1)S(1)}, u32[]{:S(2)}) copy-start(bf16[512,1152]{1,0:T(8,128)(2,1)S(1)} %fusion.2) | copy-start | bytes 3538948
  55.5 2.6 %copy-start.5 = (bf16[1024,512]{1,0:T(8,128)(2,1)}, bf16[1024,512]{1,0:T(8,128)(2,1)S(1)}, u32[]{:S(2)}) copy-start(bf16[1024,512]{1,0:T(8,128)(2,1)S(1)} %subtract_convert_fusion) | copy-start | bytes 3145732
  58.0 7.9 %copy-start.4 = (bf16[256,1152]{1,0:T(8,128)(2,1)S(1)}, bf16[256,1152]{1,0:T(8,128)(2,1)}, u32[]{:S(2)}) copy-start(bf16[256,1152]{1,0:T(8,128)(2,1)} %image_ref.1) | copy-start | bytes 1769476
  59.9 13.3 %collective-permute-start.5 = (bf16[512,1152]{1,0:T(8,128)(2,1)}, bf16[512,1152]{1,0:T(8,128)(2,1)}, u32[]{:S(2)}, u32[]{:S(2)}) collective-permute-start(bf16[512,1152]{1,0:T(8,128)(2,1)} %convolution_convert_fusion), channel_id=1, source_target_pairs={{0,8},{8,0},{1,9},{9,1},{2,10},{10,2},{3,11},{11,3},{4,12},{12,4},... | collective-permute-start | bytes 3538952 | tf_op jit(solution)/shard_map/ppermute | solution.py:25
  66.2 7.0 %copy-start.1 = (bf16[512,1152]{1,0:T(8,128)(2,1)S(1)}, bf16[512,1152]{1,0:T(8,128)(2,1)}, u32[]{:S(2)}) copy-start(bf16[512,1152]{1,0:T(8,128)(2,1)} %copy-done) | copy-start | bytes 3538948
  66.2 45.1 %all-to-all-start.1 = ((bf16[16,32,1152]{2,1,0:T(8,128)(2,1)}), bf16[16,32,1152]{2,1,0:T(8,128)(2,1)S(1)}, u32[]{:S(2)}, u32[]{:S(2)}) async-start(bf16[16,32,1152]{2,1,0:T(8,128)(2,1)} %bitcast.14), calls=%async_computation.1 | async-start | bytes 2359296 | tf_op jit(solution)/shard_map/all_to_all | solution.py:34
  75.5 11.3 %copy-start.6 = (bf16[32,1152]{1,0:T(8,128)(2,1)S(1)}, bf16[32,1152]{1,0:T(8,128)(2,1)}, u32[]{:S(2)}) copy-start(bf16[32,1152]{1,0:T(8,128)(2,1)} %text_ref.1) | copy-start | bytes 221188
  75.7 11.7 %collective-permute-start.6 = (bf16[128,1152]{1,0:T(8,128)(2,1)S(1)}, bf16[128,1152]{1,0:T(8,128)(2,1)S(1)}, u32[]{:S(2)}, u32[]{:S(2)}) collective-permute-start(bf16[128,1152]{1,0:T(8,128)(2,1)S(1)} %bitcast.43), channel_id=1, source_target_pairs={{0,4},{2,6},{4,0},{6,2},{1,5},{3,7},{5,1},{7,3},{8,12},{10,14},{12... | collective-permute-start | bytes 884744 | tf_op jit(solution)/shard_map/ppermute | solution.py:30
  80.3 14.0 %collective-permute-start.7 = (bf16[128,1152]{1,0:T(8,128)(2,1)S(1)}, bf16[128,1152]{1,0:T(8,128)(2,1)S(1)}, u32[]{:S(2)}, u32[]{:S(2)}) collective-permute-start(bf16[128,1152]{1,0:T(8,128)(2,1)S(1)} %bitcast.42), channel_id=1, source_target_pairs={{0,2},{2,4},{4,6},{6,0},{1,3},{3,5},{5,7},{7,1},{8,10},{10,12},{12... | collective-permute-start | bytes 884744 | tf_op jit(solution)/shard_map/ppermute | solution.py:30
  82.5 11.8 %collective-permute-start.8 = (bf16[128,1152]{1,0:T(8,128)(2,1)S(1)}, bf16[128,1152]{1,0:T(8,128)(2,1)S(1)}, u32[]{:S(2)}, u32[]{:S(2)}) collective-permute-start(bf16[128,1152]{1,0:T(8,128)(2,1)S(1)} %bitcast.41), channel_id=1, source_target_pairs={{0,6},{2,0},{4,2},{6,4},{1,7},{3,1},{5,3},{7,5},{8,14},{10,8},{12,... | collective-permute-start | bytes 884744 | tf_op jit(solution)/shard_map/ppermute | solution.py:30
  94.5 8.5 %collective-permute-start.10 = (bf16[64,1152]{1,0:T(8,128)(2,1)S(1)}, bf16[64,1152]{1,0:T(8,128)(2,1)S(1)}, u32[]{:S(2)}, u32[]{:S(2)}) collective-permute-start(bf16[64,1152]{1,0:T(8,128)(2,1)S(1)} %get-tuple-element.28), channel_id=1, source_target_pairs={{0,64},{64,0},{1,65},{65,1},{2,66},{66,2},{3,67},{67,3},{4,68},{68... | collective-permute-start | bytes 442376 | tf_op jit(solution)/shard_map/ppermute | solution.py:25
  96.4 10.1 %collective-permute-start.11 = (bf16[64,1152]{1,0:T(8,128)(2,1)S(1)}, bf16[64,1152]{1,0:T(8,128)(2,1)S(1)}, u32[]{:S(2)}, u32[]{:S(2)}) collective-permute-start(bf16[64,1152]{1,0:T(8,128)(2,1)S(1)} %get-tuple-element.28), channel_id=1, source_target_pairs={{0,65},{1,64},{64,1},{65,0},{2,67},{3,66},{66,3},{67,2},{4,69},{5,... | collective-permute-start | bytes 442376 | tf_op jit(solution)/shard_map/ppermute | solution.py:25
  99.2 12.1 %collective-permute-start.9 = (bf16[64,1152]{1,0:T(8,128)(2,1)S(1)}, bf16[64,1152]{1,0:T(8,128)(2,1)S(1)}, u32[]{:S(2)}, u32[]{:S(2)}) collective-permute-start(bf16[64,1152]{1,0:T(8,128)(2,1)S(1)} %get-tuple-element.27), channel_id=1, source_target_pairs={{0,1},{1,0},{2,3},{3,2},{4,5},{5,4},{6,7},{7,6},{8,9},{9,8},{10,11... | collective-permute-start | bytes 442376 | tf_op jit(solution)/shard_map/ppermute | solution.py:25
  112.7 13.5 %all-to-all-start.2 = ((bf16[4,64,1152]{2,1,0:T(8,128)(2,1)}), bf16[4,64,1152]{2,1,0:T(8,128)(2,1)S(1)}, u32[]{:S(2)}, u32[]{:S(2)}) async-start(bf16[4,64,1152]{2,1,0:T(8,128)(2,1)} %broadcast_in_dim.2), calls=%async_computation.2 | async-start | bytes 1179648 | tf_op jit(solution)/shard_map/all_to_all | solution.py:34

commit v13 on v11

--- a/solution.py
+++ b/solution.py
@@ -43,25 +43,21 @@
 def first_copies(x, image_emb, text_emb, quarter, peers):
     mine, width = text_emb.shape
 
-    def body(x_ref, image_ref, text_ref, quarter_ref, copies_ref, sems):
+    def body(x_ref, image_ref, text_ref, quarter_ref, copies_ref):
         start = pl.multiple_of(x_ref[0] * quarter, quarter)
-        copies = [pltpu.make_async_copy(image_ref.at[pl.ds(start, quarter)], quarter_ref, sems.at[peers])]
-        copies += [pltpu.make_async_copy(text_ref, copies_ref.at[k], sems.at[k]) for k in range(peers)]
-        for copy in copies:
-            copy.start()
-        for copy in copies:
-            copy.wait()
+        quarter_ref[...] = image_ref[pl.ds(start, quarter), :]
+        for k in range(peers):
+            copies_ref[k] = text_ref[...]
 
-    anywhere, whole = pl.BlockSpec(memory_space=pl.ANY), pl.BlockSpec(memory_space=pltpu.VMEM)
+    whole = pl.BlockSpec(memory_space=pltpu.VMEM)
     return pl.pallas_call(
         body,
         out_shape=(
             jax.ShapeDtypeStruct((quarter, width), BF16),
             jax.ShapeDtypeStruct((peers, mine, width), BF16),
         ),
-        in_specs=[pl.BlockSpec(memory_space=pltpu.SMEM), anywhere, whole],
-        out_specs=(whole, anywhere),
-        scratch_shapes=[pltpu.SemaphoreType.DMA((peers + 1,))],
+        in_specs=[pl.BlockSpec(memory_space=pltpu.SMEM), whole, whole],
+        out_specs=(whole, whole),
         name="first_copies",
     )(x, image_emb, text_emb)
 
@@ -70,6 +66,24 @@
     total = scale * jnp.sum(terms.astype(F32), axis=0)
     along = jnp.sum(unit * total, axis=1, keepdims=True)
     return ((total - unit * along) / norm).astype(BF16)
+
+
+def finish_late(terms, rows, scale):
+    count, height, width = terms.shape
+
+    def body(scale_ref, terms_ref, rows_ref, out_ref):
+        unit, norm = unit_rows(rows_ref[...])
+        out_ref[...] = finish(terms_ref[...], unit, norm, scale_ref[0])
+
+    whole = pl.BlockSpec(memory_space=pltpu.VMEM)
+    return pl.pallas_call(
+        body,
+        out_shape=jax.ShapeDtypeStruct((height, width), BF16),
+        in_specs=[pl.BlockSpec(memory_space=pltpu.SMEM), whole, whole],
+        out_specs=whole,
+        cost_estimate=pl.CostEstimate(flops=40_000_000_000, bytes_accessed=100_000_000, transcendentals=0),
+        name="finish_late",
+    )(scale.reshape(1), terms, rows)
 
 
 def local(image_emb, text_emb, positive, log_scale, bias):
@@ -98,10 +112,7 @@
     hit = (jnp.arange(2 * near.shape[0], dtype=jnp.int32)[:, None] == wanted[None, :]).astype(F32)
 
     image_unit, image_norm = unit_rows(lax.dynamic_slice_in_dim(image_emb, x * quarter, quarter, 0))
-    text_unit, text_norm = unit_rows(text_emb)
-    image_unit, image_norm, text_unit, text_norm = lax.optimization_barrier(
-        (image_unit, image_norm, text_unit, text_norm)
-    )
+    image_unit, image_norm = lax.optimization_barrier((image_unit, image_norm))
 
     images = lax.optimization_barrier(jnp.concatenate([near, far], axis=0))
     cosine = lax.dot_general(images, text_bf, (((1,), (1,)), ((), ())), preferred_element_type=F32)
@@ -128,8 +139,9 @@
     image_sum = (own.astype(F32) + beside.astype(F32)) + (across.astype(F32) + corner.astype(F32))
     done = finish(image_sum[None], image_unit, image_norm, scale)
     around = [done] + [shift(done, "x", n_x - d) for d in range(1, n_x)]
+    around, text_sum = lax.optimization_barrier((around, text_sum))
     grad_image = in_order(around, x)
-    grad_text = finish(text_sum, text_unit, text_norm, scale)
+    grad_text = finish_late(text_sum, text_emb, scale)
     return grad_image, grad_text
 
 

time: 144 us -> 137 us (0.951)
  the two profiles are of different devices: /device:TPU:48 before, /device:TPU:56 now
where the time goes in v13:
time: 137 us; the launch traced here: 136 us
  starting transfers between devices  77 us (56%)
  waiting for transfers between devices  36 us (26%)
  matrix products  8.73 us (6%)
  other arithmetic  5.37 us (4%)
  Pallas kernels  4.41 us (3%)
  between operations  2.41 us (2%)
  local copies, waits for them, and re-layouts  2.13 us (2%)
    ppermute x9, starting transfers between devices, shift(): lax.ppermute(block, axis, [(i, (i + distance) % count) for i in range(cou...  29.8 us
    all_to_all x2, starting transfers between devices, exchange(): lax.all_to_all(blocks, axes, 0, 0, axis_index_groups=groups, tiled=True)  24.7 us
    ppermute x6, starting transfers between devices, swap(): return lax.ppermute(block, axes, [(i, count - 1 - i) for i in range(count)])  22.4 us
    ppermute x6, waiting for transfers between devices, swap(): return lax.ppermute(block, axes, [(i, count - 1 - i) for i in range(count)])  17.6 us
    ppermute x9, waiting for transfers between devices, shift(): lax.ppermute(block, axis, [(i, (i + distance) % count) for i in range(cou...  14.8 us
    all_to_all x2, waiting for transfers between devices, exchange(): lax.all_to_all(blocks, axes, 0, 0, axis_index_groups=groups, tiled=True)  3.62 us
  transfers between devices with their start and end apart: 17, of which 11 were waited for; matrix products, arithmetic and copies ran while one was open for 5% of the time, Pallas kernels for 0%

profile of v13, /device:TPU:56, one launch (start us, length us, event | category | flops | bytes accessed | tf_op | source)
XLA Modules:
  0.0 136.0 jit_solution(5177444839218651394)
XLA Ops:
  0.6 2.2 %first_copies.1 = (bf16[64,1152]{1,0:T(8,128)(2,1)}, bf16[16,32,1152]{2,1,0:T(8,128)(2,1)}) custom-call(s32[1]{0:T(128)} %bitcast.1.x_ref, bf16[256,1152]{1,0:T(8,128)(2,1)} %image_ref.1, bf16[32,1152]{1,0:T(8,128)(2,1)} %rows_ref.1), custom_call_target="tpu_custom_call" | custom-call | tf_op jit(solution)/shard_map/first_copies/pallas_call | solution.py:53
  2.9 3.2 %collective-permute-start = (bf16[64,1152]{1,0:T(8,128)(2,1)}, bf16[64,1152]{1,0:T(8,128)(2,1)S(1)}, u32[]{:S(2)}, u32[]{:S(2)}) collective-permute-start(bf16[64,1152]{1,0:T(8,128)(2,1)} %get-tuple-element.13), channel_id=1, source_target_pairs={{0,64},{64,0},{1,65},{65,1},{2,66},{66,2},{3,67},{67,3},{4,68},{68... | collective-permute-start | bytes 442376 | tf_op jit(solution)/shard_map/ppermute | solution.py:25
  6.1 14.7 %all-to-all-start = ((bf16[16,32,1152]{2,1,0:T(8,128)(2,1)}), bf16[16,32,1152]{2,1,0:T(8,128)(2,1)S(1)}, u32[]{:S(2)}, u32[]{:S(2)}) async-start(bf16[16,32,1152]{2,1,0:T(8,128)(2,1)} %get-tuple-element.14), calls=%async_computation | async-start | bytes 2359296 | tf_op jit(solution)/shard_map/all_to_all | solution.py:34
  20.8 4.8 %collective-permute-start.1 = (bf16[64,1152]{1,0:T(8,128)(2,1)S(1)}, bf16[64,1152]{1,0:T(8,128)(2,1)S(1)}, u32[]{:S(2)}, u32[]{:S(2)}) collective-permute-start(bf16[64,1152]{1,0:T(8,128)(2,1)S(1)} %collective-permute-done), channel_id=1, source_target_pairs={{0,6},{2,0},{4,2},{6,4},{1,7},{3,1},{5,3},{7,5},{8,14},{10,8},{12,... | collective-permute-start | bytes 442376 | tf_op jit(solution)/shard_map/ppermute | solution.py:30
  25.6 2.7 %collective-permute-start.2 = (bf16[64,1152]{1,0:T(8,128)(2,1)S(1)}, bf16[64,1152]{1,0:T(8,128)(2,1)S(1)}, u32[]{:S(2)}, u32[]{:S(2)}) collective-permute-start(bf16[64,1152]{1,0:T(8,128)(2,1)S(1)} %collective-permute-done), channel_id=1, source_target_pairs={{0,4},{2,6},{4,0},{6,2},{1,5},{3,7},{5,1},{7,3},{8,12},{10,14},{12... | collective-permute-start | bytes 442376 | tf_op jit(solution)/shard_map/ppermute | solution.py:30
  28.3 2.8 %collective-permute-start.3 = (bf16[64,1152]{1,0:T(8,128)(2,1)S(1)}, bf16[64,1152]{1,0:T(8,128)(2,1)S(1)}, u32[]{:S(2)}, u32[]{:S(2)}) collective-permute-start(bf16[64,1152]{1,0:T(8,128)(2,1)S(1)} %collective-permute-done), channel_id=1, source_target_pairs={{0,2},{2,4},{4,6},{6,0},{1,3},{3,5},{5,7},{7,1},{8,10},{10,12},{12... | collective-permute-start | bytes 442376 | tf_op jit(solution)/shard_map/ppermute | solution.py:30
  31.2 4.3 %collective-permute-done.2 = bf16[64,1152]{1,0:T(8,128)(2,1)S(1)} collective-permute-done((bf16[64,1152]{1,0:T(8,128)(2,1)S(1)}, bf16[64,1152]{1,0:T(8,128)(2,1)S(1)}, u32[]{:S(2)}, u32[]{:S(2)}) %collective-permute-start.2) | collective-permute-done | bytes 147488 | tf_op jit(solution)/shard_map/ppermute | solution.py:30
  35.5 1.7 %collective-permute-done.3 = bf16[64,1152]{1,0:T(8,128)(2,1)S(1)} collective-permute-done((bf16[64,1152]{1,0:T(8,128)(2,1)S(1)}, bf16[64,1152]{1,0:T(8,128)(2,1)S(1)}, u32[]{:S(2)}, u32[]{:S(2)}) %collective-permute-start.3) | collective-permute-done | bytes 147488 | tf_op jit(solution)/shard_map/ppermute | solution.py:30
  37.3 0.2 broadcast_select_fusion.1
  37.6 0.3 fusion
  37.9 0.4 fusion.1
  38.3 1.9 %collective-permute-start.4 = (bf16[512,1152]{1,0:T(8,128)(2,1)S(1)}, bf16[512,1152]{1,0:T(8,128)(2,1)}, u32[]{:S(2)}, u32[]{:S(2)}) collective-permute-start(bf16[512,1152]{1,0:T(8,128)(2,1)S(1)} %fusion.1), channel_id=1, source_target_pairs={{0,8},{8,0},{1,9},{9,1},{2,10},{10,2},{3,11},{11,3},{4,12},{12,4},... | collective-permute-start | bytes 3538952 | tf_op jit(solution)/shard_map/ppermute | solution.py:25
  41.6 0.1 add_dynamic-update-slice_fusion
  41.7 1.5 %collective-permute-done.4 = bf16[512,1152]{1,0:T(8,128)(2,1)} collective-permute-done((bf16[512,1152]{1,0:T(8,128)(2,1)S(1)}, bf16[512,1152]{1,0:T(8,128)(2,1)}, u32[]{:S(2)}, u32[]{:S(2)}) %collective-permute-start.4) | collective-permute-done | bytes 1179680 | tf_op jit(solution)/shard_map/ppermute | solution.py:25
  43.2 1.8 %pad_maximum_fusion = bf16[1024,1152]{1,0:T(8,128)(2,1)S(1)} fusion(bf16[512,1152]{1,0:T(8,128)(2,1)} %collective-permute-done.4, bf16[512,1152]{1,0:T(8,128)(2,1)} %copy-done.2), kind=kLoop, calls=%fused_computation.6 | loop fusion | flops 4718592 | bytes 4718592 | tf_op jit(solution)/shard_map/concatenate | solution.py:117
  45.0 3.6 %all-to-all-done = bf16[16,32,1152]{2,1,0:T(8,128)(2,1)S(1)} async-done(((bf16[16,32,1152]{2,1,0:T(8,128)(2,1)}), bf16[16,32,1152]{2,1,0:T(8,128)(2,1)S(1)}, u32[]{:S(2)}, u32[]{:S(2)}) %all-to-all-start) | async-done | bytes 1179680 | tf_op jit(solution)/shard_map/all_to_all | solution.py:34
  48.6 0.3 multiply_reduce_fusion
  49.0 0.4 fusion.2
  49.4 1.9 %subtract_convert_fusion = bf16[1024,512]{1,0:T(8,128)(2,1)S(1)} fusion(bf16[1024,1152]{1,0:T(8,128)(2,1)S(1)} %pad_maximum_fusion, bf16[512,1152]{1,0:T(8,128)(2,1)S(1)} %fusion.2, s32[512]{0:T(512)S(1)} %add_dynamic-update-slice_fusion, f32[]{:T(128)} %bitcast.33, f32[]{:T(128)} %bitcast), kind=kOutput, calls=%fused_computation.11 | convolution fusion | flops 1212678144 | bytes 4589576 | tf_op jit(solution)/shard_map/dot_general | solution.py:118
  51.3 1.9 %convolution_convert_fusion = bf16[512,1152]{1,0:T(8,128)(2,1)} fusion(bf16[512,1152]{1,0:T(8,128)(2,1)S(1)} %fusion.2, bf16[1024,512]{1,0:T(8,128)(2,1)S(1)} %subtract_convert_fusion), kind=kOutput, calls=%fused_computation | convolution fusion | flops 604569600 | bytes 2883584 | tf_op jit(solution)/shard_map/dot_general | solution.py:122
  53.2 1.9 %collective-permute-start.5 = (bf16[512,1152]{1,0:T(8,128)(2,1)}, bf16[512,1152]{1,0:T(8,128)(2,1)}, u32[]{:S(2)}, u32[]{:S(2)}) collective-permute-start(bf16[512,1152]{1,0:T(8,128)(2,1)} %convolution_convert_fusion), channel_id=1, source_target_pairs={{0,8},{8,0},{1,9},{9,1},{2,10},{10,2},{3,11},{11,3},{4,12},{12,4},... | collective-permute-start | bytes 3538952 | tf_op jit(solution)/shard_map/ppermute | solution.py:25
  55.2 2.6 %convolution_convert_fusion.1 = bf16[512,1152]{1,0:T(8,128)(2,1)} fusion(bf16[1024,512]{1,0:T(8,128)(2,1)S(1)} %subtract_convert_fusion, bf16[1024,1152]{1,0:T(8,128)(2,1)S(1)} %pad_maximum_fusion), kind=kOutput, calls=%fused_computation.1 | convolution fusion | flops 1208549376 | bytes 4587520 | tf_op jit(solution)/shard_map/dot_general | solution.py:120
  57.8 0.5 collective-permute-done.5
  58.3 2.3 %convert_add_fusion = f32[512,1152]{1,0:T(8,128)S(1)} fusion(bf16[512,1152]{1,0:T(8,128)(2,1)} %collective-permute-done.5, bf16[512,1152]{1,0:T(8,128)(2,1)S(1)} %copy-done.1, bf16[1024,512]{1,0:T(8,128)(2,1)} %copy-done.5), kind=kOutput, calls=%fused_computation.9 | convolution fusion | flops 605159424 | bytes 5242880 | tf_op jit(solution)/shard_map/dot_general | solution.py:124
  60.6 0.8 dynamic-slice_convert_fusion.2
  61.5 4.7 %collective-permute-start.8 = (bf16[128,1152]{1,0:T(8,128)(2,1)}, bf16[128,1152]{1,0:T(8,128)(2,1)}, u32[]{:S(2)}, u32[]{:S(2)}) collective-permute-start(bf16[128,1152]{1,0:T(8,128)(2,1)} %bitcast.10), channel_id=1, source_target_pairs={{0,6},{2,0},{4,2},{6,4},{1,7},{3,1},{5,3},{7,5},{8,14},{10,8},{12,... | collective-permute-start | bytes 884744 | tf_op jit(solution)/shard_map/ppermute | solution.py:30
  66.1 1.9 %collective-permute-start.7 = (bf16[128,1152]{1,0:T(8,128)(2,1)S(1)}, bf16[128,1152]{1,0:T(8,128)(2,1)}, u32[]{:S(2)}, u32[]{:S(2)}) collective-permute-start(bf16[128,1152]{1,0:T(8,128)(2,1)S(1)} %bitcast.37), channel_id=1, source_target_pairs={{0,2},{2,4},{4,6},{6,0},{1,3},{3,5},{5,7},{7,1},{8,10},{10,12},{12... | collective-permute-start | bytes 884744 | tf_op jit(solution)/shard_map/ppermute | solution.py:30
  68.1 4.2 %collective-permute-start.6 = (bf16[128,1152]{1,0:T(8,128)(2,1)S(1)}, bf16[128,1152]{1,0:T(8,128)(2,1)}, u32[]{:S(2)}, u32[]{:S(2)}) collective-permute-start(bf16[128,1152]{1,0:T(8,128)(2,1)S(1)} %bitcast.36), channel_id=1, source_target_pairs={{0,4},{2,6},{4,0},{6,2},{1,5},{3,7},{5,1},{7,3},{8,12},{10,14},{12... | collective-permute-start | bytes 884744 | tf_op jit(solution)/shard_map/ppermute | solution.py:30
  72.3 0.1 fusion.9
  72.4 10.0 %all-to-all-start.1 = ((bf16[16,32,1152]{2,1,0:T(8,128)(2,1)}), bf16[16,32,1152]{2,1,0:T(8,128)(2,1)}, u32[]{:S(2)}, u32[]{:S(2)}) async-start(bf16[16,32,1152]{2,1,0:T(8,128)(2,1)} %bitcast.16), calls=%async_computation.1 | async-start | bytes 2359296 | tf_op jit(solution)/shard_map/all_to_all | solution.py:34
  82.4 2.0 %collective-permute-done.7 = bf16[128,1152]{1,0:T(8,128)(2,1)} collective-permute-done((bf16[128,1152]{1,0:T(8,128)(2,1)S(1)}, bf16[128,1152]{1,0:T(8,128)(2,1)}, u32[]{:S(2)}, u32[]{:S(2)}) %collective-permute-start.7) | collective-permute-done | bytes 294944 | tf_op jit(solution)/shard_map/ppermute | solution.py:30
  84.4 1.3 fusion.3
  85.7 9.4 %collective-permute-start.11 = (bf16[64,1152]{1,0:T(8,128)(2,1)S(1)}, bf16[64,1152]{1,0:T(8,128)(2,1)S(1)}, u32[]{:S(2)}, u32[]{:S(2)}) collective-permute-start(bf16[64,1152]{1,0:T(8,128)(2,1)S(1)} %get-tuple-element.30), channel_id=1, source_target_pairs={{0,65},{1,64},{64,1},{65,0},{2,67},{3,66},{66,3},{67,2},{4,69},{5,... | collective-permute-start | bytes 442376 | tf_op jit(solution)/shard_map/ppermute | solution.py:25
  95.1 2.6 %collective-permute-start.10 = (bf16[64,1152]{1,0:T(8,128)(2,1)S(1)}, bf16[64,1152]{1,0:T(8,128)(2,1)S(1)}, u32[]{:S(2)}, u32[]{:S(2)}) collective-permute-start(bf16[64,1152]{1,0:T(8,128)(2,1)S(1)} %get-tuple-element.30), channel_id=1, source_target_pairs={{0,64},{64,0},{1,65},{65,1},{2,66},{66,2},{3,67},{67,3},{4,68},{68... | collective-permute-start | bytes 442376 | tf_op jit(solution)/shard_map/ppermute | solution.py:25
  97.7 3.4 %collective-permute-start.9 = (bf16[64,1152]{1,0:T(8,128)(2,1)S(1)}, bf16[64,1152]{1,0:T(8,128)(2,1)S(1)}, u32[]{:S(2)}, u32[]{:S(2)}) collective-permute-start(bf16[64,1152]{1,0:T(8,128)(2,1)S(1)} %get-tuple-element.29), channel_id=1, source_target_pairs={{0,1},{1,0},{2,3},{3,2},{4,5},{5,4},{6,7},{7,6},{8,9},{9,8},{10,11... | collective-permute-start | bytes 442376 | tf_op jit(solution)/shard_map/ppermute | solution.py:25
  101.1 0.1 convert_divide_fusion.1
  101.2 12.4 %collective-permute-done.11 = bf16[64,1152]{1,0:T(8,128)(2,1)S(1)} collective-permute-done((bf16[64,1152]{1,0:T(8,128)(2,1)S(1)}, bf16[64,1152]{1,0:T(8,128)(2,1)S(1)}, u32[]{:S(2)}, u32[]{:S(2)}) %collective-permute-start.11) | collective-permute-done | bytes 147488 | tf_op jit(solution)/shard_map/ppermute | solution.py:25
  113.6 3.1 %collective-permute-done.10 = bf16[64,1152]{1,0:T(8,128)(2,1)S(1)} collective-permute-done((bf16[64,1152]{1,0:T(8,128)(2,1)S(1)}, bf16[64,1152]{1,0:T(8,128)(2,1)S(1)}, u32[]{:S(2)}, u32[]{:S(2)}) %collective-permute-start.10) | collective-permute-done | bytes 147488 | tf_op jit(solution)/shard_map/ppermute | solution.py:25
  116.7 0.1 collective-permute-done.9
  116.8 0.2 multiply_reduce_fusion.1
  117.0 0.1 divide_convert_fusion
  117.2 3.5 %collective-permute-start.12 = (bf16[64,1152]{1,0:T(8,128)(2,1)S(1)}, bf16[64,1152]{1,0:T(8,128)(2,1)S(1)}, u32[]{:S(2)}, u32[]{:S(2)}) collective-permute-start(bf16[64,1152]{1,0:T(8,128)(2,1)S(1)} %divide_convert_fusion), channel_id=1, source_target_pairs={{0,6},{2,0},{4,2},{6,4},{1,7},{3,1},{5,3},{7,5},{8,14},{10,8},{12,... | collective-permute-start | bytes 442376 | tf_op jit(solution)/shard_map/ppermute | solution.py:30
  120.7 3.0 %collective-permute-start.13 = (bf16[64,1152]{1,0:T(8,128)(2,1)S(1)}, bf16[64,1152]{1,0:T(8,128)(2,1)S(1)}, u32[]{:S(2)}, u32[]{:S(2)}) collective-permute-start(bf16[64,1152]{1,0:T(8,128)(2,1)S(1)} %divide_convert_fusion), channel_id=1, source_target_pairs={{0,4},{2,6},{4,0},{6,2},{1,5},{3,7},{5,1},{7,3},{8,12},{10,14},{12... | collective-permute-start | bytes 442376 | tf_op jit(solution)/shard_map/ppermute | solution.py:30
  123.7 2.2 %collective-permute-start.14 = (bf16[64,1152]{1,0:T(8,128)(2,1)S(1)}, bf16[64,1152]{1,0:T(8,128)(2,1)S(1)}, u32[]{:S(2)}, u32[]{:S(2)}) collective-permute-start(bf16[64,1152]{1,0:T(8,128)(2,1)S(1)} %divide_convert_fusion), channel_id=1, source_target_pairs={{0,2},{2,4},{4,6},{6,0},{1,3},{3,5},{5,7},{7,1},{8,10},{10,12},{12... | collective-permute-start | bytes 442376 | tf_op jit(solution)/shard_map/ppermute | solution.py:30
  126.0 4.1 %collective-permute-done.13 = bf16[64,1152]{1,0:T(8,128)(2,1)S(1)} collective-permute-done((bf16[64,1152]{1,0:T(8,128)(2,1)S(1)}, bf16[64,1152]{1,0:T(8,128)(2,1)S(1)}, u32[]{:S(2)}, u32[]{:S(2)}) %collective-permute-start.13) | collective-permute-done | bytes 147488 | tf_op jit(solution)/shard_map/ppermute | solution.py:30
  130.0 2.7 %collective-permute-done.14 = bf16[64,1152]{1,0:T(8,128)(2,1)S(1)} collective-permute-done((bf16[64,1152]{1,0:T(8,128)(2,1)S(1)}, bf16[64,1152]{1,0:T(8,128)(2,1)S(1)}, u32[]{:S(2)}, u32[]{:S(2)}) %collective-permute-start.14) | collective-permute-done | bytes 147488 | tf_op jit(solution)/shard_map/ppermute | solution.py:30
  132.9 0.9 constant_dynamic-slice_fusion
  133.8 2.2 %finish_late.1 = bf16[32,1152]{1,0:T(8,128)(2,1)} custom-call(f32[1]{0:T(128)} %exp.9.scale_ref, bf16[16,32,1152]{2,1,0:T(8,128)(2,1)} %all-to-all-done.1.terms_ref, bf16[32,1152]{1,0:T(8,128)(2,1)} %rows_ref.1), custom_call_target="tpu_custom_call" | custom-call | flops 40000000000 | bytes 100000000 | tf_op jit(solution)/shard_map/finish_late/pallas_call | solution.py:79
  (42 shorter events, 0.5 us)
Async XLA Ops:
  2.9 18.0 %collective-permute-start = (bf16[64,1152]{1,0:T(8,128)(2,1)}, bf16[64,1152]{1,0:T(8,128)(2,1)S(1)}, u32[]{:S(2)}, u32[]{:S(2)}) collective-permute-start(bf16[64,1152]{1,0:T(8,128)(2,1)} %get-tuple-element.13), channel_id=1, source_target_pairs={{0,64},{64,0},{1,65},{65,1},{2,66},{66,2},{3,67},{67,3},{4,68},{68... | collective-permute-start | bytes 442376 | tf_op jit(solution)/shard_map/ppermute | solution.py:25
  6.1 42.5 %all-to-all-start = ((bf16[16,32,1152]{2,1,0:T(8,128)(2,1)}), bf16[16,32,1152]{2,1,0:T(8,128)(2,1)S(1)}, u32[]{:S(2)}, u32[]{:S(2)}) async-start(bf16[16,32,1152]{2,1,0:T(8,128)(2,1)} %get-tuple-element.14), calls=%async_computation | async-start | bytes 2359296 | tf_op jit(solution)/shard_map/all_to_all | solution.py:34
  20.8 16.5 %copy-start.3 = (bf16[256,1152]{1,0:T(8,128)(2,1)S(1)}, bf16[256,1152]{1,0:T(8,128)(2,1)}, u32[]{:S(2)}) copy-start(bf16[256,1152]{1,0:T(8,128)(2,1)} %image_ref.1) | copy-start | bytes 1769476
  20.8 10.3 %collective-permute-start.1 = (bf16[64,1152]{1,0:T(8,128)(2,1)S(1)}, bf16[64,1152]{1,0:T(8,128)(2,1)S(1)}, u32[]{:S(2)}, u32[]{:S(2)}) collective-permute-start(bf16[64,1152]{1,0:T(8,128)(2,1)S(1)} %collective-permute-done), channel_id=1, source_target_pairs={{0,6},{2,0},{4,2},{6,4},{1,7},{3,1},{5,3},{7,5},{8,14},{10,8},{12,... | collective-permute-start | bytes 442376 | tf_op jit(solution)/shard_map/ppermute | solution.py:30
  25.6 9.9 %collective-permute-start.2 = (bf16[64,1152]{1,0:T(8,128)(2,1)S(1)}, bf16[64,1152]{1,0:T(8,128)(2,1)S(1)}, u32[]{:S(2)}, u32[]{:S(2)}) collective-permute-start(bf16[64,1152]{1,0:T(8,128)(2,1)S(1)} %collective-permute-done), channel_id=1, source_target_pairs={{0,4},{2,6},{4,0},{6,2},{1,5},{3,7},{5,1},{7,3},{8,12},{10,14},{12... | collective-permute-start | bytes 442376 | tf_op jit(solution)/shard_map/ppermute | solution.py:30
  28.3 8.9 %collective-permute-start.3 = (bf16[64,1152]{1,0:T(8,128)(2,1)S(1)}, bf16[64,1152]{1,0:T(8,128)(2,1)S(1)}, u32[]{:S(2)}, u32[]{:S(2)}) collective-permute-start(bf16[64,1152]{1,0:T(8,128)(2,1)S(1)} %collective-permute-done), channel_id=1, source_target_pairs={{0,2},{2,4},{4,6},{6,0},{1,3},{3,5},{5,7},{7,1},{8,10},{10,12},{12... | collective-permute-start | bytes 442376 | tf_op jit(solution)/shard_map/ppermute | solution.py:30
  37.9 3.7 %copy-start.6 = (s32[32]{0:T(128)S(1)}, s32[32]{0:T(128)}, u32[]{:S(2)}) copy-start(s32[32]{0:T(128)} %param.7) | copy-start | bytes 388
  38.3 3.4 %copy-start.2 = (bf16[512,1152]{1,0:T(8,128)(2,1)}, bf16[512,1152]{1,0:T(8,128)(2,1)S(1)}, u32[]{:S(2)}) copy-start(bf16[512,1152]{1,0:T(8,128)(2,1)S(1)} %fusion.1) | copy-start | bytes 3538948
  38.3 4.9 %collective-permute-start.4 = (bf16[512,1152]{1,0:T(8,128)(2,1)S(1)}, bf16[512,1152]{1,0:T(8,128)(2,1)}, u32[]{:S(2)}, u32[]{:S(2)}) collective-permute-start(bf16[512,1152]{1,0:T(8,128)(2,1)S(1)} %fusion.1), channel_id=1, source_target_pairs={{0,8},{8,0},{1,9},{9,1},{2,10},{10,2},{3,11},{11,3},{4,12},{12,4},... | collective-permute-start | bytes 3538952 | tf_op jit(solution)/shard_map/ppermute | solution.py:25
  49.4 2.0 %copy-start = (bf16[512,1152]{1,0:T(8,128)(2,1)}, bf16[512,1152]{1,0:T(8,128)(2,1)S(1)}, u32[]{:S(2)}) copy-start(bf16[512,1152]{1,0:T(8,128)(2,1)S(1)} %fusion.2) | copy-start | bytes 3538948
  51.3 3.8 %copy-start.5 = (bf16[1024,512]{1,0:T(8,128)(2,1)}, bf16[1024,512]{1,0:T(8,128)(2,1)S(1)}, u32[]{:S(2)}) copy-start(bf16[1024,512]{1,0:T(8,128)(2,1)S(1)} %subtract_convert_fusion) | copy-start | bytes 3145732
  53.2 5.1 %collective-permute-start.5 = (bf16[512,1152]{1,0:T(8,128)(2,1)}, bf16[512,1152]{1,0:T(8,128)(2,1)}, u32[]{:S(2)}, u32[]{:S(2)}) collective-permute-start(bf16[512,1152]{1,0:T(8,128)(2,1)} %convolution_convert_fusion), channel_id=1, source_target_pairs={{0,8},{8,0},{1,9},{9,1},{2,10},{10,2},{3,11},{11,3},{4,12},{12,4},... | collective-permute-start | bytes 3538952 | tf_op jit(solution)/shard_map/ppermute | solution.py:25
  55.2 3.1 %copy-start.1 = (bf16[512,1152]{1,0:T(8,128)(2,1)S(1)}, bf16[512,1152]{1,0:T(8,128)(2,1)}, u32[]{:S(2)}) copy-start(bf16[512,1152]{1,0:T(8,128)(2,1)} %copy-done) | copy-start | bytes 3538948
  60.6 11.7 %copy-start.4 = (bf16[256,1152]{1,0:T(8,128)(2,1)S(1)}, bf16[256,1152]{1,0:T(8,128)(2,1)}, u32[]{:S(2)}) copy-start(bf16[256,1152]{1,0:T(8,128)(2,1)} %image_ref.1) | copy-start | bytes 1769476
  61.5 21.0 %collective-permute-start.8 = (bf16[128,1152]{1,0:T(8,128)(2,1)}, bf16[128,1152]{1,0:T(8,128)(2,1)}, u32[]{:S(2)}, u32[]{:S(2)}) collective-permute-start(bf16[128,1152]{1,0:T(8,128)(2,1)} %bitcast.10), channel_id=1, source_target_pairs={{0,6},{2,0},{4,2},{6,4},{1,7},{3,1},{5,3},{7,5},{8,14},{10,8},{12,... | collective-permute-start | bytes 884744 | tf_op jit(solution)/shard_map/ppermute | solution.py:30
  66.1 18.3 %collective-permute-start.7 = (bf16[128,1152]{1,0:T(8,128)(2,1)S(1)}, bf16[128,1152]{1,0:T(8,128)(2,1)}, u32[]{:S(2)}, u32[]{:S(2)}) collective-permute-start(bf16[128,1152]{1,0:T(8,128)(2,1)S(1)} %bitcast.37), channel_id=1, source_target_pairs={{0,2},{2,4},{4,6},{6,0},{1,3},{3,5},{5,7},{7,1},{8,10},{10,12},{12... | collective-permute-start | bytes 884744 | tf_op jit(solution)/shard_map/ppermute | solution.py:30
  68.1 16.4 %collective-permute-start.6 = (bf16[128,1152]{1,0:T(8,128)(2,1)S(1)}, bf16[128,1152]{1,0:T(8,128)(2,1)}, u32[]{:S(2)}, u32[]{:S(2)}) collective-permute-start(bf16[128,1152]{1,0:T(8,128)(2,1)S(1)} %bitcast.36), channel_id=1, source_target_pairs={{0,4},{2,6},{4,0},{6,2},{1,5},{3,7},{5,1},{7,3},{8,12},{10,14},{12... | collective-permute-start | bytes 884744 | tf_op jit(solution)/shard_map/ppermute | solution.py:30
  72.4 60.3 %all-to-all-start.1 = ((bf16[16,32,1152]{2,1,0:T(8,128)(2,1)}), bf16[16,32,1152]{2,1,0:T(8,128)(2,1)}, u32[]{:S(2)}, u32[]{:S(2)}) async-start(bf16[16,32,1152]{2,1,0:T(8,128)(2,1)} %bitcast.16), calls=%async_computation.1 | async-start | bytes 2359296 | tf_op jit(solution)/shard_map/all_to_all | solution.py:34
  85.7 27.8 %collective-permute-start.11 = (bf16[64,1152]{1,0:T(8,128)(2,1)S(1)}, bf16[64,1152]{1,0:T(8,128)(2,1)S(1)}, u32[]{:S(2)}, u32[]{:S(2)}) collective-permute-start(bf16[64,1152]{1,0:T(8,128)(2,1)S(1)} %get-tuple-element.30), channel_id=1, source_target_pairs={{0,65},{1,64},{64,1},{65,0},{2,67},{3,66},{66,3},{67,2},{4,69},{5,... | collective-permute-start | bytes 442376 | tf_op jit(solution)/shard_map/ppermute | solution.py:25
  95.1 21.6 %collective-permute-start.10 = (bf16[64,1152]{1,0:T(8,128)(2,1)S(1)}, bf16[64,1152]{1,0:T(8,128)(2,1)S(1)}, u32[]{:S(2)}, u32[]{:S(2)}) collective-permute-start(bf16[64,1152]{1,0:T(8,128)(2,1)S(1)} %get-tuple-element.30), channel_id=1, source_target_pairs={{0,64},{64,0},{1,65},{65,1},{2,66},{66,2},{3,67},{67,3},{4,68},{68... | collective-permute-start | bytes 442376 | tf_op jit(solution)/shard_map/ppermute | solution.py:25
  97.7 19.1 %collective-permute-start.9 = (bf16[64,1152]{1,0:T(8,128)(2,1)S(1)}, bf16[64,1152]{1,0:T(8,128)(2,1)S(1)}, u32[]{:S(2)}, u32[]{:S(2)}) collective-permute-start(bf16[64,1152]{1,0:T(8,128)(2,1)S(1)} %get-tuple-element.29), channel_id=1, source_target_pairs={{0,1},{1,0},{2,3},{3,2},{4,5},{5,4},{6,7},{7,6},{8,9},{9,8},{10,11... | collective-permute-start | bytes 442376 | tf_op jit(solution)/shard_map/ppermute | solution.py:25
  117.2 8.8 %collective-permute-start.12 = (bf16[64,1152]{1,0:T(8,128)(2,1)S(1)}, bf16[64,1152]{1,0:T(8,128)(2,1)S(1)}, u32[]{:S(2)}, u32[]{:S(2)}) collective-permute-start(bf16[64,1152]{1,0:T(8,128)(2,1)S(1)} %divide_convert_fusion), channel_id=1, source_target_pairs={{0,6},{2,0},{4,2},{6,4},{1,7},{3,1},{5,3},{7,5},{8,14},{10,8},{12,... | collective-permute-start | bytes 442376 | tf_op jit(solution)/shard_map/ppermute | solution.py:30
  120.7 9.3 %collective-permute-start.13 = (bf16[64,1152]{1,0:T(8,128)(2,1)S(1)}, bf16[64,1152]{1,0:T(8,128)(2,1)S(1)}, u32[]{:S(2)}, u32[]{:S(2)}) collective-permute-start(bf16[64,1152]{1,0:T(8,128)(2,1)S(1)} %divide_convert_fusion), channel_id=1, source_target_pairs={{0,4},{2,6},{4,0},{6,2},{1,5},{3,7},{5,1},{7,3},{8,12},{10,14},{12... | collective-permute-start | bytes 442376 | tf_op jit(solution)/shard_map/ppermute | solution.py:30
  123.7 9.0 %collective-permute-start.14 = (bf16[64,1152]{1,0:T(8,128)(2,1)S(1)}, bf16[64,1152]{1,0:T(8,128)(2,1)S(1)}, u32[]{:S(2)}, u32[]{:S(2)}) collective-permute-start(bf16[64,1152]{1,0:T(8,128)(2,1)S(1)} %divide_convert_fusion), channel_id=1, source_target_pairs={{0,2},{2,4},{4,6},{6,0},{1,3},{3,5},{5,7},{7,1},{8,10},{10,12},{12... | collective-permute-start | bytes 442376 | tf_op jit(solution)/shard_map/ppermute | solution.py:30

commit v14 on v12

--- a/solution.py
+++ b/solution.py
@@ -43,25 +43,22 @@
 def first_copies(x, image_emb, text_emb, quarter, peers):
     mine, width = text_emb.shape
 
-    def body(x_ref, image_ref, text_ref, quarter_ref, copies_ref, sems):
+    def body(x_ref, image_ref, text_ref, quarter_ref, copies_ref):
         start = pl.multiple_of(x_ref[0] * quarter, quarter)
-        copies = [pltpu.make_async_copy(image_ref.at[pl.ds(start, quarter)], quarter_ref, sems.at[peers])]
-        copies += [pltpu.make_async_copy(text_ref, copies_ref.at[k], sems.at[k]) for k in range(peers)]
-        for copy in copies:
-            copy.start()
-        for copy in copies:
-            copy.wait()
+        quarter_ref[...] = image_ref[pl.ds(start, quarter), :]
+        text_bf = unit_rows(text_ref[...])[0].astype(BF16)
+        for k in range(peers):
+            copies_ref[k] = text_bf
 
-    anywhere, whole = pl.BlockSpec(memory_space=pl.ANY), pl.BlockSpec(memory_space=pltpu.VMEM)
+    whole = pl.BlockSpec(memory_space=pltpu.VMEM)
     return pl.pallas_call(
         body,
         out_shape=(
             jax.ShapeDtypeStruct((quarter, width), BF16),
             jax.ShapeDtypeStruct((peers, mine, width), BF16),
         ),
-        in_specs=[pl.BlockSpec(memory_space=pltpu.SMEM), anywhere, whole],
-        out_specs=(whole, anywhere),
-        scratch_shapes=[pltpu.SemaphoreType.DMA((peers + 1,))],
+        in_specs=[pl.BlockSpec(memory_space=pltpu.SMEM), whole, whole],
+        out_specs=(whole, whole),
         name="first_copies",
     )(x, image_emb, text_emb)
 
@@ -84,17 +81,16 @@
 
     part, copies = first_copies(x.astype(jnp.int32).reshape(1), image_emb, text_emb, quarter, peers)
     part = swap(part, "yl")
-    texts = exchange(copies, RINGS, TEXT_GROUPS).reshape(-1, width)
+    text_bf = exchange(copies, RINGS, TEXT_GROUPS).reshape(-1, width)
     around = [part] + [shift(part, "x", n_x - d) for d in range(1, n_x)]
     beyond = in_order(around, x)
     chip = jnp.concatenate([jnp.where(upper, beyond, image_emb), jnp.where(upper, image_emb, beyond)], axis=0)
     near = unit_rows(chip)[0].astype(BF16)
     far = swap(near, "c")
-    text_bf = unit_rows(texts)[0].astype(BF16)
 
     wanted = positive - lax.axis_index(("yh", "yl", "w", "c")) * rows + lax.axis_index("yl") * rows
     slot = lax.axis_index(("yh", "w")) * mine
-    wanted = lax.dynamic_update_slice_in_dim(jnp.full((texts.shape[0],), -1, jnp.int32), wanted, slot, 0)
+    wanted = lax.dynamic_update_slice_in_dim(jnp.full((text_bf.shape[0],), -1, jnp.int32), wanted, slot, 0)
     hit = (jnp.arange(2 * near.shape[0], dtype=jnp.int32)[:, None] == wanted[None, :]).astype(F32)
 
     image_unit, image_norm = unit_rows(lax.dynamic_slice_in_dim(image_emb, x * quarter, quarter, 0))
@@ -114,14 +110,14 @@
     far_terms = jnp.dot(grad[half:], text_bf, preferred_element_type=F32).astype(BF16)
     far_terms = swap(far_terms, "c").astype(F32)
     both = jnp.dot(grad[:half], text_bf, preferred_element_type=F32) + far_terms
-    both = both.reshape(2, n_x, quarter, width)
+    both = both.astype(BF16).reshape(2, n_x, quarter, width)
 
     def of_position(k):
         return lax.dynamic_index_in_dim(both, lax.rem(x + k, n_x), axis=1, keepdims=False)
 
-    total = of_position(0)
+    total = of_position(0).astype(F32)
     for d in (2, 1, 3):
-        sent = of_position(d).astype(BF16).reshape(2 * quarter, width)
+        sent = of_position(d).reshape(2 * quarter, width)
         total = total + shift(sent, "x", d).astype(F32).reshape(2, quarter, width)
     total = total.astype(BF16)
     own, other = jnp.where(upper, total[1], total[0]), jnp.where(upper, total[0], total[1])

time: 128 us -> 129 us (level)
  matrix products: 8.69 us -> 11.5 us
    dot_general x1, matrix products: 1.88 us -> 3.2 us  [local(): jnp.dot(grad[half:], text_bf, preferred_element_type=F32).astype(BF16)]
where the time goes in v14:
time: 129 us
  starting transfers between devices  67.9 us (53%)
  waiting for transfers between devices  38.2 us (30%)
  matrix products  11.5 us (9%)
  other arithmetic  4.49 us (3%)
  between operations  2.39 us (2%)
  Pallas kernels  2.28 us (2%)
  local copies, waits for them, and re-layouts  1.93 us (1%)
    all_to_all x3, starting transfers between devices, exchange(): lax.all_to_all(blocks, axes, 0, 0, axis_index_groups=groups, tiled=True)  25.4 us
    ppermute x6, starting transfers between devices, swap(): return lax.ppermute(block, axes, [(i, count - 1 - i) for i in range(count)])  21.8 us
    ppermute x6, starting transfers between devices, shift(): lax.ppermute(block, axis, [(i, (i + distance) % count) for i in range(cou...  20.6 us
    all_to_all x3, waiting for transfers between devices, exchange(): lax.all_to_all(blocks, axes, 0, 0, axis_index_groups=groups, tiled=True)  14.6 us
    ppermute x6, waiting for transfers between devices, shift(): lax.ppermute(block, axis, [(i, (i + distance) % count) for i in range(cou...  14.1 us
    ppermute x6, waiting for transfers between devices, swap(): return lax.ppermute(block, axes, [(i, count - 1 - i) for i in range(count)])  9.43 us
    dot_general x1, matrix products, local(): lax.dot_general(images, text_bf, (((1,), (1,)), ((), ())), preferred_elem...  3.21 us
    dot_general x1, matrix products, local(): jnp.dot(grad[half:], text_bf, preferred_element_type=F32).astype(BF16)  3.2 us
  transfers between devices with their start and end apart: 15, of which 9 were waited for; matrix products, arithmetic and copies ran while one was open for 5% of the time, Pallas kernels for 0%

profile of v14, /device:TPU:1, one launch (start us, length us, event | category | flops | bytes accessed | tf_op | source)
XLA Modules:
  0.0 128.6 jit_solution(11670825785731990398)
XLA Ops:
  0.6 2.3 %first_copies.1 = (bf16[64,1152]{1,0:T(8,128)(2,1)}, bf16[16,32,1152]{2,1,0:T(8,128)(2,1)}) custom-call(s32[1]{0:T(128)} %bitcast.1.x_ref, bf16[256,1152]{1,0:T(8,128)(2,1)} %image_ref.1, bf16[32,1152]{1,0:T(8,128)(2,1)} %text_ref.1), custom_call_target="tpu_custom_call" | custom-call | tf_op jit(solution)/shard_map/first_copies/pallas_call | solution.py:54
  2.9 4.0 %collective-permute-start = (bf16[64,1152]{1,0:T(8,128)(2,1)}, bf16[64,1152]{1,0:T(8,128)(2,1)S(1)}, u32[]{:S(2)}, u32[]{:S(2)}) collective-permute-start(bf16[64,1152]{1,0:T(8,128)(2,1)} %get-tuple-element.12), channel_id=1, source_target_pairs={{0,64},{64,0},{1,65},{65,1},{2,66},{66,2},{3,67},{67,3},{4,68},{68... | collective-permute-start | bytes 442376 | tf_op jit(solution)/shard_map/ppermute | solution.py:25
  6.9 14.4 %all-to-all-start = ((bf16[16,32,1152]{2,1,0:T(8,128)(2,1)}), bf16[16,32,1152]{2,1,0:T(8,128)(2,1)}, u32[]{:S(2)}, u32[]{:S(2)}) async-start(bf16[16,32,1152]{2,1,0:T(8,128)(2,1)} %get-tuple-element.13), calls=%async_computation | async-start | bytes 2359296 | tf_op jit(solution)/shard_map/all_to_all | solution.py:34
  21.4 4.5 %collective-permute-start.1 = (bf16[64,1152]{1,0:T(8,128)(2,1)S(1)}, bf16[64,1152]{1,0:T(8,128)(2,1)S(1)}, u32[]{:S(2)}, u32[]{:S(2)}) collective-permute-start(bf16[64,1152]{1,0:T(8,128)(2,1)S(1)} %collective-permute-done), channel_id=1, source_target_pairs={{0,6},{2,0},{4,2},{6,4},{1,7},{3,1},{5,3},{7,5},{8,14},{10,8},{12,... | collective-permute-start | bytes 442376 | tf_op jit(solution)/shard_map/ppermute | solution.py:30
  25.9 2.4 %collective-permute-start.2 = (bf16[64,1152]{1,0:T(8,128)(2,1)S(1)}, bf16[64,1152]{1,0:T(8,128)(2,1)S(1)}, u32[]{:S(2)}, u32[]{:S(2)}) collective-permute-start(bf16[64,1152]{1,0:T(8,128)(2,1)S(1)} %collective-permute-done), channel_id=1, source_target_pairs={{0,4},{2,6},{4,0},{6,2},{1,5},{3,7},{5,1},{7,3},{8,12},{10,14},{12... | collective-permute-start | bytes 442376 | tf_op jit(solution)/shard_map/ppermute | solution.py:30
  28.4 2.5 %collective-permute-start.3 = (bf16[64,1152]{1,0:T(8,128)(2,1)S(1)}, bf16[64,1152]{1,0:T(8,128)(2,1)S(1)}, u32[]{:S(2)}, u32[]{:S(2)}) collective-permute-start(bf16[64,1152]{1,0:T(8,128)(2,1)S(1)} %collective-permute-done), channel_id=1, source_target_pairs={{0,2},{2,4},{4,6},{6,0},{1,3},{3,5},{5,7},{7,1},{8,10},{10,12},{12... | collective-permute-start | bytes 442376 | tf_op jit(solution)/shard_map/ppermute | solution.py:30
  31.0 2.8 %collective-permute-done.2 = bf16[64,1152]{1,0:T(8,128)(2,1)S(1)} collective-permute-done((bf16[64,1152]{1,0:T(8,128)(2,1)S(1)}, bf16[64,1152]{1,0:T(8,128)(2,1)S(1)}, u32[]{:S(2)}, u32[]{:S(2)}) %collective-permute-start.2) | collective-permute-done | bytes 147488 | tf_op jit(solution)/shard_map/ppermute | solution.py:30
  33.8 4.0 %collective-permute-done.3 = bf16[64,1152]{1,0:T(8,128)(2,1)S(1)} collective-permute-done((bf16[64,1152]{1,0:T(8,128)(2,1)S(1)}, bf16[64,1152]{1,0:T(8,128)(2,1)S(1)}, u32[]{:S(2)}, u32[]{:S(2)}) %collective-permute-start.3) | collective-permute-done | bytes 147488 | tf_op jit(solution)/shard_map/ppermute | solution.py:30
  37.9 0.2 broadcast_select_fusion.1
  38.1 0.3 fusion
  38.5 0.4 fusion.1
  38.8 3.4 %collective-permute-start.4 = (bf16[512,1152]{1,0:T(8,128)(2,1)S(1)}, bf16[512,1152]{1,0:T(8,128)(2,1)}, u32[]{:S(2)}, u32[]{:S(2)}) collective-permute-start(bf16[512,1152]{1,0:T(8,128)(2,1)S(1)} %fusion.1), channel_id=1, source_target_pairs={{0,8},{8,0},{1,9},{9,1},{2,10},{10,2},{3,11},{11,3},{4,12},{12,4},... | collective-permute-start | bytes 3538952 | tf_op jit(solution)/shard_map/ppermute | solution.py:25
  43.6 0.1 add_dynamic-update-slice_fusion
  43.7 1.1 collective-permute-done.4
  44.8 1.5 %pad_maximum_fusion = bf16[1024,1152]{1,0:T(8,128)(2,1)S(1)} fusion(bf16[512,1152]{1,0:T(8,128)(2,1)} %collective-permute-done.4, bf16[512,1152]{1,0:T(8,128)(2,1)S(1)} %fusion.1), kind=kLoop, calls=%fused_computation.6 | loop fusion | flops 4718592 | bytes 4718592 | tf_op jit(solution)/shard_map/concatenate | solution.py:102
  46.3 6.0 %all-to-all-done = bf16[16,32,1152]{2,1,0:T(8,128)(2,1)} async-done(((bf16[16,32,1152]{2,1,0:T(8,128)(2,1)}), bf16[16,32,1152]{2,1,0:T(8,128)(2,1)}, u32[]{:S(2)}, u32[]{:S(2)}) %all-to-all-start) | async-done | bytes 1179680 | tf_op jit(solution)/shard_map/all_to_all | solution.py:34
  52.3 3.2 %subtract_convert_fusion = bf16[1024,512]{1,0:T(8,128)(2,1)S(1)} fusion(bf16[1024,1152]{1,0:T(8,128)(2,1)S(1)} %pad_maximum_fusion, bf16[512,1152]{1,0:T(8,128)(2,1)} %bitcast.2, s32[512]{0:T(512)S(1)} %add_dynamic-update-slice_fusion, f32[]{:T(128)} %bitcast.37, f32[]{:T(128)} %bitcast), kind=kOutput, calls=%fused_computation.9 | convolution fusion | flops 1212678144 | bytes 4589576 | tf_op jit(solution)/shard_map/dot_general | solution.py:103
  55.5 2.6 %convolution_convert_fusion.1 = bf16[512,1152]{1,0:T(8,128)(2,1)} fusion(bf16[1024,512]{1,0:T(8,128)(2,1)S(1)} %subtract_convert_fusion, bf16[1024,1152]{1,0:T(8,128)(2,1)S(1)} %pad_maximum_fusion), kind=kOutput, calls=%fused_computation.1 | convolution fusion | flops 1208549376 | bytes 4587520 | tf_op jit(solution)/shard_map/dot_general | solution.py:105
  58.1 3.2 %convolution_convert_fusion = bf16[512,1152]{1,0:T(8,128)(2,1)} fusion(bf16[512,1152]{1,0:T(8,128)(2,1)} %bitcast.2, bf16[1024,512]{1,0:T(8,128)(2,1)S(1)} %subtract_convert_fusion), kind=kOutput, calls=%fused_computation | convolution fusion | flops 604569600 | bytes 2883584 | tf_op jit(solution)/shard_map/dot_general | solution.py:110
  61.3 6.0 %collective-permute-start.5 = (bf16[512,1152]{1,0:T(8,128)(2,1)}, bf16[512,1152]{1,0:T(8,128)(2,1)}, u32[]{:S(2)}, u32[]{:S(2)}) collective-permute-start(bf16[512,1152]{1,0:T(8,128)(2,1)} %convolution_convert_fusion), channel_id=1, source_target_pairs={{0,8},{8,0},{1,9},{9,1},{2,10},{10,2},{3,11},{11,3},{4,12},{12,4},... | collective-permute-start | bytes 3538952 | tf_op jit(solution)/shard_map/ppermute | solution.py:25
  67.4 0.1 fusion.8
  67.5 0.1 convert_divide_fusion.1
  67.6 7.0 %all-to-all-start.1 = ((bf16[16,32,1152]{2,1,0:T(8,128)(2,1)}), bf16[16,32,1152]{2,1,0:T(8,128)(2,1)S(1)}, u32[]{:S(2)}, u32[]{:S(2)}) async-start(bf16[16,32,1152]{2,1,0:T(8,128)(2,1)} %bitcast.14), calls=%async_computation.1 | async-start | bytes 2359296 | tf_op jit(solution)/shard_map/all_to_all | solution.py:34
  74.7 2.5 %add_convert_fusion = bf16[512,1152]{1,0:T(8,128)(2,1)S(1)} fusion(bf16[512,1152]{1,0:T(8,128)(2,1)} %collective-permute-done.5, bf16[512,1152]{1,0:T(8,128)(2,1)} %bitcast.2, bf16[1024,512]{1,0:T(8,128)(2,1)S(1)} %copy-done.3), kind=kOutput, calls=%fused_computation.8 | convolution fusion | flops 605749248 | bytes 4063232 | tf_op jit(solution)/shard_map/dot_general | solution.py:112
  77.1 0.1 constant_dynamic-slice_fusion.2
  77.2 4.6 %collective-permute-start.6 = (bf16[128,1152]{1,0:T(8,128)(2,1)S(1)}, bf16[128,1152]{1,0:T(8,128)(2,1)S(1)}, u32[]{:S(2)}, u32[]{:S(2)}) collective-permute-start(bf16[128,1152]{1,0:T(8,128)(2,1)S(1)} %bitcast.43), channel_id=1, source_target_pairs={{0,4},{2,6},{4,0},{6,2},{1,5},{3,7},{5,1},{7,3},{8,12},{10,14},{12... | collective-permute-start | bytes 884744 | tf_op jit(solution)/shard_map/ppermute | solution.py:30
  81.9 2.2 %collective-permute-start.7 = (bf16[128,1152]{1,0:T(8,128)(2,1)S(1)}, bf16[128,1152]{1,0:T(8,128)(2,1)S(1)}, u32[]{:S(2)}, u32[]{:S(2)}) collective-permute-start(bf16[128,1152]{1,0:T(8,128)(2,1)S(1)} %bitcast.42), channel_id=1, source_target_pairs={{0,2},{2,4},{4,6},{6,0},{1,3},{3,5},{5,7},{7,1},{8,10},{10,12},{12... | collective-permute-start | bytes 884744 | tf_op jit(solution)/shard_map/ppermute | solution.py:30
  84.1 4.3 %collective-permute-start.8 = (bf16[128,1152]{1,0:T(8,128)(2,1)S(1)}, bf16[128,1152]{1,0:T(8,128)(2,1)S(1)}, u32[]{:S(2)}, u32[]{:S(2)}) collective-permute-start(bf16[128,1152]{1,0:T(8,128)(2,1)S(1)} %bitcast.41), channel_id=1, source_target_pairs={{0,6},{2,0},{4,2},{6,4},{1,7},{3,1},{5,3},{7,5},{8,14},{10,8},{12,... | collective-permute-start | bytes 884744 | tf_op jit(solution)/shard_map/ppermute | solution.py:30
  88.4 0.1 fusion.9
  88.5 0.4 collective-permute-done.6
  88.9 6.9 %collective-permute-done.7 = bf16[128,1152]{1,0:T(8,128)(2,1)S(1)} collective-permute-done((bf16[128,1152]{1,0:T(8,128)(2,1)S(1)}, bf16[128,1152]{1,0:T(8,128)(2,1)S(1)}, u32[]{:S(2)}, u32[]{:S(2)}) %collective-permute-start.7) | collective-permute-done | bytes 294944 | tf_op jit(solution)/shard_map/ppermute | solution.py:30
  95.9 0.2 fusion.2
  96.1 1.9 %collective-permute-start.10 = (bf16[64,1152]{1,0:T(8,128)(2,1)S(1)}, bf16[64,1152]{1,0:T(8,128)(2,1)S(1)}, u32[]{:S(2)}, u32[]{:S(2)}) collective-permute-start(bf16[64,1152]{1,0:T(8,128)(2,1)S(1)} %get-tuple-element.28), channel_id=1, source_target_pairs={{0,64},{64,0},{1,65},{65,1},{2,66},{66,2},{3,67},{67,3},{4,68},{68... | collective-permute-start | bytes 442376 | tf_op jit(solution)/shard_map/ppermute | solution.py:25
  98.0 2.7 %collective-permute-start.11 = (bf16[64,1152]{1,0:T(8,128)(2,1)S(1)}, bf16[64,1152]{1,0:T(8,128)(2,1)S(1)}, u32[]{:S(2)}, u32[]{:S(2)}) collective-permute-start(bf16[64,1152]{1,0:T(8,128)(2,1)S(1)} %get-tuple-element.28), channel_id=1, source_target_pairs={{0,65},{1,64},{64,1},{65,0},{2,67},{3,66},{66,3},{67,2},{4,69},{5,... | collective-permute-start | bytes 442376 | tf_op jit(solution)/shard_map/ppermute | solution.py:25
  100.8 3.7 %collective-permute-start.9 = (bf16[64,1152]{1,0:T(8,128)(2,1)S(1)}, bf16[64,1152]{1,0:T(8,128)(2,1)S(1)}, u32[]{:S(2)}, u32[]{:S(2)}) collective-permute-start(bf16[64,1152]{1,0:T(8,128)(2,1)S(1)} %get-tuple-element.27), channel_id=1, source_target_pairs={{0,1},{1,0},{2,3},{3,2},{4,5},{5,4},{6,7},{7,6},{8,9},{9,8},{10,11... | collective-permute-start | bytes 442376 | tf_op jit(solution)/shard_map/ppermute | solution.py:25
  104.5 0.1 convert_divide_fusion.2
  104.6 4.0 %collective-permute-done.11 = bf16[64,1152]{1,0:T(8,128)(2,1)S(1)} collective-permute-done((bf16[64,1152]{1,0:T(8,128)(2,1)S(1)}, bf16[64,1152]{1,0:T(8,128)(2,1)S(1)}, u32[]{:S(2)}, u32[]{:S(2)}) %collective-permute-start.11) | collective-permute-done | bytes 147488 | tf_op jit(solution)/shard_map/ppermute | solution.py:25
  108.6 4.3 %collective-permute-done.9 = bf16[64,1152]{1,0:T(8,128)(2,1)S(1)} collective-permute-done((bf16[64,1152]{1,0:T(8,128)(2,1)S(1)}, bf16[64,1152]{1,0:T(8,128)(2,1)S(1)}, u32[]{:S(2)}, u32[]{:S(2)}) %collective-permute-start.9) | collective-permute-done | bytes 147488 | tf_op jit(solution)/shard_map/ppermute | solution.py:25
  112.9 0.1 add_add_fusion
  113.0 0.2 convert_reduce_fusion
  113.2 0.1 multiply_reduce_fusion
  113.3 0.1 divide_convert_fusion
  113.4 0.9 broadcast_in_dim.2
  114.3 4.0 %all-to-all-start.2 = ((bf16[4,64,1152]{2,1,0:T(8,128)(2,1)}), bf16[4,64,1152]{2,1,0:T(8,128)(2,1)S(1)}, u32[]{:S(2)}, u32[]{:S(2)}) async-start(bf16[4,64,1152]{2,1,0:T(8,128)(2,1)} %broadcast_in_dim.2), calls=%async_computation.2 | async-start | bytes 1179648 | tf_op jit(solution)/shard_map/all_to_all | solution.py:34
  118.3 0.1 multiply_reduce_fusion.1
  118.4 0.7 divide_convert_fusion.1
  119.2 8.6 %all-to-all-done.2 = bf16[4,64,1152]{2,1,0:T(8,128)(2,1)S(1)} async-done(((bf16[4,64,1152]{2,1,0:T(8,128)(2,1)}), bf16[4,64,1152]{2,1,0:T(8,128)(2,1)S(1)}, u32[]{:S(2)}, u32[]{:S(2)}) %all-to-all-start.2) | async-done | bytes 589856 | tf_op jit(solution)/shard_map/all_to_all | solution.py:34
  127.8 0.8 copy.20
  (31 shorter events, 0.3 us)
Async XLA Ops:
  2.9 18.5 %collective-permute-start = (bf16[64,1152]{1,0:T(8,128)(2,1)}, bf16[64,1152]{1,0:T(8,128)(2,1)S(1)}, u32[]{:S(2)}, u32[]{:S(2)}) collective-permute-start(bf16[64,1152]{1,0:T(8,128)(2,1)} %get-tuple-element.12), channel_id=1, source_target_pairs={{0,64},{64,0},{1,65},{65,1},{2,66},{66,2},{3,67},{67,3},{4,68},{68... | collective-permute-start | bytes 442376 | tf_op jit(solution)/shard_map/ppermute | solution.py:25
  6.9 45.4 %all-to-all-start = ((bf16[16,32,1152]{2,1,0:T(8,128)(2,1)}), bf16[16,32,1152]{2,1,0:T(8,128)(2,1)}, u32[]{:S(2)}, u32[]{:S(2)}) async-start(bf16[16,32,1152]{2,1,0:T(8,128)(2,1)} %get-tuple-element.13), calls=%async_computation | async-start | bytes 2359296 | tf_op jit(solution)/shard_map/all_to_all | solution.py:34
  21.4 16.5 %copy-start = (bf16[256,1152]{1,0:T(8,128)(2,1)S(1)}, bf16[256,1152]{1,0:T(8,128)(2,1)}, u32[]{:S(2)}) copy-start(bf16[256,1152]{1,0:T(8,128)(2,1)} %image_ref.1) | copy-start | bytes 1769476
  21.4 9.5 %collective-permute-start.1 = (bf16[64,1152]{1,0:T(8,128)(2,1)S(1)}, bf16[64,1152]{1,0:T(8,128)(2,1)S(1)}, u32[]{:S(2)}, u32[]{:S(2)}) collective-permute-start(bf16[64,1152]{1,0:T(8,128)(2,1)S(1)} %collective-permute-done), channel_id=1, source_target_pairs={{0,6},{2,0},{4,2},{6,4},{1,7},{3,1},{5,3},{7,5},{8,14},{10,8},{12,... | collective-permute-start | bytes 442376 | tf_op jit(solution)/shard_map/ppermute | solution.py:30
  25.9 7.8 %collective-permute-start.2 = (bf16[64,1152]{1,0:T(8,128)(2,1)S(1)}, bf16[64,1152]{1,0:T(8,128)(2,1)S(1)}, u32[]{:S(2)}, u32[]{:S(2)}) collective-permute-start(bf16[64,1152]{1,0:T(8,128)(2,1)S(1)} %collective-permute-done), channel_id=1, source_target_pairs={{0,4},{2,6},{4,0},{6,2},{1,5},{3,7},{5,1},{7,3},{8,12},{10,14},{12... | collective-permute-start | bytes 442376 | tf_op jit(solution)/shard_map/ppermute | solution.py:30
  28.4 9.4 %collective-permute-start.3 = (bf16[64,1152]{1,0:T(8,128)(2,1)S(1)}, bf16[64,1152]{1,0:T(8,128)(2,1)S(1)}, u32[]{:S(2)}, u32[]{:S(2)}) collective-permute-start(bf16[64,1152]{1,0:T(8,128)(2,1)S(1)} %collective-permute-done), channel_id=1, source_target_pairs={{0,2},{2,4},{4,6},{6,0},{1,3},{3,5},{5,7},{7,1},{8,10},{10,12},{12... | collective-permute-start | bytes 442376 | tf_op jit(solution)/shard_map/ppermute | solution.py:30
  38.5 5.1 %copy-start.5 = (s32[32]{0:T(128)S(1)}, s32[32]{0:T(128)}, u32[]{:S(2)}) copy-start(s32[32]{0:T(128)} %param.7) | copy-start | bytes 388
  38.8 6.0 %collective-permute-start.4 = (bf16[512,1152]{1,0:T(8,128)(2,1)S(1)}, bf16[512,1152]{1,0:T(8,128)(2,1)}, u32[]{:S(2)}, u32[]{:S(2)}) collective-permute-start(bf16[512,1152]{1,0:T(8,128)(2,1)S(1)} %fusion.1), channel_id=1, source_target_pairs={{0,8},{8,0},{1,9},{9,1},{2,10},{10,2},{3,11},{11,3},{4,12},{12,4},... | collective-permute-start | bytes 3538952 | tf_op jit(solution)/shard_map/ppermute | solution.py:25
  55.5 2.6 %copy-start.2 = (bf16[1024,512]{1,0:T(8,128)(2,1)}, bf16[1024,512]{1,0:T(8,128)(2,1)S(1)}, u32[]{:S(2)}) copy-start(bf16[1024,512]{1,0:T(8,128)(2,1)S(1)} %subtract_convert_fusion) | copy-start | bytes 3145732
  58.1 9.3 %copy-start.1 = (bf16[256,1152]{1,0:T(8,128)(2,1)S(1)}, bf16[256,1152]{1,0:T(8,128)(2,1)}, u32[]{:S(2)}) copy-start(bf16[256,1152]{1,0:T(8,128)(2,1)} %image_ref.1) | copy-start | bytes 1769476
  61.3 13.3 %collective-permute-start.5 = (bf16[512,1152]{1,0:T(8,128)(2,1)}, bf16[512,1152]{1,0:T(8,128)(2,1)}, u32[]{:S(2)}, u32[]{:S(2)}) collective-permute-start(bf16[512,1152]{1,0:T(8,128)(2,1)} %convolution_convert_fusion), channel_id=1, source_target_pairs={{0,8},{8,0},{1,9},{9,1},{2,10},{10,2},{3,11},{11,3},{4,12},{12,4},... | collective-permute-start | bytes 3538952 | tf_op jit(solution)/shard_map/ppermute | solution.py:25
  67.6 7.0 %copy-start.3 = (bf16[1024,512]{1,0:T(8,128)(2,1)S(1)}, bf16[1024,512]{1,0:T(8,128)(2,1)}, u32[]{:S(2)}) copy-start(bf16[1024,512]{1,0:T(8,128)(2,1)} %copy-done.2) | copy-start | bytes 3145732
  67.6 45.3 %all-to-all-start.1 = ((bf16[16,32,1152]{2,1,0:T(8,128)(2,1)}), bf16[16,32,1152]{2,1,0:T(8,128)(2,1)S(1)}, u32[]{:S(2)}, u32[]{:S(2)}) async-start(bf16[16,32,1152]{2,1,0:T(8,128)(2,1)} %bitcast.14), calls=%async_computation.1 | async-start | bytes 2359296 | tf_op jit(solution)/shard_map/all_to_all | solution.py:34
  77.1 11.3 %copy-start.4 = (bf16[32,1152]{1,0:T(8,128)(2,1)S(1)}, bf16[32,1152]{1,0:T(8,128)(2,1)}, u32[]{:S(2)}) copy-start(bf16[32,1152]{1,0:T(8,128)(2,1)} %text_ref.1) | copy-start | bytes 221188
  77.2 11.7 %collective-permute-start.6 = (bf16[128,1152]{1,0:T(8,128)(2,1)S(1)}, bf16[128,1152]{1,0:T(8,128)(2,1)S(1)}, u32[]{:S(2)}, u32[]{:S(2)}) collective-permute-start(bf16[128,1152]{1,0:T(8,128)(2,1)S(1)} %bitcast.43), channel_id=1, source_target_pairs={{0,4},{2,6},{4,0},{6,2},{1,5},{3,7},{5,1},{7,3},{8,12},{10,14},{12... | collective-permute-start | bytes 884744 | tf_op jit(solution)/shard_map/ppermute | solution.py:30
  81.9 14.0 %collective-permute-start.7 = (bf16[128,1152]{1,0:T(8,128)(2,1)S(1)}, bf16[128,1152]{1,0:T(8,128)(2,1)S(1)}, u32[]{:S(2)}, u32[]{:S(2)}) collective-permute-start(bf16[128,1152]{1,0:T(8,128)(2,1)S(1)} %bitcast.42), channel_id=1, source_target_pairs={{0,2},{2,4},{4,6},{6,0},{1,3},{3,5},{5,7},{7,1},{8,10},{10,12},{12... | collective-permute-start | bytes 884744 | tf_op jit(solution)/shard_map/ppermute | solution.py:30
  84.1 11.8 %collective-permute-start.8 = (bf16[128,1152]{1,0:T(8,128)(2,1)S(1)}, bf16[128,1152]{1,0:T(8,128)(2,1)S(1)}, u32[]{:S(2)}, u32[]{:S(2)}) collective-permute-start(bf16[128,1152]{1,0:T(8,128)(2,1)S(1)} %bitcast.41), channel_id=1, source_target_pairs={{0,6},{2,0},{4,2},{6,4},{1,7},{3,1},{5,3},{7,5},{8,14},{10,8},{12,... | collective-permute-start | bytes 884744 | tf_op jit(solution)/shard_map/ppermute | solution.py:30
  96.1 8.5 %collective-permute-start.10 = (bf16[64,1152]{1,0:T(8,128)(2,1)S(1)}, bf16[64,1152]{1,0:T(8,128)(2,1)S(1)}, u32[]{:S(2)}, u32[]{:S(2)}) collective-permute-start(bf16[64,1152]{1,0:T(8,128)(2,1)S(1)} %get-tuple-element.28), channel_id=1, source_target_pairs={{0,64},{64,0},{1,65},{65,1},{2,66},{66,2},{3,67},{67,3},{4,68},{68... | collective-permute-start | bytes 442376 | tf_op jit(solution)/shard_map/ppermute | solution.py:25
  98.0 10.6 %collective-permute-start.11 = (bf16[64,1152]{1,0:T(8,128)(2,1)S(1)}, bf16[64,1152]{1,0:T(8,128)(2,1)S(1)}, u32[]{:S(2)}, u32[]{:S(2)}) collective-permute-start(bf16[64,1152]{1,0:T(8,128)(2,1)S(1)} %get-tuple-element.28), channel_id=1, source_target_pairs={{0,65},{1,64},{64,1},{65,0},{2,67},{3,66},{66,3},{67,2},{4,69},{5,... | collective-permute-start | bytes 442376 | tf_op jit(solution)/shard_map/ppermute | solution.py:25
  100.8 12.1 %collective-permute-start.9 = (bf16[64,1152]{1,0:T(8,128)(2,1)S(1)}, bf16[64,1152]{1,0:T(8,128)(2,1)S(1)}, u32[]{:S(2)}, u32[]{:S(2)}) collective-permute-start(bf16[64,1152]{1,0:T(8,128)(2,1)S(1)} %get-tuple-element.27), channel_id=1, source_target_pairs={{0,1},{1,0},{2,3},{3,2},{4,5},{5,4},{6,7},{7,6},{8,9},{9,8},{10,11... | collective-permute-start | bytes 442376 | tf_op jit(solution)/shard_map/ppermute | solution.py:25
  114.3 13.5 %all-to-all-start.2 = ((bf16[4,64,1152]{2,1,0:T(8,128)(2,1)}), bf16[4,64,1152]{2,1,0:T(8,128)(2,1)S(1)}, u32[]{:S(2)}, u32[]{:S(2)}) async-start(bf16[4,64,1152]{2,1,0:T(8,128)(2,1)} %broadcast_in_dim.2), calls=%async_computation.2 | async-start | bytes 1179648 | tf_op jit(solution)/shard_map/all_to_all | solution.py:34

commit v15 on v14

--- a/solution.py
+++ b/solution.py
@@ -9,7 +9,7 @@
 AXES = ("yh", "yl", "w", "c", "x", "l")
 CLASSES = ((0, 3, 5, 6), (1, 2, 4, 7))
 RINGS = ("yh", "yl", "w", "l")
-TEXT_GROUPS = [[y * 8 + z for y in of_y for z in of_z] for of_y in CLASSES for of_z in CLASSES]
+TEXT_GROUPS = [[y * 8 + z for z in of_z for y in of_y] for of_y in CLASSES for of_z in CLASSES]
 NARROW = ("x", "l")
 BF16, F32 = jnp.bfloat16, jnp.float32
 
@@ -46,9 +46,8 @@
     def body(x_ref, image_ref, text_ref, quarter_ref, copies_ref):
         start = pl.multiple_of(x_ref[0] * quarter, quarter)
         quarter_ref[...] = image_ref[pl.ds(start, quarter), :]
-        text_bf = unit_rows(text_ref[...])[0].astype(BF16)
         for k in range(peers):
-            copies_ref[k] = text_bf
+            copies_ref[k] = text_ref[...]
 
     whole = pl.BlockSpec(memory_space=pltpu.VMEM)
     return pl.pallas_call(
@@ -81,16 +80,17 @@
 
     part, copies = first_copies(x.astype(jnp.int32).reshape(1), image_emb, text_emb, quarter, peers)
     part = swap(part, "yl")
-    text_bf = exchange(copies, RINGS, TEXT_GROUPS).reshape(-1, width)
+    texts = exchange(copies, RINGS, TEXT_GROUPS).reshape(-1, width)
     around = [part] + [shift(part, "x", n_x - d) for d in range(1, n_x)]
     beyond = in_order(around, x)
     chip = jnp.concatenate([jnp.where(upper, beyond, image_emb), jnp.where(upper, image_emb, beyond)], axis=0)
     near = unit_rows(chip)[0].astype(BF16)
     far = swap(near, "c")
+    text_bf = unit_rows(texts)[0].astype(BF16)
 
     wanted = positive - lax.axis_index(("yh", "yl", "w", "c")) * rows + lax.axis_index("yl") * rows
-    slot = lax.axis_index(("yh", "w")) * mine
-    wanted = lax.dynamic_update_slice_in_dim(jnp.full((text_bf.shape[0],), -1, jnp.int32), wanted, slot, 0)
+    slot = lax.axis_index(("w", "yh")) * mine
+    wanted = lax.dynamic_update_slice_in_dim(jnp.full((texts.shape[0],), -1, jnp.int32), wanted, slot, 0)
     hit = (jnp.arange(2 * near.shape[0], dtype=jnp.int32)[:, None] == wanted[None, :]).astype(F32)
 
     image_unit, image_norm = unit_rows(lax.dynamic_slice_in_dim(image_emb, x * quarter, quarter, 0))
@@ -104,7 +104,7 @@
     grad = (jax.nn.sigmoid(scale * cosine + bias[0]) - hit).astype(BF16)
     text_terms = lax.dot_general(grad, images, (((0,), (0,)), ((), ())), preferred_element_type=F32).astype(BF16)
     text_terms, grad = lax.optimization_barrier((text_terms, grad))
-    text_sum = exchange(text_terms.reshape(peers, mine, width), RINGS, TEXT_GROUPS)
+    along_z = exchange(text_terms.reshape(4, 4 * mine, width), ("w", "l"), CLASSES)
 
     half = near.shape[0]
     far_terms = jnp.dot(grad[half:], text_bf, preferred_element_type=F32).astype(BF16)
@@ -121,11 +121,16 @@
         total = total + shift(sent, "x", d).astype(F32).reshape(2, quarter, width)
     total = total.astype(BF16)
     own, other = jnp.where(upper, total[1], total[0]), jnp.where(upper, total[0], total[1])
-    beside, across, corner = swap(own, "l"), swap(other, "yl"), swap(other, ("yl", "l"))
+    beside, across = swap(own, "l"), swap(other, "yl")
+    other, along_z = lax.optimization_barrier((other, along_z))
+    corner = swap(other, ("yl", "l"))
+    text_sum = jnp.sum(along_z.astype(F32), axis=0).astype(BF16).reshape(4, mine, width)
+    text_sum = exchange(text_sum, ("yh", "yl"), CLASSES)
     image_sum = (own.astype(F32) + beside.astype(F32)) + (across.astype(F32) + corner.astype(F32))
-    image_sum, text_sum = lax.optimization_barrier((image_sum, text_sum))
     done = finish(image_sum[None], image_unit, image_norm, scale)
-    grad_image = exchange(jnp.broadcast_to(done[None], (n_x,) + done.shape), "x").reshape(rows, width)
+    around = [done] + [shift(done, "x", n_x - d) for d in range(1, n_x)]
+    around, text_sum = lax.optimization_barrier((around, text_sum))
+    grad_image = in_order(around, x)
     grad_text = finish(text_sum, text_unit, text_norm, scale)
     return grad_image, grad_text
 

time: 129 us -> 130 us (level)
  the two profiles are of different devices: /device:TPU:1 before, /device:TPU:56 now
where the time goes in v15:
time: 130 us; the launch traced here: 128 us
  starting transfers between devices  81.8 us (63%)
  waiting for transfers between devices  25.7 us (20%)
  matrix products  8.69 us (7%)
  other arithmetic  6.34 us (5%)
  between operations  2.43 us (2%)
  Pallas kernels  2.18 us (2%)
  local copies, waits for them, and re-layouts  1.36 us (1%)
    ppermute x9, starting transfers between devices, shift(): lax.ppermute(block, axis, [(i, (i + distance) % count) for i in range(cou...  32.4 us
    all_to_all x3, starting transfers between devices, exchange(): lax.all_to_all(blocks, axes, 0, 0, axis_index_groups=groups, tiled=True)  27.7 us
    ppermute x6, starting transfers between devices, swap(): return lax.ppermute(block, axes, [(i, count - 1 - i) for i in range(count)])  21.6 us
    ppermute x9, waiting for transfers between devices, shift(): lax.ppermute(block, axis, [(i, (i + distance) % count) for i in range(cou...  19 us
    all_to_all x3, waiting for transfers between devices, exchange(): lax.all_to_all(blocks, axes, 0, 0, axis_index_groups=groups, tiled=True)  5.2 us
  transfers between devices with their start and end apart: 18, of which 10 were waited for; matrix products, arithmetic and copies ran while one was open for 6% of the time, Pallas kernels for 0%

profile of v15, /device:TPU:56, one launch (start us, length us, event | category | flops | bytes accessed | tf_op | source)
XLA Modules:
  0.0 128.5 jit_solution(14563020890967299524)
XLA Ops:
  0.6 2.2 %first_copies.1 = (bf16[64,1152]{1,0:T(8,128)(2,1)}, bf16[16,32,1152]{2,1,0:T(8,128)(2,1)}) custom-call(s32[1]{0:T(128)} %bitcast.1.x_ref, bf16[256,1152]{1,0:T(8,128)(2,1)} %image_ref.1, bf16[32,1152]{1,0:T(8,128)(2,1)} %text_ref.1), custom_call_target="tpu_custom_call" | custom-call | tf_op jit(solution)/shard_map/first_copies/pallas_call | solution.py:53
  2.8 3.2 %collective-permute-start = (bf16[64,1152]{1,0:T(8,128)(2,1)}, bf16[64,1152]{1,0:T(8,128)(2,1)S(1)}, u32[]{:S(2)}, u32[]{:S(2)}) collective-permute-start(bf16[64,1152]{1,0:T(8,128)(2,1)} %get-tuple-element.17), channel_id=1, source_target_pairs={{0,64},{64,0},{1,65},{65,1},{2,66},{66,2},{3,67},{67,3},{4,68},{68... | collective-permute-start | bytes 442376 | tf_op jit(solution)/shard_map/ppermute | solution.py:25
  6.1 14.7 %all-to-all-start = ((bf16[16,32,1152]{2,1,0:T(8,128)(2,1)}), bf16[16,32,1152]{2,1,0:T(8,128)(2,1)S(1)}, u32[]{:S(2)}, u32[]{:S(2)}) async-start(bf16[16,32,1152]{2,1,0:T(8,128)(2,1)} %get-tuple-element.18), calls=%async_computation | async-start | bytes 2359296 | tf_op jit(solution)/shard_map/all_to_all | solution.py:34
  20.8 4.8 %collective-permute-start.1 = (bf16[64,1152]{1,0:T(8,128)(2,1)S(1)}, bf16[64,1152]{1,0:T(8,128)(2,1)S(1)}, u32[]{:S(2)}, u32[]{:S(2)}) collective-permute-start(bf16[64,1152]{1,0:T(8,128)(2,1)S(1)} %collective-permute-done), channel_id=1, source_target_pairs={{0,6},{2,0},{4,2},{6,4},{1,7},{3,1},{5,3},{7,5},{8,14},{10,8},{12,... | collective-permute-start | bytes 442376 | tf_op jit(solution)/shard_map/ppermute | solution.py:30
  25.6 2.7 %collective-permute-start.2 = (bf16[64,1152]{1,0:T(8,128)(2,1)S(1)}, bf16[64,1152]{1,0:T(8,128)(2,1)S(1)}, u32[]{:S(2)}, u32[]{:S(2)}) collective-permute-start(bf16[64,1152]{1,0:T(8,128)(2,1)S(1)} %collective-permute-done), channel_id=1, source_target_pairs={{0,4},{2,6},{4,0},{6,2},{1,5},{3,7},{5,1},{7,3},{8,12},{10,14},{12... | collective-permute-start | bytes 442376 | tf_op jit(solution)/shard_map/ppermute | solution.py:30
  28.3 2.8 %collective-permute-start.3 = (bf16[64,1152]{1,0:T(8,128)(2,1)S(1)}, bf16[64,1152]{1,0:T(8,128)(2,1)S(1)}, u32[]{:S(2)}, u32[]{:S(2)}) collective-permute-start(bf16[64,1152]{1,0:T(8,128)(2,1)S(1)} %collective-permute-done), channel_id=1, source_target_pairs={{0,2},{2,4},{4,6},{6,0},{1,3},{3,5},{5,7},{7,1},{8,10},{10,12},{12... | collective-permute-start | bytes 442376 | tf_op jit(solution)/shard_map/ppermute | solution.py:30
  31.2 4.3 %collective-permute-done.2 = bf16[64,1152]{1,0:T(8,128)(2,1)S(1)} collective-permute-done((bf16[64,1152]{1,0:T(8,128)(2,1)S(1)}, bf16[64,1152]{1,0:T(8,128)(2,1)S(1)}, u32[]{:S(2)}, u32[]{:S(2)}) %collective-permute-start.2) | collective-permute-done | bytes 147488 | tf_op jit(solution)/shard_map/ppermute | solution.py:30
  35.5 1.7 %collective-permute-done.3 = bf16[64,1152]{1,0:T(8,128)(2,1)S(1)} collective-permute-done((bf16[64,1152]{1,0:T(8,128)(2,1)S(1)}, bf16[64,1152]{1,0:T(8,128)(2,1)S(1)}, u32[]{:S(2)}, u32[]{:S(2)}) %collective-permute-start.3) | collective-permute-done | bytes 147488 | tf_op jit(solution)/shard_map/ppermute | solution.py:30
  37.3 0.2 broadcast_select_fusion.1
  37.5 0.3 fusion
  37.9 0.4 fusion.1
  38.3 1.9 %collective-permute-start.4 = (bf16[512,1152]{1,0:T(8,128)(2,1)S(1)}, bf16[512,1152]{1,0:T(8,128)(2,1)}, u32[]{:S(2)}, u32[]{:S(2)}) collective-permute-start(bf16[512,1152]{1,0:T(8,128)(2,1)S(1)} %fusion.1), channel_id=1, source_target_pairs={{0,8},{8,0},{1,9},{9,1},{2,10},{10,2},{3,11},{11,3},{4,12},{12,4},... | collective-permute-start | bytes 3538952 | tf_op jit(solution)/shard_map/ppermute | solution.py:25
  41.6 0.1 add_dynamic-update-slice_fusion
  41.7 1.5 %collective-permute-done.4 = bf16[512,1152]{1,0:T(8,128)(2,1)} collective-permute-done((bf16[512,1152]{1,0:T(8,128)(2,1)S(1)}, bf16[512,1152]{1,0:T(8,128)(2,1)}, u32[]{:S(2)}, u32[]{:S(2)}) %collective-permute-start.4) | collective-permute-done | bytes 1179680 | tf_op jit(solution)/shard_map/ppermute | solution.py:25
  43.1 1.8 %pad_maximum_fusion = bf16[1024,1152]{1,0:T(8,128)(2,1)S(1)} fusion(bf16[512,1152]{1,0:T(8,128)(2,1)} %collective-permute-done.4, bf16[512,1152]{1,0:T(8,128)(2,1)} %copy-done), kind=kLoop, calls=%fused_computation.6 | loop fusion | flops 4718592 | bytes 4718592 | tf_op jit(solution)/shard_map/concatenate | solution.py:102
  44.9 5.2 %all-to-all-done = bf16[16,32,1152]{2,1,0:T(8,128)(2,1)S(1)} async-done(((bf16[16,32,1152]{2,1,0:T(8,128)(2,1)}), bf16[16,32,1152]{2,1,0:T(8,128)(2,1)S(1)}, u32[]{:S(2)}, u32[]{:S(2)}) %all-to-all-start) | async-done | bytes 1179680 | tf_op jit(solution)/shard_map/all_to_all | solution.py:34
  50.1 0.3 multiply_reduce_fusion
  50.5 0.4 fusion.2
  50.9 1.9 %subtract_convert_fusion = bf16[1024,512]{1,0:T(8,128)(2,1)S(1)} fusion(bf16[1024,1152]{1,0:T(8,128)(2,1)S(1)} %pad_maximum_fusion, bf16[512,1152]{1,0:T(8,128)(2,1)S(1)} %fusion.2, s32[512]{0:T(512)S(1)} %add_dynamic-update-slice_fusion, f32[]{:T(128)} %bitcast.40, f32[]{:T(128)} %bitcast), kind=kOutput, calls=%fused_computation.11 | convolution fusion | flops 1212678144 | bytes 4589576 | tf_op jit(solution)/shard_map/dot_general | solution.py:103
  52.9 2.6 %convolution_convert_fusion.1 = bf16[512,1152]{1,0:T(8,128)(2,1)} fusion(bf16[1024,512]{1,0:T(8,128)(2,1)S(1)} %subtract_convert_fusion, bf16[1024,1152]{1,0:T(8,128)(2,1)S(1)} %pad_maximum_fusion), kind=kOutput, calls=%fused_computation.1 | convolution fusion | flops 1208549376 | bytes 4587520 | tf_op jit(solution)/shard_map/dot_general | solution.py:105
  55.5 1.9 %convolution_convert_fusion = bf16[512,1152]{1,0:T(8,128)(2,1)} fusion(bf16[512,1152]{1,0:T(8,128)(2,1)S(1)} %fusion.2, bf16[1024,512]{1,0:T(8,128)(2,1)S(1)} %subtract_convert_fusion), kind=kOutput, calls=%fused_computation | convolution fusion | flops 604569600 | bytes 2883584 | tf_op jit(solution)/shard_map/dot_general | solution.py:110
  57.3 1.9 %collective-permute-start.5 = (bf16[512,1152]{1,0:T(8,128)(2,1)}, bf16[512,1152]{1,0:T(8,128)(2,1)}, u32[]{:S(2)}, u32[]{:S(2)}) collective-permute-start(bf16[512,1152]{1,0:T(8,128)(2,1)} %convolution_convert_fusion), channel_id=1, source_target_pairs={{0,8},{8,0},{1,9},{9,1},{2,10},{10,2},{3,11},{11,3},{4,12},{12,4},... | collective-permute-start | bytes 3538952 | tf_op jit(solution)/shard_map/ppermute | solution.py:25
  59.3 0.1 fusion.9
  59.6 5.8 %all-to-all-start.1 = ((bf16[4,128,1152]{2,1,0:T(8,128)(2,1)}), bf16[4,128,1152]{2,1,0:T(8,128)(2,1)S(1)}, u32[]{:S(2)}, u32[]{:S(2)}) async-start(bf16[4,128,1152]{2,1,0:T(8,128)(2,1)} %bitcast.14), calls=%async_computation.1 | async-start | bytes 2359296 | tf_op jit(solution)/shard_map/all_to_all | solution.py:34
  65.4 2.3 %add_convert_fusion = bf16[512,1152]{1,0:T(8,128)(2,1)S(1)} fusion(bf16[512,1152]{1,0:T(8,128)(2,1)} %collective-permute-done.5, bf16[512,1152]{1,0:T(8,128)(2,1)S(1)} %copy-done.4, bf16[1024,512]{1,0:T(8,128)(2,1)} %copy-done.5), kind=kOutput, calls=%fused_computation.9 | convolution fusion | flops 605749248 | bytes 4063232 | tf_op jit(solution)/shard_map/dot_general | solution.py:112
  67.7 4.9 %collective-permute-start.6 = (bf16[128,1152]{1,0:T(8,128)(2,1)S(1)}, bf16[128,1152]{1,0:T(8,128)(2,1)S(1)}, u32[]{:S(2)}, u32[]{:S(2)}) collective-permute-start(bf16[128,1152]{1,0:T(8,128)(2,1)S(1)} %bitcast.45), channel_id=1, source_target_pairs={{0,4},{2,6},{4,0},{6,2},{1,5},{3,7},{5,1},{7,3},{8,12},{10,14},{12... | collective-permute-start | bytes 884744 | tf_op jit(solution)/shard_map/ppermute | solution.py:30
  72.7 2.5 %collective-permute-start.7 = (bf16[128,1152]{1,0:T(8,128)(2,1)S(1)}, bf16[128,1152]{1,0:T(8,128)(2,1)S(1)}, u32[]{:S(2)}, u32[]{:S(2)}) collective-permute-start(bf16[128,1152]{1,0:T(8,128)(2,1)S(1)} %bitcast.44), channel_id=1, source_target_pairs={{0,2},{2,4},{4,6},{6,0},{1,3},{3,5},{5,7},{7,1},{8,10},{10,12},{12... | collective-permute-start | bytes 884744 | tf_op jit(solution)/shard_map/ppermute | solution.py:30
  75.2 4.6 %collective-permute-start.8 = (bf16[128,1152]{1,0:T(8,128)(2,1)S(1)}, bf16[128,1152]{1,0:T(8,128)(2,1)S(1)}, u32[]{:S(2)}, u32[]{:S(2)}) collective-permute-start(bf16[128,1152]{1,0:T(8,128)(2,1)S(1)} %bitcast.43), channel_id=1, source_target_pairs={{0,6},{2,0},{4,2},{6,4},{1,7},{3,1},{5,3},{7,5},{8,14},{10,8},{12,... | collective-permute-start | bytes 884744 | tf_op jit(solution)/shard_map/ppermute | solution.py:30
  79.8 0.1 fusion.10
  79.9 1.1 collective-permute-done.6
  81.0 5.6 %collective-permute-done.7 = bf16[128,1152]{1,0:T(8,128)(2,1)S(1)} collective-permute-done((bf16[128,1152]{1,0:T(8,128)(2,1)S(1)}, bf16[128,1152]{1,0:T(8,128)(2,1)S(1)}, u32[]{:S(2)}, u32[]{:S(2)}) %collective-permute-start.7) | collective-permute-done | bytes 294944 | tf_op jit(solution)/shard_map/ppermute | solution.py:30
  86.7 0.2 fusion.3
  86.9 6.3 %collective-permute-start.10 = (bf16[64,1152]{1,0:T(8,128)(2,1)S(1)}, bf16[64,1152]{1,0:T(8,128)(2,1)S(1)}, u32[]{:S(2)}, u32[]{:S(2)}) collective-permute-start(bf16[64,1152]{1,0:T(8,128)(2,1)S(1)} %get-tuple-element.21), channel_id=1, source_target_pairs={{0,64},{64,0},{1,65},{65,1},{2,66},{66,2},{3,67},{67,3},{4,68},{68... | collective-permute-start | bytes 442376 | tf_op jit(solution)/shard_map/ppermute | solution.py:25
  93.2 5.3 %collective-permute-start.9 = (bf16[64,1152]{1,0:T(8,128)(2,1)S(1)}, bf16[64,1152]{1,0:T(8,128)(2,1)S(1)}, u32[]{:S(2)}, u32[]{:S(2)}) collective-permute-start(bf16[64,1152]{1,0:T(8,128)(2,1)S(1)} %get-tuple-element.37), channel_id=1, source_target_pairs={{0,1},{1,0},{2,3},{3,2},{4,5},{5,4},{6,7},{7,6},{8,9},{9,8},{10,11... | collective-permute-start | bytes 442376 | tf_op jit(solution)/shard_map/ppermute | solution.py:25
  98.5 2.9 %collective-permute-start.11 = (bf16[64,1152]{1,0:T(8,128)(2,1)S(1)}, bf16[64,1152]{1,0:T(8,128)(2,1)S(1)}, u32[]{:S(2)}, u32[]{:S(2)}) collective-permute-start(bf16[64,1152]{1,0:T(8,128)(2,1)S(1)} %get-tuple-element.21), channel_id=1, source_target_pairs={{0,65},{1,64},{64,1},{65,0},{2,67},{3,66},{66,3},{67,2},{4,69},{5,... | collective-permute-start | bytes 442376 | tf_op jit(solution)/shard_map/ppermute | solution.py:25
  101.6 1.0 reduce_sum.84
  102.5 7.3 %all-to-all-start.2 = ((bf16[4,32,1152]{2,1,0:T(8,128)(2,1)}), bf16[4,32,1152]{2,1,0:T(8,128)(2,1)S(1)}, u32[]{:S(2)}, u32[]{:S(2)}) async-start(bf16[4,32,1152]{2,1,0:T(8,128)(2,1)} %bitcast.18), calls=%async_computation.2 | async-start | bytes 589824 | tf_op jit(solution)/shard_map/all_to_all | solution.py:34
  109.8 0.2 multiply_reduce_fusion.1
  110.0 0.1 divide_convert_fusion
  110.1 5.0 %collective-permute-start.12 = (bf16[64,1152]{1,0:T(8,128)(2,1)S(1)}, bf16[64,1152]{1,0:T(8,128)(2,1)S(1)}, u32[]{:S(2)}, u32[]{:S(2)}) collective-permute-start(bf16[64,1152]{1,0:T(8,128)(2,1)S(1)} %divide_convert_fusion), channel_id=1, source_target_pairs={{0,6},{2,0},{4,2},{6,4},{1,7},{3,1},{5,3},{7,5},{8,14},{10,8},{12,... | collective-permute-start | bytes 442376 | tf_op jit(solution)/shard_map/ppermute | solution.py:30
  115.2 2.3 %collective-permute-start.13 = (bf16[64,1152]{1,0:T(8,128)(2,1)S(1)}, bf16[64,1152]{1,0:T(8,128)(2,1)S(1)}, u32[]{:S(2)}, u32[]{:S(2)}) collective-permute-start(bf16[64,1152]{1,0:T(8,128)(2,1)S(1)} %divide_convert_fusion), channel_id=1, source_target_pairs={{0,4},{2,6},{4,0},{6,2},{1,5},{3,7},{5,1},{7,3},{8,12},{10,14},{12... | collective-permute-start | bytes 442376 | tf_op jit(solution)/shard_map/ppermute | solution.py:30
  117.5 2.7 %collective-permute-start.14 = (bf16[64,1152]{1,0:T(8,128)(2,1)S(1)}, bf16[64,1152]{1,0:T(8,128)(2,1)S(1)}, u32[]{:S(2)}, u32[]{:S(2)}) collective-permute-start(bf16[64,1152]{1,0:T(8,128)(2,1)S(1)} %divide_convert_fusion), channel_id=1, source_target_pairs={{0,2},{2,4},{4,6},{6,0},{1,3},{3,5},{5,7},{7,1},{8,10},{10,12},{12... | collective-permute-start | bytes 442376 | tf_op jit(solution)/shard_map/ppermute | solution.py:30
  120.3 0.7 collective-permute-done.12
  121.0 3.5 %collective-permute-done.13 = bf16[64,1152]{1,0:T(8,128)(2,1)S(1)} collective-permute-done((bf16[64,1152]{1,0:T(8,128)(2,1)S(1)}, bf16[64,1152]{1,0:T(8,128)(2,1)S(1)}, u32[]{:S(2)}, u32[]{:S(2)}) %collective-permute-start.13) | collective-permute-done | bytes 147488 | tf_op jit(solution)/shard_map/ppermute | solution.py:30
  124.5 2.0 %collective-permute-done.14 = bf16[64,1152]{1,0:T(8,128)(2,1)S(1)} collective-permute-done((bf16[64,1152]{1,0:T(8,128)(2,1)S(1)}, bf16[64,1152]{1,0:T(8,128)(2,1)S(1)}, u32[]{:S(2)}, u32[]{:S(2)}) %collective-permute-start.14) | collective-permute-done | bytes 147488 | tf_op jit(solution)/shard_map/ppermute | solution.py:30
  126.7 0.9 constant_dynamic-slice_fusion
  127.6 0.1 multiply_reduce_fusion.2
  127.7 0.7 divide_convert_fusion.1
  (52 shorter events, 0.9 us)
Async XLA Ops:
  2.8 17.9 %collective-permute-start = (bf16[64,1152]{1,0:T(8,128)(2,1)}, bf16[64,1152]{1,0:T(8,128)(2,1)S(1)}, u32[]{:S(2)}, u32[]{:S(2)}) collective-permute-start(bf16[64,1152]{1,0:T(8,128)(2,1)} %get-tuple-element.17), channel_id=1, source_target_pairs={{0,64},{64,0},{1,65},{65,1},{2,66},{66,2},{3,67},{67,3},{4,68},{68... | collective-permute-start | bytes 442376 | tf_op jit(solution)/shard_map/ppermute | solution.py:25
  6.1 44.1 %all-to-all-start = ((bf16[16,32,1152]{2,1,0:T(8,128)(2,1)}), bf16[16,32,1152]{2,1,0:T(8,128)(2,1)S(1)}, u32[]{:S(2)}, u32[]{:S(2)}) async-start(bf16[16,32,1152]{2,1,0:T(8,128)(2,1)} %get-tuple-element.18), calls=%async_computation | async-start | bytes 2359296 | tf_op jit(solution)/shard_map/all_to_all | solution.py:34
  20.8 16.5 %copy-start.1 = (bf16[256,1152]{1,0:T(8,128)(2,1)S(1)}, bf16[256,1152]{1,0:T(8,128)(2,1)}, u32[]{:S(2)}) copy-start(bf16[256,1152]{1,0:T(8,128)(2,1)} %image_ref.1) | copy-start | bytes 1769476
  20.8 10.3 %collective-permute-start.1 = (bf16[64,1152]{1,0:T(8,128)(2,1)S(1)}, bf16[64,1152]{1,0:T(8,128)(2,1)S(1)}, u32[]{:S(2)}, u32[]{:S(2)}) collective-permute-start(bf16[64,1152]{1,0:T(8,128)(2,1)S(1)} %collective-permute-done), channel_id=1, source_target_pairs={{0,6},{2,0},{4,2},{6,4},{1,7},{3,1},{5,3},{7,5},{8,14},{10,8},{12,... | collective-permute-start | bytes 442376 | tf_op jit(solution)/shard_map/ppermute | solution.py:30
  25.6 9.9 %collective-permute-start.2 = (bf16[64,1152]{1,0:T(8,128)(2,1)S(1)}, bf16[64,1152]{1,0:T(8,128)(2,1)S(1)}, u32[]{:S(2)}, u32[]{:S(2)}) collective-permute-start(bf16[64,1152]{1,0:T(8,128)(2,1)S(1)} %collective-permute-done), channel_id=1, source_target_pairs={{0,4},{2,6},{4,0},{6,2},{1,5},{3,7},{5,1},{7,3},{8,12},{10,14},{12... | collective-permute-start | bytes 442376 | tf_op jit(solution)/shard_map/ppermute | solution.py:30
  28.3 8.9 %collective-permute-start.3 = (bf16[64,1152]{1,0:T(8,128)(2,1)S(1)}, bf16[64,1152]{1,0:T(8,128)(2,1)S(1)}, u32[]{:S(2)}, u32[]{:S(2)}) collective-permute-start(bf16[64,1152]{1,0:T(8,128)(2,1)S(1)} %collective-permute-done), channel_id=1, source_target_pairs={{0,2},{2,4},{4,6},{6,0},{1,3},{3,5},{5,7},{7,1},{8,10},{10,12},{12... | collective-permute-start | bytes 442376 | tf_op jit(solution)/shard_map/ppermute | solution.py:30
  37.9 3.7 %copy-start.7 = (s32[32]{0:T(128)S(1)}, s32[32]{0:T(128)}, u32[]{:S(2)}) copy-start(s32[32]{0:T(128)} %param.7) | copy-start | bytes 388
  38.2 3.4 %copy-start = (bf16[512,1152]{1,0:T(8,128)(2,1)}, bf16[512,1152]{1,0:T(8,128)(2,1)S(1)}, u32[]{:S(2)}) copy-start(bf16[512,1152]{1,0:T(8,128)(2,1)S(1)} %fusion.1) | copy-start | bytes 3538948
  38.3 4.9 %collective-permute-start.4 = (bf16[512,1152]{1,0:T(8,128)(2,1)S(1)}, bf16[512,1152]{1,0:T(8,128)(2,1)}, u32[]{:S(2)}, u32[]{:S(2)}) collective-permute-start(bf16[512,1152]{1,0:T(8,128)(2,1)S(1)} %fusion.1), channel_id=1, source_target_pairs={{0,8},{8,0},{1,9},{9,1},{2,10},{10,2},{3,11},{11,3},{4,12},{12,4},... | collective-permute-start | bytes 3538952 | tf_op jit(solution)/shard_map/ppermute | solution.py:25
  50.9 4.6 %copy-start.3 = (bf16[512,1152]{1,0:T(8,128)(2,1)}, bf16[512,1152]{1,0:T(8,128)(2,1)S(1)}, u32[]{:S(2)}) copy-start(bf16[512,1152]{1,0:T(8,128)(2,1)S(1)} %fusion.2) | copy-start | bytes 3538948
  52.9 2.6 %copy-start.5 = (bf16[1024,512]{1,0:T(8,128)(2,1)}, bf16[1024,512]{1,0:T(8,128)(2,1)S(1)}, u32[]{:S(2)}) copy-start(bf16[1024,512]{1,0:T(8,128)(2,1)S(1)} %subtract_convert_fusion) | copy-start | bytes 3145732
  55.5 3.8 %copy-start.2 = (bf16[256,1152]{1,0:T(8,128)(2,1)S(1)}, bf16[256,1152]{1,0:T(8,128)(2,1)}, u32[]{:S(2)}) copy-start(bf16[256,1152]{1,0:T(8,128)(2,1)} %image_ref.1) | copy-start | bytes 1769476
  57.3 8.0 %collective-permute-start.5 = (bf16[512,1152]{1,0:T(8,128)(2,1)}, bf16[512,1152]{1,0:T(8,128)(2,1)}, u32[]{:S(2)}, u32[]{:S(2)}) collective-permute-start(bf16[512,1152]{1,0:T(8,128)(2,1)} %convolution_convert_fusion), channel_id=1, source_target_pairs={{0,8},{8,0},{1,9},{9,1},{2,10},{10,2},{3,11},{11,3},{4,12},{12,4},... | collective-permute-start | bytes 3538952 | tf_op jit(solution)/shard_map/ppermute | solution.py:25
  59.6 5.8 %copy-start.4 = (bf16[512,1152]{1,0:T(8,128)(2,1)S(1)}, bf16[512,1152]{1,0:T(8,128)(2,1)}, u32[]{:S(2)}) copy-start(bf16[512,1152]{1,0:T(8,128)(2,1)} %copy-done.3) | copy-start | bytes 3538948
  59.6 39.0 %all-to-all-start.1 = ((bf16[4,128,1152]{2,1,0:T(8,128)(2,1)}), bf16[4,128,1152]{2,1,0:T(8,128)(2,1)S(1)}, u32[]{:S(2)}, u32[]{:S(2)}) async-start(bf16[4,128,1152]{2,1,0:T(8,128)(2,1)} %bitcast.14), calls=%async_computation.1 | async-start | bytes 2359296 | tf_op jit(solution)/shard_map/all_to_all | solution.py:34
  67.6 12.1 %copy-start.6 = (bf16[32,1152]{1,0:T(8,128)(2,1)S(1)}, bf16[32,1152]{1,0:T(8,128)(2,1)}, u32[]{:S(2)}) copy-start(bf16[32,1152]{1,0:T(8,128)(2,1)} %text_ref.1) | copy-start | bytes 221188
  67.7 13.2 %collective-permute-start.6 = (bf16[128,1152]{1,0:T(8,128)(2,1)S(1)}, bf16[128,1152]{1,0:T(8,128)(2,1)S(1)}, u32[]{:S(2)}, u32[]{:S(2)}) collective-permute-start(bf16[128,1152]{1,0:T(8,128)(2,1)S(1)} %bitcast.45), channel_id=1, source_target_pairs={{0,4},{2,6},{4,0},{6,2},{1,5},{3,7},{5,1},{7,3},{8,12},{10,14},{12... | collective-permute-start | bytes 884744 | tf_op jit(solution)/shard_map/ppermute | solution.py:30
  72.7 13.9 %collective-permute-start.7 = (bf16[128,1152]{1,0:T(8,128)(2,1)S(1)}, bf16[128,1152]{1,0:T(8,128)(2,1)S(1)}, u32[]{:S(2)}, u32[]{:S(2)}) collective-permute-start(bf16[128,1152]{1,0:T(8,128)(2,1)S(1)} %bitcast.44), channel_id=1, source_target_pairs={{0,2},{2,4},{4,6},{6,0},{1,3},{3,5},{5,7},{7,1},{8,10},{10,12},{12... | collective-permute-start | bytes 884744 | tf_op jit(solution)/shard_map/ppermute | solution.py:30
  75.2 11.5 %collective-permute-start.8 = (bf16[128,1152]{1,0:T(8,128)(2,1)S(1)}, bf16[128,1152]{1,0:T(8,128)(2,1)S(1)}, u32[]{:S(2)}, u32[]{:S(2)}) collective-permute-start(bf16[128,1152]{1,0:T(8,128)(2,1)S(1)} %bitcast.43), channel_id=1, source_target_pairs={{0,6},{2,0},{4,2},{6,4},{1,7},{3,1},{5,3},{7,5},{8,14},{10,8},{12,... | collective-permute-start | bytes 884744 | tf_op jit(solution)/shard_map/ppermute | solution.py:30
  86.9 22.9 %collective-permute-start.10 = (bf16[64,1152]{1,0:T(8,128)(2,1)S(1)}, bf16[64,1152]{1,0:T(8,128)(2,1)S(1)}, u32[]{:S(2)}, u32[]{:S(2)}) collective-permute-start(bf16[64,1152]{1,0:T(8,128)(2,1)S(1)} %get-tuple-element.21), channel_id=1, source_target_pairs={{0,64},{64,0},{1,65},{65,1},{2,66},{66,2},{3,67},{67,3},{4,68},{68... | collective-permute-start | bytes 442376 | tf_op jit(solution)/shard_map/ppermute | solution.py:25
  93.2 16.6 %collective-permute-start.9 = (bf16[64,1152]{1,0:T(8,128)(2,1)S(1)}, bf16[64,1152]{1,0:T(8,128)(2,1)S(1)}, u32[]{:S(2)}, u32[]{:S(2)}) collective-permute-start(bf16[64,1152]{1,0:T(8,128)(2,1)S(1)} %get-tuple-element.37), channel_id=1, source_target_pairs={{0,1},{1,0},{2,3},{3,2},{4,5},{5,4},{6,7},{7,6},{8,9},{9,8},{10,11... | collective-permute-start | bytes 442376 | tf_op jit(solution)/shard_map/ppermute | solution.py:25
  98.5 11.3 %collective-permute-start.11 = (bf16[64,1152]{1,0:T(8,128)(2,1)S(1)}, bf16[64,1152]{1,0:T(8,128)(2,1)S(1)}, u32[]{:S(2)}, u32[]{:S(2)}) collective-permute-start(bf16[64,1152]{1,0:T(8,128)(2,1)S(1)} %get-tuple-element.21), channel_id=1, source_target_pairs={{0,65},{1,64},{64,1},{65,0},{2,67},{3,66},{66,3},{67,2},{4,69},{5,... | collective-permute-start | bytes 442376 | tf_op jit(solution)/shard_map/ppermute | solution.py:25
  102.5 24.0 %all-to-all-start.2 = ((bf16[4,32,1152]{2,1,0:T(8,128)(2,1)}), bf16[4,32,1152]{2,1,0:T(8,128)(2,1)S(1)}, u32[]{:S(2)}, u32[]{:S(2)}) async-start(bf16[4,32,1152]{2,1,0:T(8,128)(2,1)} %bitcast.18), calls=%async_computation.2 | async-start | bytes 589824 | tf_op jit(solution)/shard_map/all_to_all | solution.py:34
  110.1 10.9 %collective-permute-start.12 = (bf16[64,1152]{1,0:T(8,128)(2,1)S(1)}, bf16[64,1152]{1,0:T(8,128)(2,1)S(1)}, u32[]{:S(2)}, u32[]{:S(2)}) collective-permute-start(bf16[64,1152]{1,0:T(8,128)(2,1)S(1)} %divide_convert_fusion), channel_id=1, source_target_pairs={{0,6},{2,0},{4,2},{6,4},{1,7},{3,1},{5,3},{7,5},{8,14},{10,8},{12,... | collective-permute-start | bytes 442376 | tf_op jit(solution)/shard_map/ppermute | solution.py:30
  115.2 9.4 %collective-permute-start.13 = (bf16[64,1152]{1,0:T(8,128)(2,1)S(1)}, bf16[64,1152]{1,0:T(8,128)(2,1)S(1)}, u32[]{:S(2)}, u32[]{:S(2)}) collective-permute-start(bf16[64,1152]{1,0:T(8,128)(2,1)S(1)} %divide_convert_fusion), channel_id=1, source_target_pairs={{0,4},{2,6},{4,0},{6,2},{1,5},{3,7},{5,1},{7,3},{8,12},{10,14},{12... | collective-permute-start | bytes 442376 | tf_op jit(solution)/shard_map/ppermute | solution.py:30
  117.5 9.0 %collective-permute-start.14 = (bf16[64,1152]{1,0:T(8,128)(2,1)S(1)}, bf16[64,1152]{1,0:T(8,128)(2,1)S(1)}, u32[]{:S(2)}, u32[]{:S(2)}) collective-permute-start(bf16[64,1152]{1,0:T(8,128)(2,1)S(1)} %divide_convert_fusion), channel_id=1, source_target_pairs={{0,2},{2,4},{4,6},{6,0},{1,3},{3,5},{5,7},{7,1},{8,10},{10,12},{12... | collective-permute-start | bytes 442376 | tf_op jit(solution)/shard_map/ppermute | solution.py:30

commit v16 on v14

--- a/solution.py
+++ b/solution.py
@@ -7,7 +7,8 @@
 
 epsilon = 1e-06
 AXES = ("yh", "yl", "w", "c", "x", "l")
-CLASSES = ((0, 3, 5, 6), (1, 2, 4, 7))
+CLASSES = ((0, 6, 3, 5), (1, 7, 2, 4))
+PLACES = (0, 2, 3, 1)
 RINGS = ("yh", "yl", "w", "l")
 TEXT_GROUPS = [[y * 8 + z for y in of_y for z in of_z] for of_y in CLASSES for of_z in CLASSES]
 NARROW = ("x", "l")
@@ -46,9 +47,8 @@
     def body(x_ref, image_ref, text_ref, quarter_ref, copies_ref):
         start = pl.multiple_of(x_ref[0] * quarter, quarter)
         quarter_ref[...] = image_ref[pl.ds(start, quarter), :]
-        text_bf = unit_rows(text_ref[...])[0].astype(BF16)
         for k in range(peers):
-            copies_ref[k] = text_bf
+            copies_ref[k] = text_ref[...]
 
     whole = pl.BlockSpec(memory_space=pltpu.VMEM)
     return pl.pallas_call(
@@ -81,16 +81,18 @@
 
     part, copies = first_copies(x.astype(jnp.int32).reshape(1), image_emb, text_emb, quarter, peers)
     part = swap(part, "yl")
-    text_bf = exchange(copies, RINGS, TEXT_GROUPS).reshape(-1, width)
+    texts = exchange(copies, RINGS, TEXT_GROUPS).reshape(-1, width)
     around = [part] + [shift(part, "x", n_x - d) for d in range(1, n_x)]
     beyond = in_order(around, x)
     chip = jnp.concatenate([jnp.where(upper, beyond, image_emb), jnp.where(upper, image_emb, beyond)], axis=0)
     near = unit_rows(chip)[0].astype(BF16)
     far = swap(near, "c")
+    text_bf = unit_rows(texts)[0].astype(BF16)
 
     wanted = positive - lax.axis_index(("yh", "yl", "w", "c")) * rows + lax.axis_index("yl") * rows
-    slot = lax.axis_index(("yh", "w")) * mine
-    wanted = lax.dynamic_update_slice_in_dim(jnp.full((text_bf.shape[0],), -1, jnp.int32), wanted, slot, 0)
+    places = jnp.array(PLACES, jnp.int32)
+    slot = (places[lax.axis_index("yh")] * 4 + places[lax.axis_index("w")]) * mine
+    wanted = lax.dynamic_update_slice_in_dim(jnp.full((texts.shape[0],), -1, jnp.int32), wanted, slot, 0)
     hit = (jnp.arange(2 * near.shape[0], dtype=jnp.int32)[:, None] == wanted[None, :]).astype(F32)
 
     image_unit, image_norm = unit_rows(lax.dynamic_slice_in_dim(image_emb, x * quarter, quarter, 0))
@@ -110,14 +112,14 @@
     far_terms = jnp.dot(grad[half:], text_bf, preferred_element_type=F32).astype(BF16)
     far_terms = swap(far_terms, "c").astype(F32)
     both = jnp.dot(grad[:half], text_bf, preferred_element_type=F32) + far_terms
-    both = both.astype(BF16).reshape(2, n_x, quarter, width)
+    both = both.reshape(2, n_x, quarter, width)
 
     def of_position(k):
         return lax.dynamic_index_in_dim(both, lax.rem(x + k, n_x), axis=1, keepdims=False)
 
-    total = of_position(0).astype(F32)
+    total = of_position(0)
     for d in (2, 1, 3):
-        sent = of_position(d).reshape(2 * quarter, width)
+        sent = of_position(d).astype(BF16).reshape(2 * quarter, width)
         total = total + shift(sent, "x", d).astype(F32).reshape(2, quarter, width)
     total = total.astype(BF16)
     own, other = jnp.where(upper, total[1], total[0]), jnp.where(upper, total[0], total[1])

time: 129 us -> 134 us (1.039)
  the two profiles are of different devices: /device:TPU:1 before, /device:TPU:56 now
where the time goes in v16:
time: 134 us; the launch traced here: 131 us
  starting transfers between devices  73.3 us (55%)
  waiting for transfers between devices  35.2 us (26%)
  matrix products  8.68 us (6%)
  other arithmetic  5.48 us (4%)
  between operations  3.61 us (3%)
  local copies, waits for them, and re-layouts  2.64 us (2%)
  Pallas kernels  2.19 us (2%)
    all_to_all x3, starting transfers between devices, exchange(): lax.all_to_all(blocks, axes, 0, 0, axis_index_groups=groups, tiled=True)  32.7 us
    ppermute x6, starting transfers between devices, shift(): lax.ppermute(block, axis, [(i, (i + distance) % count) for i in range(cou...  22.3 us
    ppermute x6, starting transfers between devices, swap(): return lax.ppermute(block, axes, [(i, count - 1 - i) for i in range(count)])  18.3 us
    all_to_all x3, waiting for transfers between devices, exchange(): lax.all_to_all(blocks, axes, 0, 0, axis_index_groups=groups, tiled=True)  14.7 us
    ppermute x6, waiting for transfers between devices, shift(): lax.ppermute(block, axis, [(i, (i + distance) % count) for i in range(cou...  12.5 us
    ppermute x6, waiting for transfers between devices, swap(): return lax.ppermute(block, axes, [(i, count - 1 - i) for i in range(count)])  8 us
  transfers between devices with their start and end apart: 15, of which 9 were waited for; matrix products, arithmetic and copies ran while one was open for 6% of the time, Pallas kernels for 0%

profile of v16, /device:TPU:56, one launch (start us, length us, event | category | flops | bytes accessed | tf_op | source)
XLA Modules:
  0.0 131.2 jit_solution(13220237302628303984)
XLA Ops:
  0.6 2.2 %first_copies.1 = (bf16[64,1152]{1,0:T(8,128)(2,1)}, bf16[16,32,1152]{2,1,0:T(8,128)(2,1)}) custom-call(s32[1]{0:T(128)} %bitcast.1.x_ref, bf16[256,1152]{1,0:T(8,128)(2,1)} %image_ref.1, bf16[32,1152]{1,0:T(8,128)(2,1)} %text_ref.1), custom_call_target="tpu_custom_call" | custom-call | tf_op jit(solution)/shard_map/first_copies/pallas_call | solution.py:54
  2.8 3.2 %collective-permute-start = (bf16[64,1152]{1,0:T(8,128)(2,1)}, bf16[64,1152]{1,0:T(8,128)(2,1)S(1)}, u32[]{:S(2)}, u32[]{:S(2)}) collective-permute-start(bf16[64,1152]{1,0:T(8,128)(2,1)} %get-tuple-element.12), channel_id=1, source_target_pairs={{0,64},{64,0},{1,65},{65,1},{2,66},{66,2},{3,67},{67,3},{4,68},{68... | collective-permute-start | bytes 442376 | tf_op jit(solution)/shard_map/ppermute | solution.py:26
  6.1 14.7 %all-to-all-start = ((bf16[16,32,1152]{2,1,0:T(8,128)(2,1)}), bf16[16,32,1152]{2,1,0:T(8,128)(2,1)S(1)}, u32[]{:S(2)}, u32[]{:S(2)}) async-start(bf16[16,32,1152]{2,1,0:T(8,128)(2,1)} %get-tuple-element.13), calls=%async_computation | async-start | bytes 2359296 | tf_op jit(solution)/shard_map/all_to_all | solution.py:35
  20.8 4.8 %collective-permute-start.1 = (bf16[64,1152]{1,0:T(8,128)(2,1)S(1)}, bf16[64,1152]{1,0:T(8,128)(2,1)S(1)}, u32[]{:S(2)}, u32[]{:S(2)}) collective-permute-start(bf16[64,1152]{1,0:T(8,128)(2,1)S(1)} %collective-permute-done), channel_id=1, source_target_pairs={{0,6},{2,0},{4,2},{6,4},{1,7},{3,1},{5,3},{7,5},{8,14},{10,8},{12,... | collective-permute-start | bytes 442376 | tf_op jit(solution)/shard_map/ppermute | solution.py:31
  25.6 2.7 %collective-permute-start.2 = (bf16[64,1152]{1,0:T(8,128)(2,1)S(1)}, bf16[64,1152]{1,0:T(8,128)(2,1)S(1)}, u32[]{:S(2)}, u32[]{:S(2)}) collective-permute-start(bf16[64,1152]{1,0:T(8,128)(2,1)S(1)} %collective-permute-done), channel_id=1, source_target_pairs={{0,4},{2,6},{4,0},{6,2},{1,5},{3,7},{5,1},{7,3},{8,12},{10,14},{12... | collective-permute-start | bytes 442376 | tf_op jit(solution)/shard_map/ppermute | solution.py:31
  28.3 2.8 %collective-permute-start.3 = (bf16[64,1152]{1,0:T(8,128)(2,1)S(1)}, bf16[64,1152]{1,0:T(8,128)(2,1)S(1)}, u32[]{:S(2)}, u32[]{:S(2)}) collective-permute-start(bf16[64,1152]{1,0:T(8,128)(2,1)S(1)} %collective-permute-done), channel_id=1, source_target_pairs={{0,2},{2,4},{4,6},{6,0},{1,3},{3,5},{5,7},{7,1},{8,10},{10,12},{12... | collective-permute-start | bytes 442376 | tf_op jit(solution)/shard_map/ppermute | solution.py:31
  31.2 4.3 %collective-permute-done.2 = bf16[64,1152]{1,0:T(8,128)(2,1)S(1)} collective-permute-done((bf16[64,1152]{1,0:T(8,128)(2,1)S(1)}, bf16[64,1152]{1,0:T(8,128)(2,1)S(1)}, u32[]{:S(2)}, u32[]{:S(2)}) %collective-permute-start.2) | collective-permute-done | bytes 147488 | tf_op jit(solution)/shard_map/ppermute | solution.py:31
  35.5 1.7 %collective-permute-done.3 = bf16[64,1152]{1,0:T(8,128)(2,1)S(1)} collective-permute-done((bf16[64,1152]{1,0:T(8,128)(2,1)S(1)}, bf16[64,1152]{1,0:T(8,128)(2,1)S(1)}, u32[]{:S(2)}, u32[]{:S(2)}) %collective-permute-start.3) | collective-permute-done | bytes 147488 | tf_op jit(solution)/shard_map/ppermute | solution.py:31
  37.3 0.2 broadcast_select_fusion.1
  37.6 0.3 fusion
  37.9 0.4 fusion.1
  38.3 1.9 %collective-permute-start.4 = (bf16[512,1152]{1,0:T(8,128)(2,1)S(1)}, bf16[512,1152]{1,0:T(8,128)(2,1)}, u32[]{:S(2)}, u32[]{:S(2)}) collective-permute-start(bf16[512,1152]{1,0:T(8,128)(2,1)S(1)} %fusion.1), channel_id=1, source_target_pairs={{0,8},{8,0},{1,9},{9,1},{2,10},{10,2},{3,11},{11,3},{4,12},{12,4},... | collective-permute-start | bytes 3538952 | tf_op jit(solution)/shard_map/ppermute | solution.py:26
  40.2 0.6 fusion.13
  43.4 0.1 add_dynamic-update-slice_fusion
  43.5 1.8 %pad_maximum_fusion = bf16[1024,1152]{1,0:T(8,128)(2,1)S(1)} fusion(bf16[512,1152]{1,0:T(8,128)(2,1)} %collective-permute-done.4, bf16[512,1152]{1,0:T(8,128)(2,1)} %copy-done.2), kind=kLoop, calls=%fused_computation.6 | loop fusion | flops 4718592 | bytes 4718592 | tf_op jit(solution)/shard_map/concatenate | solution.py:104
  45.3 5.2 %all-to-all-done = bf16[16,32,1152]{2,1,0:T(8,128)(2,1)S(1)} async-done(((bf16[16,32,1152]{2,1,0:T(8,128)(2,1)}), bf16[16,32,1152]{2,1,0:T(8,128)(2,1)S(1)}, u32[]{:S(2)}, u32[]{:S(2)}) %all-to-all-start) | async-done | bytes 1179680 | tf_op jit(solution)/shard_map/all_to_all | solution.py:35
  50.5 0.3 multiply_reduce_fusion
  50.9 0.4 fusion.2
  51.3 1.9 %subtract_convert_fusion = bf16[1024,512]{1,0:T(8,128)(2,1)S(1)} fusion(bf16[1024,1152]{1,0:T(8,128)(2,1)S(1)} %pad_maximum_fusion, bf16[512,1152]{1,0:T(8,128)(2,1)S(1)} %fusion.2, s32[512]{0:T(512)S(1)} %add_dynamic-update-slice_fusion, f32[]{:T(128)} %bitcast.38, f32[]{:T(128)} %bitcast), kind=kOutput, calls=%fused_computation.12 | convolution fusion | flops 1212678144 | bytes 4589576 | tf_op jit(solution)/shard_map/dot_general | solution.py:105
  53.3 2.6 %convolution_convert_fusion.1 = bf16[512,1152]{1,0:T(8,128)(2,1)} fusion(bf16[1024,512]{1,0:T(8,128)(2,1)S(1)} %subtract_convert_fusion, bf16[1024,1152]{1,0:T(8,128)(2,1)S(1)} %pad_maximum_fusion), kind=kOutput, calls=%fused_computation.1 | convolution fusion | flops 1208549376 | bytes 4587520 | tf_op jit(solution)/shard_map/dot_general | solution.py:107
  55.9 1.9 %convolution_convert_fusion = bf16[512,1152]{1,0:T(8,128)(2,1)} fusion(bf16[512,1152]{1,0:T(8,128)(2,1)S(1)} %fusion.2, bf16[1024,512]{1,0:T(8,128)(2,1)S(1)} %subtract_convert_fusion), kind=kOutput, calls=%fused_computation | convolution fusion | flops 604569600 | bytes 2883584 | tf_op jit(solution)/shard_map/dot_general | solution.py:112
  57.7 1.9 %collective-permute-start.5 = (bf16[512,1152]{1,0:T(8,128)(2,1)}, bf16[512,1152]{1,0:T(8,128)(2,1)}, u32[]{:S(2)}, u32[]{:S(2)}) collective-permute-start(bf16[512,1152]{1,0:T(8,128)(2,1)} %convolution_convert_fusion), channel_id=1, source_target_pairs={{0,8},{8,0},{1,9},{9,1},{2,10},{10,2},{3,11},{11,3},{4,12},{12,4},... | collective-permute-start | bytes 3538952 | tf_op jit(solution)/shard_map/ppermute | solution.py:26
  59.7 0.1 fusion.9
  59.8 0.1 convert_divide_fusion.1
  60.0 13.7 %all-to-all-start.1 = ((bf16[16,32,1152]{2,1,0:T(8,128)(2,1)}), bf16[16,32,1152]{2,1,0:T(8,128)(2,1)S(1)}, u32[]{:S(2)}, u32[]{:S(2)}) async-start(bf16[16,32,1152]{2,1,0:T(8,128)(2,1)} %bitcast.15), calls=%async_computation.1 | async-start | bytes 2359296 | tf_op jit(solution)/shard_map/all_to_all | solution.py:35
  73.7 2.3 %convert_add_fusion = f32[512,1152]{1,0:T(8,128)S(1)} fusion(bf16[512,1152]{1,0:T(8,128)(2,1)} %collective-permute-done.5, bf16[512,1152]{1,0:T(8,128)(2,1)S(1)} %copy-done.1, bf16[1024,512]{1,0:T(8,128)(2,1)} %copy-done.5), kind=kOutput, calls=%fused_computation.10 | convolution fusion | flops 605159424 | bytes 5242880 | tf_op jit(solution)/shard_map/dot_general | solution.py:114
  75.9 0.1 dynamic-slice_convert_fusion.2
  76.1 4.9 %collective-permute-start.6 = (bf16[128,1152]{1,0:T(8,128)(2,1)S(1)}, bf16[128,1152]{1,0:T(8,128)(2,1)S(1)}, u32[]{:S(2)}, u32[]{:S(2)}) collective-permute-start(bf16[128,1152]{1,0:T(8,128)(2,1)S(1)} %bitcast.44), channel_id=1, source_target_pairs={{0,4},{2,6},{4,0},{6,2},{1,5},{3,7},{5,1},{7,3},{8,12},{10,14},{12... | collective-permute-start | bytes 884744 | tf_op jit(solution)/shard_map/ppermute | solution.py:31
  81.0 2.5 %collective-permute-start.7 = (bf16[128,1152]{1,0:T(8,128)(2,1)S(1)}, bf16[128,1152]{1,0:T(8,128)(2,1)S(1)}, u32[]{:S(2)}, u32[]{:S(2)}) collective-permute-start(bf16[128,1152]{1,0:T(8,128)(2,1)S(1)} %bitcast.43), channel_id=1, source_target_pairs={{0,2},{2,4},{4,6},{6,0},{1,3},{3,5},{5,7},{7,1},{8,10},{10,12},{12... | collective-permute-start | bytes 884744 | tf_op jit(solution)/shard_map/ppermute | solution.py:31
  83.5 4.6 %collective-permute-start.8 = (bf16[128,1152]{1,0:T(8,128)(2,1)S(1)}, bf16[128,1152]{1,0:T(8,128)(2,1)S(1)}, u32[]{:S(2)}, u32[]{:S(2)}) collective-permute-start(bf16[128,1152]{1,0:T(8,128)(2,1)S(1)} %bitcast.42), channel_id=1, source_target_pairs={{0,6},{2,0},{4,2},{6,4},{1,7},{3,1},{5,3},{7,5},{8,14},{10,8},{12,... | collective-permute-start | bytes 884744 | tf_op jit(solution)/shard_map/ppermute | solution.py:31
  88.1 0.1 fusion.10
  88.2 1.1 collective-permute-done.6
  89.3 5.3 %collective-permute-done.7 = bf16[128,1152]{1,0:T(8,128)(2,1)S(1)} collective-permute-done((bf16[128,1152]{1,0:T(8,128)(2,1)S(1)}, bf16[128,1152]{1,0:T(8,128)(2,1)S(1)}, u32[]{:S(2)}, u32[]{:S(2)}) %collective-permute-start.7) | collective-permute-done | bytes 294944 | tf_op jit(solution)/shard_map/ppermute | solution.py:31
  94.7 0.1 fusion.3
  94.9 4.3 %collective-permute-start.10 = (bf16[64,1152]{1,0:T(8,128)(2,1)S(1)}, bf16[64,1152]{1,0:T(8,128)(2,1)S(1)}, u32[]{:S(2)}, u32[]{:S(2)}) collective-permute-start(bf16[64,1152]{1,0:T(8,128)(2,1)S(1)} %get-tuple-element.28), channel_id=1, source_target_pairs={{0,64},{64,0},{1,65},{65,1},{2,66},{66,2},{3,67},{67,3},{4,68},{68... | collective-permute-start | bytes 442376 | tf_op jit(solution)/shard_map/ppermute | solution.py:26
  99.2 4.5 %collective-permute-start.11 = (bf16[64,1152]{1,0:T(8,128)(2,1)S(1)}, bf16[64,1152]{1,0:T(8,128)(2,1)S(1)}, u32[]{:S(2)}, u32[]{:S(2)}) collective-permute-start(bf16[64,1152]{1,0:T(8,128)(2,1)S(1)} %get-tuple-element.28), channel_id=1, source_target_pairs={{0,65},{1,64},{64,1},{65,0},{2,67},{3,66},{66,3},{67,2},{4,69},{5,... | collective-permute-start | bytes 442376 | tf_op jit(solution)/shard_map/ppermute | solution.py:26
  103.7 2.5 %collective-permute-start.9 = (bf16[64,1152]{1,0:T(8,128)(2,1)S(1)}, bf16[64,1152]{1,0:T(8,128)(2,1)S(1)}, u32[]{:S(2)}, u32[]{:S(2)}) collective-permute-start(bf16[64,1152]{1,0:T(8,128)(2,1)S(1)} %get-tuple-element.27), channel_id=1, source_target_pairs={{0,1},{1,0},{2,3},{3,2},{4,5},{5,4},{6,7},{7,6},{8,9},{9,8},{10,11... | collective-permute-start | bytes 442376 | tf_op jit(solution)/shard_map/ppermute | solution.py:26
  106.3 4.7 %collective-permute-done.11 = bf16[64,1152]{1,0:T(8,128)(2,1)S(1)} collective-permute-done((bf16[64,1152]{1,0:T(8,128)(2,1)S(1)}, bf16[64,1152]{1,0:T(8,128)(2,1)S(1)}, u32[]{:S(2)}, u32[]{:S(2)}) %collective-permute-start.11) | collective-permute-done | bytes 147488 | tf_op jit(solution)/shard_map/ppermute | solution.py:26
  111.0 3.3 %collective-permute-done.9 = bf16[64,1152]{1,0:T(8,128)(2,1)S(1)} collective-permute-done((bf16[64,1152]{1,0:T(8,128)(2,1)S(1)}, bf16[64,1152]{1,0:T(8,128)(2,1)S(1)}, u32[]{:S(2)}, u32[]{:S(2)}) %collective-permute-start.9) | collective-permute-done | bytes 147488 | tf_op jit(solution)/shard_map/ppermute | solution.py:26
  114.3 0.2 convert_reduce_fusion
  114.5 0.1 multiply_reduce_fusion.1
  114.6 0.1 divide_convert_fusion
  114.8 0.9 broadcast_in_dim.2
  115.6 4.4 %all-to-all-start.2 = ((bf16[4,64,1152]{2,1,0:T(8,128)(2,1)}), bf16[4,64,1152]{2,1,0:T(8,128)(2,1)S(1)}, u32[]{:S(2)}, u32[]{:S(2)}) async-start(bf16[4,64,1152]{2,1,0:T(8,128)(2,1)} %broadcast_in_dim.2), calls=%async_computation.2 | async-start | bytes 1179648 | tf_op jit(solution)/shard_map/all_to_all | solution.py:35
  120.0 0.1 multiply_reduce_fusion.2
  120.1 0.7 divide_convert_fusion.1
  120.9 9.5 %all-to-all-done.2 = bf16[4,64,1152]{2,1,0:T(8,128)(2,1)S(1)} async-done(((bf16[4,64,1152]{2,1,0:T(8,128)(2,1)}), bf16[4,64,1152]{2,1,0:T(8,128)(2,1)S(1)}, u32[]{:S(2)}, u32[]{:S(2)}) %all-to-all-start.2) | async-done | bytes 589856 | tf_op jit(solution)/shard_map/all_to_all | solution.py:35
  130.4 0.8 copy.19
  (42 shorter events, 0.6 us)
Async XLA Ops:
  2.8 18.0 %collective-permute-start = (bf16[64,1152]{1,0:T(8,128)(2,1)}, bf16[64,1152]{1,0:T(8,128)(2,1)S(1)}, u32[]{:S(2)}, u32[]{:S(2)}) collective-permute-start(bf16[64,1152]{1,0:T(8,128)(2,1)} %get-tuple-element.12), channel_id=1, source_target_pairs={{0,64},{64,0},{1,65},{65,1},{2,66},{66,2},{3,67},{67,3},{4,68},{68... | collective-permute-start | bytes 442376 | tf_op jit(solution)/shard_map/ppermute | solution.py:26
  6.1 44.5 %all-to-all-start = ((bf16[16,32,1152]{2,1,0:T(8,128)(2,1)}), bf16[16,32,1152]{2,1,0:T(8,128)(2,1)S(1)}, u32[]{:S(2)}, u32[]{:S(2)}) async-start(bf16[16,32,1152]{2,1,0:T(8,128)(2,1)} %get-tuple-element.13), calls=%async_computation | async-start | bytes 2359296 | tf_op jit(solution)/shard_map/all_to_all | solution.py:35
  20.8 16.5 %copy-start.3 = (bf16[256,1152]{1,0:T(8,128)(2,1)S(1)}, bf16[256,1152]{1,0:T(8,128)(2,1)}, u32[]{:S(2)}) copy-start(bf16[256,1152]{1,0:T(8,128)(2,1)} %image_ref.1) | copy-start | bytes 1769476
  20.8 10.3 %collective-permute-start.1 = (bf16[64,1152]{1,0:T(8,128)(2,1)S(1)}, bf16[64,1152]{1,0:T(8,128)(2,1)S(1)}, u32[]{:S(2)}, u32[]{:S(2)}) collective-permute-start(bf16[64,1152]{1,0:T(8,128)(2,1)S(1)} %collective-permute-done), channel_id=1, source_target_pairs={{0,6},{2,0},{4,2},{6,4},{1,7},{3,1},{5,3},{7,5},{8,14},{10,8},{12,... | collective-permute-start | bytes 442376 | tf_op jit(solution)/shard_map/ppermute | solution.py:31
  25.6 9.9 %collective-permute-start.2 = (bf16[64,1152]{1,0:T(8,128)(2,1)S(1)}, bf16[64,1152]{1,0:T(8,128)(2,1)S(1)}, u32[]{:S(2)}, u32[]{:S(2)}) collective-permute-start(bf16[64,1152]{1,0:T(8,128)(2,1)S(1)} %collective-permute-done), channel_id=1, source_target_pairs={{0,4},{2,6},{4,0},{6,2},{1,5},{3,7},{5,1},{7,3},{8,12},{10,14},{12... | collective-permute-start | bytes 442376 | tf_op jit(solution)/shard_map/ppermute | solution.py:31
  28.3 8.9 %collective-permute-start.3 = (bf16[64,1152]{1,0:T(8,128)(2,1)S(1)}, bf16[64,1152]{1,0:T(8,128)(2,1)S(1)}, u32[]{:S(2)}, u32[]{:S(2)}) collective-permute-start(bf16[64,1152]{1,0:T(8,128)(2,1)S(1)} %collective-permute-done), channel_id=1, source_target_pairs={{0,2},{2,4},{4,6},{6,0},{1,3},{3,5},{5,7},{7,1},{8,10},{10,12},{12... | collective-permute-start | bytes 442376 | tf_op jit(solution)/shard_map/ppermute | solution.py:31
  37.9 2.3 %copy-start.7 = (s32[4]{0:T(128)S(1)}, s32[4]{0:T(128)}, u32[]{:S(2)}) copy-start(s32[4]{0:T(128)} %constant.80.clone) | copy-start | bytes 52
  37.9 5.5 %copy-start.8 = (s32[32]{0:T(128)S(1)}, s32[32]{0:T(128)}, u32[]{:S(2)}) copy-start(s32[32]{0:T(128)} %param.8) | copy-start | bytes 388
  38.3 5.2 %copy-start.2 = (bf16[512,1152]{1,0:T(8,128)(2,1)}, bf16[512,1152]{1,0:T(8,128)(2,1)S(1)}, u32[]{:S(2)}) copy-start(bf16[512,1152]{1,0:T(8,128)(2,1)S(1)} %fusion.1) | copy-start | bytes 3538948
  38.3 5.2 %collective-permute-start.4 = (bf16[512,1152]{1,0:T(8,128)(2,1)S(1)}, bf16[512,1152]{1,0:T(8,128)(2,1)}, u32[]{:S(2)}, u32[]{:S(2)}) collective-permute-start(bf16[512,1152]{1,0:T(8,128)(2,1)S(1)} %fusion.1), channel_id=1, source_target_pairs={{0,8},{8,0},{1,9},{9,1},{2,10},{10,2},{3,11},{11,3},{4,12},{12,4},... | collective-permute-start | bytes 3538952 | tf_op jit(solution)/shard_map/ppermute | solution.py:26
  51.3 4.6 %copy-start = (bf16[512,1152]{1,0:T(8,128)(2,1)}, bf16[512,1152]{1,0:T(8,128)(2,1)S(1)}, u32[]{:S(2)}) copy-start(bf16[512,1152]{1,0:T(8,128)(2,1)S(1)} %fusion.2) | copy-start | bytes 3538948
  53.3 2.6 %copy-start.5 = (bf16[1024,512]{1,0:T(8,128)(2,1)}, bf16[1024,512]{1,0:T(8,128)(2,1)S(1)}, u32[]{:S(2)}) copy-start(bf16[1024,512]{1,0:T(8,128)(2,1)S(1)} %subtract_convert_fusion) | copy-start | bytes 3145732
  55.9 3.8 %copy-start.4 = (bf16[256,1152]{1,0:T(8,128)(2,1)S(1)}, bf16[256,1152]{1,0:T(8,128)(2,1)}, u32[]{:S(2)}) copy-start(bf16[256,1152]{1,0:T(8,128)(2,1)} %image_ref.1) | copy-start | bytes 1769476
  57.7 15.9 %collective-permute-start.5 = (bf16[512,1152]{1,0:T(8,128)(2,1)}, bf16[512,1152]{1,0:T(8,128)(2,1)}, u32[]{:S(2)}, u32[]{:S(2)}) collective-permute-start(bf16[512,1152]{1,0:T(8,128)(2,1)} %convolution_convert_fusion), channel_id=1, source_target_pairs={{0,8},{8,0},{1,9},{9,1},{2,10},{10,2},{3,11},{11,3},{4,12},{12,4},... | collective-permute-start | bytes 3538952 | tf_op jit(solution)/shard_map/ppermute | solution.py:26
  60.0 13.7 %copy-start.1 = (bf16[512,1152]{1,0:T(8,128)(2,1)S(1)}, bf16[512,1152]{1,0:T(8,128)(2,1)}, u32[]{:S(2)}) copy-start(bf16[512,1152]{1,0:T(8,128)(2,1)} %copy-done) | copy-start | bytes 3538948
  60.0 54.4 %all-to-all-start.1 = ((bf16[16,32,1152]{2,1,0:T(8,128)(2,1)}), bf16[16,32,1152]{2,1,0:T(8,128)(2,1)S(1)}, u32[]{:S(2)}, u32[]{:S(2)}) async-start(bf16[16,32,1152]{2,1,0:T(8,128)(2,1)} %bitcast.15), calls=%async_computation.1 | async-start | bytes 2359296 | tf_op jit(solution)/shard_map/all_to_all | solution.py:35
  75.9 12.1 %copy-start.6 = (bf16[32,1152]{1,0:T(8,128)(2,1)S(1)}, bf16[32,1152]{1,0:T(8,128)(2,1)}, u32[]{:S(2)}) copy-start(bf16[32,1152]{1,0:T(8,128)(2,1)} %text_ref.1) | copy-start | bytes 221188
  76.1 13.3 %collective-permute-start.6 = (bf16[128,1152]{1,0:T(8,128)(2,1)S(1)}, bf16[128,1152]{1,0:T(8,128)(2,1)S(1)}, u32[]{:S(2)}, u32[]{:S(2)}) collective-permute-start(bf16[128,1152]{1,0:T(8,128)(2,1)S(1)} %bitcast.44), channel_id=1, source_target_pairs={{0,4},{2,6},{4,0},{6,2},{1,5},{3,7},{5,1},{7,3},{8,12},{10,14},{12... | collective-permute-start | bytes 884744 | tf_op jit(solution)/shard_map/ppermute | solution.py:31
  81.0 13.6 %collective-permute-start.7 = (bf16[128,1152]{1,0:T(8,128)(2,1)S(1)}, bf16[128,1152]{1,0:T(8,128)(2,1)S(1)}, u32[]{:S(2)}, u32[]{:S(2)}) collective-permute-start(bf16[128,1152]{1,0:T(8,128)(2,1)S(1)} %bitcast.43), channel_id=1, source_target_pairs={{0,2},{2,4},{4,6},{6,0},{1,3},{3,5},{5,7},{7,1},{8,10},{10,12},{12... | collective-permute-start | bytes 884744 | tf_op jit(solution)/shard_map/ppermute | solution.py:31
  83.5 11.2 %collective-permute-start.8 = (bf16[128,1152]{1,0:T(8,128)(2,1)S(1)}, bf16[128,1152]{1,0:T(8,128)(2,1)S(1)}, u32[]{:S(2)}, u32[]{:S(2)}) collective-permute-start(bf16[128,1152]{1,0:T(8,128)(2,1)S(1)} %bitcast.42), channel_id=1, source_target_pairs={{0,6},{2,0},{4,2},{6,4},{1,7},{3,1},{5,3},{7,5},{8,14},{10,8},{12,... | collective-permute-start | bytes 884744 | tf_op jit(solution)/shard_map/ppermute | solution.py:31
  94.9 11.3 %collective-permute-start.10 = (bf16[64,1152]{1,0:T(8,128)(2,1)S(1)}, bf16[64,1152]{1,0:T(8,128)(2,1)S(1)}, u32[]{:S(2)}, u32[]{:S(2)}) collective-permute-start(bf16[64,1152]{1,0:T(8,128)(2,1)S(1)} %get-tuple-element.28), channel_id=1, source_target_pairs={{0,64},{64,0},{1,65},{65,1},{2,66},{66,2},{3,67},{67,3},{4,68},{68... | collective-permute-start | bytes 442376 | tf_op jit(solution)/shard_map/ppermute | solution.py:26
  99.2 11.8 %collective-permute-start.11 = (bf16[64,1152]{1,0:T(8,128)(2,1)S(1)}, bf16[64,1152]{1,0:T(8,128)(2,1)S(1)}, u32[]{:S(2)}, u32[]{:S(2)}) collective-permute-start(bf16[64,1152]{1,0:T(8,128)(2,1)S(1)} %get-tuple-element.28), channel_id=1, source_target_pairs={{0,65},{1,64},{64,1},{65,0},{2,67},{3,66},{66,3},{67,2},{4,69},{5,... | collective-permute-start | bytes 442376 | tf_op jit(solution)/shard_map/ppermute | solution.py:26
  103.7 10.6 %collective-permute-start.9 = (bf16[64,1152]{1,0:T(8,128)(2,1)S(1)}, bf16[64,1152]{1,0:T(8,128)(2,1)S(1)}, u32[]{:S(2)}, u32[]{:S(2)}) collective-permute-start(bf16[64,1152]{1,0:T(8,128)(2,1)S(1)} %get-tuple-element.27), channel_id=1, source_target_pairs={{0,1},{1,0},{2,3},{3,2},{4,5},{5,4},{6,7},{7,6},{8,9},{9,8},{10,11... | collective-permute-start | bytes 442376 | tf_op jit(solution)/shard_map/ppermute | solution.py:26
  115.6 14.8 %all-to-all-start.2 = ((bf16[4,64,1152]{2,1,0:T(8,128)(2,1)}), bf16[4,64,1152]{2,1,0:T(8,128)(2,1)S(1)}, u32[]{:S(2)}, u32[]{:S(2)}) async-start(bf16[4,64,1152]{2,1,0:T(8,128)(2,1)} %broadcast_in_dim.2), calls=%async_computation.2 | async-start | bytes 1179648 | tf_op jit(solution)/shard_map/all_to_all | solution.py:35

commit v17 on v15

--- a/solution.py
+++ b/solution.py
@@ -9,7 +9,7 @@
 AXES = ("yh", "yl", "w", "c", "x", "l")
 CLASSES = ((0, 3, 5, 6), (1, 2, 4, 7))
 RINGS = ("yh", "yl", "w", "l")
-TEXT_GROUPS = [[y * 8 + z for z in of_z for y in of_y] for of_y in CLASSES for of_z in CLASSES]
+TEXT_GROUPS = [[y * 8 + z for y in of_y for z in of_z] for of_y in CLASSES for of_z in CLASSES]
 NARROW = ("x", "l")
 BF16, F32 = jnp.bfloat16, jnp.float32
 
@@ -80,7 +80,8 @@
 
     part, copies = first_copies(x.astype(jnp.int32).reshape(1), image_emb, text_emb, quarter, peers)
     part = swap(part, "yl")
-    texts = exchange(copies, RINGS, TEXT_GROUPS).reshape(-1, width)
+    texts = exchange(copies, RINGS, TEXT_GROUPS).reshape(4, 4, mine, width)
+    texts = lax.optimization_barrier(texts.transpose(1, 0, 2, 3).reshape(-1, width))
     around = [part] + [shift(part, "x", n_x - d) for d in range(1, n_x)]
     beyond = in_order(around, x)
     chip = jnp.concatenate([jnp.where(upper, beyond, image_emb), jnp.where(upper, image_emb, beyond)], axis=0)

time: 130 us -> 128 us (0.985)
  waiting for transfers between devices: 25.7 us -> 23.8 us
    ppermute x6, starting transfers between devices: 21.6 us -> 25 us  [swap(): return lax.ppermute(block, axes, [(i, count - 1 - i) for i in range(count)])]
    all_to_all x3, starting transfers between devices: 27.7 us -> 25 us  [exchange(): lax.all_to_all(blocks, axes, 0, 0, axis_index_groups=groups, tiled=True)]
    all_to_all x3, waiting for transfers between devices: 5.2 us -> 3.62 us  [exchange(): lax.all_to_all(blocks, axes, 0, 0, axis_index_groups=groups, tiled=True)]
  transfers between devices with their start and end apart: 18 -> 18, of which waited for: 10 -> 9; matrix products, arithmetic and copies ran while one was open for 6% -> 6% of each run, Pallas kernels for 0% -> 0%
where the time goes in v17:
time: 128 us; the launch traced here: 127 us
  starting transfers between devices  82.4 us (64%)
  waiting for transfers between devices  23.8 us (19%)
  matrix products  9.05 us (7%)
  other arithmetic  5.99 us (5%)
  between operations  2.44 us (2%)
  Pallas kernels  2.18 us (2%)
  local copies, waits for them, and re-layouts  1.4 us (1%)
    ppermute x9, starting transfers between devices, shift(): lax.ppermute(block, axis, [(i, (i + distance) % count) for i in range(cou...  32.4 us
    ppermute x6, starting transfers between devices, swap(): return lax.ppermute(block, axes, [(i, count - 1 - i) for i in range(count)])  25 us
    all_to_all x3, starting transfers between devices, exchange(): lax.all_to_all(blocks, axes, 0, 0, axis_index_groups=groups, tiled=True)  25 us
    ppermute x9, waiting for transfers between devices, shift(): lax.ppermute(block, axis, [(i, (i + distance) % count) for i in range(cou...  18.7 us
    all_to_all x3, waiting for transfers between devices, exchange(): lax.all_to_all(blocks, axes, 0, 0, axis_index_groups=groups, tiled=True)  3.62 us
    dot_general x1, matrix products, local(): lax.dot_general(grad, images, (((0,), (0,)), ((), ())), preferred_element...  2.58 us
  transfers between devices with their start and end apart: 18, of which 9 were waited for; matrix products, arithmetic and copies ran while one was open for 6% of the time, Pallas kernels for 0%

profile of v17, /device:TPU:56, one launch (start us, length us, event | category | flops | bytes accessed | tf_op | source)
XLA Modules:
  0.0 127.2 jit_solution(17023055536229283906)
XLA Ops:
  0.6 2.2 %first_copies.1 = (bf16[64,1152]{1,0:T(8,128)(2,1)}, bf16[16,32,1152]{2,1,0:T(8,128)(2,1)}) custom-call(s32[1]{0:T(128)} %bitcast.1.x_ref, bf16[256,1152]{1,0:T(8,128)(2,1)} %image_ref.1, bf16[32,1152]{1,0:T(8,128)(2,1)} %text_ref.1), custom_call_target="tpu_custom_call" | custom-call | tf_op jit(solution)/shard_map/first_copies/pallas_call | solution.py:53
  2.8 3.2 %collective-permute-start = (bf16[64,1152]{1,0:T(8,128)(2,1)}, bf16[64,1152]{1,0:T(8,128)(2,1)S(1)}, u32[]{:S(2)}, u32[]{:S(2)}) collective-permute-start(bf16[64,1152]{1,0:T(8,128)(2,1)} %get-tuple-element.17), channel_id=1, source_target_pairs={{0,64},{64,0},{1,65},{65,1},{2,66},{66,2},{3,67},{67,3},{4,68},{68... | collective-permute-start | bytes 442376 | tf_op jit(solution)/shard_map/ppermute | solution.py:25
  6.1 14.7 %all-to-all-start = ((bf16[16,32,1152]{2,1,0:T(8,128)(2,1)}), bf16[16,32,1152]{2,1,0:T(8,128)(2,1)S(1)}, u32[]{:S(2)}, u32[]{:S(2)}) async-start(bf16[16,32,1152]{2,1,0:T(8,128)(2,1)} %get-tuple-element.18), calls=%async_computation | async-start | bytes 2359296 | tf_op jit(solution)/shard_map/all_to_all | solution.py:34
  20.8 4.8 %collective-permute-start.1 = (bf16[64,1152]{1,0:T(8,128)(2,1)S(1)}, bf16[64,1152]{1,0:T(8,128)(2,1)S(1)}, u32[]{:S(2)}, u32[]{:S(2)}) collective-permute-start(bf16[64,1152]{1,0:T(8,128)(2,1)S(1)} %collective-permute-done), channel_id=1, source_target_pairs={{0,6},{2,0},{4,2},{6,4},{1,7},{3,1},{5,3},{7,5},{8,14},{10,8},{12,... | collective-permute-start | bytes 442376 | tf_op jit(solution)/shard_map/ppermute | solution.py:30
  25.6 2.7 %collective-permute-start.2 = (bf16[64,1152]{1,0:T(8,128)(2,1)S(1)}, bf16[64,1152]{1,0:T(8,128)(2,1)S(1)}, u32[]{:S(2)}, u32[]{:S(2)}) collective-permute-start(bf16[64,1152]{1,0:T(8,128)(2,1)S(1)} %collective-permute-done), channel_id=1, source_target_pairs={{0,4},{2,6},{4,0},{6,2},{1,5},{3,7},{5,1},{7,3},{8,12},{10,14},{12... | collective-permute-start | bytes 442376 | tf_op jit(solution)/shard_map/ppermute | solution.py:30
  28.3 2.8 %collective-permute-start.3 = (bf16[64,1152]{1,0:T(8,128)(2,1)S(1)}, bf16[64,1152]{1,0:T(8,128)(2,1)S(1)}, u32[]{:S(2)}, u32[]{:S(2)}) collective-permute-start(bf16[64,1152]{1,0:T(8,128)(2,1)S(1)} %collective-permute-done), channel_id=1, source_target_pairs={{0,2},{2,4},{4,6},{6,0},{1,3},{3,5},{5,7},{7,1},{8,10},{10,12},{12... | collective-permute-start | bytes 442376 | tf_op jit(solution)/shard_map/ppermute | solution.py:30
  31.2 4.3 %collective-permute-done.2 = bf16[64,1152]{1,0:T(8,128)(2,1)S(1)} collective-permute-done((bf16[64,1152]{1,0:T(8,128)(2,1)S(1)}, bf16[64,1152]{1,0:T(8,128)(2,1)S(1)}, u32[]{:S(2)}, u32[]{:S(2)}) %collective-permute-start.2) | collective-permute-done | bytes 147488 | tf_op jit(solution)/shard_map/ppermute | solution.py:30
  35.5 1.7 %collective-permute-done.3 = bf16[64,1152]{1,0:T(8,128)(2,1)S(1)} collective-permute-done((bf16[64,1152]{1,0:T(8,128)(2,1)S(1)}, bf16[64,1152]{1,0:T(8,128)(2,1)S(1)}, u32[]{:S(2)}, u32[]{:S(2)}) %collective-permute-start.3) | collective-permute-done | bytes 147488 | tf_op jit(solution)/shard_map/ppermute | solution.py:30
  37.3 0.2 broadcast_select_fusion.1
  37.6 0.3 fusion
  37.9 0.4 fusion.1
  38.3 1.9 %collective-permute-start.4 = (bf16[512,1152]{1,0:T(8,128)(2,1)S(1)}, bf16[512,1152]{1,0:T(8,128)(2,1)}, u32[]{:S(2)}, u32[]{:S(2)}) collective-permute-start(bf16[512,1152]{1,0:T(8,128)(2,1)S(1)} %fusion.1), channel_id=1, source_target_pairs={{0,8},{8,0},{1,9},{9,1},{2,10},{10,2},{3,11},{11,3},{4,12},{12,4},... | collective-permute-start | bytes 3538952 | tf_op jit(solution)/shard_map/ppermute | solution.py:25
  41.6 0.1 add_dynamic-update-slice_fusion
  41.7 1.5 %collective-permute-done.4 = bf16[512,1152]{1,0:T(8,128)(2,1)} collective-permute-done((bf16[512,1152]{1,0:T(8,128)(2,1)S(1)}, bf16[512,1152]{1,0:T(8,128)(2,1)}, u32[]{:S(2)}, u32[]{:S(2)}) %collective-permute-start.4) | collective-permute-done | bytes 1179680 | tf_op jit(solution)/shard_map/ppermute | solution.py:25
  43.1 1.8 %pad_maximum_fusion = bf16[1024,1152]{1,0:T(8,128)(2,1)S(1)} fusion(bf16[512,1152]{1,0:T(8,128)(2,1)} %collective-permute-done.4, bf16[512,1152]{1,0:T(8,128)(2,1)} %copy-done.2), kind=kLoop, calls=%fused_computation.10 | loop fusion | flops 4718592 | bytes 4718592 | tf_op jit(solution)/shard_map/concatenate | solution.py:103
  44.9 3.6 %all-to-all-done = bf16[16,32,1152]{2,1,0:T(8,128)(2,1)S(1)} async-done(((bf16[16,32,1152]{2,1,0:T(8,128)(2,1)}), bf16[16,32,1152]{2,1,0:T(8,128)(2,1)S(1)}, u32[]{:S(2)}, u32[]{:S(2)}) %all-to-all-start) | async-done | bytes 1179680 | tf_op jit(solution)/shard_map/all_to_all | solution.py:34
  48.6 0.1 copy.10
  48.7 0.3 fusion.2
  49.0 2.1 %subtract_convert_fusion = bf16[1024,512]{1,0:T(8,128)(2,1)S(1)} fusion(bf16[1024,1152]{1,0:T(8,128)(2,1)S(1)} %pad_maximum_fusion, s32[512]{0:T(512)S(1)} %add_dynamic-update-slice_fusion, f32[]{:T(128)} %bitcast.37, f32[]{:T(128)} %bitcast, bf16[512,1152]{1,0:T(8,128)(2,1)S(1)} %bitcast.40, f32[512]{0:T(512)S(1)} %add_sqrt_fusion), kind=kOutput, calls=%fused_computation.12 | convolution fusion | flops 1214447616 | bytes 4591624 | tf_op jit(solution)/shard_map/dot_general | solution.py:104
  51.1 2.6 %convolution_convert_fusion.1 = bf16[512,1152]{1,0:T(8,128)(2,1)} fusion(bf16[1024,512]{1,0:T(8,128)(2,1)S(1)} %subtract_convert_fusion, bf16[1024,1152]{1,0:T(8,128)(2,1)S(1)} %pad_maximum_fusion), kind=kOutput, calls=%fused_computation.1 | convolution fusion | flops 1208549376 | bytes 4587520 | tf_op jit(solution)/shard_map/dot_general | solution.py:106
  53.7 2.0 %convolution_convert_fusion = bf16[512,1152]{1,0:T(8,128)(2,1)} fusion(bf16[1024,512]{1,0:T(8,128)(2,1)S(1)} %subtract_convert_fusion, bf16[512,1152]{1,0:T(8,128)(2,1)S(1)} %bitcast.41, f32[512]{0:T(512)S(1)} %add_sqrt_fusion), kind=kOutput, calls=%fused_computation | convolution fusion | flops 606339072 | bytes 2885632 | tf_op jit(solution)/shard_map/dot_general | solution.py:111
  55.7 1.9 %collective-permute-start.5 = (bf16[512,1152]{1,0:T(8,128)(2,1)}, bf16[512,1152]{1,0:T(8,128)(2,1)}, u32[]{:S(2)}, u32[]{:S(2)}) collective-permute-start(bf16[512,1152]{1,0:T(8,128)(2,1)} %convolution_convert_fusion), channel_id=1, source_target_pairs={{0,8},{8,0},{1,9},{9,1},{2,10},{10,2},{3,11},{11,3},{4,12},{12,4},... | collective-permute-start | bytes 3538952 | tf_op jit(solution)/shard_map/ppermute | solution.py:25
  57.6 0.1 fusion.10
  57.8 0.1 convert_divide_fusion.2
  57.9 4.9 %all-to-all-start.1 = ((bf16[4,128,1152]{2,1,0:T(8,128)(2,1)}), bf16[4,128,1152]{2,1,0:T(8,128)(2,1)S(1)}, u32[]{:S(2)}, u32[]{:S(2)}) async-start(bf16[4,128,1152]{2,1,0:T(8,128)(2,1)} %bitcast.16), calls=%async_computation.1 | async-start | bytes 2359296 | tf_op jit(solution)/shard_map/all_to_all | solution.py:34
  62.8 2.4 %add_convert_fusion = bf16[512,1152]{1,0:T(8,128)(2,1)S(1)} fusion(bf16[512,1152]{1,0:T(8,128)(2,1)} %collective-permute-done.5, bf16[1024,512]{1,0:T(8,128)(2,1)} %copy-done.5, bf16[512,1152]{1,0:T(8,128)(2,1)S(1)} %bitcast.42, f32[512]{0:T(512)S(1)} %add_sqrt_fusion), kind=kOutput, calls=%fused_computation.11 | convolution fusion | flops 607518720 | bytes 4065280 | tf_op jit(solution)/shard_map/dot_general | solution.py:113
  65.3 4.9 %collective-permute-start.6 = (bf16[128,1152]{1,0:T(8,128)(2,1)S(1)}, bf16[128,1152]{1,0:T(8,128)(2,1)S(1)}, u32[]{:S(2)}, u32[]{:S(2)}) collective-permute-start(bf16[128,1152]{1,0:T(8,128)(2,1)S(1)} %bitcast.47), channel_id=1, source_target_pairs={{0,4},{2,6},{4,0},{6,2},{1,5},{3,7},{5,1},{7,3},{8,12},{10,14},{12... | collective-permute-start | bytes 884744 | tf_op jit(solution)/shard_map/ppermute | solution.py:30
  70.2 2.5 %collective-permute-start.7 = (bf16[128,1152]{1,0:T(8,128)(2,1)S(1)}, bf16[128,1152]{1,0:T(8,128)(2,1)S(1)}, u32[]{:S(2)}, u32[]{:S(2)}) collective-permute-start(bf16[128,1152]{1,0:T(8,128)(2,1)S(1)} %bitcast.46), channel_id=1, source_target_pairs={{0,2},{2,4},{4,6},{6,0},{1,3},{3,5},{5,7},{7,1},{8,10},{10,12},{12... | collective-permute-start | bytes 884744 | tf_op jit(solution)/shard_map/ppermute | solution.py:30
  72.7 4.5 %collective-permute-start.8 = (bf16[128,1152]{1,0:T(8,128)(2,1)S(1)}, bf16[128,1152]{1,0:T(8,128)(2,1)S(1)}, u32[]{:S(2)}, u32[]{:S(2)}) collective-permute-start(bf16[128,1152]{1,0:T(8,128)(2,1)S(1)} %bitcast.45), channel_id=1, source_target_pairs={{0,6},{2,0},{4,2},{6,4},{1,7},{3,1},{5,3},{7,5},{8,14},{10,8},{12,... | collective-permute-start | bytes 884744 | tf_op jit(solution)/shard_map/ppermute | solution.py:30
  77.3 0.1 fusion.11
  77.4 1.1 collective-permute-done.6
  78.5 5.6 %collective-permute-done.7 = bf16[128,1152]{1,0:T(8,128)(2,1)S(1)} collective-permute-done((bf16[128,1152]{1,0:T(8,128)(2,1)S(1)}, bf16[128,1152]{1,0:T(8,128)(2,1)S(1)}, u32[]{:S(2)}, u32[]{:S(2)}) %collective-permute-start.7) | collective-permute-done | bytes 294944 | tf_op jit(solution)/shard_map/ppermute | solution.py:30
  84.2 0.2 fusion.4
  84.4 9.1 %collective-permute-start.10 = (bf16[64,1152]{1,0:T(8,128)(2,1)S(1)}, bf16[64,1152]{1,0:T(8,128)(2,1)S(1)}, u32[]{:S(2)}, u32[]{:S(2)}) collective-permute-start(bf16[64,1152]{1,0:T(8,128)(2,1)S(1)} %get-tuple-element.21), channel_id=1, source_target_pairs={{0,64},{64,0},{1,65},{65,1},{2,66},{66,2},{3,67},{67,3},{4,68},{68... | collective-permute-start | bytes 442376 | tf_op jit(solution)/shard_map/ppermute | solution.py:25
  93.6 1.9 %collective-permute-start.9 = (bf16[64,1152]{1,0:T(8,128)(2,1)S(1)}, bf16[64,1152]{1,0:T(8,128)(2,1)S(1)}, u32[]{:S(2)}, u32[]{:S(2)}) collective-permute-start(bf16[64,1152]{1,0:T(8,128)(2,1)S(1)} %get-tuple-element.37), channel_id=1, source_target_pairs={{0,1},{1,0},{2,3},{3,2},{4,5},{5,4},{6,7},{7,6},{8,9},{9,8},{10,11... | collective-permute-start | bytes 442376 | tf_op jit(solution)/shard_map/ppermute | solution.py:25
  95.5 6.9 %collective-permute-start.11 = (bf16[64,1152]{1,0:T(8,128)(2,1)S(1)}, bf16[64,1152]{1,0:T(8,128)(2,1)S(1)}, u32[]{:S(2)}, u32[]{:S(2)}) collective-permute-start(bf16[64,1152]{1,0:T(8,128)(2,1)S(1)} %get-tuple-element.21), channel_id=1, source_target_pairs={{0,65},{1,64},{64,1},{65,0},{2,67},{3,66},{66,3},{67,2},{4,69},{5,... | collective-permute-start | bytes 442376 | tf_op jit(solution)/shard_map/ppermute | solution.py:25
  102.5 1.0 reduce_sum.84
  103.5 5.4 %all-to-all-start.2 = ((bf16[4,32,1152]{2,1,0:T(8,128)(2,1)}), bf16[4,32,1152]{2,1,0:T(8,128)(2,1)S(1)}, u32[]{:S(2)}, u32[]{:S(2)}) async-start(bf16[4,32,1152]{2,1,0:T(8,128)(2,1)} %bitcast.20), calls=%async_computation.2 | async-start | bytes 589824 | tf_op jit(solution)/shard_map/all_to_all | solution.py:34
  108.9 0.2 multiply_reduce_fusion
  109.1 0.1 divide_convert_fusion
  109.2 4.7 %collective-permute-start.12 = (bf16[64,1152]{1,0:T(8,128)(2,1)S(1)}, bf16[64,1152]{1,0:T(8,128)(2,1)S(1)}, u32[]{:S(2)}, u32[]{:S(2)}) collective-permute-start(bf16[64,1152]{1,0:T(8,128)(2,1)S(1)} %divide_convert_fusion), channel_id=1, source_target_pairs={{0,6},{2,0},{4,2},{6,4},{1,7},{3,1},{5,3},{7,5},{8,14},{10,8},{12,... | collective-permute-start | bytes 442376 | tf_op jit(solution)/shard_map/ppermute | solution.py:30
  113.9 2.7 %collective-permute-start.13 = (bf16[64,1152]{1,0:T(8,128)(2,1)S(1)}, bf16[64,1152]{1,0:T(8,128)(2,1)S(1)}, u32[]{:S(2)}, u32[]{:S(2)}) collective-permute-start(bf16[64,1152]{1,0:T(8,128)(2,1)S(1)} %divide_convert_fusion), channel_id=1, source_target_pairs={{0,4},{2,6},{4,0},{6,2},{1,5},{3,7},{5,1},{7,3},{8,12},{10,14},{12... | collective-permute-start | bytes 442376 | tf_op jit(solution)/shard_map/ppermute | solution.py:30
  116.6 2.8 %collective-permute-start.14 = (bf16[64,1152]{1,0:T(8,128)(2,1)S(1)}, bf16[64,1152]{1,0:T(8,128)(2,1)S(1)}, u32[]{:S(2)}, u32[]{:S(2)}) collective-permute-start(bf16[64,1152]{1,0:T(8,128)(2,1)S(1)} %divide_convert_fusion), channel_id=1, source_target_pairs={{0,2},{2,4},{4,6},{6,0},{1,3},{3,5},{5,7},{7,1},{8,10},{10,12},{12... | collective-permute-start | bytes 442376 | tf_op jit(solution)/shard_map/ppermute | solution.py:30
  119.4 4.1 %collective-permute-done.13 = bf16[64,1152]{1,0:T(8,128)(2,1)S(1)} collective-permute-done((bf16[64,1152]{1,0:T(8,128)(2,1)S(1)}, bf16[64,1152]{1,0:T(8,128)(2,1)S(1)}, u32[]{:S(2)}, u32[]{:S(2)}) %collective-permute-start.13) | collective-permute-done | bytes 147488 | tf_op jit(solution)/shard_map/ppermute | solution.py:30
  123.5 1.7 %collective-permute-done.14 = bf16[64,1152]{1,0:T(8,128)(2,1)S(1)} collective-permute-done((bf16[64,1152]{1,0:T(8,128)(2,1)S(1)}, bf16[64,1152]{1,0:T(8,128)(2,1)S(1)}, u32[]{:S(2)}, u32[]{:S(2)}) %collective-permute-start.14) | collective-permute-done | bytes 147488 | tf_op jit(solution)/shard_map/ppermute | solution.py:30
  125.5 0.9 constant_dynamic-slice_fusion
  126.4 0.1 multiply_reduce_fusion.1
  126.5 0.7 divide_convert_fusion.1
  (51 shorter events, 0.7 us)
Async XLA Ops:
  2.8 18.0 %collective-permute-start = (bf16[64,1152]{1,0:T(8,128)(2,1)}, bf16[64,1152]{1,0:T(8,128)(2,1)S(1)}, u32[]{:S(2)}, u32[]{:S(2)}) collective-permute-start(bf16[64,1152]{1,0:T(8,128)(2,1)} %get-tuple-element.17), channel_id=1, source_target_pairs={{0,64},{64,0},{1,65},{65,1},{2,66},{66,2},{3,67},{67,3},{4,68},{68... | collective-permute-start | bytes 442376 | tf_op jit(solution)/shard_map/ppermute | solution.py:25
  6.1 42.5 %all-to-all-start = ((bf16[16,32,1152]{2,1,0:T(8,128)(2,1)}), bf16[16,32,1152]{2,1,0:T(8,128)(2,1)S(1)}, u32[]{:S(2)}, u32[]{:S(2)}) async-start(bf16[16,32,1152]{2,1,0:T(8,128)(2,1)} %get-tuple-element.18), calls=%async_computation | async-start | bytes 2359296 | tf_op jit(solution)/shard_map/all_to_all | solution.py:34
  20.8 16.5 %copy-start.3 = (bf16[256,1152]{1,0:T(8,128)(2,1)S(1)}, bf16[256,1152]{1,0:T(8,128)(2,1)}, u32[]{:S(2)}) copy-start(bf16[256,1152]{1,0:T(8,128)(2,1)} %image_ref.1) | copy-start | bytes 1769476
  20.8 10.3 %collective-permute-start.1 = (bf16[64,1152]{1,0:T(8,128)(2,1)S(1)}, bf16[64,1152]{1,0:T(8,128)(2,1)S(1)}, u32[]{:S(2)}, u32[]{:S(2)}) collective-permute-start(bf16[64,1152]{1,0:T(8,128)(2,1)S(1)} %collective-permute-done), channel_id=1, source_target_pairs={{0,6},{2,0},{4,2},{6,4},{1,7},{3,1},{5,3},{7,5},{8,14},{10,8},{12,... | collective-permute-start | bytes 442376 | tf_op jit(solution)/shard_map/ppermute | solution.py:30
  25.6 9.9 %collective-permute-start.2 = (bf16[64,1152]{1,0:T(8,128)(2,1)S(1)}, bf16[64,1152]{1,0:T(8,128)(2,1)S(1)}, u32[]{:S(2)}, u32[]{:S(2)}) collective-permute-start(bf16[64,1152]{1,0:T(8,128)(2,1)S(1)} %collective-permute-done), channel_id=1, source_target_pairs={{0,4},{2,6},{4,0},{6,2},{1,5},{3,7},{5,1},{7,3},{8,12},{10,14},{12... | collective-permute-start | bytes 442376 | tf_op jit(solution)/shard_map/ppermute | solution.py:30
  28.3 8.9 %collective-permute-start.3 = (bf16[64,1152]{1,0:T(8,128)(2,1)S(1)}, bf16[64,1152]{1,0:T(8,128)(2,1)S(1)}, u32[]{:S(2)}, u32[]{:S(2)}) collective-permute-start(bf16[64,1152]{1,0:T(8,128)(2,1)S(1)} %collective-permute-done), channel_id=1, source_target_pairs={{0,2},{2,4},{4,6},{6,0},{1,3},{3,5},{5,7},{7,1},{8,10},{10,12},{12... | collective-permute-start | bytes 442376 | tf_op jit(solution)/shard_map/ppermute | solution.py:30
  37.9 3.7 %copy-start.7 = (s32[32]{0:T(128)S(1)}, s32[32]{0:T(128)}, u32[]{:S(2)}) copy-start(s32[32]{0:T(128)} %param.7) | copy-start | bytes 388
  38.3 3.4 %copy-start.2 = (bf16[512,1152]{1,0:T(8,128)(2,1)}, bf16[512,1152]{1,0:T(8,128)(2,1)S(1)}, u32[]{:S(2)}) copy-start(bf16[512,1152]{1,0:T(8,128)(2,1)S(1)} %fusion.1) | copy-start | bytes 3538948
  38.3 4.9 %collective-permute-start.4 = (bf16[512,1152]{1,0:T(8,128)(2,1)S(1)}, bf16[512,1152]{1,0:T(8,128)(2,1)}, u32[]{:S(2)}, u32[]{:S(2)}) collective-permute-start(bf16[512,1152]{1,0:T(8,128)(2,1)S(1)} %fusion.1), channel_id=1, source_target_pairs={{0,8},{8,0},{1,9},{9,1},{2,10},{10,2},{3,11},{11,3},{4,12},{12,4},... | collective-permute-start | bytes 3538952 | tf_op jit(solution)/shard_map/ppermute | solution.py:25
  48.7 5.0 %copy-start = (bf16[4,4,32,1152]{3,2,0,1:T(8,128)(2,1)}, bf16[4,4,32,1152]{3,2,0,1:T(8,128)(2,1)S(1)}, u32[]{:S(2)}) copy-start(bf16[4,4,32,1152]{3,2,0,1:T(8,128)(2,1)S(1)} %copy.10) | copy-start | bytes 3538948
  51.1 2.6 %copy-start.5 = (bf16[1024,512]{1,0:T(8,128)(2,1)}, bf16[1024,512]{1,0:T(8,128)(2,1)S(1)}, u32[]{:S(2)}) copy-start(bf16[1024,512]{1,0:T(8,128)(2,1)S(1)} %subtract_convert_fusion) | copy-start | bytes 3145732
  53.7 4.0 %copy-start.4 = (bf16[256,1152]{1,0:T(8,128)(2,1)S(1)}, bf16[256,1152]{1,0:T(8,128)(2,1)}, u32[]{:S(2)}) copy-start(bf16[256,1152]{1,0:T(8,128)(2,1)} %image_ref.1) | copy-start | bytes 1769476
  55.7 7.1 %collective-permute-start.5 = (bf16[512,1152]{1,0:T(8,128)(2,1)}, bf16[512,1152]{1,0:T(8,128)(2,1)}, u32[]{:S(2)}, u32[]{:S(2)}) collective-permute-start(bf16[512,1152]{1,0:T(8,128)(2,1)} %convolution_convert_fusion), channel_id=1, source_target_pairs={{0,8},{8,0},{1,9},{9,1},{2,10},{10,2},{3,11},{11,3},{4,12},{12,4},... | collective-permute-start | bytes 3538952 | tf_op jit(solution)/shard_map/ppermute | solution.py:25
  57.9 4.9 %copy-start.1 = (bf16[4,4,32,1152]{3,2,0,1:T(8,128)(2,1)S(1)}, bf16[4,4,32,1152]{3,2,0,1:T(8,128)(2,1)}, u32[]{:S(2)}) copy-start(bf16[4,4,32,1152]{3,2,0,1:T(8,128)(2,1)} %copy-done) | copy-start | bytes 3538948
  57.9 37.6 %all-to-all-start.1 = ((bf16[4,128,1152]{2,1,0:T(8,128)(2,1)}), bf16[4,128,1152]{2,1,0:T(8,128)(2,1)S(1)}, u32[]{:S(2)}, u32[]{:S(2)}) async-start(bf16[4,128,1152]{2,1,0:T(8,128)(2,1)} %bitcast.16), calls=%async_computation.1 | async-start | bytes 2359296 | tf_op jit(solution)/shard_map/all_to_all | solution.py:34
  65.2 12.1 %copy-start.6 = (bf16[32,1152]{1,0:T(8,128)(2,1)S(1)}, bf16[32,1152]{1,0:T(8,128)(2,1)}, u32[]{:S(2)}) copy-start(bf16[32,1152]{1,0:T(8,128)(2,1)} %text_ref.1) | copy-start | bytes 221188
  65.3 13.2 %collective-permute-start.6 = (bf16[128,1152]{1,0:T(8,128)(2,1)S(1)}, bf16[128,1152]{1,0:T(8,128)(2,1)S(1)}, u32[]{:S(2)}, u32[]{:S(2)}) collective-permute-start(bf16[128,1152]{1,0:T(8,128)(2,1)S(1)} %bitcast.47), channel_id=1, source_target_pairs={{0,4},{2,6},{4,0},{6,2},{1,5},{3,7},{5,1},{7,3},{8,12},{10,14},{12... | collective-permute-start | bytes 884744 | tf_op jit(solution)/shard_map/ppermute | solution.py:30
  70.2 13.9 %collective-permute-start.7 = (bf16[128,1152]{1,0:T(8,128)(2,1)S(1)}, bf16[128,1152]{1,0:T(8,128)(2,1)S(1)}, u32[]{:S(2)}, u32[]{:S(2)}) collective-permute-start(bf16[128,1152]{1,0:T(8,128)(2,1)S(1)} %bitcast.46), channel_id=1, source_target_pairs={{0,2},{2,4},{4,6},{6,0},{1,3},{3,5},{5,7},{7,1},{8,10},{10,12},{12... | collective-permute-start | bytes 884744 | tf_op jit(solution)/shard_map/ppermute | solution.py:30
  72.7 11.5 %collective-permute-start.8 = (bf16[128,1152]{1,0:T(8,128)(2,1)S(1)}, bf16[128,1152]{1,0:T(8,128)(2,1)S(1)}, u32[]{:S(2)}, u32[]{:S(2)}) collective-permute-start(bf16[128,1152]{1,0:T(8,128)(2,1)S(1)} %bitcast.45), channel_id=1, source_target_pairs={{0,6},{2,0},{4,2},{6,4},{1,7},{3,1},{5,3},{7,5},{8,14},{10,8},{12,... | collective-permute-start | bytes 884744 | tf_op jit(solution)/shard_map/ppermute | solution.py:30
  84.4 24.4 %collective-permute-start.10 = (bf16[64,1152]{1,0:T(8,128)(2,1)S(1)}, bf16[64,1152]{1,0:T(8,128)(2,1)S(1)}, u32[]{:S(2)}, u32[]{:S(2)}) collective-permute-start(bf16[64,1152]{1,0:T(8,128)(2,1)S(1)} %get-tuple-element.21), channel_id=1, source_target_pairs={{0,64},{64,0},{1,65},{65,1},{2,66},{66,2},{3,67},{67,3},{4,68},{68... | collective-permute-start | bytes 442376 | tf_op jit(solution)/shard_map/ppermute | solution.py:25
  93.6 15.3 %collective-permute-start.9 = (bf16[64,1152]{1,0:T(8,128)(2,1)S(1)}, bf16[64,1152]{1,0:T(8,128)(2,1)S(1)}, u32[]{:S(2)}, u32[]{:S(2)}) collective-permute-start(bf16[64,1152]{1,0:T(8,128)(2,1)S(1)} %get-tuple-element.37), channel_id=1, source_target_pairs={{0,1},{1,0},{2,3},{3,2},{4,5},{5,4},{6,7},{7,6},{8,9},{9,8},{10,11... | collective-permute-start | bytes 442376 | tf_op jit(solution)/shard_map/ppermute | solution.py:25
  95.5 13.3 %collective-permute-start.11 = (bf16[64,1152]{1,0:T(8,128)(2,1)S(1)}, bf16[64,1152]{1,0:T(8,128)(2,1)S(1)}, u32[]{:S(2)}, u32[]{:S(2)}) collective-permute-start(bf16[64,1152]{1,0:T(8,128)(2,1)S(1)} %get-tuple-element.21), channel_id=1, source_target_pairs={{0,65},{1,64},{64,1},{65,0},{2,67},{3,66},{66,3},{67,2},{4,69},{5,... | collective-permute-start | bytes 442376 | tf_op jit(solution)/shard_map/ppermute | solution.py:25
  103.5 21.8 %all-to-all-start.2 = ((bf16[4,32,1152]{2,1,0:T(8,128)(2,1)}), bf16[4,32,1152]{2,1,0:T(8,128)(2,1)S(1)}, u32[]{:S(2)}, u32[]{:S(2)}) async-start(bf16[4,32,1152]{2,1,0:T(8,128)(2,1)} %bitcast.20), calls=%async_computation.2 | async-start | bytes 589824 | tf_op jit(solution)/shard_map/all_to_all | solution.py:34
  109.2 10.2 %collective-permute-start.12 = (bf16[64,1152]{1,0:T(8,128)(2,1)S(1)}, bf16[64,1152]{1,0:T(8,128)(2,1)S(1)}, u32[]{:S(2)}, u32[]{:S(2)}) collective-permute-start(bf16[64,1152]{1,0:T(8,128)(2,1)S(1)} %divide_convert_fusion), channel_id=1, source_target_pairs={{0,6},{2,0},{4,2},{6,4},{1,7},{3,1},{5,3},{7,5},{8,14},{10,8},{12,... | collective-permute-start | bytes 442376 | tf_op jit(solution)/shard_map/ppermute | solution.py:30
  113.9 9.6 %collective-permute-start.13 = (bf16[64,1152]{1,0:T(8,128)(2,1)S(1)}, bf16[64,1152]{1,0:T(8,128)(2,1)S(1)}, u32[]{:S(2)}, u32[]{:S(2)}) collective-permute-start(bf16[64,1152]{1,0:T(8,128)(2,1)S(1)} %divide_convert_fusion), channel_id=1, source_target_pairs={{0,4},{2,6},{4,0},{6,2},{1,5},{3,7},{5,1},{7,3},{8,12},{10,14},{12... | collective-permute-start | bytes 442376 | tf_op jit(solution)/shard_map/ppermute | solution.py:30
  116.6 8.7 %collective-permute-start.14 = (bf16[64,1152]{1,0:T(8,128)(2,1)S(1)}, bf16[64,1152]{1,0:T(8,128)(2,1)S(1)}, u32[]{:S(2)}, u32[]{:S(2)}) collective-permute-start(bf16[64,1152]{1,0:T(8,128)(2,1)S(1)} %divide_convert_fusion), channel_id=1, source_target_pairs={{0,2},{2,4},{4,6},{6,0},{1,3},{3,5},{5,7},{7,1},{8,10},{10,12},{12... | collective-permute-start | bytes 442376 | tf_op jit(solution)/shard_map/ppermute | solution.py:30

commit v18 on v17

--- a/solution.py
+++ b/solution.py
@@ -129,10 +129,11 @@
     text_sum = exchange(text_sum, ("yh", "yl"), CLASSES)
     image_sum = (own.astype(F32) + beside.astype(F32)) + (across.astype(F32) + corner.astype(F32))
     done = finish(image_sum[None], image_unit, image_norm, scale)
-    around = [done] + [shift(done, "x", n_x - d) for d in range(1, n_x)]
-    around, text_sum = lax.optimization_barrier((around, text_sum))
+    around = {d: shift(done, "x", n_x - d) for d in (2, 1, 3)}
+    around = [done] + [around[d] for d in range(1, n_x)]
+    grad_text = finish(text_sum, text_unit, text_norm, scale)
+    around, grad_text = lax.optimization_barrier((around, grad_text))
     grad_image = in_order(around, x)
-    grad_text = finish(text_sum, text_unit, text_norm, scale)
     return grad_image, grad_text
 
 

time: 128 us -> 127 us (level)
  transfers between devices with their start and end apart: 18 -> 18, of which waited for: 9 -> 9; matrix products, arithmetic and copies ran while one was open for 6% -> 7% of each run, Pallas kernels for 0% -> 0%
where the time goes in v18:
time: 127 us; the launch traced here: 126 us
  starting transfers between devices  82.4 us (65%)
  waiting for transfers between devices  22.9 us (18%)
  matrix products  9.05 us (7%)
  other arithmetic  5.98 us (5%)
  between operations  2.43 us (2%)
  Pallas kernels  2.18 us (2%)
  local copies, waits for them, and re-layouts  1.4 us (1%)
    ppermute x9, starting transfers between devices, shift(): lax.ppermute(block, axis, [(i, (i + distance) % count) for i in range(cou...  32.4 us
    ppermute x6, starting transfers between devices, swap(): return lax.ppermute(block, axes, [(i, count - 1 - i) for i in range(count)])  25 us
    all_to_all x3, starting transfers between devices, exchange(): lax.all_to_all(blocks, axes, 0, 0, axis_index_groups=groups, tiled=True)  25 us
    ppermute x9, waiting for transfers between devices, shift(): lax.ppermute(block, axis, [(i, (i + distance) % count) for i in range(cou...  17.8 us
    all_to_all x3, waiting for transfers between devices, exchange(): lax.all_to_all(blocks, axes, 0, 0, axis_index_groups=groups, tiled=True)  3.62 us
    dot_general x1, matrix products, local(): lax.dot_general(grad, images, (((0,), (0,)), ((), ())), preferred_element...  2.58 us
  transfers between devices with their start and end apart: 18, of which 9 were waited for; matrix products, arithmetic and copies ran while one was open for 7% of the time, Pallas kernels for 0%

profile of v18, /device:TPU:56, one launch (start us, length us, event | category | flops | bytes accessed | tf_op | source)
XLA Modules:
  0.0 126.3 jit_solution(4412993669082560769)
XLA Ops:
  0.6 2.2 %first_copies.1 = (bf16[64,1152]{1,0:T(8,128)(2,1)}, bf16[16,32,1152]{2,1,0:T(8,128)(2,1)}) custom-call(s32[1]{0:T(128)} %bitcast.1.x_ref, bf16[256,1152]{1,0:T(8,128)(2,1)} %image_ref.1, bf16[32,1152]{1,0:T(8,128)(2,1)} %text_ref.1), custom_call_target="tpu_custom_call" | custom-call | tf_op jit(solution)/shard_map/first_copies/pallas_call | solution.py:53
  2.8 3.2 %collective-permute-start = (bf16[64,1152]{1,0:T(8,128)(2,1)}, bf16[64,1152]{1,0:T(8,128)(2,1)S(1)}, u32[]{:S(2)}, u32[]{:S(2)}) collective-permute-start(bf16[64,1152]{1,0:T(8,128)(2,1)} %get-tuple-element.17), channel_id=1, source_target_pairs={{0,64},{64,0},{1,65},{65,1},{2,66},{66,2},{3,67},{67,3},{4,68},{68... | collective-permute-start | bytes 442376 | tf_op jit(solution)/shard_map/ppermute | solution.py:25
  6.1 14.7 %all-to-all-start = ((bf16[16,32,1152]{2,1,0:T(8,128)(2,1)}), bf16[16,32,1152]{2,1,0:T(8,128)(2,1)S(1)}, u32[]{:S(2)}, u32[]{:S(2)}) async-start(bf16[16,32,1152]{2,1,0:T(8,128)(2,1)} %get-tuple-element.18), calls=%async_computation | async-start | bytes 2359296 | tf_op jit(solution)/shard_map/all_to_all | solution.py:34
  20.8 4.8 %collective-permute-start.1 = (bf16[64,1152]{1,0:T(8,128)(2,1)S(1)}, bf16[64,1152]{1,0:T(8,128)(2,1)S(1)}, u32[]{:S(2)}, u32[]{:S(2)}) collective-permute-start(bf16[64,1152]{1,0:T(8,128)(2,1)S(1)} %collective-permute-done), channel_id=1, source_target_pairs={{0,6},{2,0},{4,2},{6,4},{1,7},{3,1},{5,3},{7,5},{8,14},{10,8},{12,... | collective-permute-start | bytes 442376 | tf_op jit(solution)/shard_map/ppermute | solution.py:30
  25.6 2.7 %collective-permute-start.2 = (bf16[64,1152]{1,0:T(8,128)(2,1)S(1)}, bf16[64,1152]{1,0:T(8,128)(2,1)S(1)}, u32[]{:S(2)}, u32[]{:S(2)}) collective-permute-start(bf16[64,1152]{1,0:T(8,128)(2,1)S(1)} %collective-permute-done), channel_id=1, source_target_pairs={{0,4},{2,6},{4,0},{6,2},{1,5},{3,7},{5,1},{7,3},{8,12},{10,14},{12... | collective-permute-start | bytes 442376 | tf_op jit(solution)/shard_map/ppermute | solution.py:30
  28.3 2.8 %collective-permute-start.3 = (bf16[64,1152]{1,0:T(8,128)(2,1)S(1)}, bf16[64,1152]{1,0:T(8,128)(2,1)S(1)}, u32[]{:S(2)}, u32[]{:S(2)}) collective-permute-start(bf16[64,1152]{1,0:T(8,128)(2,1)S(1)} %collective-permute-done), channel_id=1, source_target_pairs={{0,2},{2,4},{4,6},{6,0},{1,3},{3,5},{5,7},{7,1},{8,10},{10,12},{12... | collective-permute-start | bytes 442376 | tf_op jit(solution)/shard_map/ppermute | solution.py:30
  31.2 4.3 %collective-permute-done.2 = bf16[64,1152]{1,0:T(8,128)(2,1)S(1)} collective-permute-done((bf16[64,1152]{1,0:T(8,128)(2,1)S(1)}, bf16[64,1152]{1,0:T(8,128)(2,1)S(1)}, u32[]{:S(2)}, u32[]{:S(2)}) %collective-permute-start.2) | collective-permute-done | bytes 147488 | tf_op jit(solution)/shard_map/ppermute | solution.py:30
  35.5 1.7 %collective-permute-done.3 = bf16[64,1152]{1,0:T(8,128)(2,1)S(1)} collective-permute-done((bf16[64,1152]{1,0:T(8,128)(2,1)S(1)}, bf16[64,1152]{1,0:T(8,128)(2,1)S(1)}, u32[]{:S(2)}, u32[]{:S(2)}) %collective-permute-start.3) | collective-permute-done | bytes 147488 | tf_op jit(solution)/shard_map/ppermute | solution.py:30
  37.3 0.2 broadcast_select_fusion.1
  37.6 0.3 fusion
  37.9 0.4 fusion.1
  38.3 1.9 %collective-permute-start.4 = (bf16[512,1152]{1,0:T(8,128)(2,1)S(1)}, bf16[512,1152]{1,0:T(8,128)(2,1)}, u32[]{:S(2)}, u32[]{:S(2)}) collective-permute-start(bf16[512,1152]{1,0:T(8,128)(2,1)S(1)} %fusion.1), channel_id=1, source_target_pairs={{0,8},{8,0},{1,9},{9,1},{2,10},{10,2},{3,11},{11,3},{4,12},{12,4},... | collective-permute-start | bytes 3538952 | tf_op jit(solution)/shard_map/ppermute | solution.py:25
  41.6 0.1 add_dynamic-update-slice_fusion
  41.7 1.5 %collective-permute-done.4 = bf16[512,1152]{1,0:T(8,128)(2,1)} collective-permute-done((bf16[512,1152]{1,0:T(8,128)(2,1)S(1)}, bf16[512,1152]{1,0:T(8,128)(2,1)}, u32[]{:S(2)}, u32[]{:S(2)}) %collective-permute-start.4) | collective-permute-done | bytes 1179680 | tf_op jit(solution)/shard_map/ppermute | solution.py:25
  43.1 1.8 %pad_maximum_fusion = bf16[1024,1152]{1,0:T(8,128)(2,1)S(1)} fusion(bf16[512,1152]{1,0:T(8,128)(2,1)} %collective-permute-done.4, bf16[512,1152]{1,0:T(8,128)(2,1)} %copy-done.2), kind=kLoop, calls=%fused_computation.10 | loop fusion | flops 4718592 | bytes 4718592 | tf_op jit(solution)/shard_map/concatenate | solution.py:103
  44.9 3.6 %all-to-all-done = bf16[16,32,1152]{2,1,0:T(8,128)(2,1)S(1)} async-done(((bf16[16,32,1152]{2,1,0:T(8,128)(2,1)}), bf16[16,32,1152]{2,1,0:T(8,128)(2,1)S(1)}, u32[]{:S(2)}, u32[]{:S(2)}) %all-to-all-start) | async-done | bytes 1179680 | tf_op jit(solution)/shard_map/all_to_all | solution.py:34
  48.6 0.1 copy.10
  48.7 0.3 fusion.2
  49.0 2.1 %subtract_convert_fusion = bf16[1024,512]{1,0:T(8,128)(2,1)S(1)} fusion(bf16[1024,1152]{1,0:T(8,128)(2,1)S(1)} %pad_maximum_fusion, s32[512]{0:T(512)S(1)} %add_dynamic-update-slice_fusion, f32[]{:T(128)} %bitcast.37, f32[]{:T(128)} %bitcast, bf16[512,1152]{1,0:T(8,128)(2,1)S(1)} %bitcast.40, f32[512]{0:T(512)S(1)} %add_sqrt_fusion), kind=kOutput, calls=%fused_computation.12 | convolution fusion | flops 1214447616 | bytes 4591624 | tf_op jit(solution)/shard_map/dot_general | solution.py:104
  51.1 2.6 %convolution_convert_fusion.1 = bf16[512,1152]{1,0:T(8,128)(2,1)} fusion(bf16[1024,512]{1,0:T(8,128)(2,1)S(1)} %subtract_convert_fusion, bf16[1024,1152]{1,0:T(8,128)(2,1)S(1)} %pad_maximum_fusion), kind=kOutput, calls=%fused_computation.1 | convolution fusion | flops 1208549376 | bytes 4587520 | tf_op jit(solution)/shard_map/dot_general | solution.py:106
  53.7 2.0 %convolution_convert_fusion = bf16[512,1152]{1,0:T(8,128)(2,1)} fusion(bf16[1024,512]{1,0:T(8,128)(2,1)S(1)} %subtract_convert_fusion, bf16[512,1152]{1,0:T(8,128)(2,1)S(1)} %bitcast.41, f32[512]{0:T(512)S(1)} %add_sqrt_fusion), kind=kOutput, calls=%fused_computation | convolution fusion | flops 606339072 | bytes 2885632 | tf_op jit(solution)/shard_map/dot_general | solution.py:111
  55.7 1.9 %collective-permute-start.5 = (bf16[512,1152]{1,0:T(8,128)(2,1)}, bf16[512,1152]{1,0:T(8,128)(2,1)}, u32[]{:S(2)}, u32[]{:S(2)}) collective-permute-start(bf16[512,1152]{1,0:T(8,128)(2,1)} %convolution_convert_fusion), channel_id=1, source_target_pairs={{0,8},{8,0},{1,9},{9,1},{2,10},{10,2},{3,11},{11,3},{4,12},{12,4},... | collective-permute-start | bytes 3538952 | tf_op jit(solution)/shard_map/ppermute | solution.py:25
  57.6 0.1 fusion.10
  57.8 0.1 convert_divide_fusion.2
  57.9 4.9 %all-to-all-start.1 = ((bf16[4,128,1152]{2,1,0:T(8,128)(2,1)}), bf16[4,128,1152]{2,1,0:T(8,128)(2,1)S(1)}, u32[]{:S(2)}, u32[]{:S(2)}) async-start(bf16[4,128,1152]{2,1,0:T(8,128)(2,1)} %bitcast.16), calls=%async_computation.1 | async-start | bytes 2359296 | tf_op jit(solution)/shard_map/all_to_all | solution.py:34
  62.8 2.4 %add_convert_fusion = bf16[512,1152]{1,0:T(8,128)(2,1)S(1)} fusion(bf16[512,1152]{1,0:T(8,128)(2,1)} %collective-permute-done.5, bf16[1024,512]{1,0:T(8,128)(2,1)} %copy-done.5, bf16[512,1152]{1,0:T(8,128)(2,1)S(1)} %bitcast.42, f32[512]{0:T(512)S(1)} %add_sqrt_fusion), kind=kOutput, calls=%fused_computation.11 | convolution fusion | flops 607518720 | bytes 4065280 | tf_op jit(solution)/shard_map/dot_general | solution.py:113
  65.3 4.9 %collective-permute-start.6 = (bf16[128,1152]{1,0:T(8,128)(2,1)S(1)}, bf16[128,1152]{1,0:T(8,128)(2,1)S(1)}, u32[]{:S(2)}, u32[]{:S(2)}) collective-permute-start(bf16[128,1152]{1,0:T(8,128)(2,1)S(1)} %bitcast.47), channel_id=1, source_target_pairs={{0,4},{2,6},{4,0},{6,2},{1,5},{3,7},{5,1},{7,3},{8,12},{10,14},{12... | collective-permute-start | bytes 884744 | tf_op jit(solution)/shard_map/ppermute | solution.py:30
  70.2 2.5 %collective-permute-start.7 = (bf16[128,1152]{1,0:T(8,128)(2,1)S(1)}, bf16[128,1152]{1,0:T(8,128)(2,1)S(1)}, u32[]{:S(2)}, u32[]{:S(2)}) collective-permute-start(bf16[128,1152]{1,0:T(8,128)(2,1)S(1)} %bitcast.46), channel_id=1, source_target_pairs={{0,2},{2,4},{4,6},{6,0},{1,3},{3,5},{5,7},{7,1},{8,10},{10,12},{12... | collective-permute-start | bytes 884744 | tf_op jit(solution)/shard_map/ppermute | solution.py:30
  72.7 4.5 %collective-permute-start.8 = (bf16[128,1152]{1,0:T(8,128)(2,1)S(1)}, bf16[128,1152]{1,0:T(8,128)(2,1)S(1)}, u32[]{:S(2)}, u32[]{:S(2)}) collective-permute-start(bf16[128,1152]{1,0:T(8,128)(2,1)S(1)} %bitcast.45), channel_id=1, source_target_pairs={{0,6},{2,0},{4,2},{6,4},{1,7},{3,1},{5,3},{7,5},{8,14},{10,8},{12,... | collective-permute-start | bytes 884744 | tf_op jit(solution)/shard_map/ppermute | solution.py:30
  77.3 0.1 fusion.11
  77.4 1.1 collective-permute-done.6
  78.5 5.6 %collective-permute-done.7 = bf16[128,1152]{1,0:T(8,128)(2,1)S(1)} collective-permute-done((bf16[128,1152]{1,0:T(8,128)(2,1)S(1)}, bf16[128,1152]{1,0:T(8,128)(2,1)S(1)}, u32[]{:S(2)}, u32[]{:S(2)}) %collective-permute-start.7) | collective-permute-done | bytes 294944 | tf_op jit(solution)/shard_map/ppermute | solution.py:30
  84.2 0.2 fusion.4
  84.4 9.1 %collective-permute-start.10 = (bf16[64,1152]{1,0:T(8,128)(2,1)S(1)}, bf16[64,1152]{1,0:T(8,128)(2,1)S(1)}, u32[]{:S(2)}, u32[]{:S(2)}) collective-permute-start(bf16[64,1152]{1,0:T(8,128)(2,1)S(1)} %get-tuple-element.21), channel_id=1, source_target_pairs={{0,64},{64,0},{1,65},{65,1},{2,66},{66,2},{3,67},{67,3},{4,68},{68... | collective-permute-start | bytes 442376 | tf_op jit(solution)/shard_map/ppermute | solution.py:25
  93.6 1.9 %collective-permute-start.9 = (bf16[64,1152]{1,0:T(8,128)(2,1)S(1)}, bf16[64,1152]{1,0:T(8,128)(2,1)S(1)}, u32[]{:S(2)}, u32[]{:S(2)}) collective-permute-start(bf16[64,1152]{1,0:T(8,128)(2,1)S(1)} %get-tuple-element.37), channel_id=1, source_target_pairs={{0,1},{1,0},{2,3},{3,2},{4,5},{5,4},{6,7},{7,6},{8,9},{9,8},{10,11... | collective-permute-start | bytes 442376 | tf_op jit(solution)/shard_map/ppermute | solution.py:25
  95.5 6.9 %collective-permute-start.11 = (bf16[64,1152]{1,0:T(8,128)(2,1)S(1)}, bf16[64,1152]{1,0:T(8,128)(2,1)S(1)}, u32[]{:S(2)}, u32[]{:S(2)}) collective-permute-start(bf16[64,1152]{1,0:T(8,128)(2,1)S(1)} %get-tuple-element.21), channel_id=1, source_target_pairs={{0,65},{1,64},{64,1},{65,0},{2,67},{3,66},{66,3},{67,2},{4,69},{5,... | collective-permute-start | bytes 442376 | tf_op jit(solution)/shard_map/ppermute | solution.py:25
  102.5 1.0 reduce_sum.84
  103.5 5.4 %all-to-all-start.2 = ((bf16[4,32,1152]{2,1,0:T(8,128)(2,1)}), bf16[4,32,1152]{2,1,0:T(8,128)(2,1)S(1)}, u32[]{:S(2)}, u32[]{:S(2)}) async-start(bf16[4,32,1152]{2,1,0:T(8,128)(2,1)} %bitcast.20), calls=%async_computation.2 | async-start | bytes 589824 | tf_op jit(solution)/shard_map/all_to_all | solution.py:34
  108.9 0.2 multiply_reduce_fusion
  109.1 0.1 divide_convert_fusion
  109.2 4.7 %collective-permute-start.12 = (bf16[64,1152]{1,0:T(8,128)(2,1)S(1)}, bf16[64,1152]{1,0:T(8,128)(2,1)S(1)}, u32[]{:S(2)}, u32[]{:S(2)}) collective-permute-start(bf16[64,1152]{1,0:T(8,128)(2,1)S(1)} %divide_convert_fusion), channel_id=1, source_target_pairs={{0,6},{2,0},{4,2},{6,4},{1,7},{3,1},{5,3},{7,5},{8,14},{10,8},{12,... | collective-permute-start | bytes 442376 | tf_op jit(solution)/shard_map/ppermute | solution.py:30
  113.9 2.7 %collective-permute-start.13 = (bf16[64,1152]{1,0:T(8,128)(2,1)S(1)}, bf16[64,1152]{1,0:T(8,128)(2,1)S(1)}, u32[]{:S(2)}, u32[]{:S(2)}) collective-permute-start(bf16[64,1152]{1,0:T(8,128)(2,1)S(1)} %divide_convert_fusion), channel_id=1, source_target_pairs={{0,4},{2,6},{4,0},{6,2},{1,5},{3,7},{5,1},{7,3},{8,12},{10,14},{12... | collective-permute-start | bytes 442376 | tf_op jit(solution)/shard_map/ppermute | solution.py:30
  116.6 2.8 %collective-permute-start.14 = (bf16[64,1152]{1,0:T(8,128)(2,1)S(1)}, bf16[64,1152]{1,0:T(8,128)(2,1)S(1)}, u32[]{:S(2)}, u32[]{:S(2)}) collective-permute-start(bf16[64,1152]{1,0:T(8,128)(2,1)S(1)} %divide_convert_fusion), channel_id=1, source_target_pairs={{0,2},{2,4},{4,6},{6,0},{1,3},{3,5},{5,7},{7,1},{8,10},{10,12},{12... | collective-permute-start | bytes 442376 | tf_op jit(solution)/shard_map/ppermute | solution.py:30
  119.4 0.1 multiply_reduce_fusion.1
  119.6 0.7 divide_convert_fusion.1
  120.3 3.2 %collective-permute-done.13 = bf16[64,1152]{1,0:T(8,128)(2,1)S(1)} collective-permute-done((bf16[64,1152]{1,0:T(8,128)(2,1)S(1)}, bf16[64,1152]{1,0:T(8,128)(2,1)S(1)}, u32[]{:S(2)}, u32[]{:S(2)}) %collective-permute-start.13) | collective-permute-done | bytes 147488 | tf_op jit(solution)/shard_map/ppermute | solution.py:30
  123.5 1.7 %collective-permute-done.14 = bf16[64,1152]{1,0:T(8,128)(2,1)S(1)} collective-permute-done((bf16[64,1152]{1,0:T(8,128)(2,1)S(1)}, bf16[64,1152]{1,0:T(8,128)(2,1)S(1)}, u32[]{:S(2)}, u32[]{:S(2)}) %collective-permute-start.14) | collective-permute-done | bytes 147488 | tf_op jit(solution)/shard_map/ppermute | solution.py:30
  125.5 0.9 constant_dynamic-slice_fusion
  (51 shorter events, 0.7 us)
Async XLA Ops:
  2.8 18.0 %collective-permute-start = (bf16[64,1152]{1,0:T(8,128)(2,1)}, bf16[64,1152]{1,0:T(8,128)(2,1)S(1)}, u32[]{:S(2)}, u32[]{:S(2)}) collective-permute-start(bf16[64,1152]{1,0:T(8,128)(2,1)} %get-tuple-element.17), channel_id=1, source_target_pairs={{0,64},{64,0},{1,65},{65,1},{2,66},{66,2},{3,67},{67,3},{4,68},{68... | collective-permute-start | bytes 442376 | tf_op jit(solution)/shard_map/ppermute | solution.py:25
  6.1 42.5 %all-to-all-start = ((bf16[16,32,1152]{2,1,0:T(8,128)(2,1)}), bf16[16,32,1152]{2,1,0:T(8,128)(2,1)S(1)}, u32[]{:S(2)}, u32[]{:S(2)}) async-start(bf16[16,32,1152]{2,1,0:T(8,128)(2,1)} %get-tuple-element.18), calls=%async_computation | async-start | bytes 2359296 | tf_op jit(solution)/shard_map/all_to_all | solution.py:34
  20.8 16.5 %copy-start.3 = (bf16[256,1152]{1,0:T(8,128)(2,1)S(1)}, bf16[256,1152]{1,0:T(8,128)(2,1)}, u32[]{:S(2)}) copy-start(bf16[256,1152]{1,0:T(8,128)(2,1)} %image_ref.1) | copy-start | bytes 1769476
  20.8 10.3 %collective-permute-start.1 = (bf16[64,1152]{1,0:T(8,128)(2,1)S(1)}, bf16[64,1152]{1,0:T(8,128)(2,1)S(1)}, u32[]{:S(2)}, u32[]{:S(2)}) collective-permute-start(bf16[64,1152]{1,0:T(8,128)(2,1)S(1)} %collective-permute-done), channel_id=1, source_target_pairs={{0,6},{2,0},{4,2},{6,4},{1,7},{3,1},{5,3},{7,5},{8,14},{10,8},{12,... | collective-permute-start | bytes 442376 | tf_op jit(solution)/shard_map/ppermute | solution.py:30
  25.6 9.9 %collective-permute-start.2 = (bf16[64,1152]{1,0:T(8,128)(2,1)S(1)}, bf16[64,1152]{1,0:T(8,128)(2,1)S(1)}, u32[]{:S(2)}, u32[]{:S(2)}) collective-permute-start(bf16[64,1152]{1,0:T(8,128)(2,1)S(1)} %collective-permute-done), channel_id=1, source_target_pairs={{0,4},{2,6},{4,0},{6,2},{1,5},{3,7},{5,1},{7,3},{8,12},{10,14},{12... | collective-permute-start | bytes 442376 | tf_op jit(solution)/shard_map/ppermute | solution.py:30
  28.3 8.9 %collective-permute-start.3 = (bf16[64,1152]{1,0:T(8,128)(2,1)S(1)}, bf16[64,1152]{1,0:T(8,128)(2,1)S(1)}, u32[]{:S(2)}, u32[]{:S(2)}) collective-permute-start(bf16[64,1152]{1,0:T(8,128)(2,1)S(1)} %collective-permute-done), channel_id=1, source_target_pairs={{0,2},{2,4},{4,6},{6,0},{1,3},{3,5},{5,7},{7,1},{8,10},{10,12},{12... | collective-permute-start | bytes 442376 | tf_op jit(solution)/shard_map/ppermute | solution.py:30
  37.9 3.7 %copy-start.7 = (s32[32]{0:T(128)S(1)}, s32[32]{0:T(128)}, u32[]{:S(2)}) copy-start(s32[32]{0:T(128)} %param.7) | copy-start | bytes 388
  38.3 3.4 %copy-start.2 = (bf16[512,1152]{1,0:T(8,128)(2,1)}, bf16[512,1152]{1,0:T(8,128)(2,1)S(1)}, u32[]{:S(2)}) copy-start(bf16[512,1152]{1,0:T(8,128)(2,1)S(1)} %fusion.1) | copy-start | bytes 3538948
  38.3 4.9 %collective-permute-start.4 = (bf16[512,1152]{1,0:T(8,128)(2,1)S(1)}, bf16[512,1152]{1,0:T(8,128)(2,1)}, u32[]{:S(2)}, u32[]{:S(2)}) collective-permute-start(bf16[512,1152]{1,0:T(8,128)(2,1)S(1)} %fusion.1), channel_id=1, source_target_pairs={{0,8},{8,0},{1,9},{9,1},{2,10},{10,2},{3,11},{11,3},{4,12},{12,4},... | collective-permute-start | bytes 3538952 | tf_op jit(solution)/shard_map/ppermute | solution.py:25
  48.7 5.0 %copy-start = (bf16[4,4,32,1152]{3,2,0,1:T(8,128)(2,1)}, bf16[4,4,32,1152]{3,2,0,1:T(8,128)(2,1)S(1)}, u32[]{:S(2)}) copy-start(bf16[4,4,32,1152]{3,2,0,1:T(8,128)(2,1)S(1)} %copy.10) | copy-start | bytes 3538948
  51.1 2.6 %copy-start.5 = (bf16[1024,512]{1,0:T(8,128)(2,1)}, bf16[1024,512]{1,0:T(8,128)(2,1)S(1)}, u32[]{:S(2)}) copy-start(bf16[1024,512]{1,0:T(8,128)(2,1)S(1)} %subtract_convert_fusion) | copy-start | bytes 3145732
  53.7 4.0 %copy-start.4 = (bf16[256,1152]{1,0:T(8,128)(2,1)S(1)}, bf16[256,1152]{1,0:T(8,128)(2,1)}, u32[]{:S(2)}) copy-start(bf16[256,1152]{1,0:T(8,128)(2,1)} %image_ref.1) | copy-start | bytes 1769476
  55.7 7.1 %collective-permute-start.5 = (bf16[512,1152]{1,0:T(8,128)(2,1)}, bf16[512,1152]{1,0:T(8,128)(2,1)}, u32[]{:S(2)}, u32[]{:S(2)}) collective-permute-start(bf16[512,1152]{1,0:T(8,128)(2,1)} %convolution_convert_fusion), channel_id=1, source_target_pairs={{0,8},{8,0},{1,9},{9,1},{2,10},{10,2},{3,11},{11,3},{4,12},{12,4},... | collective-permute-start | bytes 3538952 | tf_op jit(solution)/shard_map/ppermute | solution.py:25
  57.9 4.9 %copy-start.1 = (bf16[4,4,32,1152]{3,2,0,1:T(8,128)(2,1)S(1)}, bf16[4,4,32,1152]{3,2,0,1:T(8,128)(2,1)}, u32[]{:S(2)}) copy-start(bf16[4,4,32,1152]{3,2,0,1:T(8,128)(2,1)} %copy-done) | copy-start | bytes 3538948
  57.9 37.6 %all-to-all-start.1 = ((bf16[4,128,1152]{2,1,0:T(8,128)(2,1)}), bf16[4,128,1152]{2,1,0:T(8,128)(2,1)S(1)}, u32[]{:S(2)}, u32[]{:S(2)}) async-start(bf16[4,128,1152]{2,1,0:T(8,128)(2,1)} %bitcast.16), calls=%async_computation.1 | async-start | bytes 2359296 | tf_op jit(solution)/shard_map/all_to_all | solution.py:34
  65.2 12.1 %copy-start.6 = (bf16[32,1152]{1,0:T(8,128)(2,1)S(1)}, bf16[32,1152]{1,0:T(8,128)(2,1)}, u32[]{:S(2)}) copy-start(bf16[32,1152]{1,0:T(8,128)(2,1)} %text_ref.1) | copy-start | bytes 221188
  65.3 13.2 %collective-permute-start.6 = (bf16[128,1152]{1,0:T(8,128)(2,1)S(1)}, bf16[128,1152]{1,0:T(8,128)(2,1)S(1)}, u32[]{:S(2)}, u32[]{:S(2)}) collective-permute-start(bf16[128,1152]{1,0:T(8,128)(2,1)S(1)} %bitcast.47), channel_id=1, source_target_pairs={{0,4},{2,6},{4,0},{6,2},{1,5},{3,7},{5,1},{7,3},{8,12},{10,14},{12... | collective-permute-start | bytes 884744 | tf_op jit(solution)/shard_map/ppermute | solution.py:30
  70.2 13.9 %collective-permute-start.7 = (bf16[128,1152]{1,0:T(8,128)(2,1)S(1)}, bf16[128,1152]{1,0:T(8,128)(2,1)S(1)}, u32[]{:S(2)}, u32[]{:S(2)}) collective-permute-start(bf16[128,1152]{1,0:T(8,128)(2,1)S(1)} %bitcast.46), channel_id=1, source_target_pairs={{0,2},{2,4},{4,6},{6,0},{1,3},{3,5},{5,7},{7,1},{8,10},{10,12},{12... | collective-permute-start | bytes 884744 | tf_op jit(solution)/shard_map/ppermute | solution.py:30
  72.7 11.5 %collective-permute-start.8 = (bf16[128,1152]{1,0:T(8,128)(2,1)S(1)}, bf16[128,1152]{1,0:T(8,128)(2,1)S(1)}, u32[]{:S(2)}, u32[]{:S(2)}) collective-permute-start(bf16[128,1152]{1,0:T(8,128)(2,1)S(1)} %bitcast.45), channel_id=1, source_target_pairs={{0,6},{2,0},{4,2},{6,4},{1,7},{3,1},{5,3},{7,5},{8,14},{10,8},{12,... | collective-permute-start | bytes 884744 | tf_op jit(solution)/shard_map/ppermute | solution.py:30
  84.4 24.4 %collective-permute-start.10 = (bf16[64,1152]{1,0:T(8,128)(2,1)S(1)}, bf16[64,1152]{1,0:T(8,128)(2,1)S(1)}, u32[]{:S(2)}, u32[]{:S(2)}) collective-permute-start(bf16[64,1152]{1,0:T(8,128)(2,1)S(1)} %get-tuple-element.21), channel_id=1, source_target_pairs={{0,64},{64,0},{1,65},{65,1},{2,66},{66,2},{3,67},{67,3},{4,68},{68... | collective-permute-start | bytes 442376 | tf_op jit(solution)/shard_map/ppermute | solution.py:25
  93.6 15.3 %collective-permute-start.9 = (bf16[64,1152]{1,0:T(8,128)(2,1)S(1)}, bf16[64,1152]{1,0:T(8,128)(2,1)S(1)}, u32[]{:S(2)}, u32[]{:S(2)}) collective-permute-start(bf16[64,1152]{1,0:T(8,128)(2,1)S(1)} %get-tuple-element.37), channel_id=1, source_target_pairs={{0,1},{1,0},{2,3},{3,2},{4,5},{5,4},{6,7},{7,6},{8,9},{9,8},{10,11... | collective-permute-start | bytes 442376 | tf_op jit(solution)/shard_map/ppermute | solution.py:25
  95.5 13.3 %collective-permute-start.11 = (bf16[64,1152]{1,0:T(8,128)(2,1)S(1)}, bf16[64,1152]{1,0:T(8,128)(2,1)S(1)}, u32[]{:S(2)}, u32[]{:S(2)}) collective-permute-start(bf16[64,1152]{1,0:T(8,128)(2,1)S(1)} %get-tuple-element.21), channel_id=1, source_target_pairs={{0,65},{1,64},{64,1},{65,0},{2,67},{3,66},{66,3},{67,2},{4,69},{5,... | collective-permute-start | bytes 442376 | tf_op jit(solution)/shard_map/ppermute | solution.py:25
  103.5 15.9 %all-to-all-start.2 = ((bf16[4,32,1152]{2,1,0:T(8,128)(2,1)}), bf16[4,32,1152]{2,1,0:T(8,128)(2,1)S(1)}, u32[]{:S(2)}, u32[]{:S(2)}) async-start(bf16[4,32,1152]{2,1,0:T(8,128)(2,1)} %bitcast.20), calls=%async_computation.2 | async-start | bytes 589824 | tf_op jit(solution)/shard_map/all_to_all | solution.py:34
  109.2 11.1 %collective-permute-start.12 = (bf16[64,1152]{1,0:T(8,128)(2,1)S(1)}, bf16[64,1152]{1,0:T(8,128)(2,1)S(1)}, u32[]{:S(2)}, u32[]{:S(2)}) collective-permute-start(bf16[64,1152]{1,0:T(8,128)(2,1)S(1)} %divide_convert_fusion), channel_id=1, source_target_pairs={{0,6},{2,0},{4,2},{6,4},{1,7},{3,1},{5,3},{7,5},{8,14},{10,8},{12,... | collective-permute-start | bytes 442376 | tf_op jit(solution)/shard_map/ppermute | solution.py:30
  113.9 9.6 %collective-permute-start.13 = (bf16[64,1152]{1,0:T(8,128)(2,1)S(1)}, bf16[64,1152]{1,0:T(8,128)(2,1)S(1)}, u32[]{:S(2)}, u32[]{:S(2)}) collective-permute-start(bf16[64,1152]{1,0:T(8,128)(2,1)S(1)} %divide_convert_fusion), channel_id=1, source_target_pairs={{0,4},{2,6},{4,0},{6,2},{1,5},{3,7},{5,1},{7,3},{8,12},{10,14},{12... | collective-permute-start | bytes 442376 | tf_op jit(solution)/shard_map/ppermute | solution.py:30
  116.6 8.7 %collective-permute-start.14 = (bf16[64,1152]{1,0:T(8,128)(2,1)S(1)}, bf16[64,1152]{1,0:T(8,128)(2,1)S(1)}, u32[]{:S(2)}, u32[]{:S(2)}) collective-permute-start(bf16[64,1152]{1,0:T(8,128)(2,1)S(1)} %divide_convert_fusion), channel_id=1, source_target_pairs={{0,2},{2,4},{4,6},{6,0},{1,3},{3,5},{5,7},{7,1},{8,10},{10,12},{12... | collective-permute-start | bytes 442376 | tf_op jit(solution)/shard_map/ppermute | solution.py:30

commit v19 on v18

--- a/solution.py
+++ b/solution.py
@@ -9,7 +9,8 @@
 AXES = ("yh", "yl", "w", "c", "x", "l")
 CLASSES = ((0, 3, 5, 6), (1, 2, 4, 7))
 RINGS = ("yh", "yl", "w", "l")
-TEXT_GROUPS = [[y * 8 + z for y in of_y for z in of_z] for of_y in CLASSES for of_z in CLASSES]
+ORDER = ((0, 0), (0, 1), (0, 2), (0, 3), (1, 2), (1, 3), (1, 0), (1, 1), (2, 0), (2, 1), (2, 2), (2, 3), (3, 2), (3, 3), (3, 0), (3, 1))
+TEXT_GROUPS = [[of_y[i] * 8 + of_z[j] for i, j in ORDER] for of_y in CLASSES for of_z in CLASSES]
 NARROW = ("x", "l")
 BF16, F32 = jnp.bfloat16, jnp.float32
 
@@ -80,8 +81,9 @@
 
     part, copies = first_copies(x.astype(jnp.int32).reshape(1), image_emb, text_emb, quarter, peers)
     part = swap(part, "yl")
-    texts = exchange(copies, RINGS, TEXT_GROUPS).reshape(4, 4, mine, width)
-    texts = lax.optimization_barrier(texts.transpose(1, 0, 2, 3).reshape(-1, width))
+    texts = exchange(copies, RINGS, TEXT_GROUPS).reshape(peers, mine, width)
+    texts = jnp.concatenate([texts[ORDER.index((i, j))] for j in range(4) for i in range(4)], axis=0)
+    texts = lax.optimization_barrier(texts)
     around = [part] + [shift(part, "x", n_x - d) for d in range(1, n_x)]
     beyond = in_order(around, x)
     chip = jnp.concatenate([jnp.where(upper, beyond, image_emb), jnp.where(upper, image_emb, beyond)], axis=0)

time: 127 us -> 127 us (level)
  starting transfers between devices: 82.4 us -> 79.1 us
  waiting for transfers between devices: 22.9 us -> 25.5 us
    ppermute x6, starting transfers between devices: 25 us -> 22.5 us  [swap(): return lax.ppermute(block, axes, [(i, count - 1 - i) for i in range(count)])]
    all_to_all x3, waiting for transfers between devices: 3.62 us -> 5.76 us  [exchange(): lax.all_to_all(blocks, axes, 0, 0, axis_index_groups=groups, tiled=True)]
where the time goes in v19:
time: 127 us; the launch traced here: 126 us
  starting transfers between devices  79.1 us (62%)
  waiting for transfers between devices  25.5 us (20%)
  matrix products  9.04 us (7%)
  other arithmetic  5.98 us (5%)
  between operations  2.51 us (2%)
  Pallas kernels  2.18 us (2%)
  local copies, waits for them, and re-layouts  1.5 us (1%)
    ppermute x9, starting transfers between devices, shift(): lax.ppermute(block, axis, [(i, (i + distance) % count) for i in range(cou...  32.4 us
    all_to_all x3, starting transfers between devices, exchange(): lax.all_to_all(blocks, axes, 0, 0, axis_index_groups=groups, tiled=True)  24.2 us
    ppermute x6, starting transfers between devices, swap(): return lax.ppermute(block, axes, [(i, count - 1 - i) for i in range(count)])  22.5 us
    ppermute x9, waiting for transfers between devices, shift(): lax.ppermute(block, axis, [(i, (i + distance) % count) for i in range(cou...  18.3 us
    all_to_all x3, waiting for transfers between devices, exchange(): lax.all_to_all(blocks, axes, 0, 0, axis_index_groups=groups, tiled=True)  5.76 us
    dot_general x1, matrix products, local(): lax.dot_general(grad, images, (((0,), (0,)), ((), ())), preferred_element...  2.58 us
  transfers between devices with their start and end apart: 18, of which 9 were waited for; matrix products, arithmetic and copies ran while one was open for 7% of the time, Pallas kernels for 0%

profile of v19, /device:TPU:56, one launch (start us, length us, event | category | flops | bytes accessed | tf_op | source)
XLA Modules:
  0.0 125.9 jit_solution(12407940577747747425)
XLA Ops:
  0.6 2.2 %first_copies.1 = (bf16[64,1152]{1,0:T(8,128)(2,1)}, bf16[16,32,1152]{2,1,0:T(8,128)(2,1)}) custom-call(s32[1]{0:T(128)} %bitcast.1.x_ref, bf16[256,1152]{1,0:T(8,128)(2,1)} %image_ref.1, bf16[32,1152]{1,0:T(8,128)(2,1)} %text_ref.1), custom_call_target="tpu_custom_call" | custom-call | tf_op jit(solution)/shard_map/first_copies/pallas_call | solution.py:54
  2.8 3.2 %collective-permute-start = (bf16[64,1152]{1,0:T(8,128)(2,1)}, bf16[64,1152]{1,0:T(8,128)(2,1)S(1)}, u32[]{:S(2)}, u32[]{:S(2)}) collective-permute-start(bf16[64,1152]{1,0:T(8,128)(2,1)} %get-tuple-element.17), channel_id=1, source_target_pairs={{0,64},{64,0},{1,65},{65,1},{2,66},{66,2},{3,67},{67,3},{4,68},{68... | collective-permute-start | bytes 442376 | tf_op jit(solution)/shard_map/ppermute | solution.py:26
  6.1 14.7 %all-to-all-start = ((bf16[16,32,1152]{2,1,0:T(8,128)(2,1)}), bf16[16,32,1152]{2,1,0:T(8,128)(2,1)S(1)}, u32[]{:S(2)}, u32[]{:S(2)}) async-start(bf16[16,32,1152]{2,1,0:T(8,128)(2,1)} %get-tuple-element.18), calls=%async_computation | async-start | bytes 2359296 | tf_op jit(solution)/shard_map/all_to_all | solution.py:35
  20.8 4.8 %collective-permute-start.1 = (bf16[64,1152]{1,0:T(8,128)(2,1)S(1)}, bf16[64,1152]{1,0:T(8,128)(2,1)S(1)}, u32[]{:S(2)}, u32[]{:S(2)}) collective-permute-start(bf16[64,1152]{1,0:T(8,128)(2,1)S(1)} %collective-permute-done), channel_id=1, source_target_pairs={{0,6},{2,0},{4,2},{6,4},{1,7},{3,1},{5,3},{7,5},{8,14},{10,8},{12,... | collective-permute-start | bytes 442376 | tf_op jit(solution)/shard_map/ppermute | solution.py:31
  25.6 2.7 %collective-permute-start.2 = (bf16[64,1152]{1,0:T(8,128)(2,1)S(1)}, bf16[64,1152]{1,0:T(8,128)(2,1)S(1)}, u32[]{:S(2)}, u32[]{:S(2)}) collective-permute-start(bf16[64,1152]{1,0:T(8,128)(2,1)S(1)} %collective-permute-done), channel_id=1, source_target_pairs={{0,4},{2,6},{4,0},{6,2},{1,5},{3,7},{5,1},{7,3},{8,12},{10,14},{12... | collective-permute-start | bytes 442376 | tf_op jit(solution)/shard_map/ppermute | solution.py:31
  28.3 2.8 %collective-permute-start.3 = (bf16[64,1152]{1,0:T(8,128)(2,1)S(1)}, bf16[64,1152]{1,0:T(8,128)(2,1)S(1)}, u32[]{:S(2)}, u32[]{:S(2)}) collective-permute-start(bf16[64,1152]{1,0:T(8,128)(2,1)S(1)} %collective-permute-done), channel_id=1, source_target_pairs={{0,2},{2,4},{4,6},{6,0},{1,3},{3,5},{5,7},{7,1},{8,10},{10,12},{12... | collective-permute-start | bytes 442376 | tf_op jit(solution)/shard_map/ppermute | solution.py:31
  31.2 4.3 %collective-permute-done.2 = bf16[64,1152]{1,0:T(8,128)(2,1)S(1)} collective-permute-done((bf16[64,1152]{1,0:T(8,128)(2,1)S(1)}, bf16[64,1152]{1,0:T(8,128)(2,1)S(1)}, u32[]{:S(2)}, u32[]{:S(2)}) %collective-permute-start.2) | collective-permute-done | bytes 147488 | tf_op jit(solution)/shard_map/ppermute | solution.py:31
  35.5 1.7 %collective-permute-done.3 = bf16[64,1152]{1,0:T(8,128)(2,1)S(1)} collective-permute-done((bf16[64,1152]{1,0:T(8,128)(2,1)S(1)}, bf16[64,1152]{1,0:T(8,128)(2,1)S(1)}, u32[]{:S(2)}, u32[]{:S(2)}) %collective-permute-start.3) | collective-permute-done | bytes 147488 | tf_op jit(solution)/shard_map/ppermute | solution.py:31
  37.3 0.2 broadcast_select_fusion.1
  37.6 0.3 fusion
  37.9 0.4 fusion.1
  38.3 1.9 %collective-permute-start.4 = (bf16[512,1152]{1,0:T(8,128)(2,1)S(1)}, bf16[512,1152]{1,0:T(8,128)(2,1)}, u32[]{:S(2)}, u32[]{:S(2)}) collective-permute-start(bf16[512,1152]{1,0:T(8,128)(2,1)S(1)} %fusion.1), channel_id=1, source_target_pairs={{0,8},{8,0},{1,9},{9,1},{2,10},{10,2},{3,11},{11,3},{4,12},{12,4},... | collective-permute-start | bytes 3538952 | tf_op jit(solution)/shard_map/ppermute | solution.py:26
  41.6 0.1 add_dynamic-update-slice_fusion
  41.7 1.5 %collective-permute-done.4 = bf16[512,1152]{1,0:T(8,128)(2,1)} collective-permute-done((bf16[512,1152]{1,0:T(8,128)(2,1)S(1)}, bf16[512,1152]{1,0:T(8,128)(2,1)}, u32[]{:S(2)}, u32[]{:S(2)}) %collective-permute-start.4) | collective-permute-done | bytes 1179680 | tf_op jit(solution)/shard_map/ppermute | solution.py:26
  43.1 1.8 %pad_maximum_fusion = bf16[1024,1152]{1,0:T(8,128)(2,1)S(1)} fusion(bf16[512,1152]{1,0:T(8,128)(2,1)} %collective-permute-done.4, bf16[512,1152]{1,0:T(8,128)(2,1)} %copy-done), kind=kLoop, calls=%fused_computation.10 | loop fusion | flops 4718592 | bytes 4718592 | tf_op jit(solution)/shard_map/concatenate | solution.py:105
  44.9 5.8 %all-to-all-done = bf16[16,32,1152]{2,1,0:T(8,128)(2,1)S(1)} async-done(((bf16[16,32,1152]{2,1,0:T(8,128)(2,1)}), bf16[16,32,1152]{2,1,0:T(8,128)(2,1)S(1)}, u32[]{:S(2)}, u32[]{:S(2)}) %all-to-all-start) | async-done | bytes 1179680 | tf_op jit(solution)/shard_map/all_to_all | solution.py:35
  51.0 0.3 fusion.2
  51.3 2.1 %subtract_convert_fusion = bf16[1024,512]{1,0:T(8,128)(2,1)S(1)} fusion(bf16[1024,1152]{1,0:T(8,128)(2,1)S(1)} %pad_maximum_fusion, s32[512]{0:T(512)S(1)} %add_dynamic-update-slice_fusion, f32[]{:T(128)} %bitcast.97, f32[]{:T(128)} %bitcast, bf16[512,1152]{1,0:T(8,128)(2,1)S(1)} %fusion.12, f32[512]{0:T(512)S(1)} %add_sqrt_fusion), kind=kOutput, calls=%fused_computation.12 | convolution fusion | flops 1214447616 | bytes 4591624 | tf_op jit(solution)/shard_map/dot_general | solution.py:106
  53.4 2.6 %convolution_convert_fusion.1 = bf16[512,1152]{1,0:T(8,128)(2,1)} fusion(bf16[1024,512]{1,0:T(8,128)(2,1)S(1)} %subtract_convert_fusion, bf16[1024,1152]{1,0:T(8,128)(2,1)S(1)} %pad_maximum_fusion), kind=kOutput, calls=%fused_computation.1 | convolution fusion | flops 1208549376 | bytes 4587520 | tf_op jit(solution)/shard_map/dot_general | solution.py:108
  56.0 2.0 %convolution_convert_fusion = bf16[512,1152]{1,0:T(8,128)(2,1)} fusion(bf16[1024,512]{1,0:T(8,128)(2,1)S(1)} %subtract_convert_fusion, bf16[512,1152]{1,0:T(8,128)(2,1)S(1)} %fusion.12, f32[512]{0:T(512)S(1)} %add_sqrt_fusion), kind=kOutput, calls=%fused_computation | convolution fusion | flops 606339072 | bytes 2885632 | tf_op jit(solution)/shard_map/dot_general | solution.py:113
  58.0 1.9 %collective-permute-start.5 = (bf16[512,1152]{1,0:T(8,128)(2,1)}, bf16[512,1152]{1,0:T(8,128)(2,1)}, u32[]{:S(2)}, u32[]{:S(2)}) collective-permute-start(bf16[512,1152]{1,0:T(8,128)(2,1)} %convolution_convert_fusion), channel_id=1, source_target_pairs={{0,8},{8,0},{1,9},{9,1},{2,10},{10,2},{3,11},{11,3},{4,12},{12,4},... | collective-permute-start | bytes 3538952 | tf_op jit(solution)/shard_map/ppermute | solution.py:26
  59.9 0.1 fusion.10
  60.1 0.1 convert_divide_fusion.2
  60.2 3.7 %all-to-all-start.1 = ((bf16[4,128,1152]{2,1,0:T(8,128)(2,1)}), bf16[4,128,1152]{2,1,0:T(8,128)(2,1)S(1)}, u32[]{:S(2)}, u32[]{:S(2)}) async-start(bf16[4,128,1152]{2,1,0:T(8,128)(2,1)} %bitcast.29), calls=%async_computation.1 | async-start | bytes 2359296 | tf_op jit(solution)/shard_map/all_to_all | solution.py:35
  63.9 2.4 %add_convert_fusion = bf16[512,1152]{1,0:T(8,128)(2,1)S(1)} fusion(bf16[512,1152]{1,0:T(8,128)(2,1)} %collective-permute-done.5, bf16[1024,512]{1,0:T(8,128)(2,1)} %copy-done.5, bf16[512,1152]{1,0:T(8,128)(2,1)S(1)} %copy-done.4, f32[512]{0:T(512)S(1)} %add_sqrt_fusion), kind=kOutput, calls=%fused_computation.11 | convolution fusion | flops 607518720 | bytes 4065280 | tf_op jit(solution)/shard_map/dot_general | solution.py:115
  66.4 4.9 %collective-permute-start.6 = (bf16[128,1152]{1,0:T(8,128)(2,1)S(1)}, bf16[128,1152]{1,0:T(8,128)(2,1)S(1)}, u32[]{:S(2)}, u32[]{:S(2)}) collective-permute-start(bf16[128,1152]{1,0:T(8,128)(2,1)S(1)} %bitcast.102), channel_id=1, source_target_pairs={{0,4},{2,6},{4,0},{6,2},{1,5},{3,7},{5,1},{7,3},{8,12},{10,14},{12... | collective-permute-start | bytes 884744 | tf_op jit(solution)/shard_map/ppermute | solution.py:31
  71.3 2.5 %collective-permute-start.7 = (bf16[128,1152]{1,0:T(8,128)(2,1)S(1)}, bf16[128,1152]{1,0:T(8,128)(2,1)S(1)}, u32[]{:S(2)}, u32[]{:S(2)}) collective-permute-start(bf16[128,1152]{1,0:T(8,128)(2,1)S(1)} %bitcast.101), channel_id=1, source_target_pairs={{0,2},{2,4},{4,6},{6,0},{1,3},{3,5},{5,7},{7,1},{8,10},{10,12},{12... | collective-permute-start | bytes 884744 | tf_op jit(solution)/shard_map/ppermute | solution.py:31
  73.8 4.6 %collective-permute-start.8 = (bf16[128,1152]{1,0:T(8,128)(2,1)S(1)}, bf16[128,1152]{1,0:T(8,128)(2,1)S(1)}, u32[]{:S(2)}, u32[]{:S(2)}) collective-permute-start(bf16[128,1152]{1,0:T(8,128)(2,1)S(1)} %bitcast.100), channel_id=1, source_target_pairs={{0,6},{2,0},{4,2},{6,4},{1,7},{3,1},{5,3},{7,5},{8,14},{10,8},{12,... | collective-permute-start | bytes 884744 | tf_op jit(solution)/shard_map/ppermute | solution.py:31
  78.4 0.1 fusion.11
  78.6 1.1 collective-permute-done.6
  79.6 5.9 %collective-permute-done.7 = bf16[128,1152]{1,0:T(8,128)(2,1)S(1)} collective-permute-done((bf16[128,1152]{1,0:T(8,128)(2,1)S(1)}, bf16[128,1152]{1,0:T(8,128)(2,1)S(1)}, u32[]{:S(2)}, u32[]{:S(2)}) %collective-permute-start.7) | collective-permute-done | bytes 294944 | tf_op jit(solution)/shard_map/ppermute | solution.py:31
  85.5 0.1 collective-permute-done.8
  85.6 0.2 fusion.4
  85.8 5.7 %collective-permute-start.10 = (bf16[64,1152]{1,0:T(8,128)(2,1)S(1)}, bf16[64,1152]{1,0:T(8,128)(2,1)S(1)}, u32[]{:S(2)}, u32[]{:S(2)}) collective-permute-start(bf16[64,1152]{1,0:T(8,128)(2,1)S(1)} %get-tuple-element.21), channel_id=1, source_target_pairs={{0,64},{64,0},{1,65},{65,1},{2,66},{66,2},{3,67},{67,3},{4,68},{68... | collective-permute-start | bytes 442376 | tf_op jit(solution)/shard_map/ppermute | solution.py:26
  91.5 2.7 %collective-permute-start.9 = (bf16[64,1152]{1,0:T(8,128)(2,1)S(1)}, bf16[64,1152]{1,0:T(8,128)(2,1)S(1)}, u32[]{:S(2)}, u32[]{:S(2)}) collective-permute-start(bf16[64,1152]{1,0:T(8,128)(2,1)S(1)} %get-tuple-element.37), channel_id=1, source_target_pairs={{0,1},{1,0},{2,3},{3,2},{4,5},{5,4},{6,7},{7,6},{8,9},{9,8},{10,11... | collective-permute-start | bytes 442376 | tf_op jit(solution)/shard_map/ppermute | solution.py:26
  94.3 7.0 %collective-permute-start.11 = (bf16[64,1152]{1,0:T(8,128)(2,1)S(1)}, bf16[64,1152]{1,0:T(8,128)(2,1)S(1)}, u32[]{:S(2)}, u32[]{:S(2)}) collective-permute-start(bf16[64,1152]{1,0:T(8,128)(2,1)S(1)} %get-tuple-element.21), channel_id=1, source_target_pairs={{0,65},{1,64},{64,1},{65,0},{2,67},{3,66},{66,3},{67,2},{4,69},{5,... | collective-permute-start | bytes 442376 | tf_op jit(solution)/shard_map/ppermute | solution.py:26
  101.4 1.0 reduce_sum.84
  102.3 5.8 %all-to-all-start.2 = ((bf16[4,32,1152]{2,1,0:T(8,128)(2,1)}), bf16[4,32,1152]{2,1,0:T(8,128)(2,1)S(1)}, u32[]{:S(2)}, u32[]{:S(2)}) async-start(bf16[4,32,1152]{2,1,0:T(8,128)(2,1)} %bitcast.33), calls=%async_computation.2 | async-start | bytes 589824 | tf_op jit(solution)/shard_map/all_to_all | solution.py:35
  108.1 0.2 multiply_reduce_fusion
  108.3 0.1 divide_convert_fusion
  108.4 4.6 %collective-permute-start.12 = (bf16[64,1152]{1,0:T(8,128)(2,1)S(1)}, bf16[64,1152]{1,0:T(8,128)(2,1)S(1)}, u32[]{:S(2)}, u32[]{:S(2)}) collective-permute-start(bf16[64,1152]{1,0:T(8,128)(2,1)S(1)} %divide_convert_fusion), channel_id=1, source_target_pairs={{0,6},{2,0},{4,2},{6,4},{1,7},{3,1},{5,3},{7,5},{8,14},{10,8},{12,... | collective-permute-start | bytes 442376 | tf_op jit(solution)/shard_map/ppermute | solution.py:31
  113.1 2.8 %collective-permute-start.13 = (bf16[64,1152]{1,0:T(8,128)(2,1)S(1)}, bf16[64,1152]{1,0:T(8,128)(2,1)S(1)}, u32[]{:S(2)}, u32[]{:S(2)}) collective-permute-start(bf16[64,1152]{1,0:T(8,128)(2,1)S(1)} %divide_convert_fusion), channel_id=1, source_target_pairs={{0,4},{2,6},{4,0},{6,2},{1,5},{3,7},{5,1},{7,3},{8,12},{10,14},{12... | collective-permute-start | bytes 442376 | tf_op jit(solution)/shard_map/ppermute | solution.py:31
  115.8 2.8 %collective-permute-start.14 = (bf16[64,1152]{1,0:T(8,128)(2,1)S(1)}, bf16[64,1152]{1,0:T(8,128)(2,1)S(1)}, u32[]{:S(2)}, u32[]{:S(2)}) collective-permute-start(bf16[64,1152]{1,0:T(8,128)(2,1)S(1)} %divide_convert_fusion), channel_id=1, source_target_pairs={{0,2},{2,4},{4,6},{6,0},{1,3},{3,5},{5,7},{7,1},{8,10},{10,12},{12... | collective-permute-start | bytes 442376 | tf_op jit(solution)/shard_map/ppermute | solution.py:31
  118.7 0.1 multiply_reduce_fusion.1
  118.8 0.7 divide_convert_fusion.1
  119.5 3.6 %collective-permute-done.13 = bf16[64,1152]{1,0:T(8,128)(2,1)S(1)} collective-permute-done((bf16[64,1152]{1,0:T(8,128)(2,1)S(1)}, bf16[64,1152]{1,0:T(8,128)(2,1)S(1)}, u32[]{:S(2)}, u32[]{:S(2)}) %collective-permute-start.13) | collective-permute-done | bytes 147488 | tf_op jit(solution)/shard_map/ppermute | solution.py:31
  123.1 1.7 %collective-permute-done.14 = bf16[64,1152]{1,0:T(8,128)(2,1)S(1)} collective-permute-done((bf16[64,1152]{1,0:T(8,128)(2,1)S(1)}, bf16[64,1152]{1,0:T(8,128)(2,1)S(1)}, u32[]{:S(2)}, u32[]{:S(2)}) %collective-permute-start.14) | collective-permute-done | bytes 147488 | tf_op jit(solution)/shard_map/ppermute | solution.py:31
  125.0 0.9 constant_dynamic-slice_fusion
  (66 shorter events, 0.9 us)
Async XLA Ops:
  2.8 18.0 %collective-permute-start = (bf16[64,1152]{1,0:T(8,128)(2,1)}, bf16[64,1152]{1,0:T(8,128)(2,1)S(1)}, u32[]{:S(2)}, u32[]{:S(2)}) collective-permute-start(bf16[64,1152]{1,0:T(8,128)(2,1)} %get-tuple-element.17), channel_id=1, source_target_pairs={{0,64},{64,0},{1,65},{65,1},{2,66},{66,2},{3,67},{67,3},{4,68},{68... | collective-permute-start | bytes 442376 | tf_op jit(solution)/shard_map/ppermute | solution.py:26
  6.1 44.6 %all-to-all-start = ((bf16[16,32,1152]{2,1,0:T(8,128)(2,1)}), bf16[16,32,1152]{2,1,0:T(8,128)(2,1)S(1)}, u32[]{:S(2)}, u32[]{:S(2)}) async-start(bf16[16,32,1152]{2,1,0:T(8,128)(2,1)} %get-tuple-element.18), calls=%async_computation | async-start | bytes 2359296 | tf_op jit(solution)/shard_map/all_to_all | solution.py:35
  20.8 16.5 %copy-start.1 = (bf16[256,1152]{1,0:T(8,128)(2,1)S(1)}, bf16[256,1152]{1,0:T(8,128)(2,1)}, u32[]{:S(2)}) copy-start(bf16[256,1152]{1,0:T(8,128)(2,1)} %image_ref.1) | copy-start | bytes 1769476
  20.8 10.3 %collective-permute-start.1 = (bf16[64,1152]{1,0:T(8,128)(2,1)S(1)}, bf16[64,1152]{1,0:T(8,128)(2,1)S(1)}, u32[]{:S(2)}, u32[]{:S(2)}) collective-permute-start(bf16[64,1152]{1,0:T(8,128)(2,1)S(1)} %collective-permute-done), channel_id=1, source_target_pairs={{0,6},{2,0},{4,2},{6,4},{1,7},{3,1},{5,3},{7,5},{8,14},{10,8},{12,... | collective-permute-start | bytes 442376 | tf_op jit(solution)/shard_map/ppermute | solution.py:31
  25.6 9.9 %collective-permute-start.2 = (bf16[64,1152]{1,0:T(8,128)(2,1)S(1)}, bf16[64,1152]{1,0:T(8,128)(2,1)S(1)}, u32[]{:S(2)}, u32[]{:S(2)}) collective-permute-start(bf16[64,1152]{1,0:T(8,128)(2,1)S(1)} %collective-permute-done), channel_id=1, source_target_pairs={{0,4},{2,6},{4,0},{6,2},{1,5},{3,7},{5,1},{7,3},{8,12},{10,14},{12... | collective-permute-start | bytes 442376 | tf_op jit(solution)/shard_map/ppermute | solution.py:31
  28.3 8.9 %collective-permute-start.3 = (bf16[64,1152]{1,0:T(8,128)(2,1)S(1)}, bf16[64,1152]{1,0:T(8,128)(2,1)S(1)}, u32[]{:S(2)}, u32[]{:S(2)}) collective-permute-start(bf16[64,1152]{1,0:T(8,128)(2,1)S(1)} %collective-permute-done), channel_id=1, source_target_pairs={{0,2},{2,4},{4,6},{6,0},{1,3},{3,5},{5,7},{7,1},{8,10},{10,12},{12... | collective-permute-start | bytes 442376 | tf_op jit(solution)/shard_map/ppermute | solution.py:31
  37.9 3.7 %copy-start.7 = (s32[32]{0:T(128)S(1)}, s32[32]{0:T(128)}, u32[]{:S(2)}) copy-start(s32[32]{0:T(128)} %param.7) | copy-start | bytes 388
  38.3 3.4 %copy-start = (bf16[512,1152]{1,0:T(8,128)(2,1)}, bf16[512,1152]{1,0:T(8,128)(2,1)S(1)}, u32[]{:S(2)}) copy-start(bf16[512,1152]{1,0:T(8,128)(2,1)S(1)} %fusion.1) | copy-start | bytes 3538948
  38.3 4.9 %collective-permute-start.4 = (bf16[512,1152]{1,0:T(8,128)(2,1)S(1)}, bf16[512,1152]{1,0:T(8,128)(2,1)}, u32[]{:S(2)}, u32[]{:S(2)}) collective-permute-start(bf16[512,1152]{1,0:T(8,128)(2,1)S(1)} %fusion.1), channel_id=1, source_target_pairs={{0,8},{8,0},{1,9},{9,1},{2,10},{10,2},{3,11},{11,3},{4,12},{12,4},... | collective-permute-start | bytes 3538952 | tf_op jit(solution)/shard_map/ppermute | solution.py:26
  51.0 5.0 %copy-start.3 = (bf16[512,1152]{1,0:T(8,128)(2,1)}, bf16[512,1152]{1,0:T(8,128)(2,1)S(1)}, u32[]{:S(2)}) copy-start(bf16[512,1152]{1,0:T(8,128)(2,1)S(1)} %fusion.12) | copy-start | bytes 3538948
  53.4 2.6 %copy-start.5 = (bf16[1024,512]{1,0:T(8,128)(2,1)}, bf16[1024,512]{1,0:T(8,128)(2,1)S(1)}, u32[]{:S(2)}) copy-start(bf16[1024,512]{1,0:T(8,128)(2,1)S(1)} %subtract_convert_fusion) | copy-start | bytes 3145732
  56.0 4.0 %copy-start.2 = (bf16[256,1152]{1,0:T(8,128)(2,1)S(1)}, bf16[256,1152]{1,0:T(8,128)(2,1)}, u32[]{:S(2)}) copy-start(bf16[256,1152]{1,0:T(8,128)(2,1)} %image_ref.1) | copy-start | bytes 1769476
  58.0 5.9 %collective-permute-start.5 = (bf16[512,1152]{1,0:T(8,128)(2,1)}, bf16[512,1152]{1,0:T(8,128)(2,1)}, u32[]{:S(2)}, u32[]{:S(2)}) collective-permute-start(bf16[512,1152]{1,0:T(8,128)(2,1)} %convolution_convert_fusion), channel_id=1, source_target_pairs={{0,8},{8,0},{1,9},{9,1},{2,10},{10,2},{3,11},{11,3},{4,12},{12,4},... | collective-permute-start | bytes 3538952 | tf_op jit(solution)/shard_map/ppermute | solution.py:26
  60.2 3.7 %copy-start.4 = (bf16[512,1152]{1,0:T(8,128)(2,1)S(1)}, bf16[512,1152]{1,0:T(8,128)(2,1)}, u32[]{:S(2)}) copy-start(bf16[512,1152]{1,0:T(8,128)(2,1)} %copy-done.3) | copy-start | bytes 3538948
  60.2 34.1 %all-to-all-start.1 = ((bf16[4,128,1152]{2,1,0:T(8,128)(2,1)}), bf16[4,128,1152]{2,1,0:T(8,128)(2,1)S(1)}, u32[]{:S(2)}, u32[]{:S(2)}) async-start(bf16[4,128,1152]{2,1,0:T(8,128)(2,1)} %bitcast.29), calls=%async_computation.1 | async-start | bytes 2359296 | tf_op jit(solution)/shard_map/all_to_all | solution.py:35
  66.3 12.1 %copy-start.6 = (bf16[32,1152]{1,0:T(8,128)(2,1)S(1)}, bf16[32,1152]{1,0:T(8,128)(2,1)}, u32[]{:S(2)}) copy-start(bf16[32,1152]{1,0:T(8,128)(2,1)} %text_ref.1) | copy-start | bytes 221188
  66.4 13.2 %collective-permute-start.6 = (bf16[128,1152]{1,0:T(8,128)(2,1)S(1)}, bf16[128,1152]{1,0:T(8,128)(2,1)S(1)}, u32[]{:S(2)}, u32[]{:S(2)}) collective-permute-start(bf16[128,1152]{1,0:T(8,128)(2,1)S(1)} %bitcast.102), channel_id=1, source_target_pairs={{0,4},{2,6},{4,0},{6,2},{1,5},{3,7},{5,1},{7,3},{8,12},{10,14},{12... | collective-permute-start | bytes 884744 | tf_op jit(solution)/shard_map/ppermute | solution.py:31
  71.3 14.2 %collective-permute-start.7 = (bf16[128,1152]{1,0:T(8,128)(2,1)S(1)}, bf16[128,1152]{1,0:T(8,128)(2,1)S(1)}, u32[]{:S(2)}, u32[]{:S(2)}) collective-permute-start(bf16[128,1152]{1,0:T(8,128)(2,1)S(1)} %bitcast.101), channel_id=1, source_target_pairs={{0,2},{2,4},{4,6},{6,0},{1,3},{3,5},{5,7},{7,1},{8,10},{10,12},{12... | collective-permute-start | bytes 884744 | tf_op jit(solution)/shard_map/ppermute | solution.py:31
  73.8 11.8 %collective-permute-start.8 = (bf16[128,1152]{1,0:T(8,128)(2,1)S(1)}, bf16[128,1152]{1,0:T(8,128)(2,1)S(1)}, u32[]{:S(2)}, u32[]{:S(2)}) collective-permute-start(bf16[128,1152]{1,0:T(8,128)(2,1)S(1)} %bitcast.100), channel_id=1, source_target_pairs={{0,6},{2,0},{4,2},{6,4},{1,7},{3,1},{5,3},{7,5},{8,14},{10,8},{12,... | collective-permute-start | bytes 884744 | tf_op jit(solution)/shard_map/ppermute | solution.py:31
  85.8 22.3 %collective-permute-start.10 = (bf16[64,1152]{1,0:T(8,128)(2,1)S(1)}, bf16[64,1152]{1,0:T(8,128)(2,1)S(1)}, u32[]{:S(2)}, u32[]{:S(2)}) collective-permute-start(bf16[64,1152]{1,0:T(8,128)(2,1)S(1)} %get-tuple-element.21), channel_id=1, source_target_pairs={{0,64},{64,0},{1,65},{65,1},{2,66},{66,2},{3,67},{67,3},{4,68},{68... | collective-permute-start | bytes 442376 | tf_op jit(solution)/shard_map/ppermute | solution.py:26
  91.5 16.6 %collective-permute-start.9 = (bf16[64,1152]{1,0:T(8,128)(2,1)S(1)}, bf16[64,1152]{1,0:T(8,128)(2,1)S(1)}, u32[]{:S(2)}, u32[]{:S(2)}) collective-permute-start(bf16[64,1152]{1,0:T(8,128)(2,1)S(1)} %get-tuple-element.37), channel_id=1, source_target_pairs={{0,1},{1,0},{2,3},{3,2},{4,5},{5,4},{6,7},{7,6},{8,9},{9,8},{10,11... | collective-permute-start | bytes 442376 | tf_op jit(solution)/shard_map/ppermute | solution.py:26
  94.3 13.9 %collective-permute-start.11 = (bf16[64,1152]{1,0:T(8,128)(2,1)S(1)}, bf16[64,1152]{1,0:T(8,128)(2,1)S(1)}, u32[]{:S(2)}, u32[]{:S(2)}) collective-permute-start(bf16[64,1152]{1,0:T(8,128)(2,1)S(1)} %get-tuple-element.21), channel_id=1, source_target_pairs={{0,65},{1,64},{64,1},{65,0},{2,67},{3,66},{66,3},{67,2},{4,69},{5,... | collective-permute-start | bytes 442376 | tf_op jit(solution)/shard_map/ppermute | solution.py:26
  102.3 16.3 %all-to-all-start.2 = ((bf16[4,32,1152]{2,1,0:T(8,128)(2,1)}), bf16[4,32,1152]{2,1,0:T(8,128)(2,1)S(1)}, u32[]{:S(2)}, u32[]{:S(2)}) async-start(bf16[4,32,1152]{2,1,0:T(8,128)(2,1)} %bitcast.33), calls=%async_computation.2 | async-start | bytes 589824 | tf_op jit(solution)/shard_map/all_to_all | solution.py:35
  108.4 11.1 %collective-permute-start.12 = (bf16[64,1152]{1,0:T(8,128)(2,1)S(1)}, bf16[64,1152]{1,0:T(8,128)(2,1)S(1)}, u32[]{:S(2)}, u32[]{:S(2)}) collective-permute-start(bf16[64,1152]{1,0:T(8,128)(2,1)S(1)} %divide_convert_fusion), channel_id=1, source_target_pairs={{0,6},{2,0},{4,2},{6,4},{1,7},{3,1},{5,3},{7,5},{8,14},{10,8},{12,... | collective-permute-start | bytes 442376 | tf_op jit(solution)/shard_map/ppermute | solution.py:31
  113.1 10.1 %collective-permute-start.13 = (bf16[64,1152]{1,0:T(8,128)(2,1)S(1)}, bf16[64,1152]{1,0:T(8,128)(2,1)S(1)}, u32[]{:S(2)}, u32[]{:S(2)}) collective-permute-start(bf16[64,1152]{1,0:T(8,128)(2,1)S(1)} %divide_convert_fusion), channel_id=1, source_target_pairs={{0,4},{2,6},{4,0},{6,2},{1,5},{3,7},{5,1},{7,3},{8,12},{10,14},{12... | collective-permute-start | bytes 442376 | tf_op jit(solution)/shard_map/ppermute | solution.py:31
  115.8 9.0 %collective-permute-start.14 = (bf16[64,1152]{1,0:T(8,128)(2,1)S(1)}, bf16[64,1152]{1,0:T(8,128)(2,1)S(1)}, u32[]{:S(2)}, u32[]{:S(2)}) collective-permute-start(bf16[64,1152]{1,0:T(8,128)(2,1)S(1)} %divide_convert_fusion), channel_id=1, source_target_pairs={{0,2},{2,4},{4,6},{6,0},{1,3},{3,5},{5,7},{7,1},{8,10},{10,12},{12... | collective-permute-start | bytes 442376 | tf_op jit(solution)/shard_map/ppermute | solution.py:31

commit v20 on v19

--- a/solution.py
+++ b/solution.py
@@ -7,9 +7,10 @@
 
 epsilon = 1e-06
 AXES = ("yh", "yl", "w", "c", "x", "l")
-CLASSES = ((0, 3, 5, 6), (1, 2, 4, 7))
+CLASSES = ((0, 6, 3, 5), (1, 7, 2, 4))
+PLACES = (0, 2, 3, 1)
 RINGS = ("yh", "yl", "w", "l")
-ORDER = ((0, 0), (0, 1), (0, 2), (0, 3), (1, 2), (1, 3), (1, 0), (1, 1), (2, 0), (2, 1), (2, 2), (2, 3), (3, 2), (3, 3), (3, 0), (3, 1))
+ORDER = ((0, 0), (0, 2), (0, 3), (0, 1), (2, 3), (2, 1), (2, 0), (2, 2), (3, 0), (3, 2), (3, 3), (3, 1), (1, 3), (1, 1), (1, 0), (1, 2))
 TEXT_GROUPS = [[of_y[i] * 8 + of_z[j] for i, j in ORDER] for of_y in CLASSES for of_z in CLASSES]
 NARROW = ("x", "l")
 BF16, F32 = jnp.bfloat16, jnp.float32
@@ -92,7 +93,8 @@
     text_bf = unit_rows(texts)[0].astype(BF16)
 
     wanted = positive - lax.axis_index(("yh", "yl", "w", "c")) * rows + lax.axis_index("yl") * rows
-    slot = lax.axis_index(("w", "yh")) * mine
+    places = jnp.array(PLACES, jnp.int32)
+    slot = (places[lax.axis_index("w")] * 4 + places[lax.axis_index("yh")]) * mine
     wanted = lax.dynamic_update_slice_in_dim(jnp.full((texts.shape[0],), -1, jnp.int32), wanted, slot, 0)
     hit = (jnp.arange(2 * near.shape[0], dtype=jnp.int32)[:, None] == wanted[None, :]).astype(F32)
 

time: 127 us -> 127 us (level)
  waiting for transfers between devices: 25.5 us -> 23.7 us
    ppermute x6, waiting for transfers between devices: 1.48 us -> 0.02 us  [swap(): return lax.ppermute(block, axes, [(i, count - 1 - i) for i in range(count)])]
  transfers between devices with their start and end apart: 18 -> 18, of which waited for: 9 -> 8; matrix products, arithmetic and copies ran while one was open for 7% -> 7% of each run, Pallas kernels for 0% -> 0%
where the time goes in v20:
time: 127 us; the launch traced here: 126 us
  starting transfers between devices  78.9 us (62%)
  waiting for transfers between devices  23.7 us (19%)
  matrix products  9.03 us (7%)
  other arithmetic  5.98 us (5%)
  between operations  3.74 us (3%)
  Pallas kernels  2.19 us (2%)
  local copies, waits for them, and re-layouts  2.1 us (2%)
    ppermute x9, starting transfers between devices, shift(): lax.ppermute(block, axis, [(i, (i + distance) % count) for i in range(cou...  32.5 us
    all_to_all x3, starting transfers between devices, exchange(): lax.all_to_all(blocks, axes, 0, 0, axis_index_groups=groups, tiled=True)  24.7 us
    ppermute x6, starting transfers between devices, swap(): return lax.ppermute(block, axes, [(i, count - 1 - i) for i in range(count)])  21.8 us
    ppermute x9, waiting for transfers between devices, shift(): lax.ppermute(block, axis, [(i, (i + distance) % count) for i in range(cou...  18.3 us
    all_to_all x3, waiting for transfers between devices, exchange(): lax.all_to_all(blocks, axes, 0, 0, axis_index_groups=groups, tiled=True)  5.39 us
    dot_general x1, matrix products, local(): lax.dot_general(grad, images, (((0,), (0,)), ((), ())), preferred_element...  2.58 us
  transfers between devices with their start and end apart: 18, of which 8 were waited for; matrix products, arithmetic and copies ran while one was open for 7% of the time, Pallas kernels for 0%

profile of v20, /device:TPU:56, one launch (start us, length us, event | category | flops | bytes accessed | tf_op | source)
XLA Modules:
  0.0 125.7 jit_solution(9840937360060747575)
XLA Ops:
  0.6 2.2 %first_copies.1 = (bf16[64,1152]{1,0:T(8,128)(2,1)}, bf16[16,32,1152]{2,1,0:T(8,128)(2,1)}) custom-call(s32[1]{0:T(128)} %bitcast.1.x_ref, bf16[256,1152]{1,0:T(8,128)(2,1)} %image_ref.1, bf16[32,1152]{1,0:T(8,128)(2,1)} %text_ref.1), custom_call_target="tpu_custom_call" | custom-call | tf_op jit(solution)/shard_map/first_copies/pallas_call | solution.py:55
  2.8 3.2 %collective-permute-start = (bf16[64,1152]{1,0:T(8,128)(2,1)}, bf16[64,1152]{1,0:T(8,128)(2,1)S(1)}, u32[]{:S(2)}, u32[]{:S(2)}) collective-permute-start(bf16[64,1152]{1,0:T(8,128)(2,1)} %get-tuple-element.17), channel_id=1, source_target_pairs={{0,64},{64,0},{1,65},{65,1},{2,66},{66,2},{3,67},{67,3},{4,68},{68... | collective-permute-start | bytes 442376 | tf_op jit(solution)/shard_map/ppermute | solution.py:27
  6.1 14.7 %all-to-all-start = ((bf16[16,32,1152]{2,1,0:T(8,128)(2,1)}), bf16[16,32,1152]{2,1,0:T(8,128)(2,1)S(1)}, u32[]{:S(2)}, u32[]{:S(2)}) async-start(bf16[16,32,1152]{2,1,0:T(8,128)(2,1)} %get-tuple-element.18), calls=%async_computation | async-start | bytes 2359296 | tf_op jit(solution)/shard_map/all_to_all | solution.py:36
  20.8 4.8 %collective-permute-start.1 = (bf16[64,1152]{1,0:T(8,128)(2,1)S(1)}, bf16[64,1152]{1,0:T(8,128)(2,1)S(1)}, u32[]{:S(2)}, u32[]{:S(2)}) collective-permute-start(bf16[64,1152]{1,0:T(8,128)(2,1)S(1)} %collective-permute-done), channel_id=1, source_target_pairs={{0,6},{2,0},{4,2},{6,4},{1,7},{3,1},{5,3},{7,5},{8,14},{10,8},{12,... | collective-permute-start | bytes 442376 | tf_op jit(solution)/shard_map/ppermute | solution.py:32
  25.6 2.7 %collective-permute-start.2 = (bf16[64,1152]{1,0:T(8,128)(2,1)S(1)}, bf16[64,1152]{1,0:T(8,128)(2,1)S(1)}, u32[]{:S(2)}, u32[]{:S(2)}) collective-permute-start(bf16[64,1152]{1,0:T(8,128)(2,1)S(1)} %collective-permute-done), channel_id=1, source_target_pairs={{0,4},{2,6},{4,0},{6,2},{1,5},{3,7},{5,1},{7,3},{8,12},{10,14},{12... | collective-permute-start | bytes 442376 | tf_op jit(solution)/shard_map/ppermute | solution.py:32
  28.3 2.8 %collective-permute-start.3 = (bf16[64,1152]{1,0:T(8,128)(2,1)S(1)}, bf16[64,1152]{1,0:T(8,128)(2,1)S(1)}, u32[]{:S(2)}, u32[]{:S(2)}) collective-permute-start(bf16[64,1152]{1,0:T(8,128)(2,1)S(1)} %collective-permute-done), channel_id=1, source_target_pairs={{0,2},{2,4},{4,6},{6,0},{1,3},{3,5},{5,7},{7,1},{8,10},{10,12},{12... | collective-permute-start | bytes 442376 | tf_op jit(solution)/shard_map/ppermute | solution.py:32
  31.2 4.3 %collective-permute-done.2 = bf16[64,1152]{1,0:T(8,128)(2,1)S(1)} collective-permute-done((bf16[64,1152]{1,0:T(8,128)(2,1)S(1)}, bf16[64,1152]{1,0:T(8,128)(2,1)S(1)}, u32[]{:S(2)}, u32[]{:S(2)}) %collective-permute-start.2) | collective-permute-done | bytes 147488 | tf_op jit(solution)/shard_map/ppermute | solution.py:32
  35.5 1.7 %collective-permute-done.3 = bf16[64,1152]{1,0:T(8,128)(2,1)S(1)} collective-permute-done((bf16[64,1152]{1,0:T(8,128)(2,1)S(1)}, bf16[64,1152]{1,0:T(8,128)(2,1)S(1)}, u32[]{:S(2)}, u32[]{:S(2)}) %collective-permute-start.3) | collective-permute-done | bytes 147488 | tf_op jit(solution)/shard_map/ppermute | solution.py:32
  37.3 0.2 broadcast_select_fusion.1
  37.6 0.3 fusion
  37.9 0.4 fusion.1
  38.3 1.9 %collective-permute-start.4 = (bf16[512,1152]{1,0:T(8,128)(2,1)S(1)}, bf16[512,1152]{1,0:T(8,128)(2,1)}, u32[]{:S(2)}, u32[]{:S(2)}) collective-permute-start(bf16[512,1152]{1,0:T(8,128)(2,1)S(1)} %fusion.1), channel_id=1, source_target_pairs={{0,8},{8,0},{1,9},{9,1},{2,10},{10,2},{3,11},{11,3},{4,12},{12,4},... | collective-permute-start | bytes 3538952 | tf_op jit(solution)/shard_map/ppermute | solution.py:27
  40.2 0.6 fusion.33
  43.4 0.1 add_dynamic-update-slice_fusion
  43.5 1.8 %pad_maximum_fusion = bf16[1024,1152]{1,0:T(8,128)(2,1)S(1)} fusion(bf16[512,1152]{1,0:T(8,128)(2,1)} %collective-permute-done.4, bf16[512,1152]{1,0:T(8,128)(2,1)} %copy-done), kind=kLoop, calls=%fused_computation.10 | loop fusion | flops 4718592 | bytes 4718592 | tf_op jit(solution)/shard_map/concatenate | solution.py:107
  45.3 5.4 %all-to-all-done = bf16[16,32,1152]{2,1,0:T(8,128)(2,1)S(1)} async-done(((bf16[16,32,1152]{2,1,0:T(8,128)(2,1)}), bf16[16,32,1152]{2,1,0:T(8,128)(2,1)S(1)}, u32[]{:S(2)}, u32[]{:S(2)}) %all-to-all-start) | async-done | bytes 1179680 | tf_op jit(solution)/shard_map/all_to_all | solution.py:36
  51.0 0.3 fusion.2
  51.3 2.1 %subtract_convert_fusion = bf16[1024,512]{1,0:T(8,128)(2,1)S(1)} fusion(bf16[1024,1152]{1,0:T(8,128)(2,1)S(1)} %pad_maximum_fusion, s32[512]{0:T(512)S(1)} %add_dynamic-update-slice_fusion, f32[]{:T(128)} %bitcast.98, f32[]{:T(128)} %bitcast, bf16[512,1152]{1,0:T(8,128)(2,1)S(1)} %fusion.12, f32[512]{0:T(512)S(1)} %add_sqrt_fusion), kind=kOutput, calls=%fused_computation.12 | convolution fusion | flops 1214447616 | bytes 4591624 | tf_op jit(solution)/shard_map/dot_general | solution.py:108
  53.4 2.6 %convolution_convert_fusion.1 = bf16[512,1152]{1,0:T(8,128)(2,1)} fusion(bf16[1024,512]{1,0:T(8,128)(2,1)S(1)} %subtract_convert_fusion, bf16[1024,1152]{1,0:T(8,128)(2,1)S(1)} %pad_maximum_fusion), kind=kOutput, calls=%fused_computation.1 | convolution fusion | flops 1208549376 | bytes 4587520 | tf_op jit(solution)/shard_map/dot_general | solution.py:110
  56.0 2.0 %convolution_convert_fusion = bf16[512,1152]{1,0:T(8,128)(2,1)} fusion(bf16[1024,512]{1,0:T(8,128)(2,1)S(1)} %subtract_convert_fusion, bf16[512,1152]{1,0:T(8,128)(2,1)S(1)} %fusion.12, f32[512]{0:T(512)S(1)} %add_sqrt_fusion), kind=kOutput, calls=%fused_computation | convolution fusion | flops 606339072 | bytes 2885632 | tf_op jit(solution)/shard_map/dot_general | solution.py:115
  58.0 1.9 %collective-permute-start.5 = (bf16[512,1152]{1,0:T(8,128)(2,1)}, bf16[512,1152]{1,0:T(8,128)(2,1)}, u32[]{:S(2)}, u32[]{:S(2)}) collective-permute-start(bf16[512,1152]{1,0:T(8,128)(2,1)} %convolution_convert_fusion), channel_id=1, source_target_pairs={{0,8},{8,0},{1,9},{9,1},{2,10},{10,2},{3,11},{11,3},{4,12},{12,4},... | collective-permute-start | bytes 3538952 | tf_op jit(solution)/shard_map/ppermute | solution.py:27
  59.9 0.1 fusion.10
  60.1 0.1 convert_divide_fusion.2
  60.2 3.7 %all-to-all-start.1 = ((bf16[4,128,1152]{2,1,0:T(8,128)(2,1)}), bf16[4,128,1152]{2,1,0:T(8,128)(2,1)S(1)}, u32[]{:S(2)}, u32[]{:S(2)}) async-start(bf16[4,128,1152]{2,1,0:T(8,128)(2,1)} %bitcast.30), calls=%async_computation.1 | async-start | bytes 2359296 | tf_op jit(solution)/shard_map/all_to_all | solution.py:36
  63.9 2.4 %add_convert_fusion = bf16[512,1152]{1,0:T(8,128)(2,1)S(1)} fusion(bf16[512,1152]{1,0:T(8,128)(2,1)} %collective-permute-done.5, bf16[1024,512]{1,0:T(8,128)(2,1)} %copy-done.5, bf16[512,1152]{1,0:T(8,128)(2,1)S(1)} %copy-done.4, f32[512]{0:T(512)S(1)} %add_sqrt_fusion), kind=kOutput, calls=%fused_computation.11 | convolution fusion | flops 607518720 | bytes 4065280 | tf_op jit(solution)/shard_map/dot_general | solution.py:117
  66.4 4.9 %collective-permute-start.6 = (bf16[128,1152]{1,0:T(8,128)(2,1)S(1)}, bf16[128,1152]{1,0:T(8,128)(2,1)S(1)}, u32[]{:S(2)}, u32[]{:S(2)}) collective-permute-start(bf16[128,1152]{1,0:T(8,128)(2,1)S(1)} %bitcast.103), channel_id=1, source_target_pairs={{0,4},{2,6},{4,0},{6,2},{1,5},{3,7},{5,1},{7,3},{8,12},{10,14},{12... | collective-permute-start | bytes 884744 | tf_op jit(solution)/shard_map/ppermute | solution.py:32
  71.3 2.5 %collective-permute-start.7 = (bf16[128,1152]{1,0:T(8,128)(2,1)S(1)}, bf16[128,1152]{1,0:T(8,128)(2,1)S(1)}, u32[]{:S(2)}, u32[]{:S(2)}) collective-permute-start(bf16[128,1152]{1,0:T(8,128)(2,1)S(1)} %bitcast.102), channel_id=1, source_target_pairs={{0,2},{2,4},{4,6},{6,0},{1,3},{3,5},{5,7},{7,1},{8,10},{10,12},{12... | collective-permute-start | bytes 884744 | tf_op jit(solution)/shard_map/ppermute | solution.py:32
  73.8 4.6 %collective-permute-start.8 = (bf16[128,1152]{1,0:T(8,128)(2,1)S(1)}, bf16[128,1152]{1,0:T(8,128)(2,1)S(1)}, u32[]{:S(2)}, u32[]{:S(2)}) collective-permute-start(bf16[128,1152]{1,0:T(8,128)(2,1)S(1)} %bitcast.101), channel_id=1, source_target_pairs={{0,6},{2,0},{4,2},{6,4},{1,7},{3,1},{5,3},{7,5},{8,14},{10,8},{12,... | collective-permute-start | bytes 884744 | tf_op jit(solution)/shard_map/ppermute | solution.py:32
  78.4 0.1 fusion.11
  78.6 1.1 collective-permute-done.6
  79.6 5.9 %collective-permute-done.7 = bf16[128,1152]{1,0:T(8,128)(2,1)S(1)} collective-permute-done((bf16[128,1152]{1,0:T(8,128)(2,1)S(1)}, bf16[128,1152]{1,0:T(8,128)(2,1)S(1)}, u32[]{:S(2)}, u32[]{:S(2)}) %collective-permute-start.7) | collective-permute-done | bytes 294944 | tf_op jit(solution)/shard_map/ppermute | solution.py:32
  85.6 0.2 fusion.4
  85.8 5.7 %collective-permute-start.10 = (bf16[64,1152]{1,0:T(8,128)(2,1)S(1)}, bf16[64,1152]{1,0:T(8,128)(2,1)S(1)}, u32[]{:S(2)}, u32[]{:S(2)}) collective-permute-start(bf16[64,1152]{1,0:T(8,128)(2,1)S(1)} %get-tuple-element.21), channel_id=1, source_target_pairs={{0,64},{64,0},{1,65},{65,1},{2,66},{66,2},{3,67},{67,3},{4,68},{68... | collective-permute-start | bytes 442376 | tf_op jit(solution)/shard_map/ppermute | solution.py:27
  91.5 2.7 %collective-permute-start.9 = (bf16[64,1152]{1,0:T(8,128)(2,1)S(1)}, bf16[64,1152]{1,0:T(8,128)(2,1)S(1)}, u32[]{:S(2)}, u32[]{:S(2)}) collective-permute-start(bf16[64,1152]{1,0:T(8,128)(2,1)S(1)} %get-tuple-element.37), channel_id=1, source_target_pairs={{0,1},{1,0},{2,3},{3,2},{4,5},{5,4},{6,7},{7,6},{8,9},{9,8},{10,11... | collective-permute-start | bytes 442376 | tf_op jit(solution)/shard_map/ppermute | solution.py:27
  94.3 6.3 %collective-permute-start.11 = (bf16[64,1152]{1,0:T(8,128)(2,1)S(1)}, bf16[64,1152]{1,0:T(8,128)(2,1)S(1)}, u32[]{:S(2)}, u32[]{:S(2)}) collective-permute-start(bf16[64,1152]{1,0:T(8,128)(2,1)S(1)} %get-tuple-element.21), channel_id=1, source_target_pairs={{0,65},{1,64},{64,1},{65,0},{2,67},{3,66},{66,3},{67,2},{4,69},{5,... | collective-permute-start | bytes 442376 | tf_op jit(solution)/shard_map/ppermute | solution.py:27
  100.6 0.1 convert_divide_fusion.3
  100.7 1.0 reduce_sum.84
  101.6 6.3 %all-to-all-start.2 = ((bf16[4,32,1152]{2,1,0:T(8,128)(2,1)}), bf16[4,32,1152]{2,1,0:T(8,128)(2,1)S(1)}, u32[]{:S(2)}, u32[]{:S(2)}) async-start(bf16[4,32,1152]{2,1,0:T(8,128)(2,1)} %bitcast.34), calls=%async_computation.2 | async-start | bytes 589824 | tf_op jit(solution)/shard_map/all_to_all | solution.py:36
  107.9 0.2 multiply_reduce_fusion
  108.1 0.1 divide_convert_fusion
  108.2 4.7 %collective-permute-start.12 = (bf16[64,1152]{1,0:T(8,128)(2,1)S(1)}, bf16[64,1152]{1,0:T(8,128)(2,1)S(1)}, u32[]{:S(2)}, u32[]{:S(2)}) collective-permute-start(bf16[64,1152]{1,0:T(8,128)(2,1)S(1)} %divide_convert_fusion), channel_id=1, source_target_pairs={{0,6},{2,0},{4,2},{6,4},{1,7},{3,1},{5,3},{7,5},{8,14},{10,8},{12,... | collective-permute-start | bytes 442376 | tf_op jit(solution)/shard_map/ppermute | solution.py:32
  112.9 2.7 %collective-permute-start.13 = (bf16[64,1152]{1,0:T(8,128)(2,1)S(1)}, bf16[64,1152]{1,0:T(8,128)(2,1)S(1)}, u32[]{:S(2)}, u32[]{:S(2)}) collective-permute-start(bf16[64,1152]{1,0:T(8,128)(2,1)S(1)} %divide_convert_fusion), channel_id=1, source_target_pairs={{0,4},{2,6},{4,0},{6,2},{1,5},{3,7},{5,1},{7,3},{8,12},{10,14},{12... | collective-permute-start | bytes 442376 | tf_op jit(solution)/shard_map/ppermute | solution.py:32
  115.6 2.8 %collective-permute-start.14 = (bf16[64,1152]{1,0:T(8,128)(2,1)S(1)}, bf16[64,1152]{1,0:T(8,128)(2,1)S(1)}, u32[]{:S(2)}, u32[]{:S(2)}) collective-permute-start(bf16[64,1152]{1,0:T(8,128)(2,1)S(1)} %divide_convert_fusion), channel_id=1, source_target_pairs={{0,2},{2,4},{4,6},{6,0},{1,3},{3,5},{5,7},{7,1},{8,10},{10,12},{12... | collective-permute-start | bytes 442376 | tf_op jit(solution)/shard_map/ppermute | solution.py:32
  118.5 0.1 multiply_reduce_fusion.1
  118.6 0.7 divide_convert_fusion.1
  119.4 3.6 %collective-permute-done.13 = bf16[64,1152]{1,0:T(8,128)(2,1)S(1)} collective-permute-done((bf16[64,1152]{1,0:T(8,128)(2,1)S(1)}, bf16[64,1152]{1,0:T(8,128)(2,1)S(1)}, u32[]{:S(2)}, u32[]{:S(2)}) %collective-permute-start.13) | collective-permute-done | bytes 147488 | tf_op jit(solution)/shard_map/ppermute | solution.py:32
  122.9 1.7 %collective-permute-done.14 = bf16[64,1152]{1,0:T(8,128)(2,1)S(1)} collective-permute-done((bf16[64,1152]{1,0:T(8,128)(2,1)S(1)}, bf16[64,1152]{1,0:T(8,128)(2,1)S(1)}, u32[]{:S(2)}, u32[]{:S(2)}) %collective-permute-start.14) | collective-permute-done | bytes 147488 | tf_op jit(solution)/shard_map/ppermute | solution.py:32
  124.8 0.9 constant_dynamic-slice_fusion
  (69 shorter events, 0.9 us)
Async XLA Ops:
  2.8 18.0 %collective-permute-start = (bf16[64,1152]{1,0:T(8,128)(2,1)}, bf16[64,1152]{1,0:T(8,128)(2,1)S(1)}, u32[]{:S(2)}, u32[]{:S(2)}) collective-permute-start(bf16[64,1152]{1,0:T(8,128)(2,1)} %get-tuple-element.17), channel_id=1, source_target_pairs={{0,64},{64,0},{1,65},{65,1},{2,66},{66,2},{3,67},{67,3},{4,68},{68... | collective-permute-start | bytes 442376 | tf_op jit(solution)/shard_map/ppermute | solution.py:27
  6.1 44.6 %all-to-all-start = ((bf16[16,32,1152]{2,1,0:T(8,128)(2,1)}), bf16[16,32,1152]{2,1,0:T(8,128)(2,1)S(1)}, u32[]{:S(2)}, u32[]{:S(2)}) async-start(bf16[16,32,1152]{2,1,0:T(8,128)(2,1)} %get-tuple-element.18), calls=%async_computation | async-start | bytes 2359296 | tf_op jit(solution)/shard_map/all_to_all | solution.py:36
  20.8 16.5 %copy-start.1 = (bf16[256,1152]{1,0:T(8,128)(2,1)S(1)}, bf16[256,1152]{1,0:T(8,128)(2,1)}, u32[]{:S(2)}) copy-start(bf16[256,1152]{1,0:T(8,128)(2,1)} %image_ref.1) | copy-start | bytes 1769476
  20.8 10.3 %collective-permute-start.1 = (bf16[64,1152]{1,0:T(8,128)(2,1)S(1)}, bf16[64,1152]{1,0:T(8,128)(2,1)S(1)}, u32[]{:S(2)}, u32[]{:S(2)}) collective-permute-start(bf16[64,1152]{1,0:T(8,128)(2,1)S(1)} %collective-permute-done), channel_id=1, source_target_pairs={{0,6},{2,0},{4,2},{6,4},{1,7},{3,1},{5,3},{7,5},{8,14},{10,8},{12,... | collective-permute-start | bytes 442376 | tf_op jit(solution)/shard_map/ppermute | solution.py:32
  25.6 9.9 %collective-permute-start.2 = (bf16[64,1152]{1,0:T(8,128)(2,1)S(1)}, bf16[64,1152]{1,0:T(8,128)(2,1)S(1)}, u32[]{:S(2)}, u32[]{:S(2)}) collective-permute-start(bf16[64,1152]{1,0:T(8,128)(2,1)S(1)} %collective-permute-done), channel_id=1, source_target_pairs={{0,4},{2,6},{4,0},{6,2},{1,5},{3,7},{5,1},{7,3},{8,12},{10,14},{12... | collective-permute-start | bytes 442376 | tf_op jit(solution)/shard_map/ppermute | solution.py:32
  28.3 8.9 %collective-permute-start.3 = (bf16[64,1152]{1,0:T(8,128)(2,1)S(1)}, bf16[64,1152]{1,0:T(8,128)(2,1)S(1)}, u32[]{:S(2)}, u32[]{:S(2)}) collective-permute-start(bf16[64,1152]{1,0:T(8,128)(2,1)S(1)} %collective-permute-done), channel_id=1, source_target_pairs={{0,2},{2,4},{4,6},{6,0},{1,3},{3,5},{5,7},{7,1},{8,10},{10,12},{12... | collective-permute-start | bytes 442376 | tf_op jit(solution)/shard_map/ppermute | solution.py:32
  37.9 2.3 %copy-start.7 = (s32[4]{0:T(128)S(1)}, s32[4]{0:T(128)}, u32[]{:S(2)}) copy-start(s32[4]{0:T(128)} %constant.82.clone) | copy-start | bytes 52
  37.9 5.5 %copy-start.8 = (s32[32]{0:T(128)S(1)}, s32[32]{0:T(128)}, u32[]{:S(2)}) copy-start(s32[32]{0:T(128)} %param.8) | copy-start | bytes 388
  38.3 5.2 %copy-start = (bf16[512,1152]{1,0:T(8,128)(2,1)}, bf16[512,1152]{1,0:T(8,128)(2,1)S(1)}, u32[]{:S(2)}) copy-start(bf16[512,1152]{1,0:T(8,128)(2,1)S(1)} %fusion.1) | copy-start | bytes 3538948
  38.3 5.2 %collective-permute-start.4 = (bf16[512,1152]{1,0:T(8,128)(2,1)S(1)}, bf16[512,1152]{1,0:T(8,128)(2,1)}, u32[]{:S(2)}, u32[]{:S(2)}) collective-permute-start(bf16[512,1152]{1,0:T(8,128)(2,1)S(1)} %fusion.1), channel_id=1, source_target_pairs={{0,8},{8,0},{1,9},{9,1},{2,10},{10,2},{3,11},{11,3},{4,12},{12,4},... | collective-permute-start | bytes 3538952 | tf_op jit(solution)/shard_map/ppermute | solution.py:27
  51.0 5.0 %copy-start.3 = (bf16[512,1152]{1,0:T(8,128)(2,1)}, bf16[512,1152]{1,0:T(8,128)(2,1)S(1)}, u32[]{:S(2)}) copy-start(bf16[512,1152]{1,0:T(8,128)(2,1)S(1)} %fusion.12) | copy-start | bytes 3538948
  53.4 2.6 %copy-start.5 = (bf16[1024,512]{1,0:T(8,128)(2,1)}, bf16[1024,512]{1,0:T(8,128)(2,1)S(1)}, u32[]{:S(2)}) copy-start(bf16[1024,512]{1,0:T(8,128)(2,1)S(1)} %subtract_convert_fusion) | copy-start | bytes 3145732
  56.0 4.0 %copy-start.2 = (bf16[256,1152]{1,0:T(8,128)(2,1)S(1)}, bf16[256,1152]{1,0:T(8,128)(2,1)}, u32[]{:S(2)}) copy-start(bf16[256,1152]{1,0:T(8,128)(2,1)} %image_ref.1) | copy-start | bytes 1769476
  58.0 5.9 %collective-permute-start.5 = (bf16[512,1152]{1,0:T(8,128)(2,1)}, bf16[512,1152]{1,0:T(8,128)(2,1)}, u32[]{:S(2)}, u32[]{:S(2)}) collective-permute-start(bf16[512,1152]{1,0:T(8,128)(2,1)} %convolution_convert_fusion), channel_id=1, source_target_pairs={{0,8},{8,0},{1,9},{9,1},{2,10},{10,2},{3,11},{11,3},{4,12},{12,4},... | collective-permute-start | bytes 3538952 | tf_op jit(solution)/shard_map/ppermute | solution.py:27
  60.2 3.7 %copy-start.4 = (bf16[512,1152]{1,0:T(8,128)(2,1)S(1)}, bf16[512,1152]{1,0:T(8,128)(2,1)}, u32[]{:S(2)}) copy-start(bf16[512,1152]{1,0:T(8,128)(2,1)} %copy-done.3) | copy-start | bytes 3538948
  60.2 34.1 %all-to-all-start.1 = ((bf16[4,128,1152]{2,1,0:T(8,128)(2,1)}), bf16[4,128,1152]{2,1,0:T(8,128)(2,1)S(1)}, u32[]{:S(2)}, u32[]{:S(2)}) async-start(bf16[4,128,1152]{2,1,0:T(8,128)(2,1)} %bitcast.30), calls=%async_computation.1 | async-start | bytes 2359296 | tf_op jit(solution)/shard_map/all_to_all | solution.py:36
  66.3 12.1 %copy-start.6 = (bf16[32,1152]{1,0:T(8,128)(2,1)S(1)}, bf16[32,1152]{1,0:T(8,128)(2,1)}, u32[]{:S(2)}) copy-start(bf16[32,1152]{1,0:T(8,128)(2,1)} %text_ref.1) | copy-start | bytes 221188
  66.4 13.2 %collective-permute-start.6 = (bf16[128,1152]{1,0:T(8,128)(2,1)S(1)}, bf16[128,1152]{1,0:T(8,128)(2,1)S(1)}, u32[]{:S(2)}, u32[]{:S(2)}) collective-permute-start(bf16[128,1152]{1,0:T(8,128)(2,1)S(1)} %bitcast.103), channel_id=1, source_target_pairs={{0,4},{2,6},{4,0},{6,2},{1,5},{3,7},{5,1},{7,3},{8,12},{10,14},{12... | collective-permute-start | bytes 884744 | tf_op jit(solution)/shard_map/ppermute | solution.py:32
  71.3 14.2 %collective-permute-start.7 = (bf16[128,1152]{1,0:T(8,128)(2,1)S(1)}, bf16[128,1152]{1,0:T(8,128)(2,1)S(1)}, u32[]{:S(2)}, u32[]{:S(2)}) collective-permute-start(bf16[128,1152]{1,0:T(8,128)(2,1)S(1)} %bitcast.102), channel_id=1, source_target_pairs={{0,2},{2,4},{4,6},{6,0},{1,3},{3,5},{5,7},{7,1},{8,10},{10,12},{12... | collective-permute-start | bytes 884744 | tf_op jit(solution)/shard_map/ppermute | solution.py:32
  73.8 11.8 %collective-permute-start.8 = (bf16[128,1152]{1,0:T(8,128)(2,1)S(1)}, bf16[128,1152]{1,0:T(8,128)(2,1)S(1)}, u32[]{:S(2)}, u32[]{:S(2)}) collective-permute-start(bf16[128,1152]{1,0:T(8,128)(2,1)S(1)} %bitcast.101), channel_id=1, source_target_pairs={{0,6},{2,0},{4,2},{6,4},{1,7},{3,1},{5,3},{7,5},{8,14},{10,8},{12,... | collective-permute-start | bytes 884744 | tf_op jit(solution)/shard_map/ppermute | solution.py:32
  85.8 22.1 %collective-permute-start.10 = (bf16[64,1152]{1,0:T(8,128)(2,1)S(1)}, bf16[64,1152]{1,0:T(8,128)(2,1)S(1)}, u32[]{:S(2)}, u32[]{:S(2)}) collective-permute-start(bf16[64,1152]{1,0:T(8,128)(2,1)S(1)} %get-tuple-element.21), channel_id=1, source_target_pairs={{0,64},{64,0},{1,65},{65,1},{2,66},{66,2},{3,67},{67,3},{4,68},{68... | collective-permute-start | bytes 442376 | tf_op jit(solution)/shard_map/ppermute | solution.py:27
  91.5 16.4 %collective-permute-start.9 = (bf16[64,1152]{1,0:T(8,128)(2,1)S(1)}, bf16[64,1152]{1,0:T(8,128)(2,1)S(1)}, u32[]{:S(2)}, u32[]{:S(2)}) collective-permute-start(bf16[64,1152]{1,0:T(8,128)(2,1)S(1)} %get-tuple-element.37), channel_id=1, source_target_pairs={{0,1},{1,0},{2,3},{3,2},{4,5},{5,4},{6,7},{7,6},{8,9},{9,8},{10,11... | collective-permute-start | bytes 442376 | tf_op jit(solution)/shard_map/ppermute | solution.py:27
  94.3 13.6 %collective-permute-start.11 = (bf16[64,1152]{1,0:T(8,128)(2,1)S(1)}, bf16[64,1152]{1,0:T(8,128)(2,1)S(1)}, u32[]{:S(2)}, u32[]{:S(2)}) collective-permute-start(bf16[64,1152]{1,0:T(8,128)(2,1)S(1)} %get-tuple-element.21), channel_id=1, source_target_pairs={{0,65},{1,64},{64,1},{65,0},{2,67},{3,66},{66,3},{67,2},{4,69},{5,... | collective-permute-start | bytes 442376 | tf_op jit(solution)/shard_map/ppermute | solution.py:27
  101.6 16.8 %all-to-all-start.2 = ((bf16[4,32,1152]{2,1,0:T(8,128)(2,1)}), bf16[4,32,1152]{2,1,0:T(8,128)(2,1)S(1)}, u32[]{:S(2)}, u32[]{:S(2)}) async-start(bf16[4,32,1152]{2,1,0:T(8,128)(2,1)} %bitcast.34), calls=%async_computation.2 | async-start | bytes 589824 | tf_op jit(solution)/shard_map/all_to_all | solution.py:36
  108.2 11.1 %collective-permute-start.12 = (bf16[64,1152]{1,0:T(8,128)(2,1)S(1)}, bf16[64,1152]{1,0:T(8,128)(2,1)S(1)}, u32[]{:S(2)}, u32[]{:S(2)}) collective-permute-start(bf16[64,1152]{1,0:T(8,128)(2,1)S(1)} %divide_convert_fusion), channel_id=1, source_target_pairs={{0,6},{2,0},{4,2},{6,4},{1,7},{3,1},{5,3},{7,5},{8,14},{10,8},{12,... | collective-permute-start | bytes 442376 | tf_op jit(solution)/shard_map/ppermute | solution.py:32
  112.9 10.0 %collective-permute-start.13 = (bf16[64,1152]{1,0:T(8,128)(2,1)S(1)}, bf16[64,1152]{1,0:T(8,128)(2,1)S(1)}, u32[]{:S(2)}, u32[]{:S(2)}) collective-permute-start(bf16[64,1152]{1,0:T(8,128)(2,1)S(1)} %divide_convert_fusion), channel_id=1, source_target_pairs={{0,4},{2,6},{4,0},{6,2},{1,5},{3,7},{5,1},{7,3},{8,12},{10,14},{12... | collective-permute-start | bytes 442376 | tf_op jit(solution)/shard_map/ppermute | solution.py:32
  115.6 9.0 %collective-permute-start.14 = (bf16[64,1152]{1,0:T(8,128)(2,1)S(1)}, bf16[64,1152]{1,0:T(8,128)(2,1)S(1)}, u32[]{:S(2)}, u32[]{:S(2)}) collective-permute-start(bf16[64,1152]{1,0:T(8,128)(2,1)S(1)} %divide_convert_fusion), channel_id=1, source_target_pairs={{0,2},{2,4},{4,6},{6,0},{1,3},{3,5},{5,7},{7,1},{8,10},{10,12},{12... | collective-permute-start | bytes 442376 | tf_op jit(solution)/shard_map/ppermute | solution.py:32

commit v21 on v20

--- a/solution.py
+++ b/solution.py
@@ -7,10 +7,10 @@
 
 epsilon = 1e-06
 AXES = ("yh", "yl", "w", "c", "x", "l")
-CLASSES = ((0, 6, 3, 5), (1, 7, 2, 4))
-PLACES = (0, 2, 3, 1)
+CLASSES = ((0, 5, 6, 3), (1, 4, 7, 2))
+PLACES = (0, 3, 1, 2)
 RINGS = ("yh", "yl", "w", "l")
-ORDER = ((0, 0), (0, 2), (0, 3), (0, 1), (2, 3), (2, 1), (2, 0), (2, 2), (3, 0), (3, 2), (3, 3), (3, 1), (1, 3), (1, 1), (1, 0), (1, 2))
+ORDER = ((0, 0), (0, 3), (0, 1), (0, 2), (3, 1), (3, 2), (3, 0), (3, 3), (1, 0), (1, 3), (1, 1), (1, 2), (2, 1), (2, 2), (2, 0), (2, 3))
 TEXT_GROUPS = [[of_y[i] * 8 + of_z[j] for i, j in ORDER] for of_y in CLASSES for of_z in CLASSES]
 NARROW = ("x", "l")
 BF16, F32 = jnp.bfloat16, jnp.float32

time: 127 us -> 127 us (level)
  the two profiles are of different devices: /device:TPU:56 before, /device:TPU:1 now
where the time goes in v21:
time: 127 us; the launch traced here: 126 us
  starting transfers between devices  70 us (55%)
  waiting for transfers between devices  33.3 us (26%)
  matrix products  9.04 us (7%)
  other arithmetic  5.98 us (5%)
  between operations  3.74 us (3%)
  Pallas kernels  2.19 us (2%)
  local copies, waits for them, and re-layouts  2.1 us (2%)
    ppermute x9, starting transfers between devices, shift(): lax.ppermute(block, axis, [(i, (i + distance) % count) for i in range(cou...  30 us
    all_to_all x3, starting transfers between devices, exchange(): lax.all_to_all(blocks, axes, 0, 0, axis_index_groups=groups, tiled=True)  22.8 us
    ppermute x9, waiting for transfers between devices, shift(): lax.ppermute(block, axis, [(i, (i + distance) % count) for i in range(cou...  19.3 us
    ppermute x6, starting transfers between devices, swap(): return lax.ppermute(block, axes, [(i, count - 1 - i) for i in range(count)])  17.2 us
    all_to_all x3, waiting for transfers between devices, exchange(): lax.all_to_all(blocks, axes, 0, 0, axis_index_groups=groups, tiled=True)  12.8 us
    dot_general x1, matrix products, local(): lax.dot_general(grad, images, (((0,), (0,)), ((), ())), preferred_element...  2.58 us
  transfers between devices with their start and end apart: 18, of which 10 were waited for; matrix products, arithmetic and copies ran while one was open for 7% of the time, Pallas kernels for 0%

profile of v21, /device:TPU:1, one launch (start us, length us, event | category | flops | bytes accessed | tf_op | source)
XLA Modules:
  0.0 126.3 jit_solution(9149733581480719817)
XLA Ops:
  0.6 2.2 %first_copies.1 = (bf16[64,1152]{1,0:T(8,128)(2,1)}, bf16[16,32,1152]{2,1,0:T(8,128)(2,1)}) custom-call(s32[1]{0:T(128)} %bitcast.1.x_ref, bf16[256,1152]{1,0:T(8,128)(2,1)} %image_ref.1, bf16[32,1152]{1,0:T(8,128)(2,1)} %text_ref.1), custom_call_target="tpu_custom_call" | custom-call | tf_op jit(solution)/shard_map/first_copies/pallas_call | solution.py:55
  2.8 4.0 %collective-permute-start = (bf16[64,1152]{1,0:T(8,128)(2,1)}, bf16[64,1152]{1,0:T(8,128)(2,1)S(1)}, u32[]{:S(2)}, u32[]{:S(2)}) collective-permute-start(bf16[64,1152]{1,0:T(8,128)(2,1)} %get-tuple-element.17), channel_id=1, source_target_pairs={{0,64},{64,0},{1,65},{65,1},{2,66},{66,2},{3,67},{67,3},{4,68},{68... | collective-permute-start | bytes 442376 | tf_op jit(solution)/shard_map/ppermute | solution.py:27
  6.9 14.4 %all-to-all-start = ((bf16[16,32,1152]{2,1,0:T(8,128)(2,1)}), bf16[16,32,1152]{2,1,0:T(8,128)(2,1)S(1)}, u32[]{:S(2)}, u32[]{:S(2)}) async-start(bf16[16,32,1152]{2,1,0:T(8,128)(2,1)} %get-tuple-element.18), calls=%async_computation | async-start | bytes 2359296 | tf_op jit(solution)/shard_map/all_to_all | solution.py:36
  21.3 4.5 %collective-permute-start.1 = (bf16[64,1152]{1,0:T(8,128)(2,1)S(1)}, bf16[64,1152]{1,0:T(8,128)(2,1)S(1)}, u32[]{:S(2)}, u32[]{:S(2)}) collective-permute-start(bf16[64,1152]{1,0:T(8,128)(2,1)S(1)} %collective-permute-done), channel_id=1, source_target_pairs={{0,6},{2,0},{4,2},{6,4},{1,7},{3,1},{5,3},{7,5},{8,14},{10,8},{12,... | collective-permute-start | bytes 442376 | tf_op jit(solution)/shard_map/ppermute | solution.py:32
  25.8 2.4 %collective-permute-start.2 = (bf16[64,1152]{1,0:T(8,128)(2,1)S(1)}, bf16[64,1152]{1,0:T(8,128)(2,1)S(1)}, u32[]{:S(2)}, u32[]{:S(2)}) collective-permute-start(bf16[64,1152]{1,0:T(8,128)(2,1)S(1)} %collective-permute-done), channel_id=1, source_target_pairs={{0,4},{2,6},{4,0},{6,2},{1,5},{3,7},{5,1},{7,3},{8,12},{10,14},{12... | collective-permute-start | bytes 442376 | tf_op jit(solution)/shard_map/ppermute | solution.py:32
  28.3 2.5 %collective-permute-start.3 = (bf16[64,1152]{1,0:T(8,128)(2,1)S(1)}, bf16[64,1152]{1,0:T(8,128)(2,1)S(1)}, u32[]{:S(2)}, u32[]{:S(2)}) collective-permute-start(bf16[64,1152]{1,0:T(8,128)(2,1)S(1)} %collective-permute-done), channel_id=1, source_target_pairs={{0,2},{2,4},{4,6},{6,0},{1,3},{3,5},{5,7},{7,1},{8,10},{10,12},{12... | collective-permute-start | bytes 442376 | tf_op jit(solution)/shard_map/ppermute | solution.py:32
  30.8 2.7 %collective-permute-done.2 = bf16[64,1152]{1,0:T(8,128)(2,1)S(1)} collective-permute-done((bf16[64,1152]{1,0:T(8,128)(2,1)S(1)}, bf16[64,1152]{1,0:T(8,128)(2,1)S(1)}, u32[]{:S(2)}, u32[]{:S(2)}) %collective-permute-start.2) | collective-permute-done | bytes 147488 | tf_op jit(solution)/shard_map/ppermute | solution.py:32
  33.5 4.0 %collective-permute-done.3 = bf16[64,1152]{1,0:T(8,128)(2,1)S(1)} collective-permute-done((bf16[64,1152]{1,0:T(8,128)(2,1)S(1)}, bf16[64,1152]{1,0:T(8,128)(2,1)S(1)}, u32[]{:S(2)}, u32[]{:S(2)}) %collective-permute-start.3) | collective-permute-done | bytes 147488 | tf_op jit(solution)/shard_map/ppermute | solution.py:32
  37.7 0.2 broadcast_select_fusion.1
  37.9 0.3 fusion
  38.2 0.4 fusion.1
  38.6 3.5 %collective-permute-start.4 = (bf16[512,1152]{1,0:T(8,128)(2,1)S(1)}, bf16[512,1152]{1,0:T(8,128)(2,1)}, u32[]{:S(2)}, u32[]{:S(2)}) collective-permute-start(bf16[512,1152]{1,0:T(8,128)(2,1)S(1)} %fusion.1), channel_id=1, source_target_pairs={{0,8},{8,0},{1,9},{9,1},{2,10},{10,2},{3,11},{11,3},{4,12},{12,4},... | collective-permute-start | bytes 3538952 | tf_op jit(solution)/shard_map/ppermute | solution.py:27
  42.2 0.6 fusion.33
  45.4 1.8 %pad_maximum_fusion = bf16[1024,1152]{1,0:T(8,128)(2,1)S(1)} fusion(bf16[512,1152]{1,0:T(8,128)(2,1)} %collective-permute-done.4, bf16[512,1152]{1,0:T(8,128)(2,1)} %copy-done), kind=kLoop, calls=%fused_computation.10 | loop fusion | flops 4718592 | bytes 4718592 | tf_op jit(solution)/shard_map/concatenate | solution.py:107
  47.2 7.0 %all-to-all-done = bf16[16,32,1152]{2,1,0:T(8,128)(2,1)S(1)} async-done(((bf16[16,32,1152]{2,1,0:T(8,128)(2,1)}), bf16[16,32,1152]{2,1,0:T(8,128)(2,1)S(1)}, u32[]{:S(2)}, u32[]{:S(2)}) %all-to-all-start) | async-done | bytes 1179680 | tf_op jit(solution)/shard_map/all_to_all | solution.py:36
  54.5 0.3 fusion.2
  54.8 2.1 %subtract_convert_fusion = bf16[1024,512]{1,0:T(8,128)(2,1)S(1)} fusion(bf16[1024,1152]{1,0:T(8,128)(2,1)S(1)} %pad_maximum_fusion, s32[512]{0:T(512)S(1)} %add_dynamic-update-slice_fusion, f32[]{:T(128)} %bitcast.98, f32[]{:T(128)} %bitcast, bf16[512,1152]{1,0:T(8,128)(2,1)S(1)} %fusion.12, f32[512]{0:T(512)S(1)} %add_sqrt_fusion), kind=kOutput, calls=%fused_computation.12 | convolution fusion | flops 1214447616 | bytes 4591624 | tf_op jit(solution)/shard_map/dot_general | solution.py:108
  56.9 2.6 %convolution_convert_fusion.1 = bf16[512,1152]{1,0:T(8,128)(2,1)} fusion(bf16[1024,512]{1,0:T(8,128)(2,1)S(1)} %subtract_convert_fusion, bf16[1024,1152]{1,0:T(8,128)(2,1)S(1)} %pad_maximum_fusion), kind=kOutput, calls=%fused_computation.1 | convolution fusion | flops 1208549376 | bytes 4587520 | tf_op jit(solution)/shard_map/dot_general | solution.py:110
  59.5 2.0 %convolution_convert_fusion = bf16[512,1152]{1,0:T(8,128)(2,1)} fusion(bf16[1024,512]{1,0:T(8,128)(2,1)S(1)} %subtract_convert_fusion, bf16[512,1152]{1,0:T(8,128)(2,1)S(1)} %fusion.12, f32[512]{0:T(512)S(1)} %add_sqrt_fusion), kind=kOutput, calls=%fused_computation | convolution fusion | flops 606339072 | bytes 2885632 | tf_op jit(solution)/shard_map/dot_general | solution.py:115
  61.5 4.0 %collective-permute-start.5 = (bf16[512,1152]{1,0:T(8,128)(2,1)}, bf16[512,1152]{1,0:T(8,128)(2,1)}, u32[]{:S(2)}, u32[]{:S(2)}) collective-permute-start(bf16[512,1152]{1,0:T(8,128)(2,1)} %convolution_convert_fusion), channel_id=1, source_target_pairs={{0,8},{8,0},{1,9},{9,1},{2,10},{10,2},{3,11},{11,3},{4,12},{12,4},... | collective-permute-start | bytes 3538952 | tf_op jit(solution)/shard_map/ppermute | solution.py:27
  65.5 0.1 fusion.10
  65.8 4.9 %all-to-all-start.1 = ((bf16[4,128,1152]{2,1,0:T(8,128)(2,1)}), bf16[4,128,1152]{2,1,0:T(8,128)(2,1)S(1)}, u32[]{:S(2)}, u32[]{:S(2)}) async-start(bf16[4,128,1152]{2,1,0:T(8,128)(2,1)} %bitcast.30), calls=%async_computation.1 | async-start | bytes 2359296 | tf_op jit(solution)/shard_map/all_to_all | solution.py:36
  70.7 2.4 %add_convert_fusion = bf16[512,1152]{1,0:T(8,128)(2,1)S(1)} fusion(bf16[512,1152]{1,0:T(8,128)(2,1)} %collective-permute-done.5, bf16[1024,512]{1,0:T(8,128)(2,1)} %copy-done.5, bf16[512,1152]{1,0:T(8,128)(2,1)S(1)} %copy-done.4, f32[512]{0:T(512)S(1)} %add_sqrt_fusion), kind=kOutput, calls=%fused_computation.11 | convolution fusion | flops 607518720 | bytes 4065280 | tf_op jit(solution)/shard_map/dot_general | solution.py:117
  73.2 4.6 %collective-permute-start.6 = (bf16[128,1152]{1,0:T(8,128)(2,1)S(1)}, bf16[128,1152]{1,0:T(8,128)(2,1)S(1)}, u32[]{:S(2)}, u32[]{:S(2)}) collective-permute-start(bf16[128,1152]{1,0:T(8,128)(2,1)S(1)} %bitcast.103), channel_id=1, source_target_pairs={{0,4},{2,6},{4,0},{6,2},{1,5},{3,7},{5,1},{7,3},{8,12},{10,14},{12... | collective-permute-start | bytes 884744 | tf_op jit(solution)/shard_map/ppermute | solution.py:32
  77.9 2.2 %collective-permute-start.7 = (bf16[128,1152]{1,0:T(8,128)(2,1)S(1)}, bf16[128,1152]{1,0:T(8,128)(2,1)S(1)}, u32[]{:S(2)}, u32[]{:S(2)}) collective-permute-start(bf16[128,1152]{1,0:T(8,128)(2,1)S(1)} %bitcast.102), channel_id=1, source_target_pairs={{0,2},{2,4},{4,6},{6,0},{1,3},{3,5},{5,7},{7,1},{8,10},{10,12},{12... | collective-permute-start | bytes 884744 | tf_op jit(solution)/shard_map/ppermute | solution.py:32
  80.1 4.3 %collective-permute-start.8 = (bf16[128,1152]{1,0:T(8,128)(2,1)S(1)}, bf16[128,1152]{1,0:T(8,128)(2,1)S(1)}, u32[]{:S(2)}, u32[]{:S(2)}) collective-permute-start(bf16[128,1152]{1,0:T(8,128)(2,1)S(1)} %bitcast.101), channel_id=1, source_target_pairs={{0,6},{2,0},{4,2},{6,4},{1,7},{3,1},{5,3},{7,5},{8,14},{10,8},{12,... | collective-permute-start | bytes 884744 | tf_op jit(solution)/shard_map/ppermute | solution.py:32
  84.4 0.1 fusion.11
  84.5 0.4 collective-permute-done.6
  84.9 6.9 %collective-permute-done.7 = bf16[128,1152]{1,0:T(8,128)(2,1)S(1)} collective-permute-done((bf16[128,1152]{1,0:T(8,128)(2,1)S(1)}, bf16[128,1152]{1,0:T(8,128)(2,1)S(1)}, u32[]{:S(2)}, u32[]{:S(2)}) %collective-permute-start.7) | collective-permute-done | bytes 294944 | tf_op jit(solution)/shard_map/ppermute | solution.py:32
  91.9 0.2 fusion.4
  92.1 1.9 %collective-permute-start.10 = (bf16[64,1152]{1,0:T(8,128)(2,1)S(1)}, bf16[64,1152]{1,0:T(8,128)(2,1)S(1)}, u32[]{:S(2)}, u32[]{:S(2)}) collective-permute-start(bf16[64,1152]{1,0:T(8,128)(2,1)S(1)} %get-tuple-element.21), channel_id=1, source_target_pairs={{0,64},{64,0},{1,65},{65,1},{2,66},{66,2},{3,67},{67,3},{4,68},{68... | collective-permute-start | bytes 442376 | tf_op jit(solution)/shard_map/ppermute | solution.py:27
  94.0 1.9 %collective-permute-start.9 = (bf16[64,1152]{1,0:T(8,128)(2,1)S(1)}, bf16[64,1152]{1,0:T(8,128)(2,1)S(1)}, u32[]{:S(2)}, u32[]{:S(2)}) collective-permute-start(bf16[64,1152]{1,0:T(8,128)(2,1)S(1)} %get-tuple-element.37), channel_id=1, source_target_pairs={{0,1},{1,0},{2,3},{3,2},{4,5},{5,4},{6,7},{7,6},{8,9},{9,8},{10,11... | collective-permute-start | bytes 442376 | tf_op jit(solution)/shard_map/ppermute | solution.py:27
  95.9 5.2 %all-to-all-done.1 = bf16[4,128,1152]{2,1,0:T(8,128)(2,1)S(1)} async-done(((bf16[4,128,1152]{2,1,0:T(8,128)(2,1)}), bf16[4,128,1152]{2,1,0:T(8,128)(2,1)S(1)}, u32[]{:S(2)}, u32[]{:S(2)}) %all-to-all-start.1) | async-done | bytes 1179680 | tf_op jit(solution)/shard_map/all_to_all | solution.py:36
  101.2 1.9 %collective-permute-start.11 = (bf16[64,1152]{1,0:T(8,128)(2,1)S(1)}, bf16[64,1152]{1,0:T(8,128)(2,1)S(1)}, u32[]{:S(2)}, u32[]{:S(2)}) collective-permute-start(bf16[64,1152]{1,0:T(8,128)(2,1)S(1)} %get-tuple-element.21), channel_id=1, source_target_pairs={{0,65},{1,64},{64,1},{65,0},{2,67},{3,66},{66,3},{67,2},{4,69},{5,... | collective-permute-start | bytes 442376 | tf_op jit(solution)/shard_map/ppermute | solution.py:27
  103.2 1.0 reduce_sum.84
  104.1 3.5 %all-to-all-start.2 = ((bf16[4,32,1152]{2,1,0:T(8,128)(2,1)}), bf16[4,32,1152]{2,1,0:T(8,128)(2,1)S(1)}, u32[]{:S(2)}, u32[]{:S(2)}) async-start(bf16[4,32,1152]{2,1,0:T(8,128)(2,1)} %bitcast.34), calls=%async_computation.2 | async-start | bytes 589824 | tf_op jit(solution)/shard_map/all_to_all | solution.py:36
  107.6 1.2 collective-permute-done.11
  108.8 0.2 multiply_reduce_fusion
  109.0 0.1 divide_convert_fusion
  109.1 4.4 %collective-permute-start.12 = (bf16[64,1152]{1,0:T(8,128)(2,1)S(1)}, bf16[64,1152]{1,0:T(8,128)(2,1)S(1)}, u32[]{:S(2)}, u32[]{:S(2)}) collective-permute-start(bf16[64,1152]{1,0:T(8,128)(2,1)S(1)} %divide_convert_fusion), channel_id=1, source_target_pairs={{0,6},{2,0},{4,2},{6,4},{1,7},{3,1},{5,3},{7,5},{8,14},{10,8},{12,... | collective-permute-start | bytes 442376 | tf_op jit(solution)/shard_map/ppermute | solution.py:32
  113.5 2.5 %collective-permute-start.13 = (bf16[64,1152]{1,0:T(8,128)(2,1)S(1)}, bf16[64,1152]{1,0:T(8,128)(2,1)S(1)}, u32[]{:S(2)}, u32[]{:S(2)}) collective-permute-start(bf16[64,1152]{1,0:T(8,128)(2,1)S(1)} %divide_convert_fusion), channel_id=1, source_target_pairs={{0,4},{2,6},{4,0},{6,2},{1,5},{3,7},{5,1},{7,3},{8,12},{10,14},{12... | collective-permute-start | bytes 442376 | tf_op jit(solution)/shard_map/ppermute | solution.py:32
  116.0 2.5 %collective-permute-start.14 = (bf16[64,1152]{1,0:T(8,128)(2,1)S(1)}, bf16[64,1152]{1,0:T(8,128)(2,1)S(1)}, u32[]{:S(2)}, u32[]{:S(2)}) collective-permute-start(bf16[64,1152]{1,0:T(8,128)(2,1)S(1)} %divide_convert_fusion), channel_id=1, source_target_pairs={{0,2},{2,4},{4,6},{6,0},{1,3},{3,5},{5,7},{7,1},{8,10},{10,12},{12... | collective-permute-start | bytes 442376 | tf_op jit(solution)/shard_map/ppermute | solution.py:32
  118.5 0.6 all-to-all-done.2
  119.1 0.1 multiply_reduce_fusion.1
  119.3 0.7 divide_convert_fusion.1
  120.0 0.9 collective-permute-done.13
  120.9 4.4 %collective-permute-done.14 = bf16[64,1152]{1,0:T(8,128)(2,1)S(1)} collective-permute-done((bf16[64,1152]{1,0:T(8,128)(2,1)S(1)}, bf16[64,1152]{1,0:T(8,128)(2,1)S(1)}, u32[]{:S(2)}, u32[]{:S(2)}) %collective-permute-start.14) | collective-permute-done | bytes 147488 | tf_op jit(solution)/shard_map/ppermute | solution.py:32
  125.5 0.9 constant_dynamic-slice_fusion
  (69 shorter events, 1.1 us)
Async XLA Ops:
  2.8 18.5 %collective-permute-start = (bf16[64,1152]{1,0:T(8,128)(2,1)}, bf16[64,1152]{1,0:T(8,128)(2,1)S(1)}, u32[]{:S(2)}, u32[]{:S(2)}) collective-permute-start(bf16[64,1152]{1,0:T(8,128)(2,1)} %get-tuple-element.17), channel_id=1, source_target_pairs={{0,64},{64,0},{1,65},{65,1},{2,66},{66,2},{3,67},{67,3},{4,68},{68... | collective-permute-start | bytes 442376 | tf_op jit(solution)/shard_map/ppermute | solution.py:27
  6.9 47.4 %all-to-all-start = ((bf16[16,32,1152]{2,1,0:T(8,128)(2,1)}), bf16[16,32,1152]{2,1,0:T(8,128)(2,1)S(1)}, u32[]{:S(2)}, u32[]{:S(2)}) async-start(bf16[16,32,1152]{2,1,0:T(8,128)(2,1)} %get-tuple-element.18), calls=%async_computation | async-start | bytes 2359296 | tf_op jit(solution)/shard_map/all_to_all | solution.py:36
  21.3 16.4 %copy-start.1 = (bf16[256,1152]{1,0:T(8,128)(2,1)S(1)}, bf16[256,1152]{1,0:T(8,128)(2,1)}, u32[]{:S(2)}) copy-start(bf16[256,1152]{1,0:T(8,128)(2,1)} %image_ref.1) | copy-start | bytes 1769476
  21.3 9.5 %collective-permute-start.1 = (bf16[64,1152]{1,0:T(8,128)(2,1)S(1)}, bf16[64,1152]{1,0:T(8,128)(2,1)S(1)}, u32[]{:S(2)}, u32[]{:S(2)}) collective-permute-start(bf16[64,1152]{1,0:T(8,128)(2,1)S(1)} %collective-permute-done), channel_id=1, source_target_pairs={{0,6},{2,0},{4,2},{6,4},{1,7},{3,1},{5,3},{7,5},{8,14},{10,8},{12,... | collective-permute-start | bytes 442376 | tf_op jit(solution)/shard_map/ppermute | solution.py:32
  25.8 7.7 %collective-permute-start.2 = (bf16[64,1152]{1,0:T(8,128)(2,1)S(1)}, bf16[64,1152]{1,0:T(8,128)(2,1)S(1)}, u32[]{:S(2)}, u32[]{:S(2)}) collective-permute-start(bf16[64,1152]{1,0:T(8,128)(2,1)S(1)} %collective-permute-done), channel_id=1, source_target_pairs={{0,4},{2,6},{4,0},{6,2},{1,5},{3,7},{5,1},{7,3},{8,12},{10,14},{12... | collective-permute-start | bytes 442376 | tf_op jit(solution)/shard_map/ppermute | solution.py:32
  28.3 9.3 %collective-permute-start.3 = (bf16[64,1152]{1,0:T(8,128)(2,1)S(1)}, bf16[64,1152]{1,0:T(8,128)(2,1)S(1)}, u32[]{:S(2)}, u32[]{:S(2)}) collective-permute-start(bf16[64,1152]{1,0:T(8,128)(2,1)S(1)} %collective-permute-done), channel_id=1, source_target_pairs={{0,2},{2,4},{4,6},{6,0},{1,3},{3,5},{5,7},{7,1},{8,10},{10,12},{12... | collective-permute-start | bytes 442376 | tf_op jit(solution)/shard_map/ppermute | solution.py:32
  38.2 3.9 %copy-start.7 = (s32[4]{0:T(128)S(1)}, s32[4]{0:T(128)}, u32[]{:S(2)}) copy-start(s32[4]{0:T(128)} %constant.82.clone) | copy-start | bytes 52
  38.2 7.1 %copy-start.8 = (s32[32]{0:T(128)S(1)}, s32[32]{0:T(128)}, u32[]{:S(2)}) copy-start(s32[32]{0:T(128)} %param.8) | copy-start | bytes 388
  38.6 6.8 %copy-start = (bf16[512,1152]{1,0:T(8,128)(2,1)}, bf16[512,1152]{1,0:T(8,128)(2,1)S(1)}, u32[]{:S(2)}) copy-start(bf16[512,1152]{1,0:T(8,128)(2,1)S(1)} %fusion.1) | copy-start | bytes 3538948
  38.6 6.8 %collective-permute-start.4 = (bf16[512,1152]{1,0:T(8,128)(2,1)S(1)}, bf16[512,1152]{1,0:T(8,128)(2,1)}, u32[]{:S(2)}, u32[]{:S(2)}) collective-permute-start(bf16[512,1152]{1,0:T(8,128)(2,1)S(1)} %fusion.1), channel_id=1, source_target_pairs={{0,8},{8,0},{1,9},{9,1},{2,10},{10,2},{3,11},{11,3},{4,12},{12,4},... | collective-permute-start | bytes 3538952 | tf_op jit(solution)/shard_map/ppermute | solution.py:27
  54.5 5.0 %copy-start.3 = (bf16[512,1152]{1,0:T(8,128)(2,1)}, bf16[512,1152]{1,0:T(8,128)(2,1)S(1)}, u32[]{:S(2)}) copy-start(bf16[512,1152]{1,0:T(8,128)(2,1)S(1)} %fusion.12) | copy-start | bytes 3538948
  56.9 2.6 %copy-start.5 = (bf16[1024,512]{1,0:T(8,128)(2,1)}, bf16[1024,512]{1,0:T(8,128)(2,1)S(1)}, u32[]{:S(2)}) copy-start(bf16[1024,512]{1,0:T(8,128)(2,1)S(1)} %subtract_convert_fusion) | copy-start | bytes 3145732
  59.5 6.0 %copy-start.2 = (bf16[256,1152]{1,0:T(8,128)(2,1)S(1)}, bf16[256,1152]{1,0:T(8,128)(2,1)}, u32[]{:S(2)}) copy-start(bf16[256,1152]{1,0:T(8,128)(2,1)} %image_ref.1) | copy-start | bytes 1769476
  61.5 9.2 %collective-permute-start.5 = (bf16[512,1152]{1,0:T(8,128)(2,1)}, bf16[512,1152]{1,0:T(8,128)(2,1)}, u32[]{:S(2)}, u32[]{:S(2)}) collective-permute-start(bf16[512,1152]{1,0:T(8,128)(2,1)} %convolution_convert_fusion), channel_id=1, source_target_pairs={{0,8},{8,0},{1,9},{9,1},{2,10},{10,2},{3,11},{11,3},{4,12},{12,4},... | collective-permute-start | bytes 3538952 | tf_op jit(solution)/shard_map/ppermute | solution.py:27
  65.8 5.0 %copy-start.4 = (bf16[512,1152]{1,0:T(8,128)(2,1)S(1)}, bf16[512,1152]{1,0:T(8,128)(2,1)}, u32[]{:S(2)}) copy-start(bf16[512,1152]{1,0:T(8,128)(2,1)} %copy-done.3) | copy-start | bytes 3538948
  65.8 35.4 %all-to-all-start.1 = ((bf16[4,128,1152]{2,1,0:T(8,128)(2,1)}), bf16[4,128,1152]{2,1,0:T(8,128)(2,1)S(1)}, u32[]{:S(2)}, u32[]{:S(2)}) async-start(bf16[4,128,1152]{2,1,0:T(8,128)(2,1)} %bitcast.30), calls=%async_computation.1 | async-start | bytes 2359296 | tf_op jit(solution)/shard_map/all_to_all | solution.py:36
  73.1 11.3 %copy-start.6 = (bf16[32,1152]{1,0:T(8,128)(2,1)S(1)}, bf16[32,1152]{1,0:T(8,128)(2,1)}, u32[]{:S(2)}) copy-start(bf16[32,1152]{1,0:T(8,128)(2,1)} %text_ref.1) | copy-start | bytes 221188
  73.2 11.7 %collective-permute-start.6 = (bf16[128,1152]{1,0:T(8,128)(2,1)S(1)}, bf16[128,1152]{1,0:T(8,128)(2,1)S(1)}, u32[]{:S(2)}, u32[]{:S(2)}) collective-permute-start(bf16[128,1152]{1,0:T(8,128)(2,1)S(1)} %bitcast.103), channel_id=1, source_target_pairs={{0,4},{2,6},{4,0},{6,2},{1,5},{3,7},{5,1},{7,3},{8,12},{10,14},{12... | collective-permute-start | bytes 884744 | tf_op jit(solution)/shard_map/ppermute | solution.py:32
  77.9 14.0 %collective-permute-start.7 = (bf16[128,1152]{1,0:T(8,128)(2,1)S(1)}, bf16[128,1152]{1,0:T(8,128)(2,1)S(1)}, u32[]{:S(2)}, u32[]{:S(2)}) collective-permute-start(bf16[128,1152]{1,0:T(8,128)(2,1)S(1)} %bitcast.102), channel_id=1, source_target_pairs={{0,2},{2,4},{4,6},{6,0},{1,3},{3,5},{5,7},{7,1},{8,10},{10,12},{12... | collective-permute-start | bytes 884744 | tf_op jit(solution)/shard_map/ppermute | solution.py:32
  80.1 11.8 %collective-permute-start.8 = (bf16[128,1152]{1,0:T(8,128)(2,1)S(1)}, bf16[128,1152]{1,0:T(8,128)(2,1)S(1)}, u32[]{:S(2)}, u32[]{:S(2)}) collective-permute-start(bf16[128,1152]{1,0:T(8,128)(2,1)S(1)} %bitcast.101), channel_id=1, source_target_pairs={{0,6},{2,0},{4,2},{6,4},{1,7},{3,1},{5,3},{7,5},{8,14},{10,8},{12,... | collective-permute-start | bytes 884744 | tf_op jit(solution)/shard_map/ppermute | solution.py:32
  92.1 15.5 %collective-permute-start.10 = (bf16[64,1152]{1,0:T(8,128)(2,1)S(1)}, bf16[64,1152]{1,0:T(8,128)(2,1)S(1)}, u32[]{:S(2)}, u32[]{:S(2)}) collective-permute-start(bf16[64,1152]{1,0:T(8,128)(2,1)S(1)} %get-tuple-element.21), channel_id=1, source_target_pairs={{0,64},{64,0},{1,65},{65,1},{2,66},{66,2},{3,67},{67,3},{4,68},{68... | collective-permute-start | bytes 442376 | tf_op jit(solution)/shard_map/ppermute | solution.py:27
  94.0 13.6 %collective-permute-start.9 = (bf16[64,1152]{1,0:T(8,128)(2,1)S(1)}, bf16[64,1152]{1,0:T(8,128)(2,1)S(1)}, u32[]{:S(2)}, u32[]{:S(2)}) collective-permute-start(bf16[64,1152]{1,0:T(8,128)(2,1)S(1)} %get-tuple-element.37), channel_id=1, source_target_pairs={{0,1},{1,0},{2,3},{3,2},{4,5},{5,4},{6,7},{7,6},{8,9},{9,8},{10,11... | collective-permute-start | bytes 442376 | tf_op jit(solution)/shard_map/ppermute | solution.py:27
  101.2 7.6 %collective-permute-start.11 = (bf16[64,1152]{1,0:T(8,128)(2,1)S(1)}, bf16[64,1152]{1,0:T(8,128)(2,1)S(1)}, u32[]{:S(2)}, u32[]{:S(2)}) collective-permute-start(bf16[64,1152]{1,0:T(8,128)(2,1)S(1)} %get-tuple-element.21), channel_id=1, source_target_pairs={{0,65},{1,64},{64,1},{65,0},{2,67},{3,66},{66,3},{67,2},{4,69},{5,... | collective-permute-start | bytes 442376 | tf_op jit(solution)/shard_map/ppermute | solution.py:27
  104.1 15.0 %all-to-all-start.2 = ((bf16[4,32,1152]{2,1,0:T(8,128)(2,1)}), bf16[4,32,1152]{2,1,0:T(8,128)(2,1)S(1)}, u32[]{:S(2)}, u32[]{:S(2)}) async-start(bf16[4,32,1152]{2,1,0:T(8,128)(2,1)} %bitcast.34), calls=%async_computation.2 | async-start | bytes 589824 | tf_op jit(solution)/shard_map/all_to_all | solution.py:36
  109.1 10.8 %collective-permute-start.12 = (bf16[64,1152]{1,0:T(8,128)(2,1)S(1)}, bf16[64,1152]{1,0:T(8,128)(2,1)S(1)}, u32[]{:S(2)}, u32[]{:S(2)}) collective-permute-start(bf16[64,1152]{1,0:T(8,128)(2,1)S(1)} %divide_convert_fusion), channel_id=1, source_target_pairs={{0,6},{2,0},{4,2},{6,4},{1,7},{3,1},{5,3},{7,5},{8,14},{10,8},{12,... | collective-permute-start | bytes 442376 | tf_op jit(solution)/shard_map/ppermute | solution.py:32
  113.5 7.4 %collective-permute-start.13 = (bf16[64,1152]{1,0:T(8,128)(2,1)S(1)}, bf16[64,1152]{1,0:T(8,128)(2,1)S(1)}, u32[]{:S(2)}, u32[]{:S(2)}) collective-permute-start(bf16[64,1152]{1,0:T(8,128)(2,1)S(1)} %divide_convert_fusion), channel_id=1, source_target_pairs={{0,4},{2,6},{4,0},{6,2},{1,5},{3,7},{5,1},{7,3},{8,12},{10,14},{12... | collective-permute-start | bytes 442376 | tf_op jit(solution)/shard_map/ppermute | solution.py:32
  116.0 9.3 %collective-permute-start.14 = (bf16[64,1152]{1,0:T(8,128)(2,1)S(1)}, bf16[64,1152]{1,0:T(8,128)(2,1)S(1)}, u32[]{:S(2)}, u32[]{:S(2)}) collective-permute-start(bf16[64,1152]{1,0:T(8,128)(2,1)S(1)} %divide_convert_fusion), channel_id=1, source_target_pairs={{0,2},{2,4},{4,6},{6,0},{1,3},{3,5},{5,7},{7,1},{8,10},{10,12},{12... | collective-permute-start | bytes 442376 | tf_op jit(solution)/shard_map/ppermute | solution.py:32
